TPU v7x, 32 devices: a whole 2x2x4 slice. The times are simulated.
32 devices in a mesh: shell: 8 (over z, x), aux: 4 (over y, core).
Axes of the slice: x: 2, y: 2, z: 4, core: 2. Of those that a mesh axis runs over, the one named last changes fastest.
Arguments:
- integrals: bfloat16 [32, 128, 4, 128], P('shell', None, 'aux'), may hold values from -6 to 6
- pair_list: int32 [32, 3], P('shell'), may hold values from 0 to 31, as said below
- coef: bfloat16 [4096, 1024], P('shell'), may hold values from -0.5 to 0.5
- metric: bfloat16 [4, 4], replicated, may hold values from -3 to 3, as said below
- occ_slot: int32 [128], replicated, may hold values from 0 to 127, each once
Outputs:
- transformed: bfloat16 [1024, 4, 4096], P(('shell', 'aux'))
Inputs may be any that keep to these rules, and one draw needn't show every extreme that they name: `pair_list`: row d * 4 + k holds slot k of index d of shell: block row, block column, live flag. The block column lies in d * 4 to (d + 1) * 4 - 1. On every index live slots come first and at least one is live; some index has all 4 live. `metric`: lower triangular, positive on the diagonal.
All inputs are finite; a program needn't handle non-finite values.
Results may differ from a plain program's by a relative error of at most 0.0054.
Values may be sent and summed in bfloat16 or wider, within the bound.
No kernel may reach another device: no remote copies, remote signals or barrier semaphores. Data moves between devices by JAX's collectives and lax.ppermute only.
A program may use at most 64 MiB of HBM per device.

v0:
```python
import jax
import jax.numpy as jnp
from jax import lax
from jax.sharding import PartitionSpec as P

BS = 128


def per_device(integrals, pair_list, coef, metric, occ_slot):
    pairs_dev = pair_list.shape[0]
    rows_local = coef.shape[0]
    occ_count = coef.shape[1]
    blocks_dev = rows_local // BS
    shell_count = lax.axis_size("shell")
    block_count = blocks_dev * shell_count
    slot_count = occ_slot.shape[0]
    aux_dev = integrals.shape[2]
    inverse = (
        jnp.zeros((slot_count,), jnp.int32)
        .at[occ_slot]
        .set(jnp.arange(slot_count, dtype=jnp.int32))
    )
    ordered = jnp.take(
        coef.reshape(rows_local, slot_count, occ_count // slot_count), inverse, axis=1
    )
    ordered = ordered.reshape(rows_local, occ_count)

    def one_slot(item):
        int_block, column_index = item
        start = column_index % blocks_dev * BS
        column = lax.dynamic_slice_in_dim(ordered, start, BS, 0)
        product = lax.dot_general(
            column,
            int_block.reshape(BS, aux_dev * BS),
            (((0,), (0,)), ((), ())),
            preferred_element_type=jnp.float32,
        )
        return product.astype(jnp.bfloat16)

    half_blocks = lax.map(one_slot, (integrals, pair_list[:, 1]))
    half_blocks = half_blocks.reshape(pairs_dev, occ_count, aux_dev, BS)
    listing = lax.all_gather(pair_list, "shell", axis=0, tiled=True)
    targets = jnp.arange(block_count, dtype=jnp.int32)[:, None]
    selector = ((listing[:, 0][None, :] == targets) & (listing[:, 2][None, :] == 1)).astype(
        jnp.bfloat16
    )
    relayed = lax.all_to_all(
        lax.all_to_all(half_blocks, "shell", split_axis=1, concat_axis=0, tiled=True),
        "aux",
        split_axis=1,
        concat_axis=2,
        tiled=True,
    )
    summed = jnp.dot(
        selector, relayed.reshape(relayed.shape[0], -1), preferred_element_type=jnp.float32
    )
    blocks = summed.astype(jnp.bfloat16).reshape((block_count,) + relayed.shape[1:])
    result = jnp.einsum("qp,bipm->iqbm", metric, blocks, preferred_element_type=jnp.float32)
    return result.reshape(result.shape[0], result.shape[1], block_count * BS).astype(jnp.bfloat16)


def solution(mesh):
    placed = (P("shell", None, "aux", None), P("shell", None), P("shell", None), P(), P())
    return jax.shard_map(
        per_device,
        mesh=mesh,
        in_specs=placed,
        out_specs=P(("shell", "aux"), None, None),
        check_vma=False,
    )
```

profile of v0, /device:TPU:0, one launch (start us, length us, event | category | flops | bytes accessed | tf_op | source)
XLA Modules:
  0.0 88.2 jit_solution(11395942804125166634)
XLA Ops:
  0.0 0.7 compare_select_fusion.1
  0.7 1.0 %scatter_custom_fusion = s32[128]{0:T(128)S(1)} fusion(s32[128]{0:T(128)S(1)} %compare_select_fusion.1, s32[128]{0:T(128)S(1)} %iota.7, s32[]{:T(128)} %constant.63.clone.1), kind=kCustom, calls=%fused_computation.26 | custom fusion | bytes 516 | tf_op jit(solution)/shard_map/scatter | solution.py:21
  1.7 1.5 %copy.21 = bf16[512,1024]{0,1:T(8,128)(2,1)S(1)} copy(bf16[512,1024]{1,0:T(8,128)(2,1)} %param.9) | data formatting | bytes 2097152 | tf_op args[2]
  3.6 0.6 gather_fusion
  4.5 13.2 %while.12 = (s32[]{:T(128)}, bf16[4,1024,128]{2,1,0:T(8,128)(2,1)S(1)}, s32[4]{0:T(128)S(1)}, bf16[512,1024]{0,1:T(8,128)(2,1)S(1)}, bf16[4,128,1,128]{3,1,2,0:T...) while((s32[]{:T(128)}, ...), condition=%wide.region_2.3_spmd, body=%wide.region_1.2_spmd.sunk | while | flops 33685520 | bytes 558360 | solution.py:40
  4.5 0.6 dynamic_slice.31
  6.8 1.0 %fusion.21 = bf16[4,1024,128]{2,1,0:T(8,128)(2,1)S(1)} fusion(bf16[4,1024,128]{2,1,0:T(8,128)(2,1)S(1)} %get-tuple-element.140, s32[]{:T(128)} %get-tuple-element.139, bf16[512,1024]{0,1:T(8,128)(2,1)S(1)} %get-tuple-element.153, s32[]{:T(128)S(6)} %select_n.42, bf16[4,128,1,128]{3,1,2,0:T(8,128)(2,1)} %get-tuple-element.154), kind=kOutput, calls=%fused_computation.4.clone.1 | convolution fusion | flops 33685504 | bytes 558084 | tf_op jit(solution)/shard_map/while/body/eval_jaxpr/dot_general | solution.py:32
  7.8 0.6 dynamic_slice.31
  10.1 1.0 %fusion.21 = bf16[4,1024,128]{2,1,0:T(8,128)(2,1)S(1)} fusion(bf16[4,1024,128]{2,1,0:T(8,128)(2,1)S(1)} %get-tuple-element.140, s32[]{:T(128)} %get-tuple-element.139, bf16[512,1024]{0,1:T(8,128)(2,1)S(1)} %get-tuple-element.153, s32[]{:T(128)S(6)} %select_n.42, bf16[4,128,1,128]{3,1,2,0:T(8,128)(2,1)} %get-tuple-element.154), kind=kOutput, calls=%fused_computation.4.clone.1 | convolution fusion | flops 33685504 | bytes 558084 | tf_op jit(solution)/shard_map/while/body/eval_jaxpr/dot_general | solution.py:32
  11.1 0.6 dynamic_slice.31
  13.4 1.0 %fusion.21 = bf16[4,1024,128]{2,1,0:T(8,128)(2,1)S(1)} fusion(bf16[4,1024,128]{2,1,0:T(8,128)(2,1)S(1)} %get-tuple-element.140, s32[]{:T(128)} %get-tuple-element.139, bf16[512,1024]{0,1:T(8,128)(2,1)S(1)} %get-tuple-element.153, s32[]{:T(128)S(6)} %select_n.42, bf16[4,128,1,128]{3,1,2,0:T(8,128)(2,1)} %get-tuple-element.154), kind=kOutput, calls=%fused_computation.4.clone.1 | convolution fusion | flops 33685504 | bytes 558084 | tf_op jit(solution)/shard_map/while/body/eval_jaxpr/dot_general | solution.py:32
  14.4 0.6 dynamic_slice.31
  16.6 1.0 %fusion.21 = bf16[4,1024,128]{2,1,0:T(8,128)(2,1)S(1)} fusion(bf16[4,1024,128]{2,1,0:T(8,128)(2,1)S(1)} %get-tuple-element.140, s32[]{:T(128)} %get-tuple-element.139, bf16[512,1024]{0,1:T(8,128)(2,1)S(1)} %get-tuple-element.153, s32[]{:T(128)S(6)} %select_n.42, bf16[4,128,1,128]{3,1,2,0:T(8,128)(2,1)} %get-tuple-element.154), kind=kOutput, calls=%fused_computation.4.clone.1 | convolution fusion | flops 33685504 | bytes 558084 | tf_op jit(solution)/shard_map/while/body/eval_jaxpr/dot_general | solution.py:32
  17.7 0.8 copy.43
  18.5 32.8 %all_to_all.33 = bf16[4,1024,1,128]{3,0,2,1:T(4,128)(2,1)S(1)} all-to-all(bf16[4,1024,1,128]{3,0,2,1:T(4,128)(2,1)S(1)} %bitcast.50), channel_id=1, replica_groups=mesh['shell'=8,'aux'=4] {'shell'}, dimensions={1} | all-to-all | bytes 2097152 | tf_op jit(solution)/shard_map/all_to_all | solution.py:48
  51.5 1.7 %copy.26 = bf16[32,128,1,128]{3,0,2,1:T(8,128)(2,1)} copy(bf16[32,128,1,128]{3,1,0,2:T(8,128)(2,1)S(1)} %bitcast.52) | data formatting | bytes 2097152 | tf_op jit(solution)/shard_map/all_to_all | solution.py:48
  53.2 3.5 %all-to-all-start.1 = ((bf16[32,128,1,128]{3,0,2,1:T(8,128)(2,1)}), bf16[32,128,1,128]{3,0,2,1:T(8,128)(2,1)S(1)}, u32[]{:S(2)}, u32[]{:S(2)}) async-start(bf16[32,128,1,128]{3,0,2,1:T(8,128)(2,1)} %copy.26), calls=%async_computation.1 | async-start | bytes 2097152 | tf_op jit(solution)/shard_map/all_to_all | solution.py:47
  56.7 26.0 %all-gather = s32[8,4,3]{2,1,0:T(4,128)S(1)} all-gather(s32[1,4,3]{2,1,0:T(4,128)S(1)} %bitcast.56), channel_id=1, replica_groups=mesh['shell'=8,'aux'=4] {'shell'}, dimensions={0}, use_global_device_ids=true | all-gather | bytes 432 | tf_op jit(solution)/shard_map/all_gather | solution.py:42
  83.4 0.5 copy.28
  83.9 0.8 reshape.42
  84.8 0.4 convolution_convert_fusion.1
  85.2 0.8 reshape.43
  86.0 0.7 fusion.6
  86.7 1.5 %copy.42 = bf16[32,32,1,4,128]{4,3,0,2,1:T(4,128)(2,1)} copy(bf16[32,32,1,4,128]{4,3,2,1,0:T(4,128)(2,1)S(1)} %fusion.6) | data formatting | bytes 2097152 | tf_op jit(solution)/shard_map/convert_element_type | solution.py:59
  (20 shorter events, 1.5 us)
Async XLA Ops:
  0.0 86.0 %copy-start = (bf16[4,4]{1,0:T(4,128)(2,1)S(1)}, bf16[4,4]{1,0:T(4,128)(2,1)}, u32[]{:S(2)}) copy-start(bf16[4,4]{1,0:T(4,128)(2,1)} %param.10) | copy-start | bytes 100
  1.7 1.7 %copy-start.1 = (s32[4,3]{1,0:T(4,128)S(1)}, s32[4,3]{1,0:T(4,128)}, u32[]{:S(2)}) copy-start(s32[4,3]{1,0:T(4,128)} %param.8) | copy-start | bytes 148
  53.2 29.8 %all-to-all-start.1 = ((bf16[32,128,1,128]{3,0,2,1:T(8,128)(2,1)}), bf16[32,128,1,128]{3,0,2,1:T(8,128)(2,1)S(1)}, u32[]{:S(2)}, u32[]{:S(2)}) async-start(bf16[32,128,1,128]{3,0,2,1:T(8,128)(2,1)} %copy.26), calls=%async_computation.1 | async-start | bytes 2097152 | tf_op jit(solution)/shard_map/all_to_all | solution.py:47
where the time goes:
time: 88.8 us; the launch traced here: 88.2 us
  blocking collectives  58.8 us (66%)
  local copies, waits for them, and re-layouts  12.8 us (14%)
  loops' own time  6.88 us (8%)
  matrix products  5.08 us (6%)
  starting transfers between devices  3.52 us (4%)
  other arithmetic  0.97 us (1%)
    all_to_all x1, blocking collectives, per_device(): lax.all_to_all(half_blocks, 'shell', split_axis=1, concat_axis=0, tiled=T...  32.8 us
    all_gather x1, blocking collectives, per_device(): listing = lax.all_gather(pair_list, 'shell', axis=0, tiled=True)  26 us
    another operation x1, loops' own time, per_device(): half_blocks = lax.map(one_slot, (integrals, pair_list[:, 1]))  6.88 us
    dot_general x4, matrix products, one_slot(): lax.dot_general(column, int_block.reshape(BS, aux_dev * BS), (((0,), (0,)...  3.97 us
    all_to_all x1, starting transfers between devices, per_device(): lax.all_to_all(lax.all_to_all(half_blocks, 'shell', split_axis=1, concat_...  3.52 us
    dynamic_slice x4, local copies, waits for them, and re-layouts, per_device(): half_blocks = lax.map(one_slot, (integrals, pair_list[:, 1]))  2.32 us
    all_to_all x3, local copies, waits for them, and re-layouts, per_device(): lax.all_to_all(half_blocks, 'shell', split_axis=1, concat_axis=0, tiled=T...  1.89 us
  transfers between devices with their start and end apart: 1, of which 0 were waited for; matrix products, arithmetic and copies ran while one was open for 0% of the time, Pallas kernels for 0%

commit v1 on v0

--- a/solution.py
+++ b/solution.py
@@ -1,12 +1,18 @@
+import functools
+
 import jax
 import jax.numpy as jnp
 from jax import lax
+from jax.experimental import pallas as pl
+from jax.experimental.pallas import tpu as pltpu
 from jax.sharding import PartitionSpec as P
 
 BS = 128
-
-
-def per_device(integrals, pair_list, coef, metric, occ_slot):
+CODE = 128
+GATHER_LIMIT = 16 * 2**20
+
+
+def relayed_half_blocks(integrals, pair_list, coef, metric, occ_slot):
     pairs_dev = pair_list.shape[0]
     rows_local = coef.shape[0]
     occ_count = coef.shape[1]
@@ -59,6 +65,142 @@
     return result.reshape(result.shape[0], result.shape[1], block_count * BS).astype(jnp.bfloat16)
 
 
+def pieces_kernel(occ_local, aux_count, pairs, slot_row, coef, out):
+    pairs_dev = pairs.shape[0]
+    blocks_dev = coef.shape[0] // BS
+    occ_count = coef.shape[1]
+    block_total = slot_row.shape[1]
+    width = occ_count // block_total
+    rows = out.shape[0]
+    me = lax.axis_index("aux")
+
+    spread = (
+        lax.broadcasted_iota(jnp.int32, (block_total, occ_count), 1) // width
+        == lax.broadcasted_iota(jnp.int32, (block_total, occ_count), 0)
+    ).astype(jnp.bfloat16)
+    slots = jnp.broadcast_to(slot_row[...], (8, block_total)).astype(jnp.float32)
+    target = jnp.dot(slots.astype(jnp.bfloat16), spread, preferred_element_type=jnp.float32)
+    target = target.astype(jnp.int32)[:1] * width + (
+        lax.broadcasted_iota(jnp.int32, (1, occ_count), 1) % width
+    )
+    row = lax.broadcasted_iota(jnp.int32, (rows, 1), 0)
+    wanted = (row // occ_local * aux_count + me) * occ_local + row % occ_local
+    pick = (wanted == target).astype(jnp.bfloat16)
+
+    lane = lax.broadcasted_iota(jnp.int32, (1, CODE), 1)
+    code = jnp.zeros((1, CODE), jnp.int32)
+    for k in range(pairs_dev):
+        column = lax.rem(pairs[k, 1], blocks_dev)
+        block = coef[pl.ds(pl.multiple_of(column * BS, BS), BS), :]
+        piece = lax.dot_general(
+            pick, block, (((1,), (1,)), ((), ())), preferred_element_type=jnp.float32
+        )
+        live = (pairs[k, 2] == 1).astype(jnp.float32)
+        out[:, k * BS : (k + 1) * BS] = (piece * live).astype(jnp.bfloat16)
+        block_row = pairs[k, 0]
+        code = jnp.where(lane == k, block_row % 128, code)
+        code = jnp.where(lane == pairs_dev + k, block_row // 128, code)
+    out[:, pairs_dev * BS :] = jnp.broadcast_to(
+        code.astype(jnp.float32), (rows, CODE)
+    ).astype(jnp.bfloat16)
+
+
+def transform_kernel(block_rows, metric, pieces, blocks, out, total):
+    step = pl.program_id(0)
+    aux_count, pairs_dev = blocks.shape[1:3]
+    occ_local = pieces.shape[1]
+    rows = occ_local * aux_count
+
+    @pl.when(step == 0)
+    def _():
+        total[...] = jnp.zeros_like(total)
+
+    row = lax.broadcasted_iota(jnp.int32, (rows, occ_local), 0)
+    orbital = lax.broadcasted_iota(jnp.int32, (rows, occ_local), 1)
+    coefs = pieces[0, :, : pairs_dev * BS]
+    scaled = []
+    for p in range(aux_count):
+        factor = jnp.zeros((rows, occ_local), jnp.float32)
+        for q in range(aux_count):
+            factor = jnp.where(row % aux_count == q, metric[q, p], factor)
+        factor = jnp.where(row // aux_count == orbital, factor, 0.0).astype(jnp.bfloat16)
+        scaled.append(
+            jnp.dot(factor, coefs, preferred_element_type=jnp.float32).astype(jnp.bfloat16)
+        )
+    for k in range(pairs_dev):
+        left = jnp.concatenate([s[:, k * BS : (k + 1) * BS] for s in scaled], axis=1)
+        right = jnp.concatenate([blocks[0, p, k] for p in range(aux_count)], axis=0)
+        r = block_rows[step, k]
+        total[r] += jnp.dot(left, right, preferred_element_type=jnp.float32)
+
+    @pl.when(step == pl.num_programs(0) - 1)
+    def _():
+        for r in range(total.shape[0]):
+            out[:, :, r * BS : (r + 1) * BS] = (
+                total[r].reshape(occ_local, aux_count, BS).astype(jnp.bfloat16)
+            )
+
+
+def gathered_blocks(integrals, pair_list, coef, metric, occ_slot):
+    pairs_dev = pair_list.shape[0]
+    shell_count = lax.axis_size("shell")
+    aux_count = lax.axis_size("aux")
+    occ_local = coef.shape[1] // (shell_count * aux_count)
+    block_count = coef.shape[0] // BS * shell_count
+    width = pairs_dev * BS + CODE
+
+    blocks = lax.all_gather(
+        integrals.reshape(pairs_dev, BS, BS), ("shell", "aux"), axis=0, tiled=True
+    ).reshape(shell_count, aux_count, pairs_dev, BS, BS)
+    pieces = pl.pallas_call(
+        functools.partial(pieces_kernel, occ_local, aux_count),
+        out_shape=jax.ShapeDtypeStruct((shell_count * occ_local, width), jnp.bfloat16),
+        in_specs=[
+            pl.BlockSpec(memory_space=pltpu.SMEM),
+            pl.BlockSpec(memory_space=pltpu.VMEM),
+            pl.BlockSpec(memory_space=pltpu.VMEM),
+        ],
+        out_specs=pl.BlockSpec(memory_space=pltpu.VMEM),
+        compiler_params=pltpu.CompilerParams(vmem_limit_bytes=32 * 2**20),
+        name="pieces",
+    )(pair_list, occ_slot.reshape(1, -1), coef)
+    pieces = lax.all_to_all(
+        pieces.reshape(shell_count, occ_local, width), "shell", split_axis=0, concat_axis=0
+    )
+    digits = pieces[:, 0, pairs_dev * BS : pairs_dev * (BS + 2)].astype(jnp.int32)
+    block_rows = digits[:, :pairs_dev] + 128 * digits[:, pairs_dev:]
+    return pl.pallas_call(
+        transform_kernel,
+        grid_spec=pltpu.PrefetchScalarGridSpec(
+            num_scalar_prefetch=1,
+            grid=(shell_count,),
+            in_specs=[
+                pl.BlockSpec(memory_space=pltpu.SMEM),
+                pl.BlockSpec((1, occ_local, width), lambda s, rows: (s, 0, 0)),
+                pl.BlockSpec(
+                    (1, aux_count, pairs_dev, BS, BS), lambda s, rows: (s, 0, 0, 0, 0)
+                ),
+            ],
+            out_specs=pl.BlockSpec(
+                (occ_local, aux_count, block_count * BS), lambda s, rows: (0, 0, 0)
+            ),
+            scratch_shapes=[pltpu.VMEM((block_count, occ_local * aux_count, BS), jnp.float32)],
+        ),
+        out_shape=jax.ShapeDtypeStruct(
+            (occ_local, aux_count, block_count * BS), jnp.bfloat16
+        ),
+        compiler_params=pltpu.CompilerParams(vmem_limit_bytes=32 * 2**20),
+        name="transform",
+    )(block_rows, metric.astype(jnp.float32), pieces, blocks)
+
+
+def per_device(integrals, pair_list, coef, metric, occ_slot):
+    gathered_bytes = integrals.size * 2 * lax.axis_size("shell") * lax.axis_size("aux")
+    if gathered_bytes > GATHER_LIMIT:
+        return relayed_half_blocks(integrals, pair_list, coef, metric, occ_slot)
+    return gathered_blocks(integrals, pair_list, coef, metric, occ_slot)
+
+
 def solution(mesh):
     placed = (P("shell", None, "aux", None), P("shell", None), P("shell", None), P(), P())
     return jax.shard_map(

time: 88.8 us -> 92.4 us (1.041)
  blocking collectives: 58.8 us -> 0 us
  waiting for transfers between devices: 0.01 us -> 56.9 us
  between operations: 0.17 us -> 13.4 us
  Pallas kernels: 0 us -> 9.02 us
  local copies, waits for them, and re-layouts: 12.8 us -> 4.74 us
  loops' own time: 6.88 us -> 0 us
  matrix products: 5.08 us -> 0 us
  starting transfers between devices: 3.52 us -> 7.25 us
    all_gather x0 -> x1, waiting for transfers between devices: none -> 44.6 us  [gathered_blocks(): lax.all_gather(integrals.reshape(pairs_dev, BS, BS), ('shell', 'aux'), ax...]
    all_to_all x1 -> x0, blocking collectives: 32.8 us -> none  [per_device(): lax.all_to_all(half_blocks, 'shell', split_axis=1, concat_axis=0, tiled=T...]
    all_gather x1 -> x0, blocking collectives: 26 us -> none  [per_device(): listing = lax.all_gather(pair_list, 'shell', axis=0, tiled=True)]
    all_to_all x1, waiting for transfers between devices: 0.01 us -> 11.6 us  [gathered_blocks(): lax.all_to_all(pieces.reshape(shell_count, occ_local, width), 'shell', sp...]
    pallas_call x0 -> x2, Pallas kernels: none -> 9.02 us  [the longest x1 6.9 us: gathered_blocks(): pl.pallas_call(transform_kernel, grid_spec=pltpu.PrefetchScalarGridSpec(n...]
    another operation x1 -> x0, loops' own time: 6.88 us -> none  [per_device(): half_blocks = lax.map(one_slot, (integrals, pair_list[:, 1]))]
    dot_general x6 -> x0, matrix products: 5.08 us -> none  [the longest x4 3.97 us: one_slot(): lax.dot_general(column, int_block.reshape(BS, aux_dev * BS), (((0,), (0,)...]
    all_to_all x1, starting transfers between devices: 3.52 us -> 7.25 us  [gathered_blocks(): lax.all_to_all(pieces.reshape(shell_count, occ_local, width), 'shell', sp...]
  transfers between devices with their start and end apart: 1 -> 2, of which waited for: 0 -> 2; matrix products, arithmetic and copies ran while one was open for 0% -> 1% of each run, Pallas kernels for 0% -> 2%
where the time goes in v1:
time: 92.4 us; the launch traced here: 92.1 us
  waiting for transfers between devices  56.9 us (62%)
  between operations  13.4 us (15%)
  Pallas kernels  9.02 us (10%)
  starting transfers between devices  7.25 us (8%)
  local copies, waits for them, and re-layouts  4.74 us (5%)
    all_gather x1, waiting for transfers between devices, gathered_blocks(): lax.all_gather(integrals.reshape(pairs_dev, BS, BS), ('shell', 'aux'), ax...  44.6 us
    all_to_all x1, waiting for transfers between devices, gathered_blocks(): lax.all_to_all(pieces.reshape(shell_count, occ_local, width), 'shell', sp...  11.6 us
    all_to_all x1, starting transfers between devices, gathered_blocks(): lax.all_to_all(pieces.reshape(shell_count, occ_local, width), 'shell', sp...  7.25 us
    pallas_call x1, Pallas kernels, gathered_blocks(): pl.pallas_call(transform_kernel, grid_spec=pltpu.PrefetchScalarGridSpec(n...  6.9 us
    unnamed x8, local copies, waits for them, and re-layouts  4.74 us
    pallas_call x1, Pallas kernels, gathered_blocks(): pl.pallas_call(functools.partial(pieces_kernel, occ_local, aux_count), ou...  2.12 us
  transfers between devices with their start and end apart: 2, of which 2 were waited for; matrix products, arithmetic and copies ran while one was open for 1% of the time, Pallas kernels for 2%

profile of v1, /device:TPU:0, one launch (start us, length us, event | category | flops | bytes accessed | tf_op | source)
XLA Modules:
  0.0 92.1 jit_solution(12922672124821456074)
XLA Ops:
  6.5 0.0 all-gather.3.cloned.1.call-start
  6.5 0.7 all-gather.3.cloned.1.call-update
  7.3 0.0 copy-start.1
  7.3 1.2 %copy-done.1 = bf16[512,1024]{1,0:T(8,128)(2,1)S(1)} copy-done((bf16[512,1024]{1,0:T(8,128)(2,1)S(1)}, bf16[512,1024]{1,0:T(8,128)(2,1)}, u32[]{:S(2)}) %copy-start.1) | copy-done | bytes 1048600
  8.5 0.0 copy-start.2
  8.5 0.7 copy-done.2
  9.2 0.0 copy-start.3
  9.2 0.7 copy-done.3
  9.8 2.1 %pieces.1 = bf16[256,640]{1,0:T(8,128)(2,1)} custom-call(s32[4,3]{1,0:T(4,128)S(1)} %copy-done.2, s32[1,128]{1,0:T(1,128)S(1)} %bitcast.5, bf16[512,1024]{1,0:T(8,128)(2,1)S(1)} %copy-done.1), custom_call_target="tpu_custom_call" | custom-call | tf_op jit(solution)/shard_map/pieces/pallas_call | solution.py:155
  11.9 7.2 %all-to-all-start = ((bf16[8,32,640]{2,1,0:T(8,128)(2,1)}), bf16[8,32,640]{2,1,0:T(8,128)(2,1)S(1)}, u32[]{:S(2)}, u32[]{:S(2)}) async-start(bf16[8,32,640]{2,1,0:T(8,128)(2,1)} %bitcast.1), calls=%async_computation | async-start | bytes 655360 | tf_op jit(solution)/shard_map/all_to_all | solution.py:167
  19.2 0.7 convert_element_type.11.metric
  19.9 11.6 %all-to-all-done.pieces = bf16[8,32,640]{2,1,0:T(8,128)(2,1)S(1)} async-done(((bf16[8,32,640]{2,1,0:T(8,128)(2,1)}), bf16[8,32,640]{2,1,0:T(8,128)(2,1)S(1)}, u32[]{:S(2)}, u32[]{:S(2)}) %all-to-all-start) | async-done | bytes 327712 | tf_op jit(solution)/shard_map/all_to_all | solution.py:167
  31.4 0.1 multiply_add_fusion.block_rows
  31.5 44.6 %all-gather.3.cloned.1.call-done = bf16[128,128,1,128]{3,1,2,0:T(8,128)(2,1)} async-done(((bf16[4,128,1,128]{3,1,2,0:T(8,128)(2,1)}), bf16[128,128,1,128]{3,1,2,0:T(8,128)(2,1)}) %all-gather.3.cloned.1.call-update) | async-done | bytes 4194320 | tf_op jit(solution)/shard_map/all_gather | solution.py:152
  76.2 0.0 copy-start
  76.2 2.2 %copy-done = bf16[128,128,1,128]{3,1,2,0:T(8,128)(2,1)S(1)} copy-done((bf16[128,128,1,128]{3,1,2,0:T(8,128)(2,1)S(1)}, bf16[128,128,1,128]{3,1,2,0:T(8,128)(2,1)}, u32[]{:S(2)}) %copy-start) | copy-done | bytes 4194328
  78.4 6.9 %transform.1 = bf16[32,4,4096]{2,1,0:T(4,128)(2,1)} custom-call(s32[8,4]{1,0:T(8,128)S(1)} %multiply_add_fusion.block_rows, f32[4,4]{1,0:T(4,128)S(1)} %convert_element_type.11.metric, bf16[8,32,640]{2,1,0:T(8,128)(2,1)S(1)} %all-to-all-done.pieces, bf16[8,4,4,128,128]{4,3,2,1,0:T(8,128)(2,1)S(1)} %bitcast.4), custom_call_target="tpu_custom_call" | custom-call | tf_op jit(solution)/shard_map/transform/pallas_call | solution.py:172
  (1 shorter events, 0.0 us)
Async XLA Ops:
  6.5 69.6 %all-gather.3.cloned.1.call-start = ((), (), s32[]{:S(2)}) async-start(), calls=%async_computation.1 | async-start | bytes 4325376 | tf_op jit(solution)/shard_map/all_gather | solution.py:152
  7.3 1.2 %copy-start.1 = (bf16[512,1024]{1,0:T(8,128)(2,1)S(1)}, bf16[512,1024]{1,0:T(8,128)(2,1)}, u32[]{:S(2)}) copy-start(bf16[512,1024]{1,0:T(8,128)(2,1)} %coef.1) | copy-start | bytes 3145732
  8.5 0.7 copy-start.2
  9.2 0.7 copy-start.3
  11.9 19.5 %all-to-all-start = ((bf16[8,32,640]{2,1,0:T(8,128)(2,1)}), bf16[8,32,640]{2,1,0:T(8,128)(2,1)S(1)}, u32[]{:S(2)}, u32[]{:S(2)}) async-start(bf16[8,32,640]{2,1,0:T(8,128)(2,1)} %bitcast.1), calls=%async_computation | async-start | bytes 655360 | tf_op jit(solution)/shard_map/all_to_all | solution.py:167
  76.2 2.2 %copy-start = (bf16[128,128,1,128]{3,1,2,0:T(8,128)(2,1)S(1)}, bf16[128,128,1,128]{3,1,2,0:T(8,128)(2,1)}, u32[]{:S(2)}) copy-start(bf16[128,128,1,128]{3,1,2,0:T(8,128)(2,1)} %all-gather.3.cloned.1.call-done) | copy-start | bytes 12582916
Sparse Core Ops, SparseCore 0:
  10.2 65.8 all-gather.2

commit v2 on v0

--- a/solution.py
+++ b/solution.py
@@ -1,12 +1,14 @@
 import jax
 import jax.numpy as jnp
 from jax import lax
+from jax.experimental import pallas as pl
+from jax.experimental.pallas import tpu as pltpu
 from jax.sharding import PartitionSpec as P
 
 BS = 128
 
 
-def per_device(integrals, pair_list, coef, metric, occ_slot):
+def relayed_half_blocks(integrals, pair_list, coef, metric, occ_slot):
     pairs_dev = pair_list.shape[0]
     rows_local = coef.shape[0]
     occ_count = coef.shape[1]
@@ -59,6 +61,156 @@
     return result.reshape(result.shape[0], result.shape[1], block_count * BS).astype(jnp.bfloat16)
 
 
+def half_kernel(pairs_in, slot_in, coef_in, blocks_in, out, pairs, slot_row, coef, blocks, sems):
+    pairs_dev = pairs.shape[0]
+    blocks_dev = coef.shape[0] // BS
+    occ_count = coef.shape[1]
+    block_total = slot_row.shape[1]
+    width = occ_count // block_total
+    devices = out.shape[0]
+    occ_local = occ_count // devices
+
+    loads = [
+        pltpu.make_async_copy(source, target, sems.at[at])
+        for at, (source, target) in enumerate(
+            ((slot_in, slot_row), (pairs_in, pairs), (coef_in, coef), (blocks_in, blocks))
+        )
+    ]
+    for load in loads:
+        load.start()
+    loads[0].wait()
+
+    spread = (
+        lax.broadcasted_iota(jnp.int32, (block_total, occ_count), 1) // width
+        == lax.broadcasted_iota(jnp.int32, (block_total, occ_count), 0)
+    ).astype(jnp.bfloat16)
+    slots = jnp.broadcast_to(slot_row[...], (8, block_total)).astype(jnp.float32)
+    target = jnp.dot(slots.astype(jnp.bfloat16), spread, preferred_element_type=jnp.float32)
+    target = target.astype(jnp.int32)[:1] * width + (
+        lax.broadcasted_iota(jnp.int32, (1, occ_count), 1) % width
+    )
+    pick = (lax.broadcasted_iota(jnp.int32, (occ_count, 1), 0) == target).astype(jnp.bfloat16)
+
+    for load in loads[1:]:
+        load.wait()
+    rows = [
+        coef[pl.ds(pl.multiple_of(lax.rem(pairs[k, 1], blocks_dev) * BS, BS), BS), :]
+        for k in range(pairs_dev)
+    ]
+    ordered = lax.dot_general(
+        pick,
+        jnp.concatenate(rows, axis=0),
+        (((1,), (1,)), ((), ())),
+        preferred_element_type=jnp.float32,
+    ).astype(jnp.bfloat16)
+    lane = lax.broadcasted_iota(jnp.int32, (1, BS), 1)
+    code = jnp.zeros((1, BS), jnp.int32)
+    for k in range(pairs_dev):
+        half = jnp.dot(
+            ordered[:, k * BS : (k + 1) * BS], blocks[k], preferred_element_type=jnp.float32
+        )
+        live = (pairs[k, 2] == 1).astype(jnp.float32)
+        out[:, k * occ_local : (k + 1) * occ_local, :] = (
+            (half * live).astype(jnp.bfloat16).reshape(devices, occ_local, BS)
+        )
+        block_row = pairs[k, 0]
+        code = jnp.where(lane == k, block_row % 128, code)
+        code = jnp.where(lane == pairs_dev + k, block_row // 128, code)
+    digits = code.astype(jnp.float32).astype(jnp.bfloat16)
+    out[:, pairs_dev * occ_local :, :] = jnp.broadcast_to(digits[None], (devices, 8, BS))
+
+
+def collect_kernel(block_rows, metric, received, out, total):
+    shell_count, pairs_dev = block_rows.shape
+    occ_local, aux_count = out.shape[:2]
+    rows = occ_local * aux_count
+    total[...] = jnp.zeros_like(total)
+    for s in range(shell_count):
+        for k in range(pairs_dev):
+            r = block_rows[s, k]
+            for p in range(aux_count):
+                part = received[s * aux_count + p, k * occ_local : (k + 1) * occ_local, :]
+                total[r, p * occ_local : (p + 1) * occ_local, :] += part.astype(jnp.float32)
+
+    row = lax.broadcasted_iota(jnp.int32, (rows, rows), 0)
+    column = lax.broadcasted_iota(jnp.int32, (rows, rows), 1)
+    left = (
+        lax.broadcasted_iota(jnp.int32, (rows, aux_count), 0) % aux_count
+        == lax.broadcasted_iota(jnp.int32, (rows, aux_count), 1)
+    ).astype(jnp.bfloat16)
+    right = (
+        lax.broadcasted_iota(jnp.int32, (aux_count, rows), 1) // occ_local
+        == lax.broadcasted_iota(jnp.int32, (aux_count, rows), 0)
+    ).astype(jnp.bfloat16)
+    factor = jnp.dot(left, metric[...], preferred_element_type=jnp.float32).astype(jnp.bfloat16)
+    factor = jnp.dot(factor, right, preferred_element_type=jnp.float32)
+    mix = jnp.where(row // aux_count == column % occ_local, factor, 0.0).astype(jnp.bfloat16)
+    for r in range(0, total.shape[0], 2):
+        summed = jnp.concatenate([total[r], total[r + 1]], axis=1).astype(jnp.bfloat16)
+        mixed = jnp.dot(mix, summed, preferred_element_type=jnp.float32)
+        out[:, :, r * BS : (r + 2) * BS] = mixed.reshape(
+            occ_local, aux_count, 2 * BS
+        ).astype(jnp.bfloat16)
+
+
+def direct_half_blocks(integrals, pair_list, coef, metric, occ_slot):
+    pairs_dev = pair_list.shape[0]
+    shell_count = lax.axis_size("shell")
+    aux_count = lax.axis_size("aux")
+    devices = shell_count * aux_count
+    occ_local = coef.shape[1] // devices
+    block_count = coef.shape[0] // BS * shell_count
+    vmem = pl.BlockSpec(memory_space=pltpu.VMEM)
+    smem = pl.BlockSpec(memory_space=pltpu.SMEM)
+    hbm = pl.BlockSpec(memory_space=pltpu.HBM)
+    half = pl.pallas_call(
+        half_kernel,
+        out_shape=jax.ShapeDtypeStruct((devices, pairs_dev * occ_local + 8, BS), jnp.bfloat16),
+        in_specs=[hbm] * 4,
+        out_specs=vmem,
+        scratch_shapes=[
+            pltpu.SMEM(pair_list.shape, jnp.int32),
+            pltpu.VMEM((1, occ_slot.shape[0]), jnp.int32),
+            pltpu.VMEM(coef.shape, jnp.bfloat16),
+            pltpu.VMEM((pairs_dev, BS, BS), jnp.bfloat16),
+            pltpu.SemaphoreType.DMA((4,)),
+        ],
+        compiler_params=pltpu.CompilerParams(vmem_limit_bytes=40 * 2**20),
+        name="half_blocks",
+    )(
+        *(
+            pltpu.with_memory_space_constraint(operand, pltpu.HBM)
+            for operand in (
+                pair_list,
+                occ_slot.reshape(1, -1),
+                coef,
+                integrals.reshape(pairs_dev, BS, BS),
+            )
+        )
+    )
+    received = lax.all_to_all(half, ("shell", "aux"), split_axis=0, concat_axis=0)
+    digits = received[::aux_count, pairs_dev * occ_local, : 2 * pairs_dev].astype(jnp.int32)
+    block_rows = digits[:, :pairs_dev] + 128 * digits[:, pairs_dev:]
+    return pl.pallas_call(
+        collect_kernel,
+        out_shape=jax.ShapeDtypeStruct(
+            (occ_local, aux_count, block_count * BS), jnp.bfloat16
+        ),
+        in_specs=[smem, vmem, vmem],
+        out_specs=vmem,
+        scratch_shapes=[pltpu.VMEM((block_count, occ_local * aux_count, BS), jnp.float32)],
+        compiler_params=pltpu.CompilerParams(vmem_limit_bytes=40 * 2**20),
+        name="collect",
+    )(block_rows, metric, received)
+
+
+def per_device(integrals, pair_list, coef, metric, occ_slot):
+    occ_local = coef.shape[1] // (lax.axis_size("shell") * lax.axis_size("aux"))
+    if occ_local % 16:
+        return relayed_half_blocks(integrals, pair_list, coef, metric, occ_slot)
+    return direct_half_blocks(integrals, pair_list, coef, metric, occ_slot)
+
+
 def solution(mesh):
     placed = (P("shell", None, "aux", None), P("shell", None), P("shell", None), P(), P())
     return jax.shard_map(

time: 88.8 us -> 42.1 us (0.47)
  blocking collectives: 58.8 us -> 36.5 us
  local copies, waits for them, and re-layouts: 12.8 us -> 0.01 us
  loops' own time: 6.88 us -> 0 us
  Pallas kernels: 0 us -> 5.35 us
  matrix products: 5.08 us -> 0 us
  starting transfers between devices: 3.52 us -> 0 us
  other arithmetic: 0.97 us -> 0.08 us
    all_gather x1 -> x0, blocking collectives: 26 us -> none  [per_device(): listing = lax.all_gather(pair_list, 'shell', axis=0, tiled=True)]
    another operation x1 -> x0, loops' own time: 6.88 us -> none  [per_device(): half_blocks = lax.map(one_slot, (integrals, pair_list[:, 1]))]
    pallas_call x0 -> x2, Pallas kernels: none -> 5.35 us  [the longest x1 2.95 us: direct_half_blocks(): pl.pallas_call(half_kernel, out_shape=jax.ShapeDtypeStruct((devices, pair...]
    dot_general x6 -> x0, matrix products: 5.08 us -> none  [the longest x4 3.97 us: one_slot(): lax.dot_general(column, int_block.reshape(BS, aux_dev * BS), (((0,), (0,)...]
    all_to_all x1, blocking collectives: 32.8 us -> 36.5 us  [direct_half_blocks(): lax.all_to_all(half, ('shell', 'aux'), split_axis=0, concat_axis=0)]
    all_to_all x1 -> x0, starting transfers between devices: 3.52 us -> none  [per_device(): lax.all_to_all(lax.all_to_all(half_blocks, 'shell', split_axis=1, concat_...]
    all_to_all x5 -> x0, local copies, waits for them, and re-layouts: 2.85 us -> none  [the longest x3 1.89 us: per_device(): lax.all_to_all(half_blocks, 'shell', split_axis=1, concat_axis=0, tiled=T...]
    dynamic_slice x4 -> x0, local copies, waits for them, and re-layouts: 2.32 us -> none  [per_device(): half_blocks = lax.map(one_slot, (integrals, pair_list[:, 1]))]
  transfers between devices with their start and end apart: 1 -> 0, of which waited for: 0 -> 0; matrix products, arithmetic and copies ran while one was open for 0% -> 0% of each run, Pallas kernels for 0% -> 0%
where the time goes in v2:
time: 42.1 us; the launch traced here: 41.9 us
  blocking collectives  36.5 us (87%)
  Pallas kernels  5.35 us (13%)
    all_to_all x1, blocking collectives, direct_half_blocks(): lax.all_to_all(half, ('shell', 'aux'), split_axis=0, concat_axis=0)  36.5 us
    pallas_call x1, Pallas kernels, direct_half_blocks(): pl.pallas_call(half_kernel, out_shape=jax.ShapeDtypeStruct((devices, pair...  2.95 us
    pallas_call x1, Pallas kernels, direct_half_blocks(): pl.pallas_call(collect_kernel, out_shape=jax.ShapeDtypeStruct((occ_local,...  2.4 us

profile of v2, /device:TPU:0, one launch (start us, length us, event | category | flops | bytes accessed | tf_op | source)
XLA Modules:
  0.0 41.9 jit_solution(16187746376459266084)
XLA Ops:
  0.0 3.0 %half_blocks.1 = bf16[32,136,128]{2,1,0:T(8,128)(2,1)S(1)} custom-call(s32[4,3]{1,0:T(4,128)} %pairs_in.1, s32[1,128]{1,0:T(1,128)} %bitcast.5, bf16[512,1024]{1,0:T(8,128)(2,1)} %coef_in.1, bf16[4,128,128]{2,1,0:T(8,128)(2,1)} %bitcast.3), custom_call_target="tpu_custom_call" | custom-call | tf_op jit(solution)/shard_map/half_blocks/pallas_call | solution.py:166
  3.0 0.0 copy-start
  3.0 36.5 %all_to_all.5.received = bf16[32,136,128]{2,1,0:T(8,128)(2,1)S(1)} all-to-all(bf16[32,136,128]{2,1,0:T(8,128)(2,1)S(1)} %half_blocks.1), channel_id=1, replica_groups=mesh['shell'=8,'aux'=4] {'shell','aux'}, dimensions={0} | all-to-all | bytes 2228224 | tf_op jit(solution)/shard_map/all_to_all | solution.py:191
  39.4 0.1 multiply_add_fusion.block_rows
  39.5 0.0 copy-done
  39.5 2.4 %collect.1 = bf16[32,4,4096]{2,1,0:T(4,128)(2,1)} custom-call(s32[8,4]{1,0:T(8,128)S(1)} %multiply_add_fusion.block_rows, bf16[4,4]{1,0:T(4,128)(2,1)S(1)} %copy-done, bf16[32,136,128]{2,1,0:T(8,128)(2,1)S(1)} %all_to_all.5.received), custom_call_target="tpu_custom_call" | custom-call | tf_op jit(solution)/shard_map/collect/pallas_call | solution.py:194
  (1 shorter events, 0.0 us)
Async XLA Ops:
  3.0 36.6 %copy-start = (bf16[4,4]{1,0:T(4,128)(2,1)S(1)}, bf16[4,4]{1,0:T(4,128)(2,1)}, u32[]{:S(2)}) copy-start(bf16[4,4]{1,0:T(4,128)(2,1)} %metric.1) | copy-start | bytes 100

commit v3 on v0

--- a/solution.py
+++ b/solution.py
@@ -1,12 +1,16 @@
+import functools
+
 import jax
 import jax.numpy as jnp
 from jax import lax
+from jax.experimental import pallas as pl
+from jax.experimental.pallas import tpu as pltpu
 from jax.sharding import PartitionSpec as P
 
 BS = 128
 
 
-def per_device(integrals, pair_list, coef, metric, occ_slot):
+def relayed_half_blocks(integrals, pair_list, coef, metric, occ_slot):
     pairs_dev = pair_list.shape[0]
     rows_local = coef.shape[0]
     occ_count = coef.shape[1]
@@ -59,6 +63,205 @@
     return result.reshape(result.shape[0], result.shape[1], block_count * BS).astype(jnp.bfloat16)
 
 
+def targets_of(slot_row, block_total, occ_count):
+    width = occ_count // block_total
+    spread = (
+        lax.broadcasted_iota(jnp.int32, (block_total, occ_count), 1) // width
+        == lax.broadcasted_iota(jnp.int32, (block_total, occ_count), 0)
+    ).astype(jnp.bfloat16)
+    slots = jnp.broadcast_to(slot_row, (8, block_total)).astype(jnp.float32)
+    target = jnp.dot(slots.astype(jnp.bfloat16), spread, preferred_element_type=jnp.float32)
+    return target.astype(jnp.int32)[:1] * width + (
+        lax.broadcasted_iota(jnp.int32, (1, occ_count), 1) % width
+    )
+
+
+def pick_kernel(group, occ_local, aux_count, pairs_in, slot_in, coef_in, near, far, pairs, slot_row, coef, sems):
+    pairs_dev = pairs.shape[0]
+    blocks_dev = coef.shape[0] // BS
+    occ_count = coef.shape[1]
+    loads = [
+        pltpu.make_async_copy(source, target, sems.at[at])
+        for at, (source, target) in enumerate(
+            ((slot_in, slot_row), (pairs_in, pairs), (coef_in, coef))
+        )
+    ]
+    for load in loads:
+        load.start()
+    me = lax.axis_index("shell")
+    mine = lax.axis_index("aux")
+    rows = group * occ_local
+    row = lax.broadcasted_iota(jnp.int32, (2 * rows, 1), 0)
+    owner = jnp.bitwise_xor(row // occ_local, me)
+    wanted = (owner * aux_count + mine) * occ_local + row % occ_local
+    loads[0].wait()
+    target = targets_of(slot_row[...], slot_row.shape[1], occ_count)
+    pick = (wanted == target).astype(jnp.bfloat16)
+    for load in loads[1:]:
+        load.wait()
+    for k in range(pairs_dev):
+        start = pl.multiple_of(lax.rem(pairs[k, 1], blocks_dev) * BS, BS)
+        live = (pairs[k, 2] == 1).astype(jnp.float32)
+        piece = lax.dot_general(
+            pick,
+            coef[pl.ds(start, BS), :],
+            (((1,), (1,)), ((), ())),
+            preferred_element_type=jnp.float32,
+        )
+        piece = (piece * live).astype(jnp.bfloat16)
+        near[:, k * BS : (k + 1) * BS] = piece[:rows]
+        far[:, k * BS : (k + 1) * BS] = piece[rows:]
+
+
+def block_kernel(aux_count, coded, *refs):
+    if coded:
+        pairs, far_pairs, *refs = refs
+    coefs, *refs = refs
+    blocks, pieces = refs[:aux_count], refs[aux_count:]
+    pairs_dev = blocks[0].shape[0]
+    occ_local = coefs.shape[0] // len(pieces)
+    mine = lax.axis_index("aux")
+    for k in range(pairs_dev):
+        left = coefs[:, k * BS : (k + 1) * BS]
+        for j in range(0, aux_count, 2):
+            right = jnp.concatenate([blocks[j][k], blocks[j + 1][k]], axis=1)
+            half = jnp.dot(left, right, preferred_element_type=jnp.float32).astype(jnp.bfloat16)
+            for side in range(2):
+                at = k * aux_count + jnp.bitwise_xor(mine, j + side)
+                start = pl.multiple_of(at * occ_local, occ_local)
+                for f, piece in enumerate(pieces):
+                    piece[pl.ds(start, occ_local), :] = half[
+                        f * occ_local : (f + 1) * occ_local, side * BS : (side + 1) * BS
+                    ]
+    if coded:
+        lane = lax.broadcasted_iota(jnp.int32, (1, BS), 1)
+        code = jnp.zeros((1, BS), jnp.int32)
+        for at, listing in enumerate((pairs, far_pairs)):
+            for k in range(pairs_dev):
+                block_row = listing[k, 0]
+                place = 2 * (at * pairs_dev + k)
+                code = jnp.where(lane == place, block_row % 128, code)
+                code = jnp.where(lane == place + 1, block_row // 128, code)
+        digits = jnp.broadcast_to(code.astype(jnp.float32), (16, BS)).astype(jnp.bfloat16)
+        for piece in pieces:
+            piece[pairs_dev * aux_count * occ_local :, :] = digits
+
+
+def collect_kernel(block_rows, metric, *refs):
+    *received, out, total = refs
+    occ_local, aux_count = out.shape[:2]
+    rows = occ_local * aux_count
+    pairs_dev = block_rows.shape[1]
+    total[...] = jnp.zeros_like(total)
+    for at, piece in enumerate(received):
+        for k in range(pairs_dev):
+            r = block_rows[at, k]
+            total[r] += piece[k * rows : (k + 1) * rows, :].astype(jnp.float32)
+
+    row = lax.broadcasted_iota(jnp.int32, (rows, rows), 0)
+    column = lax.broadcasted_iota(jnp.int32, (rows, rows), 1)
+    left = (
+        lax.broadcasted_iota(jnp.int32, (rows, aux_count), 0) % aux_count
+        == lax.broadcasted_iota(jnp.int32, (rows, aux_count), 1)
+    ).astype(jnp.bfloat16)
+    right = (
+        lax.broadcasted_iota(jnp.int32, (aux_count, rows), 1) // occ_local
+        == lax.broadcasted_iota(jnp.int32, (aux_count, rows), 0)
+    ).astype(jnp.bfloat16)
+    factor = jnp.dot(left, metric[...], preferred_element_type=jnp.float32).astype(jnp.bfloat16)
+    factor = jnp.dot(factor, right, preferred_element_type=jnp.float32)
+    mix = jnp.where(row // aux_count == column % occ_local, factor, 0.0).astype(jnp.bfloat16)
+    for r in range(0, total.shape[0], 2):
+        summed = jnp.concatenate([total[r], total[r + 1]], axis=1).astype(jnp.bfloat16)
+        mixed = jnp.dot(mix, summed, preferred_element_type=jnp.float32)
+        out[:, :, r * BS : (r + 2) * BS] = mixed.reshape(
+            occ_local, aux_count, 2 * BS
+        ).astype(jnp.bfloat16)
+
+
+def flip(value, axis, bits):
+    count = lax.axis_size(axis)
+    return lax.ppermute(value, axis, [(at, at ^ bits) for at in range(count)])
+
+
+def in_hbm(*operands):
+    return [pltpu.with_memory_space_constraint(operand, pltpu.HBM) for operand in operands]
+
+
+def exchanged_inputs(integrals, pair_list, coef, metric, occ_slot):
+    pairs_dev = pair_list.shape[0]
+    shell_count = lax.axis_size("shell")
+    aux_count = lax.axis_size("aux")
+    group = shell_count // 2
+    occ_local = coef.shape[1] // (shell_count * aux_count)
+    block_count = coef.shape[0] // BS * shell_count
+    rows = group * occ_local
+    piece_rows = pairs_dev * aux_count * occ_local
+    vmem = pl.BlockSpec(memory_space=pltpu.VMEM)
+    smem = pl.BlockSpec(memory_space=pltpu.SMEM)
+    hbm = pl.BlockSpec(memory_space=pltpu.HBM)
+    params = pltpu.CompilerParams(vmem_limit_bytes=40 * 2**20)
+
+    blocks = integrals.reshape(pairs_dev, BS, BS)
+    far_block = flip(blocks, "shell", group)
+    far_pairs = flip(pair_list, "shell", group)
+    near_blocks = [blocks] + [flip(blocks, "aux", j) for j in range(1, aux_count)]
+    near_coef, sent_coef = pl.pallas_call(
+        functools.partial(pick_kernel, group, occ_local, aux_count),
+        out_shape=[jax.ShapeDtypeStruct((rows, pairs_dev * BS), jnp.bfloat16)] * 2,
+        in_specs=[hbm] * 3,
+        out_specs=[vmem] * 2,
+        scratch_shapes=[
+            pltpu.SMEM(pair_list.shape, jnp.int32),
+            pltpu.VMEM((1, occ_slot.shape[0]), jnp.int32),
+            pltpu.VMEM(coef.shape, jnp.bfloat16),
+            pltpu.SemaphoreType.DMA((3,)),
+        ],
+        compiler_params=params,
+        name="pick",
+    )(*in_hbm(pair_list, occ_slot.reshape(1, -1), coef))
+    far_coef = flip(sent_coef, "shell", group)
+
+    def transformed(coded, name, listings, coefs, quad):
+        pieces = pl.pallas_call(
+            functools.partial(block_kernel, aux_count, coded),
+            out_shape=[
+                jax.ShapeDtypeStruct((piece_rows + 16 * coded, BS), jnp.bfloat16)
+            ] * group,
+            in_specs=[smem] * len(listings) + [vmem] * (1 + aux_count),
+            out_specs=[vmem] * group,
+            compiler_params=params,
+            name=name,
+        )(*listings, coefs, *quad)
+        return [pieces[0]] + [flip(pieces[f], "shell", f) for f in range(1, group)]
+
+    near = transformed(True, "near_blocks", (pair_list, far_pairs), near_coef, near_blocks)
+    far_blocks = [far_block] + [flip(far_block, "aux", j) for j in range(1, aux_count)]
+    far = transformed(False, "far_blocks", (), far_coef, far_blocks)
+    digits = jnp.stack([piece[piece_rows, : 4 * pairs_dev] for piece in near])
+    digits = digits.astype(jnp.int32).reshape(group, 2, pairs_dev, 2)
+    block_rows = (digits[..., 0] + 128 * digits[..., 1]).swapaxes(0, 1)
+    return pl.pallas_call(
+        collect_kernel,
+        out_shape=jax.ShapeDtypeStruct(
+            (occ_local, aux_count, block_count * BS), jnp.bfloat16
+        ),
+        in_specs=[smem] + [vmem] * (1 + 2 * group),
+        out_specs=vmem,
+        scratch_shapes=[pltpu.VMEM((block_count, occ_local * aux_count, BS), jnp.float32)],
+        compiler_params=params,
+        name="collect",
+    )(block_rows.reshape(2 * group, pairs_dev), metric, *near, *far)
+
+
+def per_device(integrals, pair_list, coef, metric, occ_slot):
+    shell_count, aux_count = lax.axis_size("shell"), lax.axis_size("aux")
+    occ_local = coef.shape[1] // (shell_count * aux_count)
+    if occ_local % 16 or shell_count & (shell_count - 1) or aux_count & (aux_count - 1):
+        return relayed_half_blocks(integrals, pair_list, coef, metric, occ_slot)
+    return exchanged_inputs(integrals, pair_list, coef, metric, occ_slot)
+
+
 def solution(mesh):
     placed = (P("shell", None, "aux", None), P("shell", None), P("shell", None), P(), P())
     return jax.shard_map(

time: 88.8 us -> 39.4 us (0.44)
  blocking collectives: 58.8 us -> 0 us
  waiting for transfers between devices: 0.01 us -> 14.9 us
  starting transfers between devices: 3.52 us -> 17.2 us
  local copies, waits for them, and re-layouts: 12.8 us -> 1.13 us
  loops' own time: 6.88 us -> 0 us
  Pallas kernels: 0 us -> 5.6 us
  matrix products: 5.08 us -> 0 us
    all_to_all x1 -> x0, blocking collectives: 32.8 us -> none  [per_device(): lax.all_to_all(half_blocks, 'shell', split_axis=1, concat_axis=0, tiled=T...]
    all_gather x1 -> x0, blocking collectives: 26 us -> none  [per_device(): listing = lax.all_gather(pair_list, 'shell', axis=0, tiled=True)]
    ppermute x0 -> x15, starting transfers between devices: none -> 17.2 us  [flip(): return lax.ppermute(value, axis, [(at, at ^ bits) for at in range(count)])]
    ppermute x0 -> x15, waiting for transfers between devices: none -> 14.9 us  [flip(): return lax.ppermute(value, axis, [(at, at ^ bits) for at in range(count)])]
    another operation x1 -> x0, loops' own time: 6.88 us -> none  [per_device(): half_blocks = lax.map(one_slot, (integrals, pair_list[:, 1]))]
    pallas_call x0 -> x4, Pallas kernels: none -> 5.6 us  [the longest x1 2.41 us: exchanged_inputs(): pl.pallas_call(collect_kernel, out_shape=jax.ShapeDtypeStruct((occ_local,...]
    dot_general x6 -> x0, matrix products: 5.08 us -> none  [the longest x4 3.97 us: one_slot(): lax.dot_general(column, int_block.reshape(BS, aux_dev * BS), (((0,), (0,)...]
    all_to_all x1 -> x0, starting transfers between devices: 3.52 us -> none  [per_device(): lax.all_to_all(lax.all_to_all(half_blocks, 'shell', split_axis=1, concat_...]
  transfers between devices with their start and end apart: 1 -> 15, of which waited for: 0 -> 5; matrix products, arithmetic and copies ran while one was open for 0% -> 2% of each run, Pallas kernels for 0% -> 8%
where the time goes in v3:
time: 39.4 us; the launch traced here: 39.2 us
  starting transfers between devices  17.2 us (44%)
  waiting for transfers between devices  14.9 us (38%)
  Pallas kernels  5.6 us (14%)
  local copies, waits for them, and re-layouts  1.13 us (3%)
    ppermute x15, starting transfers between devices, flip(): return lax.ppermute(value, axis, [(at, at ^ bits) for at in range(count)])  17.2 us
    ppermute x15, waiting for transfers between devices, flip(): return lax.ppermute(value, axis, [(at, at ^ bits) for at in range(count)])  14.9 us
    pallas_call x1, Pallas kernels, exchanged_inputs(): pl.pallas_call(collect_kernel, out_shape=jax.ShapeDtypeStruct((occ_local,...  2.41 us
    pallas_call x1, Pallas kernels, exchanged_inputs(): pl.pallas_call(functools.partial(pick_kernel, group, occ_local, aux_count...  2.02 us
    pallas_call x2, Pallas kernels, transformed(): pl.pallas_call(functools.partial(block_kernel, aux_count, coded), out_sha...  1.17 us
  transfers between devices with their start and end apart: 15, of which 5 were waited for; matrix products, arithmetic and copies ran while one was open for 2% of the time, Pallas kernels for 8%

profile of v3, /device:TPU:0, one launch (start us, length us, event | category | flops | bytes accessed | tf_op | source)
XLA Modules:
  0.0 39.2 jit_solution(15399662336163048371)
XLA Ops:
  0.0 2.4 %collective-permute-start.3 = (bf16[4,128,128]{2,1,0:T(8,128)(2,1)}, bf16[4,128,128]{2,1,0:T(8,128)(2,1)S(1)}, u32[]{:S(2)}, u32[]{:S(2)}) collective-permute-start(bf16[4,128,128]{2,1,0:T(8,128)(2,1)} %bitcast.4), channel_id=1, source_target_pairs={{0,3},{1,2},{2,1},{3,0},{4,7},{5,6},{6,5},{7,4},{8,11},{9,10},{10,... | collective-permute-start | bytes 393224 | tf_op jit(solution)/shard_map/ppermute | solution.py:184
  2.4 0.6 %collective-permute-start.2 = (bf16[4,128,128]{2,1,0:T(8,128)(2,1)}, bf16[4,128,128]{2,1,0:T(8,128)(2,1)S(1)}, u32[]{:S(2)}, u32[]{:S(2)}) collective-permute-start(bf16[4,128,128]{2,1,0:T(8,128)(2,1)} %bitcast.5), channel_id=1, source_target_pairs={{0,2},{1,3},{2,0},{3,1},{4,6},{5,7},{6,4},{7,5},{8,10},{9,11},{10,... | collective-permute-start | bytes 393224 | tf_op jit(solution)/shard_map/ppermute | solution.py:184
  3.1 2.8 %collective-permute-start.8 = (bf16[4,128,128]{2,1,0:T(8,128)(2,1)}, bf16[4,128,128]{2,1,0:T(8,128)(2,1)S(1)}, u32[]{:S(2)}, u32[]{:S(2)}) collective-permute-start(bf16[4,128,128]{2,1,0:T(8,128)(2,1)} %bitcast.7), channel_id=1, source_target_pairs={{0,16},{4,20},{8,24},{12,28},{16,0},{20,4},{24,8},{28,12},{1,17},{... | collective-permute-start | bytes 393224 | tf_op jit(solution)/shard_map/ppermute | solution.py:184
  5.9 0.1 collective-permute-start
  6.0 2.0 %pick.1 = (bf16[128,512]{1,0:T(8,128)(2,1)S(1)}, bf16[128,512]{1,0:T(8,128)(2,1)S(1)}) custom-call(s32[4,3]{1,0:T(4,128)} %refs_0_.1, s32[1,128]{1,0:T(1,128)} %bitcast.11, bf16[512,1024]{1,0:T(8,128)(2,1)} %coef_in.1), custom_call_target="tpu_custom_call" | custom-call | tf_op jit(solution)/shard_map/pick/pallas_call | solution.py:209
  8.1 4.9 %collective-permute-done.refs_1_ = s32[4,3]{1,0:T(4,128)S(1)} collective-permute-done((s32[4,3]{1,0:T(4,128)}, s32[4,3]{1,0:T(4,128)S(1)}, u32[]{:S(2)}, u32[]{:S(2)}) %collective-permute-start) | collective-permute-done | bytes 80 | tf_op jit(solution)/shard_map/ppermute | solution.py:184
  13.0 0.9 %near_blocks.1 = (bf16[528,128]{1,0:T(8,128)(2,1)S(1)}, bf16[528,128]{1,0:T(8,128)(2,1)S(1)}, bf16[528,128]{1,0:T(8,128)(2,1)S(1)}, bf16[528,128]{1,0:T(8,128)(2,1)S(1)}) custom-call(s32[4,3]{1,0:T(4,128)S(1)} %copy-done.1, s32[4,3]{1,0:T(4,128)S(1)} %collective-permute-done.refs_1_, bf16[128,512]{1,0:T(8,128)(2,1)S(1)} %get-tuple-element.15.refs_2_, ...), custom_call_target="tpu_custom_call" | custom-call | tf_op jit(solution)/shard_map/near_blocks/pallas_call | solution.py:226
  13.9 1.5 %collective-permute-start.4 = (bf16[528,128]{1,0:T(8,128)(2,1)S(1)}, bf16[528,128]{1,0:T(8,128)(2,1)S(1)}, u32[]{:S(2)}, u32[]{:S(2)}) collective-permute-start(bf16[528,128]{1,0:T(8,128)(2,1)S(1)} %get-tuple-element.17), channel_id=1, source_target_pairs={{0,4},{4,0},{8,12},{12,8},{16,20},{20,16},{24,28},{28,24},{1,5},{5... | collective-permute-start | bytes 405512 | tf_op jit(solution)/shard_map/ppermute | solution.py:184
  15.5 1.4 %collective-permute-start.10 = (bf16[4,128,128]{2,1,0:T(8,128)(2,1)S(1)}, bf16[4,128,128]{2,1,0:T(8,128)(2,1)S(1)}, u32[]{:S(2)}, u32[]{:S(2)}) collective-permute-start(bf16[4,128,128]{2,1,0:T(8,128)(2,1)S(1)} %collective-permute-done.8.refs_1_), channel_id=1, source_target_pairs={{0,2},{1,3},{2,0},{3,1},{4,6},{5,7},{6,4},{7,5},{8,10},{9,11},{10,... | collective-permute-start | bytes 393224 | tf_op jit(solution)/shard_map/ppermute | solution.py:184
  16.9 0.4 %collective-permute-start.9 = (bf16[4,128,128]{2,1,0:T(8,128)(2,1)S(1)}, bf16[4,128,128]{2,1,0:T(8,128)(2,1)S(1)}, u32[]{:S(2)}, u32[]{:S(2)}) collective-permute-start(bf16[4,128,128]{2,1,0:T(8,128)(2,1)S(1)} %collective-permute-done.8.refs_1_), channel_id=1, source_target_pairs={{0,1},{1,0},{2,3},{3,2},{4,5},{5,4},{6,7},{7,6},{8,9},{9,8},{10,11... | collective-permute-start | bytes 393224 | tf_op jit(solution)/shard_map/ppermute | solution.py:184
  17.3 4.4 %collective-permute-done.7.refs_0_ = bf16[128,512]{1,0:T(8,128)(2,1)S(1)} collective-permute-done((bf16[128,512]{1,0:T(8,128)(2,1)S(1)}, bf16[128,512]{1,0:T(8,128)(2,1)S(1)}, u32[]{:S(2)}, u32[]{:S(2)}) %collective-permute-start.7) | collective-permute-done | bytes 131104 | tf_op jit(solution)/shard_map/ppermute | solution.py:184
  21.8 3.4 %collective-permute-start.6 = (bf16[528,128]{1,0:T(8,128)(2,1)S(1)}, bf16[528,128]{1,0:T(8,128)(2,1)S(1)}, u32[]{:S(2)}, u32[]{:S(2)}) collective-permute-start(bf16[528,128]{1,0:T(8,128)(2,1)S(1)} %get-tuple-element.19), channel_id=1, source_target_pairs={{0,12},{4,8},{8,4},{12,0},{16,28},{20,24},{24,20},{28,16},{1,13},{... | collective-permute-start | bytes 405512 | tf_op jit(solution)/shard_map/ppermute | solution.py:184
  25.2 0.3 far_blocks.1
  25.5 1.6 %collective-permute-start.12 = (bf16[512,128]{1,0:T(8,128)(2,1)S(1)}, bf16[512,128]{1,0:T(8,128)(2,1)S(1)}, u32[]{:S(2)}, u32[]{:S(2)}) collective-permute-start(bf16[512,128]{1,0:T(8,128)(2,1)S(1)} %get-tuple-element.22), channel_id=1, source_target_pairs={{0,4},{4,0},{8,12},{12,8},{16,20},{20,16},{24,28},{28,24},{1,5},{5... | collective-permute-start | bytes 393224 | tf_op jit(solution)/shard_map/ppermute | solution.py:184
  27.1 1.9 %collective-permute-start.13 = (bf16[512,128]{1,0:T(8,128)(2,1)S(1)}, bf16[512,128]{1,0:T(8,128)(2,1)S(1)}, u32[]{:S(2)}, u32[]{:S(2)}) collective-permute-start(bf16[512,128]{1,0:T(8,128)(2,1)S(1)} %get-tuple-element.23), channel_id=1, source_target_pairs={{0,8},{4,12},{8,0},{12,4},{16,24},{20,28},{24,16},{28,20},{1,9},{5... | collective-permute-start | bytes 393224 | tf_op jit(solution)/shard_map/ppermute | solution.py:184
  28.9 0.9 %collective-permute-start.14 = (bf16[512,128]{1,0:T(8,128)(2,1)S(1)}, bf16[512,128]{1,0:T(8,128)(2,1)S(1)}, u32[]{:S(2)}, u32[]{:S(2)}) collective-permute-start(bf16[512,128]{1,0:T(8,128)(2,1)S(1)} %get-tuple-element.24), channel_id=1, source_target_pairs={{0,12},{4,8},{8,4},{12,0},{16,28},{20,24},{24,20},{28,16},{1,13},{... | collective-permute-start | bytes 393224 | tf_op jit(solution)/shard_map/ppermute | solution.py:184
  29.9 0.1 stack.12
  30.1 0.4 collective-permute-done.6.refs_3_
  30.5 0.1 stack.14
  30.6 0.3 fusion.1
  30.9 2.1 %collective-permute-done.12.refs_5_ = bf16[512,128]{1,0:T(8,128)(2,1)S(1)} collective-permute-done((bf16[512,128]{1,0:T(8,128)(2,1)S(1)}, bf16[512,128]{1,0:T(8,128)(2,1)S(1)}, u32[]{:S(2)}, u32[]{:S(2)}) %collective-permute-start.12) | collective-permute-done | bytes 131104 | tf_op jit(solution)/shard_map/ppermute | solution.py:184
  33.0 3.1 %collective-permute-done.14.refs_7_ = bf16[512,128]{1,0:T(8,128)(2,1)S(1)} collective-permute-done((bf16[512,128]{1,0:T(8,128)(2,1)S(1)}, bf16[512,128]{1,0:T(8,128)(2,1)S(1)}, u32[]{:S(2)}, u32[]{:S(2)}) %collective-permute-start.14) | collective-permute-done | bytes 131104 | tf_op jit(solution)/shard_map/ppermute | solution.py:184
  36.2 0.7 %copy-done.2 = bf16[4,4]{1,0:T(4,128)(2,1)S(1)} copy-done((bf16[4,4]{1,0:T(4,128)(2,1)S(1)}, bf16[4,4]{1,0:T(4,128)(2,1)}, u32[]{:S(2)}) %copy-start.2) | copy-done | bytes 56
  36.8 2.4 %collect.1 = bf16[32,4,4096]{2,1,0:T(4,128)(2,1)} custom-call(s32[8,4]{1,0:T(8,128)S(1)} %bitcast.9, bf16[4,4]{1,0:T(4,128)(2,1)S(1)} %copy-done.2, bf16[528,128]{1,0:T(8,128)(2,1)S(1)} %get-tuple-element.16.refs_0_, bf16[528,128]{1,0:T(8,128)(2,1)S(1)} %collective-permute-done.4.refs_1_, bf16[528,128]{1,0:T(8,128)(2,1)S(1)} %collective-permute-done.5.refs_2_, ...), custom_call_target="tpu_custom_call" | custom-call | tf_op jit(solution)/shard_map/collect/pallas_call | solution.py:244
  (27 shorter events, 0.4 us)
Async XLA Ops:
  0.0 12.9 %collective-permute-start.3 = (bf16[4,128,128]{2,1,0:T(8,128)(2,1)}, bf16[4,128,128]{2,1,0:T(8,128)(2,1)S(1)}, u32[]{:S(2)}, u32[]{:S(2)}) collective-permute-start(bf16[4,128,128]{2,1,0:T(8,128)(2,1)} %bitcast.4), channel_id=1, source_target_pairs={{0,3},{1,2},{2,1},{3,0},{4,7},{5,6},{6,5},{7,4},{8,11},{9,10},{10,... | collective-permute-start | bytes 393224 | tf_op jit(solution)/shard_map/ppermute | solution.py:184
  2.4 10.5 %collective-permute-start.2 = (bf16[4,128,128]{2,1,0:T(8,128)(2,1)}, bf16[4,128,128]{2,1,0:T(8,128)(2,1)S(1)}, u32[]{:S(2)}, u32[]{:S(2)}) collective-permute-start(bf16[4,128,128]{2,1,0:T(8,128)(2,1)} %bitcast.5), channel_id=1, source_target_pairs={{0,2},{1,3},{2,0},{3,1},{4,6},{5,7},{6,4},{7,5},{8,10},{9,11},{10,... | collective-permute-start | bytes 393224 | tf_op jit(solution)/shard_map/ppermute | solution.py:184
  3.0 9.9 %collective-permute-start.1 = (bf16[4,128,128]{2,1,0:T(8,128)(2,1)}, bf16[4,128,128]{2,1,0:T(8,128)(2,1)S(1)}, u32[]{:S(2)}, u32[]{:S(2)}) collective-permute-start(bf16[4,128,128]{2,1,0:T(8,128)(2,1)} %bitcast.6), channel_id=1, source_target_pairs={{0,1},{1,0},{2,3},{3,2},{4,5},{5,4},{6,7},{7,6},{8,9},{9,8},{10,11... | collective-permute-start | bytes 393224 | tf_op jit(solution)/shard_map/ppermute | solution.py:184
  3.1 12.3 %collective-permute-start.8 = (bf16[4,128,128]{2,1,0:T(8,128)(2,1)}, bf16[4,128,128]{2,1,0:T(8,128)(2,1)S(1)}, u32[]{:S(2)}, u32[]{:S(2)}) collective-permute-start(bf16[4,128,128]{2,1,0:T(8,128)(2,1)} %bitcast.7), channel_id=1, source_target_pairs={{0,16},{4,20},{8,24},{12,28},{16,0},{20,4},{24,8},{28,12},{1,17},{... | collective-permute-start | bytes 393224 | tf_op jit(solution)/shard_map/ppermute | solution.py:184
  5.9 7.0 %collective-permute-start = (s32[4,3]{1,0:T(4,128)}, s32[4,3]{1,0:T(4,128)S(1)}, u32[]{:S(2)}, u32[]{:S(2)}) collective-permute-start(s32[4,3]{1,0:T(4,128)} %refs_0_.1), channel_id=1, source_target_pairs={{0,16},{4,20},{8,24},{12,28},{16,0},{20,4},{24,8},{28,12},{1,17},{... | collective-permute-start | bytes 152 | tf_op jit(solution)/shard_map/ppermute | solution.py:184
  6.0 6.9 %copy-start = (bf16[4,128,1,128]{3,1,2,0:T(8,128)(2,1)S(1)}, bf16[4,128,1,128]{3,1,2,0:T(8,128)(2,1)}, u32[]{:S(2)}) copy-start(bf16[4,128,1,128]{3,1,2,0:T(8,128)(2,1)} %param.5) | copy-start | bytes 393220
  8.0 4.9 %copy-start.1 = (s32[4,3]{1,0:T(4,128)S(1)}, s32[4,3]{1,0:T(4,128)}, u32[]{:S(2)}) copy-start(s32[4,3]{1,0:T(4,128)} %refs_0_.1) | copy-start | bytes 148
  12.9 8.8 %collective-permute-start.7 = (bf16[128,512]{1,0:T(8,128)(2,1)S(1)}, bf16[128,512]{1,0:T(8,128)(2,1)S(1)}, u32[]{:S(2)}, u32[]{:S(2)}) collective-permute-start(bf16[128,512]{1,0:T(8,128)(2,1)S(1)} %get-tuple-element.20), channel_id=1, source_target_pairs={{0,16},{4,20},{8,24},{12,28},{16,0},{20,4},{24,8},{28,12},{1,17},{... | collective-permute-start | bytes 393224 | tf_op jit(solution)/shard_map/ppermute | solution.py:184
  13.9 15.1 %collective-permute-start.4 = (bf16[528,128]{1,0:T(8,128)(2,1)S(1)}, bf16[528,128]{1,0:T(8,128)(2,1)S(1)}, u32[]{:S(2)}, u32[]{:S(2)}) collective-permute-start(bf16[528,128]{1,0:T(8,128)(2,1)S(1)} %get-tuple-element.17), channel_id=1, source_target_pairs={{0,4},{4,0},{8,12},{12,8},{16,20},{20,16},{24,28},{28,24},{1,5},{5... | collective-permute-start | bytes 405512 | tf_op jit(solution)/shard_map/ppermute | solution.py:184
  15.4 6.4 %collective-permute-start.11 = (bf16[4,128,128]{2,1,0:T(8,128)(2,1)S(1)}, bf16[4,128,128]{2,1,0:T(8,128)(2,1)S(1)}, u32[]{:S(2)}, u32[]{:S(2)}) collective-permute-start(bf16[4,128,128]{2,1,0:T(8,128)(2,1)S(1)} %collective-permute-done.8.refs_1_), channel_id=1, source_target_pairs={{0,3},{1,2},{2,1},{3,0},{4,7},{5,6},{6,5},{7,4},{8,11},{9,10},{10,... | collective-permute-start | bytes 393224 | tf_op jit(solution)/shard_map/ppermute | solution.py:184
  15.5 9.8 %collective-permute-start.10 = (bf16[4,128,128]{2,1,0:T(8,128)(2,1)S(1)}, bf16[4,128,128]{2,1,0:T(8,128)(2,1)S(1)}, u32[]{:S(2)}, u32[]{:S(2)}) collective-permute-start(bf16[4,128,128]{2,1,0:T(8,128)(2,1)S(1)} %collective-permute-done.8.refs_1_), channel_id=1, source_target_pairs={{0,2},{1,3},{2,0},{3,1},{4,6},{5,7},{6,4},{7,5},{8,10},{9,11},{10,... | collective-permute-start | bytes 393224 | tf_op jit(solution)/shard_map/ppermute | solution.py:184
  16.9 8.3 %collective-permute-start.9 = (bf16[4,128,128]{2,1,0:T(8,128)(2,1)S(1)}, bf16[4,128,128]{2,1,0:T(8,128)(2,1)S(1)}, u32[]{:S(2)}, u32[]{:S(2)}) collective-permute-start(bf16[4,128,128]{2,1,0:T(8,128)(2,1)S(1)} %collective-permute-done.8.refs_1_), channel_id=1, source_target_pairs={{0,1},{1,0},{2,3},{3,2},{4,5},{5,4},{6,7},{7,6},{8,9},{9,8},{10,11... | collective-permute-start | bytes 393224 | tf_op jit(solution)/shard_map/ppermute | solution.py:184
  21.7 8.3 %collective-permute-start.5 = (bf16[528,128]{1,0:T(8,128)(2,1)S(1)}, bf16[528,128]{1,0:T(8,128)(2,1)S(1)}, u32[]{:S(2)}, u32[]{:S(2)}) collective-permute-start(bf16[528,128]{1,0:T(8,128)(2,1)S(1)} %get-tuple-element.18), channel_id=1, source_target_pairs={{0,8},{4,12},{8,0},{12,4},{16,24},{20,28},{24,16},{28,20},{1,9},{5... | collective-permute-start | bytes 405512 | tf_op jit(solution)/shard_map/ppermute | solution.py:184
  21.8 8.7 %collective-permute-start.6 = (bf16[528,128]{1,0:T(8,128)(2,1)S(1)}, bf16[528,128]{1,0:T(8,128)(2,1)S(1)}, u32[]{:S(2)}, u32[]{:S(2)}) collective-permute-start(bf16[528,128]{1,0:T(8,128)(2,1)S(1)} %get-tuple-element.19), channel_id=1, source_target_pairs={{0,12},{4,8},{8,4},{12,0},{16,28},{20,24},{24,20},{28,16},{1,13},{... | collective-permute-start | bytes 405512 | tf_op jit(solution)/shard_map/ppermute | solution.py:184
  25.5 7.5 %collective-permute-start.12 = (bf16[512,128]{1,0:T(8,128)(2,1)S(1)}, bf16[512,128]{1,0:T(8,128)(2,1)S(1)}, u32[]{:S(2)}, u32[]{:S(2)}) collective-permute-start(bf16[512,128]{1,0:T(8,128)(2,1)S(1)} %get-tuple-element.22), channel_id=1, source_target_pairs={{0,4},{4,0},{8,12},{12,8},{16,20},{20,16},{24,28},{28,24},{1,5},{5... | collective-permute-start | bytes 393224 | tf_op jit(solution)/shard_map/ppermute | solution.py:184
  27.1 6.0 %collective-permute-start.13 = (bf16[512,128]{1,0:T(8,128)(2,1)S(1)}, bf16[512,128]{1,0:T(8,128)(2,1)S(1)}, u32[]{:S(2)}, u32[]{:S(2)}) collective-permute-start(bf16[512,128]{1,0:T(8,128)(2,1)S(1)} %get-tuple-element.23), channel_id=1, source_target_pairs={{0,8},{4,12},{8,0},{12,4},{16,24},{20,28},{24,16},{28,20},{1,9},{5... | collective-permute-start | bytes 393224 | tf_op jit(solution)/shard_map/ppermute | solution.py:184
  28.9 7.2 %collective-permute-start.14 = (bf16[512,128]{1,0:T(8,128)(2,1)S(1)}, bf16[512,128]{1,0:T(8,128)(2,1)S(1)}, u32[]{:S(2)}, u32[]{:S(2)}) collective-permute-start(bf16[512,128]{1,0:T(8,128)(2,1)S(1)} %get-tuple-element.24), channel_id=1, source_target_pairs={{0,12},{4,8},{8,4},{12,0},{16,28},{20,24},{24,20},{28,16},{1,13},{... | collective-permute-start | bytes 393224 | tf_op jit(solution)/shard_map/ppermute | solution.py:184
  36.2 0.7 %copy-start.2 = (bf16[4,4]{1,0:T(4,128)(2,1)S(1)}, bf16[4,4]{1,0:T(4,128)(2,1)}, u32[]{:S(2)}) copy-start(bf16[4,4]{1,0:T(4,128)(2,1)} %metric.1) | copy-start | bytes 100

commit v4 on v3

--- a/solution.py
+++ b/solution.py
@@ -109,20 +109,27 @@
             preferred_element_type=jnp.float32,
         )
         piece = (piece * live).astype(jnp.bfloat16)
-        near[:, k * BS : (k + 1) * BS] = piece[:rows]
-        far[:, k * BS : (k + 1) * BS] = piece[rows:]
-
-
-def block_kernel(aux_count, coded, *refs):
-    if coded:
-        pairs, far_pairs, *refs = refs
-    coefs, *refs = refs
+        near[:rows, k * BS : (k + 1) * BS] = piece[:rows]
+        far[:rows, k * BS : (k + 1) * BS] = piece[rows:]
+    lane = lax.broadcasted_iota(jnp.int32, (1, BS), 1)
+    code = jnp.zeros((1, BS), jnp.int32)
+    for k in range(pairs_dev):
+        code = jnp.where(lane == k, pairs[k, 0] % 128, code)
+        code = jnp.where(lane == pairs_dev + k, pairs[k, 0] // 128, code)
+    code = jnp.broadcast_to(code.astype(jnp.float32), (16, BS)).astype(jnp.bfloat16)
+    for piece in (near, far):
+        piece[rows:, :BS] = code
+        piece[rows:, BS:] = jnp.zeros((16, piece.shape[1] - BS), jnp.bfloat16)
+
+
+def block_kernel(aux_count, coefs, *refs):
     blocks, pieces = refs[:aux_count], refs[aux_count:]
     pairs_dev = blocks[0].shape[0]
-    occ_local = coefs.shape[0] // len(pieces)
+    rows = coefs.shape[0] - 16
+    occ_local = rows // len(pieces)
     mine = lax.axis_index("aux")
     for k in range(pairs_dev):
-        left = coefs[:, k * BS : (k + 1) * BS]
+        left = coefs[:rows, k * BS : (k + 1) * BS]
         for j in range(0, aux_count, 2):
             right = jnp.concatenate([blocks[j][k], blocks[j + 1][k]], axis=1)
             half = jnp.dot(left, right, preferred_element_type=jnp.float32).astype(jnp.bfloat16)
@@ -133,29 +140,29 @@
                     piece[pl.ds(start, occ_local), :] = half[
                         f * occ_local : (f + 1) * occ_local, side * BS : (side + 1) * BS
                     ]
-    if coded:
-        lane = lax.broadcasted_iota(jnp.int32, (1, BS), 1)
-        code = jnp.zeros((1, BS), jnp.int32)
-        for at, listing in enumerate((pairs, far_pairs)):
-            for k in range(pairs_dev):
-                block_row = listing[k, 0]
-                place = 2 * (at * pairs_dev + k)
-                code = jnp.where(lane == place, block_row % 128, code)
-                code = jnp.where(lane == place + 1, block_row // 128, code)
-        digits = jnp.broadcast_to(code.astype(jnp.float32), (16, BS)).astype(jnp.bfloat16)
-        for piece in pieces:
-            piece[pairs_dev * aux_count * occ_local :, :] = digits
-
-
-def collect_kernel(block_rows, metric, *refs):
-    *received, out, total = refs
+    for piece in pieces:
+        piece[pairs_dev * aux_count * occ_local :, :] = coefs[rows:, :BS]
+
+
+def collect_kernel(pairs_dev, metric_in, *refs):
+    *received, out, total, metric, codes_v, codes, sems = refs
     occ_local, aux_count = out.shape[:2]
     rows = occ_local * aux_count
-    pairs_dev = block_rows.shape[1]
+    for at, piece in enumerate(received):
+        digits = piece[pairs_dev * rows :, :].astype(jnp.float32).astype(jnp.int32)
+        codes_v[at : at + 1, :] = digits[:1]
+    loads = [
+        pltpu.make_async_copy(codes_v, codes, sems.at[0]),
+        pltpu.make_async_copy(metric_in, metric, sems.at[1]),
+    ]
+    for load in loads:
+        load.start()
     total[...] = jnp.zeros_like(total)
+    for load in loads:
+        load.wait()
     for at, piece in enumerate(received):
         for k in range(pairs_dev):
-            r = block_rows[at, k]
+            r = codes[at, k] + 128 * codes[at, pairs_dev + k]
             total[r] += piece[k * rows : (k + 1) * rows, :].astype(jnp.float32)
 
     row = lax.broadcasted_iota(jnp.int32, (rows, rows), 0)
@@ -184,6 +191,17 @@
     return lax.ppermute(value, axis, [(at, at ^ bits) for at in range(count)])
 
 
+def shared(block, after=None):
+    held, order, bits = [block], [0], lax.axis_size("aux") // 2
+    while bits:
+        held += [flip(one, "aux", bits) for one in held]
+        order += [at ^ bits for at in order]
+        bits //= 2
+        if after is not None:
+            *held, after = lax.optimization_barrier((*held, after))
+    return [held[order.index(at)] for at in range(len(held))]
+
+
 def in_hbm(*operands):
     return [pltpu.with_memory_space_constraint(operand, pltpu.HBM) for operand in operands]
 
@@ -198,17 +216,14 @@
     rows = group * occ_local
     piece_rows = pairs_dev * aux_count * occ_local
     vmem = pl.BlockSpec(memory_space=pltpu.VMEM)
-    smem = pl.BlockSpec(memory_space=pltpu.SMEM)
     hbm = pl.BlockSpec(memory_space=pltpu.HBM)
     params = pltpu.CompilerParams(vmem_limit_bytes=40 * 2**20)
 
     blocks = integrals.reshape(pairs_dev, BS, BS)
     far_block = flip(blocks, "shell", group)
-    far_pairs = flip(pair_list, "shell", group)
-    near_blocks = [blocks] + [flip(blocks, "aux", j) for j in range(1, aux_count)]
     near_coef, sent_coef = pl.pallas_call(
         functools.partial(pick_kernel, group, occ_local, aux_count),
-        out_shape=[jax.ShapeDtypeStruct((rows, pairs_dev * BS), jnp.bfloat16)] * 2,
+        out_shape=[jax.ShapeDtypeStruct((rows + 16, pairs_dev * BS), jnp.bfloat16)] * 2,
         in_specs=[hbm] * 3,
         out_specs=[vmem] * 2,
         scratch_shapes=[
@@ -220,38 +235,41 @@
         compiler_params=params,
         name="pick",
     )(*in_hbm(pair_list, occ_slot.reshape(1, -1), coef))
+    near_blocks = shared(blocks, sent_coef)
+    far_block, near_coef, sent_coef = lax.optimization_barrier((far_block, near_coef, sent_coef))
     far_coef = flip(sent_coef, "shell", group)
 
-    def transformed(coded, name, listings, coefs, quad):
+    def transformed(name, coefs, quad):
         pieces = pl.pallas_call(
-            functools.partial(block_kernel, aux_count, coded),
-            out_shape=[
-                jax.ShapeDtypeStruct((piece_rows + 16 * coded, BS), jnp.bfloat16)
-            ] * group,
-            in_specs=[smem] * len(listings) + [vmem] * (1 + aux_count),
+            functools.partial(block_kernel, aux_count),
+            out_shape=[jax.ShapeDtypeStruct((piece_rows + 16, BS), jnp.bfloat16)] * group,
+            in_specs=[vmem] * (1 + aux_count),
             out_specs=[vmem] * group,
             compiler_params=params,
             name=name,
-        )(*listings, coefs, *quad)
+        )(coefs, *quad)
         return [pieces[0]] + [flip(pieces[f], "shell", f) for f in range(1, group)]
 
-    near = transformed(True, "near_blocks", (pair_list, far_pairs), near_coef, near_blocks)
-    far_blocks = [far_block] + [flip(far_block, "aux", j) for j in range(1, aux_count)]
-    far = transformed(False, "far_blocks", (), far_coef, far_blocks)
-    digits = jnp.stack([piece[piece_rows, : 4 * pairs_dev] for piece in near])
-    digits = digits.astype(jnp.int32).reshape(group, 2, pairs_dev, 2)
-    block_rows = (digits[..., 0] + 128 * digits[..., 1]).swapaxes(0, 1)
+    near = transformed("near_blocks", near_coef, near_blocks)
+    far_blocks = shared(far_block)
+    far = transformed("far_blocks", far_coef, far_blocks)
     return pl.pallas_call(
-        collect_kernel,
+        functools.partial(collect_kernel, pairs_dev),
         out_shape=jax.ShapeDtypeStruct(
             (occ_local, aux_count, block_count * BS), jnp.bfloat16
         ),
-        in_specs=[smem] + [vmem] * (1 + 2 * group),
+        in_specs=[hbm] + [vmem] * (2 * group),
         out_specs=vmem,
-        scratch_shapes=[pltpu.VMEM((block_count, occ_local * aux_count, BS), jnp.float32)],
+        scratch_shapes=[
+            pltpu.VMEM((block_count, occ_local * aux_count, BS), jnp.float32),
+            pltpu.VMEM(metric.shape, jnp.bfloat16),
+            pltpu.VMEM((2 * group, BS), jnp.int32),
+            pltpu.SMEM((2 * group, BS), jnp.int32),
+            pltpu.SemaphoreType.DMA((2,)),
+        ],
         compiler_params=params,
         name="collect",
-    )(block_rows.reshape(2 * group, pairs_dev), metric, *near, *far)
+    )(*in_hbm(metric), *near, *far)
 
 
 def per_device(integrals, pair_list, coef, metric, occ_slot):

time: 39.4 us -> 36.4 us (0.924)
  starting transfers between devices: 17.2 us -> 14.7 us
  waiting for transfers between devices: 14.9 us -> 16.3 us
  local copies, waits for them, and re-layouts: 1.13 us -> 0.01 us
  Pallas kernels: 5.6 us -> 5.12 us
    ppermute x15 -> x14, starting transfers between devices: 17.2 us -> 14.7 us  [flip(): return lax.ppermute(value, axis, [(at, at ^ bits) for at in range(count)])]
    ppermute x15 -> x14, waiting for transfers between devices: 14.9 us -> 16.3 us  [flip(): return lax.ppermute(value, axis, [(at, at ^ bits) for at in range(count)])]
    unnamed x6 -> x2, local copies, waits for them, and re-layouts: 0.69 us -> 0.01 us
    pallas_call x3, Pallas kernels: 3.58 us -> 3.09 us  [the longest x1 2.51 us: exchanged_inputs(): pl.pallas_call(functools.partial(collect_kernel, pairs_dev), out_shape=ja...]
  transfers between devices with their start and end apart: 15 -> 14, of which waited for: 5 -> 7; matrix products, arithmetic and copies ran while one was open for 2% -> 0% of each run, Pallas kernels for 8% -> 7%
where the time goes in v4:
time: 36.4 us; the launch traced here: 36.2 us
  waiting for transfers between devices  16.3 us (45%)
  starting transfers between devices  14.7 us (40%)
  Pallas kernels  5.12 us (14%)
    ppermute x14, waiting for transfers between devices, flip(): return lax.ppermute(value, axis, [(at, at ^ bits) for at in range(count)])  16.3 us
    ppermute x14, starting transfers between devices, flip(): return lax.ppermute(value, axis, [(at, at ^ bits) for at in range(count)])  14.7 us
    pallas_call x1, Pallas kernels, exchanged_inputs(): pl.pallas_call(functools.partial(collect_kernel, pairs_dev), out_shape=ja...  2.51 us
    pallas_call x1, Pallas kernels, exchanged_inputs(): pl.pallas_call(functools.partial(pick_kernel, group, occ_local, aux_count...  2.03 us
  transfers between devices with their start and end apart: 14, of which 7 were waited for; matrix products, arithmetic and copies ran while one was open for 0% of the time, Pallas kernels for 7%

profile of v4, /device:TPU:0, one launch (start us, length us, event | category | flops | bytes accessed | tf_op | source)
XLA Modules:
  0.0 36.2 jit_solution(2428635775298108884)
XLA Ops:
  0.0 3.0 %collective-permute-start.1 = (bf16[4,128,128]{2,1,0:T(8,128)(2,1)}, bf16[4,128,128]{2,1,0:T(8,128)(2,1)S(1)}, u32[]{:S(2)}, u32[]{:S(2)}) collective-permute-start(bf16[4,128,128]{2,1,0:T(8,128)(2,1)} %bitcast.2), channel_id=1, source_target_pairs={{0,2},{1,3},{2,0},{3,1},{4,6},{5,7},{6,4},{7,5},{8,10},{9,11},{10,... | collective-permute-start | bytes 393224 | tf_op jit(solution)/shard_map/ppermute | solution.py:191
  3.0 2.6 %collective-permute-start = (bf16[4,128,128]{2,1,0:T(8,128)(2,1)}, bf16[4,128,128]{2,1,0:T(8,128)(2,1)S(1)}, u32[]{:S(2)}, u32[]{:S(2)}) collective-permute-start(bf16[4,128,128]{2,1,0:T(8,128)(2,1)} %bitcast.3), channel_id=1, source_target_pairs={{0,16},{4,20},{8,24},{12,28},{16,0},{20,4},{24,8},{28,12},{1,17},{... | collective-permute-start | bytes 393224 | tf_op jit(solution)/shard_map/ppermute | solution.py:191
  5.6 2.0 %pick.1 = (bf16[144,512]{1,0:T(8,128)(2,1)S(1)}, bf16[144,512]{1,0:T(8,128)(2,1)S(1)}) custom-call(s32[4,3]{1,0:T(4,128)} %pairs_in.1, s32[1,128]{1,0:T(1,128)} %bitcast.6, bf16[512,1024]{1,0:T(8,128)(2,1)} %coef_in.1), custom_call_target="tpu_custom_call" | custom-call | tf_op jit(solution)/shard_map/pick/pallas_call | solution.py:224
  7.6 0.0 collective-permute-done.1.refs_2_
  7.6 0.1 collective-permute-start.2
  7.7 0.5 %collective-permute-start.3 = (bf16[4,128,128]{2,1,0:T(8,128)(2,1)S(1)}, bf16[4,128,128]{2,1,0:T(8,128)(2,1)S(1)}, u32[]{:S(2)}, u32[]{:S(2)}) collective-permute-start(bf16[4,128,128]{2,1,0:T(8,128)(2,1)S(1)} %collective-permute-done.1.refs_2_), channel_id=1, source_target_pairs={{0,1},{1,0},{2,3},{3,2},{4,5},{5,4},{6,7},{7,6},{8,9},{9,8},{10,11... | collective-permute-start | bytes 393224 | tf_op jit(solution)/shard_map/ppermute | solution.py:191
  8.2 3.7 %collective-permute-done.refs_0_ = bf16[4,128,128]{2,1,0:T(8,128)(2,1)S(1)} collective-permute-done((bf16[4,128,128]{2,1,0:T(8,128)(2,1)}, bf16[4,128,128]{2,1,0:T(8,128)(2,1)S(1)}, u32[]{:S(2)}, u32[]{:S(2)}) %collective-permute-start) | collective-permute-done | bytes 131104 | tf_op jit(solution)/shard_map/ppermute | solution.py:191
  11.9 0.5 %collective-permute-start.9 = (bf16[4,128,128]{2,1,0:T(8,128)(2,1)S(1)}, bf16[4,128,128]{2,1,0:T(8,128)(2,1)S(1)}, u32[]{:S(2)}, u32[]{:S(2)}) collective-permute-start(bf16[4,128,128]{2,1,0:T(8,128)(2,1)S(1)} %collective-permute-done.refs_0_), channel_id=1, source_target_pairs={{0,2},{1,3},{2,0},{3,1},{4,6},{5,7},{6,4},{7,5},{8,10},{9,11},{10,... | collective-permute-start | bytes 393224 | tf_op jit(solution)/shard_map/ppermute | solution.py:191
  12.3 0.0 collective-permute-done.3.refs_3_
  12.3 0.3 near_blocks.1
  12.6 1.6 %collective-permute-start.4 = (bf16[528,128]{1,0:T(8,128)(2,1)S(1)}, bf16[528,128]{1,0:T(8,128)(2,1)S(1)}, u32[]{:S(2)}, u32[]{:S(2)}) collective-permute-start(bf16[528,128]{1,0:T(8,128)(2,1)S(1)} %get-tuple-element.34), channel_id=1, source_target_pairs={{0,4},{4,0},{8,12},{12,8},{16,20},{20,16},{24,28},{28,24},{1,5},{5... | collective-permute-start | bytes 405512 | tf_op jit(solution)/shard_map/ppermute | solution.py:191
  14.2 0.0 collective-permute-start.8
  14.2 2.6 %collective-permute-done.9.refs_2_ = bf16[4,128,128]{2,1,0:T(8,128)(2,1)S(1)} collective-permute-done((bf16[4,128,128]{2,1,0:T(8,128)(2,1)S(1)}, bf16[4,128,128]{2,1,0:T(8,128)(2,1)S(1)}, u32[]{:S(2)}, u32[]{:S(2)}) %collective-permute-start.9) | collective-permute-done | bytes 131104 | tf_op jit(solution)/shard_map/ppermute | solution.py:191
  16.8 1.9 %collective-permute-start.5 = (bf16[528,128]{1,0:T(8,128)(2,1)S(1)}, bf16[528,128]{1,0:T(8,128)(2,1)S(1)}, u32[]{:S(2)}, u32[]{:S(2)}) collective-permute-start(bf16[528,128]{1,0:T(8,128)(2,1)S(1)} %get-tuple-element.35), channel_id=1, source_target_pairs={{0,8},{4,12},{8,0},{12,4},{16,24},{20,28},{24,16},{28,20},{1,9},{5... | collective-permute-start | bytes 405512 | tf_op jit(solution)/shard_map/ppermute | solution.py:191
  18.8 1.0 %collective-permute-start.6 = (bf16[528,128]{1,0:T(8,128)(2,1)S(1)}, bf16[528,128]{1,0:T(8,128)(2,1)S(1)}, u32[]{:S(2)}, u32[]{:S(2)}) collective-permute-start(bf16[528,128]{1,0:T(8,128)(2,1)S(1)} %get-tuple-element.36), channel_id=1, source_target_pairs={{0,12},{4,8},{8,4},{12,0},{16,28},{20,24},{24,20},{28,16},{1,13},{... | collective-permute-start | bytes 405512 | tf_op jit(solution)/shard_map/ppermute | solution.py:191
  19.8 1.5 %collective-permute-done.7.coefs = bf16[144,512]{1,0:T(8,128)(2,1)S(1)} collective-permute-done((bf16[144,512]{1,0:T(8,128)(2,1)S(1)}, bf16[144,512]{1,0:T(8,128)(2,1)S(1)}, u32[]{:S(2)}, u32[]{:S(2)}) %collective-permute-start.7) | collective-permute-done | bytes 147488 | tf_op jit(solution)/shard_map/ppermute | solution.py:191
  21.3 0.3 far_blocks.1
  21.6 1.6 %collective-permute-start.11 = (bf16[528,128]{1,0:T(8,128)(2,1)S(1)}, bf16[528,128]{1,0:T(8,128)(2,1)S(1)}, u32[]{:S(2)}, u32[]{:S(2)}) collective-permute-start(bf16[528,128]{1,0:T(8,128)(2,1)S(1)} %get-tuple-element.40), channel_id=1, source_target_pairs={{0,4},{4,0},{8,12},{12,8},{16,20},{20,16},{24,28},{28,24},{1,5},{5... | collective-permute-start | bytes 405512 | tf_op jit(solution)/shard_map/ppermute | solution.py:191
  23.1 2.0 %collective-permute-start.13 = (bf16[528,128]{1,0:T(8,128)(2,1)S(1)}, bf16[528,128]{1,0:T(8,128)(2,1)S(1)}, u32[]{:S(2)}, u32[]{:S(2)}) collective-permute-start(bf16[528,128]{1,0:T(8,128)(2,1)S(1)} %get-tuple-element.42), channel_id=1, source_target_pairs={{0,12},{4,8},{8,4},{12,0},{16,28},{20,24},{24,20},{28,16},{1,13},{... | collective-permute-start | bytes 405512 | tf_op jit(solution)/shard_map/ppermute | solution.py:191
  25.1 2.9 %collective-permute-done.6.refs_3_ = bf16[528,128]{1,0:T(8,128)(2,1)S(1)} collective-permute-done((bf16[528,128]{1,0:T(8,128)(2,1)S(1)}, bf16[528,128]{1,0:T(8,128)(2,1)S(1)}, u32[]{:S(2)}, u32[]{:S(2)}) %collective-permute-start.6) | collective-permute-done | bytes 135200 | tf_op jit(solution)/shard_map/ppermute | solution.py:191
  28.0 1.3 %collective-permute-done.11.refs_5_ = bf16[528,128]{1,0:T(8,128)(2,1)S(1)} collective-permute-done((bf16[528,128]{1,0:T(8,128)(2,1)S(1)}, bf16[528,128]{1,0:T(8,128)(2,1)S(1)}, u32[]{:S(2)}, u32[]{:S(2)}) %collective-permute-start.11) | collective-permute-done | bytes 135200 | tf_op jit(solution)/shard_map/ppermute | solution.py:191
  29.3 0.6 %collective-permute-done.12.refs_6_ = bf16[528,128]{1,0:T(8,128)(2,1)S(1)} collective-permute-done((bf16[528,128]{1,0:T(8,128)(2,1)S(1)}, bf16[528,128]{1,0:T(8,128)(2,1)S(1)}, u32[]{:S(2)}, u32[]{:S(2)}) %collective-permute-start.12) | collective-permute-done | bytes 135200 | tf_op jit(solution)/shard_map/ppermute | solution.py:191
  29.9 3.8 %collective-permute-done.13.refs_7_ = bf16[528,128]{1,0:T(8,128)(2,1)S(1)} collective-permute-done((bf16[528,128]{1,0:T(8,128)(2,1)S(1)}, bf16[528,128]{1,0:T(8,128)(2,1)S(1)}, u32[]{:S(2)}, u32[]{:S(2)}) %collective-permute-start.13) | collective-permute-done | bytes 135200 | tf_op jit(solution)/shard_map/ppermute | solution.py:191
  33.7 2.5 %collect.1 = bf16[32,4,4096]{2,1,0:T(4,128)(2,1)} custom-call(bf16[4,4]{1,0:T(4,128)(2,1)} %metric_in.1, bf16[528,128]{1,0:T(8,128)(2,1)S(1)} %get-tuple-element.33.refs_0_, bf16[528,128]{1,0:T(8,128)(2,1)S(1)} %collective-permute-done.4.refs_1_, bf16[528,128]{1,0:T(8,128)(2,1)S(1)} %collective-permute-done.5.refs_2_, ...), custom_call_target="tpu_custom_call" | custom-call | tf_op jit(solution)/shard_map/collect/pallas_call | solution.py:256
  (10 shorter events, 0.0 us)
Async XLA Ops:
  0.0 7.6 %collective-permute-start.1 = (bf16[4,128,128]{2,1,0:T(8,128)(2,1)}, bf16[4,128,128]{2,1,0:T(8,128)(2,1)S(1)}, u32[]{:S(2)}, u32[]{:S(2)}) collective-permute-start(bf16[4,128,128]{2,1,0:T(8,128)(2,1)} %bitcast.2), channel_id=1, source_target_pairs={{0,2},{1,3},{2,0},{3,1},{4,6},{5,7},{6,4},{7,5},{8,10},{9,11},{10,... | collective-permute-start | bytes 393224 | tf_op jit(solution)/shard_map/ppermute | solution.py:191
  3.0 8.9 %collective-permute-start = (bf16[4,128,128]{2,1,0:T(8,128)(2,1)}, bf16[4,128,128]{2,1,0:T(8,128)(2,1)S(1)}, u32[]{:S(2)}, u32[]{:S(2)}) collective-permute-start(bf16[4,128,128]{2,1,0:T(8,128)(2,1)} %bitcast.3), channel_id=1, source_target_pairs={{0,16},{4,20},{8,24},{12,28},{16,0},{20,4},{24,8},{28,12},{1,17},{... | collective-permute-start | bytes 393224 | tf_op jit(solution)/shard_map/ppermute | solution.py:191
  5.6 2.1 %copy-start = (bf16[4,128,1,128]{3,1,2,0:T(8,128)(2,1)S(1)}, bf16[4,128,1,128]{3,1,2,0:T(8,128)(2,1)}, u32[]{:S(2)}) copy-start(bf16[4,128,1,128]{3,1,2,0:T(8,128)(2,1)} %param.5) | copy-start | bytes 393220
  7.6 4.7 %collective-permute-start.2 = (bf16[4,128,128]{2,1,0:T(8,128)(2,1)S(1)}, bf16[4,128,128]{2,1,0:T(8,128)(2,1)S(1)}, u32[]{:S(2)}, u32[]{:S(2)}) collective-permute-start(bf16[4,128,128]{2,1,0:T(8,128)(2,1)S(1)} %bitcast.4), channel_id=1, source_target_pairs={{0,1},{1,0},{2,3},{3,2},{4,5},{5,4},{6,7},{7,6},{8,9},{9,8},{10,11... | collective-permute-start | bytes 393224 | tf_op jit(solution)/shard_map/ppermute | solution.py:191
  7.7 4.6 %collective-permute-start.3 = (bf16[4,128,128]{2,1,0:T(8,128)(2,1)S(1)}, bf16[4,128,128]{2,1,0:T(8,128)(2,1)S(1)}, u32[]{:S(2)}, u32[]{:S(2)}) collective-permute-start(bf16[4,128,128]{2,1,0:T(8,128)(2,1)S(1)} %collective-permute-done.1.refs_2_), channel_id=1, source_target_pairs={{0,1},{1,0},{2,3},{3,2},{4,5},{5,4},{6,7},{7,6},{8,9},{9,8},{10,11... | collective-permute-start | bytes 393224 | tf_op jit(solution)/shard_map/ppermute | solution.py:191
  11.9 5.0 %collective-permute-start.9 = (bf16[4,128,128]{2,1,0:T(8,128)(2,1)S(1)}, bf16[4,128,128]{2,1,0:T(8,128)(2,1)S(1)}, u32[]{:S(2)}, u32[]{:S(2)}) collective-permute-start(bf16[4,128,128]{2,1,0:T(8,128)(2,1)S(1)} %collective-permute-done.refs_0_), channel_id=1, source_target_pairs={{0,2},{1,3},{2,0},{3,1},{4,6},{5,7},{6,4},{7,5},{8,10},{9,11},{10,... | collective-permute-start | bytes 393224 | tf_op jit(solution)/shard_map/ppermute | solution.py:191
  12.3 8.9 %collective-permute-start.7 = (bf16[144,512]{1,0:T(8,128)(2,1)S(1)}, bf16[144,512]{1,0:T(8,128)(2,1)S(1)}, u32[]{:S(2)}, u32[]{:S(2)}) collective-permute-start(bf16[144,512]{1,0:T(8,128)(2,1)S(1)} %get-tuple-element.37), channel_id=1, source_target_pairs={{0,16},{4,20},{8,24},{12,28},{16,0},{20,4},{24,8},{28,12},{1,17},{... | collective-permute-start | bytes 442376 | tf_op jit(solution)/shard_map/ppermute | solution.py:191
  12.6 10.5 %collective-permute-start.4 = (bf16[528,128]{1,0:T(8,128)(2,1)S(1)}, bf16[528,128]{1,0:T(8,128)(2,1)S(1)}, u32[]{:S(2)}, u32[]{:S(2)}) collective-permute-start(bf16[528,128]{1,0:T(8,128)(2,1)S(1)} %get-tuple-element.34), channel_id=1, source_target_pairs={{0,4},{4,0},{8,12},{12,8},{16,20},{20,16},{24,28},{28,24},{1,5},{5... | collective-permute-start | bytes 405512 | tf_op jit(solution)/shard_map/ppermute | solution.py:191
  14.2 4.5 %collective-permute-start.8 = (bf16[4,128,128]{2,1,0:T(8,128)(2,1)S(1)}, bf16[4,128,128]{2,1,0:T(8,128)(2,1)S(1)}, u32[]{:S(2)}, u32[]{:S(2)}) collective-permute-start(bf16[4,128,128]{2,1,0:T(8,128)(2,1)S(1)} %collective-permute-done.refs_0_), channel_id=1, source_target_pairs={{0,1},{1,0},{2,3},{3,2},{4,5},{5,4},{6,7},{7,6},{8,9},{9,8},{10,11... | collective-permute-start | bytes 393224 | tf_op jit(solution)/shard_map/ppermute | solution.py:191
  16.8 4.4 %collective-permute-start.10 = (bf16[4,128,128]{2,1,0:T(8,128)(2,1)S(1)}, bf16[4,128,128]{2,1,0:T(8,128)(2,1)S(1)}, u32[]{:S(2)}, u32[]{:S(2)}) collective-permute-start(bf16[4,128,128]{2,1,0:T(8,128)(2,1)S(1)} %collective-permute-done.9.refs_2_), channel_id=1, source_target_pairs={{0,1},{1,0},{2,3},{3,2},{4,5},{5,4},{6,7},{7,6},{8,9},{9,8},{10,11... | collective-permute-start | bytes 393224 | tf_op jit(solution)/shard_map/ppermute | solution.py:191
  16.8 8.3 %collective-permute-start.5 = (bf16[528,128]{1,0:T(8,128)(2,1)S(1)}, bf16[528,128]{1,0:T(8,128)(2,1)S(1)}, u32[]{:S(2)}, u32[]{:S(2)}) collective-permute-start(bf16[528,128]{1,0:T(8,128)(2,1)S(1)} %get-tuple-element.35), channel_id=1, source_target_pairs={{0,8},{4,12},{8,0},{12,4},{16,24},{20,28},{24,16},{28,20},{1,9},{5... | collective-permute-start | bytes 405512 | tf_op jit(solution)/shard_map/ppermute | solution.py:191
  18.8 9.2 %collective-permute-start.6 = (bf16[528,128]{1,0:T(8,128)(2,1)S(1)}, bf16[528,128]{1,0:T(8,128)(2,1)S(1)}, u32[]{:S(2)}, u32[]{:S(2)}) collective-permute-start(bf16[528,128]{1,0:T(8,128)(2,1)S(1)} %get-tuple-element.36), channel_id=1, source_target_pairs={{0,12},{4,8},{8,4},{12,0},{16,28},{20,24},{24,20},{28,16},{1,13},{... | collective-permute-start | bytes 405512 | tf_op jit(solution)/shard_map/ppermute | solution.py:191
  21.6 7.8 %collective-permute-start.11 = (bf16[528,128]{1,0:T(8,128)(2,1)S(1)}, bf16[528,128]{1,0:T(8,128)(2,1)S(1)}, u32[]{:S(2)}, u32[]{:S(2)}) collective-permute-start(bf16[528,128]{1,0:T(8,128)(2,1)S(1)} %get-tuple-element.40), channel_id=1, source_target_pairs={{0,4},{4,0},{8,12},{12,8},{16,20},{20,16},{24,28},{28,24},{1,5},{5... | collective-permute-start | bytes 405512 | tf_op jit(solution)/shard_map/ppermute | solution.py:191
  23.1 6.8 %collective-permute-start.12 = (bf16[528,128]{1,0:T(8,128)(2,1)S(1)}, bf16[528,128]{1,0:T(8,128)(2,1)S(1)}, u32[]{:S(2)}, u32[]{:S(2)}) collective-permute-start(bf16[528,128]{1,0:T(8,128)(2,1)S(1)} %get-tuple-element.41), channel_id=1, source_target_pairs={{0,8},{4,12},{8,0},{12,4},{16,24},{20,28},{24,16},{28,20},{1,9},{5... | collective-permute-start | bytes 405512 | tf_op jit(solution)/shard_map/ppermute | solution.py:191
  23.1 10.6 %collective-permute-start.13 = (bf16[528,128]{1,0:T(8,128)(2,1)S(1)}, bf16[528,128]{1,0:T(8,128)(2,1)S(1)}, u32[]{:S(2)}, u32[]{:S(2)}) collective-permute-start(bf16[528,128]{1,0:T(8,128)(2,1)S(1)} %get-tuple-element.42), channel_id=1, source_target_pairs={{0,12},{4,8},{8,4},{12,0},{16,28},{20,24},{24,20},{28,16},{1,13},{... | collective-permute-start | bytes 405512 | tf_op jit(solution)/shard_map/ppermute | solution.py:191

commit v5 on v4

--- a/solution.py
+++ b/solution.py
@@ -191,14 +191,17 @@
     return lax.ppermute(value, axis, [(at, at ^ bits) for at in range(count)])
 
 
-def shared(block, after=None):
+def after(value, *others):
+    return lax.optimization_barrier((value, *others))[0]
+
+
+def shared(block, *others):
     held, order, bits = [block], [0], lax.axis_size("aux") // 2
     while bits:
         held += [flip(one, "aux", bits) for one in held]
         order += [at ^ bits for at in order]
         bits //= 2
-        if after is not None:
-            *held, after = lax.optimization_barrier((*held, after))
+        held = [after(one, *others) for one in held]
     return [held[order.index(at)] for at in range(len(held))]
 
 
@@ -235,8 +238,7 @@
         compiler_params=params,
         name="pick",
     )(*in_hbm(pair_list, occ_slot.reshape(1, -1), coef))
-    near_blocks = shared(blocks, sent_coef)
-    far_block, near_coef, sent_coef = lax.optimization_barrier((far_block, near_coef, sent_coef))
+    near_blocks = [blocks] + [flip(blocks, "aux", j) for j in range(1, aux_count)]
     far_coef = flip(sent_coef, "shell", group)
 
     def transformed(name, coefs, quad):
@@ -248,11 +250,16 @@
             compiler_params=params,
             name=name,
         )(coefs, *quad)
+        return pieces
+
+    def relayed(pieces):
         return [pieces[0]] + [flip(pieces[f], "shell", f) for f in range(1, group)]
 
     near = transformed("near_blocks", near_coef, near_blocks)
-    far_blocks = shared(far_block)
-    far = transformed("far_blocks", far_coef, far_blocks)
+    far_block = after(far_block, near[0])
+    near = relayed(near)
+    far_blocks = shared(far_block, far_coef, *near[1:3])
+    far = relayed(transformed("far_blocks", after(far_coef, *near), far_blocks))
     return pl.pallas_call(
         functools.partial(collect_kernel, pairs_dev),
         out_shape=jax.ShapeDtypeStruct(

time: 36.4 us -> 36.9 us (1.014)
  starting transfers between devices: 14.7 us -> 16.7 us
  waiting for transfers between devices: 16.3 us -> 14.5 us
    ppermute x14, starting transfers between devices: 14.7 us -> 16.7 us  [flip(): return lax.ppermute(value, axis, [(at, at ^ bits) for at in range(count)])]
    ppermute x14, waiting for transfers between devices: 16.3 us -> 14.5 us  [flip(): return lax.ppermute(value, axis, [(at, at ^ bits) for at in range(count)])]
  transfers between devices with their start and end apart: 14 -> 14, of which waited for: 7 -> 7; matrix products, arithmetic and copies ran while one was open for 0% -> 0% of each run, Pallas kernels for 7% -> 6%
where the time goes in v5:
time: 36.9 us; the launch traced here: 36.4 us
  starting transfers between devices  16.7 us (45%)
  waiting for transfers between devices  14.5 us (39%)
  Pallas kernels  5.12 us (14%)
    ppermute x14, starting transfers between devices, flip(): return lax.ppermute(value, axis, [(at, at ^ bits) for at in range(count)])  16.7 us
    ppermute x14, waiting for transfers between devices, flip(): return lax.ppermute(value, axis, [(at, at ^ bits) for at in range(count)])  14.5 us
    pallas_call x1, Pallas kernels, exchanged_inputs(): pl.pallas_call(functools.partial(collect_kernel, pairs_dev), out_shape=ja...  2.51 us
    pallas_call x1, Pallas kernels, exchanged_inputs(): pl.pallas_call(functools.partial(pick_kernel, group, occ_local, aux_count...  2.03 us
  transfers between devices with their start and end apart: 14, of which 7 were waited for; matrix products, arithmetic and copies ran while one was open for 0% of the time, Pallas kernels for 6%

profile of v5, /device:TPU:0, one launch (start us, length us, event | category | flops | bytes accessed | tf_op | source)
XLA Modules:
  0.0 36.4 jit_solution(1710662478075460726)
XLA Ops:
  0.0 2.4 %collective-permute-start.2 = (bf16[4,128,128]{2,1,0:T(8,128)(2,1)}, bf16[4,128,128]{2,1,0:T(8,128)(2,1)S(1)}, u32[]{:S(2)}, u32[]{:S(2)}) collective-permute-start(bf16[4,128,128]{2,1,0:T(8,128)(2,1)} %bitcast.2), channel_id=1, source_target_pairs={{0,3},{1,2},{2,1},{3,0},{4,7},{5,6},{6,5},{7,4},{8,11},{9,10},{10,... | collective-permute-start | bytes 393224 | tf_op jit(solution)/shard_map/ppermute | solution.py:191
  2.4 0.6 %collective-permute-start.1 = (bf16[4,128,128]{2,1,0:T(8,128)(2,1)}, bf16[4,128,128]{2,1,0:T(8,128)(2,1)S(1)}, u32[]{:S(2)}, u32[]{:S(2)}) collective-permute-start(bf16[4,128,128]{2,1,0:T(8,128)(2,1)} %bitcast.3), channel_id=1, source_target_pairs={{0,2},{1,3},{2,0},{3,1},{4,6},{5,7},{6,4},{7,5},{8,10},{9,11},{10,... | collective-permute-start | bytes 393224 | tf_op jit(solution)/shard_map/ppermute | solution.py:191
  3.0 0.1 collective-permute-start
  3.1 2.8 %collective-permute-start.7 = (bf16[4,128,128]{2,1,0:T(8,128)(2,1)}, bf16[4,128,128]{2,1,0:T(8,128)(2,1)S(1)}, u32[]{:S(2)}, u32[]{:S(2)}) collective-permute-start(bf16[4,128,128]{2,1,0:T(8,128)(2,1)} %bitcast.5), channel_id=1, source_target_pairs={{0,16},{4,20},{8,24},{12,28},{16,0},{20,4},{24,8},{28,12},{1,17},{... | collective-permute-start | bytes 393224 | tf_op jit(solution)/shard_map/ppermute | solution.py:191
  5.9 2.0 %pick.1 = (bf16[144,512]{1,0:T(8,128)(2,1)S(1)}, bf16[144,512]{1,0:T(8,128)(2,1)S(1)}) custom-call(s32[4,3]{1,0:T(4,128)} %pairs_in.1, s32[1,128]{1,0:T(1,128)} %bitcast.7, bf16[512,1024]{1,0:T(8,128)(2,1)} %coef_in.1), custom_call_target="tpu_custom_call" | custom-call | tf_op jit(solution)/shard_map/pick/pallas_call | solution.py:227
  7.9 0.2 collective-permute-start.6
  8.1 1.4 %collective-permute-done.1.refs_2_ = bf16[4,128,128]{2,1,0:T(8,128)(2,1)S(1)} collective-permute-done((bf16[4,128,128]{2,1,0:T(8,128)(2,1)}, bf16[4,128,128]{2,1,0:T(8,128)(2,1)S(1)}, u32[]{:S(2)}, u32[]{:S(2)}) %collective-permute-start.1) | collective-permute-done | bytes 131104 | tf_op jit(solution)/shard_map/ppermute | solution.py:191
  9.5 0.3 near_blocks.1
  9.8 2.3 %collective-permute-start.3 = (bf16[528,128]{1,0:T(8,128)(2,1)S(1)}, bf16[528,128]{1,0:T(8,128)(2,1)S(1)}, u32[]{:S(2)}, u32[]{:S(2)}) collective-permute-start(bf16[528,128]{1,0:T(8,128)(2,1)S(1)} %get-tuple-element.25), channel_id=1, source_target_pairs={{0,4},{4,0},{8,12},{12,8},{16,20},{20,16},{24,28},{28,24},{1,5},{5... | collective-permute-start | bytes 405512 | tf_op jit(solution)/shard_map/ppermute | solution.py:191
  12.1 1.6 %collective-permute-start.4 = (bf16[528,128]{1,0:T(8,128)(2,1)S(1)}, bf16[528,128]{1,0:T(8,128)(2,1)S(1)}, u32[]{:S(2)}, u32[]{:S(2)}) collective-permute-start(bf16[528,128]{1,0:T(8,128)(2,1)S(1)} %get-tuple-element.26), channel_id=1, source_target_pairs={{0,8},{4,12},{8,0},{12,4},{16,24},{20,28},{24,16},{28,20},{1,9},{5... | collective-permute-start | bytes 405512 | tf_op jit(solution)/shard_map/ppermute | solution.py:191
  13.7 2.9 %collective-permute-done.7.refs_0_ = bf16[4,128,128]{2,1,0:T(8,128)(2,1)S(1)} collective-permute-done((bf16[4,128,128]{2,1,0:T(8,128)(2,1)}, bf16[4,128,128]{2,1,0:T(8,128)(2,1)S(1)}, u32[]{:S(2)}, u32[]{:S(2)}) %collective-permute-start.7) | collective-permute-done | bytes 131104 | tf_op jit(solution)/shard_map/ppermute | solution.py:191
  16.6 1.8 %collective-permute-start.9 = (bf16[4,128,128]{2,1,0:T(8,128)(2,1)S(1)}, bf16[4,128,128]{2,1,0:T(8,128)(2,1)S(1)}, u32[]{:S(2)}, u32[]{:S(2)}) collective-permute-start(bf16[4,128,128]{2,1,0:T(8,128)(2,1)S(1)} %collective-permute-done.7.refs_0_), channel_id=1, source_target_pairs={{0,2},{1,3},{2,0},{3,1},{4,6},{5,7},{6,4},{7,5},{8,10},{9,11},{10,... | collective-permute-start | bytes 393224 | tf_op jit(solution)/shard_map/ppermute | solution.py:191
  18.4 0.9 %collective-permute-start.5 = (bf16[528,128]{1,0:T(8,128)(2,1)S(1)}, bf16[528,128]{1,0:T(8,128)(2,1)S(1)}, u32[]{:S(2)}, u32[]{:S(2)}) collective-permute-start(bf16[528,128]{1,0:T(8,128)(2,1)S(1)} %get-tuple-element.27), channel_id=1, source_target_pairs={{0,12},{4,8},{8,4},{12,0},{16,28},{20,24},{24,20},{28,16},{1,13},{... | collective-permute-start | bytes 405512 | tf_op jit(solution)/shard_map/ppermute | solution.py:191
  19.3 2.8 %collective-permute-done.4.refs_2_ = bf16[528,128]{1,0:T(8,128)(2,1)S(1)} collective-permute-done((bf16[528,128]{1,0:T(8,128)(2,1)S(1)}, bf16[528,128]{1,0:T(8,128)(2,1)S(1)}, u32[]{:S(2)}, u32[]{:S(2)}) %collective-permute-start.4) | collective-permute-done | bytes 135200 | tf_op jit(solution)/shard_map/ppermute | solution.py:191
  22.1 0.5 %collective-permute-start.10 = (bf16[4,128,128]{2,1,0:T(8,128)(2,1)S(1)}, bf16[4,128,128]{2,1,0:T(8,128)(2,1)S(1)}, u32[]{:S(2)}, u32[]{:S(2)}) collective-permute-start(bf16[4,128,128]{2,1,0:T(8,128)(2,1)S(1)} %collective-permute-done.9.refs_2_), channel_id=1, source_target_pairs={{0,1},{1,0},{2,3},{3,2},{4,5},{5,4},{6,7},{7,6},{8,9},{9,8},{10,11... | collective-permute-start | bytes 393224 | tf_op jit(solution)/shard_map/ppermute | solution.py:191
  22.6 1.7 %collective-permute-done.5.refs_3_ = bf16[528,128]{1,0:T(8,128)(2,1)S(1)} collective-permute-done((bf16[528,128]{1,0:T(8,128)(2,1)S(1)}, bf16[528,128]{1,0:T(8,128)(2,1)S(1)}, u32[]{:S(2)}, u32[]{:S(2)}) %collective-permute-start.5) | collective-permute-done | bytes 135200 | tf_op jit(solution)/shard_map/ppermute | solution.py:191
  24.3 0.3 far_blocks.1
  24.6 1.6 %collective-permute-start.11 = (bf16[528,128]{1,0:T(8,128)(2,1)S(1)}, bf16[528,128]{1,0:T(8,128)(2,1)S(1)}, u32[]{:S(2)}, u32[]{:S(2)}) collective-permute-start(bf16[528,128]{1,0:T(8,128)(2,1)S(1)} %get-tuple-element.38), channel_id=1, source_target_pairs={{0,4},{4,0},{8,12},{12,8},{16,20},{20,16},{24,28},{28,24},{1,5},{5... | collective-permute-start | bytes 405512 | tf_op jit(solution)/shard_map/ppermute | solution.py:191
  26.1 0.1 collective-permute-start.12
  26.2 1.9 %collective-permute-start.13 = (bf16[528,128]{1,0:T(8,128)(2,1)S(1)}, bf16[528,128]{1,0:T(8,128)(2,1)S(1)}, u32[]{:S(2)}, u32[]{:S(2)}) collective-permute-start(bf16[528,128]{1,0:T(8,128)(2,1)S(1)} %get-tuple-element.40), channel_id=1, source_target_pairs={{0,12},{4,8},{8,4},{12,0},{16,28},{20,24},{24,20},{28,16},{1,13},{... | collective-permute-start | bytes 405512 | tf_op jit(solution)/shard_map/ppermute | solution.py:191
  28.1 2.1 %collective-permute-done.11.refs_5_ = bf16[528,128]{1,0:T(8,128)(2,1)S(1)} collective-permute-done((bf16[528,128]{1,0:T(8,128)(2,1)S(1)}, bf16[528,128]{1,0:T(8,128)(2,1)S(1)}, u32[]{:S(2)}, u32[]{:S(2)}) %collective-permute-start.11) | collective-permute-done | bytes 135200 | tf_op jit(solution)/shard_map/ppermute | solution.py:191
  30.3 1.6 %collective-permute-done.12.refs_6_ = bf16[528,128]{1,0:T(8,128)(2,1)S(1)} collective-permute-done((bf16[528,128]{1,0:T(8,128)(2,1)S(1)}, bf16[528,128]{1,0:T(8,128)(2,1)S(1)}, u32[]{:S(2)}, u32[]{:S(2)}) %collective-permute-start.12) | collective-permute-done | bytes 135200 | tf_op jit(solution)/shard_map/ppermute | solution.py:191
  31.8 2.1 %collective-permute-done.13.refs_7_ = bf16[528,128]{1,0:T(8,128)(2,1)S(1)} collective-permute-done((bf16[528,128]{1,0:T(8,128)(2,1)S(1)}, bf16[528,128]{1,0:T(8,128)(2,1)S(1)}, u32[]{:S(2)}, u32[]{:S(2)}) %collective-permute-start.13) | collective-permute-done | bytes 135200 | tf_op jit(solution)/shard_map/ppermute | solution.py:191
  33.9 2.5 %collect.1 = bf16[32,4,4096]{2,1,0:T(4,128)(2,1)} custom-call(bf16[4,4]{1,0:T(4,128)(2,1)} %metric_in.1, bf16[528,128]{1,0:T(8,128)(2,1)S(1)} %get-tuple-element.24.refs_0_, bf16[528,128]{1,0:T(8,128)(2,1)S(1)} %collective-permute-done.3.refs_1_, bf16[528,128]{1,0:T(8,128)(2,1)S(1)} %collective-permute-done.4.refs_2_, ...), custom_call_target="tpu_custom_call" | custom-call | tf_op jit(solution)/shard_map/collect/pallas_call | solution.py:263
  (10 shorter events, 0.0 us)
Async XLA Ops:
  0.0 8.1 %collective-permute-start.2 = (bf16[4,128,128]{2,1,0:T(8,128)(2,1)}, bf16[4,128,128]{2,1,0:T(8,128)(2,1)S(1)}, u32[]{:S(2)}, u32[]{:S(2)}) collective-permute-start(bf16[4,128,128]{2,1,0:T(8,128)(2,1)} %bitcast.2), channel_id=1, source_target_pairs={{0,3},{1,2},{2,1},{3,0},{4,7},{5,6},{6,5},{7,4},{8,11},{9,10},{10,... | collective-permute-start | bytes 393224 | tf_op jit(solution)/shard_map/ppermute | solution.py:191
  2.4 7.1 %collective-permute-start.1 = (bf16[4,128,128]{2,1,0:T(8,128)(2,1)}, bf16[4,128,128]{2,1,0:T(8,128)(2,1)S(1)}, u32[]{:S(2)}, u32[]{:S(2)}) collective-permute-start(bf16[4,128,128]{2,1,0:T(8,128)(2,1)} %bitcast.3), channel_id=1, source_target_pairs={{0,2},{1,3},{2,0},{3,1},{4,6},{5,7},{6,4},{7,5},{8,10},{9,11},{10,... | collective-permute-start | bytes 393224 | tf_op jit(solution)/shard_map/ppermute | solution.py:191
  3.0 6.5 %collective-permute-start = (bf16[4,128,128]{2,1,0:T(8,128)(2,1)}, bf16[4,128,128]{2,1,0:T(8,128)(2,1)S(1)}, u32[]{:S(2)}, u32[]{:S(2)}) collective-permute-start(bf16[4,128,128]{2,1,0:T(8,128)(2,1)} %bitcast.4), channel_id=1, source_target_pairs={{0,1},{1,0},{2,3},{3,2},{4,5},{5,4},{6,7},{7,6},{8,9},{9,8},{10,11... | collective-permute-start | bytes 393224 | tf_op jit(solution)/shard_map/ppermute | solution.py:191
  3.1 13.5 %collective-permute-start.7 = (bf16[4,128,128]{2,1,0:T(8,128)(2,1)}, bf16[4,128,128]{2,1,0:T(8,128)(2,1)S(1)}, u32[]{:S(2)}, u32[]{:S(2)}) collective-permute-start(bf16[4,128,128]{2,1,0:T(8,128)(2,1)} %bitcast.5), channel_id=1, source_target_pairs={{0,16},{4,20},{8,24},{12,28},{16,0},{20,4},{24,8},{28,12},{1,17},{... | collective-permute-start | bytes 393224 | tf_op jit(solution)/shard_map/ppermute | solution.py:191
  5.9 3.6 %copy-start = (bf16[4,128,1,128]{3,1,2,0:T(8,128)(2,1)S(1)}, bf16[4,128,1,128]{3,1,2,0:T(8,128)(2,1)}, u32[]{:S(2)}) copy-start(bf16[4,128,1,128]{3,1,2,0:T(8,128)(2,1)} %param.5) | copy-start | bytes 393220
  7.9 11.3 %collective-permute-start.6 = (bf16[144,512]{1,0:T(8,128)(2,1)S(1)}, bf16[144,512]{1,0:T(8,128)(2,1)S(1)}, u32[]{:S(2)}, u32[]{:S(2)}) collective-permute-start(bf16[144,512]{1,0:T(8,128)(2,1)S(1)} %get-tuple-element.28), channel_id=1, source_target_pairs={{0,16},{4,20},{8,24},{12,28},{16,0},{20,4},{24,8},{28,12},{1,17},{... | collective-permute-start | bytes 442376 | tf_op jit(solution)/shard_map/ppermute | solution.py:191
  9.8 9.5 %collective-permute-start.3 = (bf16[528,128]{1,0:T(8,128)(2,1)S(1)}, bf16[528,128]{1,0:T(8,128)(2,1)S(1)}, u32[]{:S(2)}, u32[]{:S(2)}) collective-permute-start(bf16[528,128]{1,0:T(8,128)(2,1)S(1)} %get-tuple-element.25), channel_id=1, source_target_pairs={{0,4},{4,0},{8,12},{12,8},{16,20},{20,16},{24,28},{28,24},{1,5},{5... | collective-permute-start | bytes 405512 | tf_op jit(solution)/shard_map/ppermute | solution.py:191
  12.1 10.0 %collective-permute-start.4 = (bf16[528,128]{1,0:T(8,128)(2,1)S(1)}, bf16[528,128]{1,0:T(8,128)(2,1)S(1)}, u32[]{:S(2)}, u32[]{:S(2)}) collective-permute-start(bf16[528,128]{1,0:T(8,128)(2,1)S(1)} %get-tuple-element.26), channel_id=1, source_target_pairs={{0,8},{4,12},{8,0},{12,4},{16,24},{20,28},{24,16},{28,20},{1,9},{5... | collective-permute-start | bytes 405512 | tf_op jit(solution)/shard_map/ppermute | solution.py:191
  16.6 5.5 %collective-permute-start.9 = (bf16[4,128,128]{2,1,0:T(8,128)(2,1)S(1)}, bf16[4,128,128]{2,1,0:T(8,128)(2,1)S(1)}, u32[]{:S(2)}, u32[]{:S(2)}) collective-permute-start(bf16[4,128,128]{2,1,0:T(8,128)(2,1)S(1)} %collective-permute-done.7.refs_0_), channel_id=1, source_target_pairs={{0,2},{1,3},{2,0},{3,1},{4,6},{5,7},{6,4},{7,5},{8,10},{9,11},{10,... | collective-permute-start | bytes 393224 | tf_op jit(solution)/shard_map/ppermute | solution.py:191
  18.4 5.9 %collective-permute-start.5 = (bf16[528,128]{1,0:T(8,128)(2,1)S(1)}, bf16[528,128]{1,0:T(8,128)(2,1)S(1)}, u32[]{:S(2)}, u32[]{:S(2)}) collective-permute-start(bf16[528,128]{1,0:T(8,128)(2,1)S(1)} %get-tuple-element.27), channel_id=1, source_target_pairs={{0,12},{4,8},{8,4},{12,0},{16,28},{20,24},{24,20},{28,16},{1,13},{... | collective-permute-start | bytes 405512 | tf_op jit(solution)/shard_map/ppermute | solution.py:191
  22.1 2.2 %collective-permute-start.8 = (bf16[4,128,128]{2,1,0:T(8,128)(2,1)S(1)}, bf16[4,128,128]{2,1,0:T(8,128)(2,1)S(1)}, u32[]{:S(2)}, u32[]{:S(2)}) collective-permute-start(bf16[4,128,128]{2,1,0:T(8,128)(2,1)S(1)} %collective-permute-done.7.refs_0_), channel_id=1, source_target_pairs={{0,1},{1,0},{2,3},{3,2},{4,5},{5,4},{6,7},{7,6},{8,9},{9,8},{10,11... | collective-permute-start | bytes 393224 | tf_op jit(solution)/shard_map/ppermute | solution.py:191
  22.1 2.2 %collective-permute-start.10 = (bf16[4,128,128]{2,1,0:T(8,128)(2,1)S(1)}, bf16[4,128,128]{2,1,0:T(8,128)(2,1)S(1)}, u32[]{:S(2)}, u32[]{:S(2)}) collective-permute-start(bf16[4,128,128]{2,1,0:T(8,128)(2,1)S(1)} %collective-permute-done.9.refs_2_), channel_id=1, source_target_pairs={{0,1},{1,0},{2,3},{3,2},{4,5},{5,4},{6,7},{7,6},{8,9},{9,8},{10,11... | collective-permute-start | bytes 393224 | tf_op jit(solution)/shard_map/ppermute | solution.py:191
  24.6 5.7 %collective-permute-start.11 = (bf16[528,128]{1,0:T(8,128)(2,1)S(1)}, bf16[528,128]{1,0:T(8,128)(2,1)S(1)}, u32[]{:S(2)}, u32[]{:S(2)}) collective-permute-start(bf16[528,128]{1,0:T(8,128)(2,1)S(1)} %get-tuple-element.38), channel_id=1, source_target_pairs={{0,4},{4,0},{8,12},{12,8},{16,20},{20,16},{24,28},{28,24},{1,5},{5... | collective-permute-start | bytes 405512 | tf_op jit(solution)/shard_map/ppermute | solution.py:191
  26.1 5.7 %collective-permute-start.12 = (bf16[528,128]{1,0:T(8,128)(2,1)S(1)}, bf16[528,128]{1,0:T(8,128)(2,1)S(1)}, u32[]{:S(2)}, u32[]{:S(2)}) collective-permute-start(bf16[528,128]{1,0:T(8,128)(2,1)S(1)} %get-tuple-element.39), channel_id=1, source_target_pairs={{0,8},{4,12},{8,0},{12,4},{16,24},{20,28},{24,16},{28,20},{1,9},{5... | collective-permute-start | bytes 405512 | tf_op jit(solution)/shard_map/ppermute | solution.py:191
  26.2 7.6 %collective-permute-start.13 = (bf16[528,128]{1,0:T(8,128)(2,1)S(1)}, bf16[528,128]{1,0:T(8,128)(2,1)S(1)}, u32[]{:S(2)}, u32[]{:S(2)}) collective-permute-start(bf16[528,128]{1,0:T(8,128)(2,1)S(1)} %get-tuple-element.40), channel_id=1, source_target_pairs={{0,12},{4,8},{8,4},{12,0},{16,28},{20,24},{24,20},{28,16},{1,13},{... | collective-permute-start | bytes 405512 | tf_op jit(solution)/shard_map/ppermute | solution.py:191

commit v6 on v0

--- a/solution.py
+++ b/solution.py
@@ -1,12 +1,16 @@
+import functools
+
 import jax
 import jax.numpy as jnp
 from jax import lax
-from jax.sharding import PartitionSpec as P
+from jax.experimental import pallas as pl
+from jax.experimental.pallas import tpu as pltpu
+from jax.sharding import Mesh, PartitionSpec as P
 
 BS = 128
 
 
-def per_device(integrals, pair_list, coef, metric, occ_slot):
+def relayed_half_blocks(integrals, pair_list, coef, metric, occ_slot):
     pairs_dev = pair_list.shape[0]
     rows_local = coef.shape[0]
     occ_count = coef.shape[1]
@@ -59,12 +63,297 @@
     return result.reshape(result.shape[0], result.shape[1], block_count * BS).astype(jnp.bfloat16)
 
 
+def targets_of(slot_row, block_total, occ_count):
+    width = occ_count // block_total
+    spread = (
+        lax.broadcasted_iota(jnp.int32, (block_total, occ_count), 1) // width
+        == lax.broadcasted_iota(jnp.int32, (block_total, occ_count), 0)
+    ).astype(jnp.bfloat16)
+    slots = jnp.broadcast_to(slot_row, (8, block_total)).astype(jnp.float32)
+    target = jnp.dot(slots.astype(jnp.bfloat16), spread, preferred_element_type=jnp.float32)
+    return target.astype(jnp.int32)[:1] * width + (
+        lax.broadcasted_iota(jnp.int32, (1, occ_count), 1) % width
+    )
+
+
+def load_all(copies, sems):
+    loads = [
+        pltpu.make_async_copy(source, target, sems.at[at])
+        for at, (source, target) in enumerate(copies)
+    ]
+    for load in loads:
+        load.start()
+    return loads
+
+
+def half_kernel(
+    occ_local,
+    aux_count,
+    pairs_in,
+    slot_in,
+    coef_in,
+    blocks_in,
+    near,
+    far_coef,
+    pairs,
+    slot_row,
+    coef,
+    blocks,
+    sems,
+):
+    loads = load_all(
+        ((slot_in, slot_row), (pairs_in, pairs), (coef_in, coef), (blocks_in, blocks)), sems
+    )
+    pairs_dev = pairs.shape[0]
+    blocks_dev = coef.shape[0] // BS
+    occ_count = coef.shape[1]
+    devices = near.shape[0]
+    near_rows = devices * occ_local
+    far_rows = far_coef.shape[0] - 16
+    half, mine = lax.axis_index("half"), lax.axis_index("aux")
+
+    near_wanted = half * near_rows + lax.broadcasted_iota(jnp.int32, (near_rows, 1), 0)
+    row = lax.broadcasted_iota(jnp.int32, (far_rows, 1), 0)
+    far_wanted = (1 - half) * near_rows + (
+        (row // occ_local * aux_count + mine) * occ_local + row % occ_local
+    )
+    loads[0].wait()
+    target = targets_of(slot_row[...], slot_row.shape[1], occ_count)
+    near_pick = (near_wanted == target).astype(jnp.bfloat16)
+    far_pick = (far_wanted == target).astype(jnp.bfloat16)
+    for load in loads[1:]:
+        load.wait()
+    lane = lax.broadcasted_iota(jnp.int32, (1, BS), 1)
+    code = jnp.zeros((1, BS), jnp.int32)
+    rows, live = [], []
+    for k in range(pairs_dev):
+        code = jnp.where(lane == k, pairs[k, 0] % 128, code)
+        code = jnp.where(lane == pairs_dev + k, pairs[k, 0] // 128, code)
+        start = pl.multiple_of(lax.rem(pairs[k, 1], blocks_dev) * BS, BS)
+        rows.append(coef[pl.ds(start, BS), :])
+        live.append((pairs[k, 2] == 1).astype(jnp.bfloat16))
+    code = jnp.broadcast_to(code.astype(jnp.float32), (16, BS)).astype(jnp.bfloat16)
+    rows = jnp.concatenate(rows, axis=0)
+    contract = (((1,), (1,)), ((), ()))
+    ordered = lax.dot_general(far_pick, rows, contract, preferred_element_type=jnp.float32)
+    ordered = ordered.astype(jnp.bfloat16)
+    for k in range(pairs_dev):
+        far_coef[:far_rows, k * BS : (k + 1) * BS] = ordered[:, k * BS : (k + 1) * BS] * live[k]
+        far_coef[far_rows:, k * BS : (k + 1) * BS] = code
+    ordered = lax.dot_general(near_pick, rows, contract, preferred_element_type=jnp.float32)
+    ordered = ordered.astype(jnp.bfloat16)
+    for k in range(pairs_dev):
+        block = jnp.dot(
+            ordered[:, k * BS : (k + 1) * BS], blocks[k], preferred_element_type=jnp.float32
+        )
+        near[:, k * occ_local : (k + 1) * occ_local, :] = (
+            block.astype(jnp.bfloat16) * live[k]
+        ).reshape(devices, occ_local, BS)
+    near[:, pairs_dev * occ_local :, :] = jnp.broadcast_to(code[None], (devices, 16, BS))
+
+
+def far_kernel(aux_count, coefs, *refs):
+    *blocks, out = refs
+    pairs_dev = blocks[0].shape[0]
+    rows = coefs.shape[0] - 16
+    places = out.shape[0]
+    occ_local = rows // places
+    mine = lax.axis_index("aux")
+    for k in range(pairs_dev):
+        left = coefs[:rows, k * BS : (k + 1) * BS]
+        for j in range(0, aux_count, 2):
+            right = jnp.concatenate([blocks[j][k], blocks[j + 1][k]], axis=1)
+            half = jnp.dot(left, right, preferred_element_type=jnp.float32).astype(jnp.bfloat16)
+            for side in range(2):
+                at = k * aux_count + jnp.bitwise_xor(mine, j + side)
+                start = pl.multiple_of(at * occ_local, occ_local)
+                out[:, pl.ds(start, occ_local), :] = half[
+                    :, side * BS : (side + 1) * BS
+                ].reshape(places, occ_local, BS)
+    out[:, pairs_dev * aux_count * occ_local :, :] = jnp.broadcast_to(
+        coefs[rows:, :BS][None], (places, 16, BS)
+    )
+
+
+def load_codes(received, step, codes_v, codes, sem):
+    tile = received.shape[1] - 16
+    for at in range(received.shape[0] // step):
+        digits = received[at * step, tile:, :].astype(jnp.float32).astype(jnp.int32)
+        codes_v[at : at + 1, :] = digits[:1]
+    load = pltpu.make_async_copy(codes_v, codes, sem)
+    load.start()
+    return load
+
+
+def near_sum_kernel(aux_count, received, total, codes_v, codes, sem):
+    load = load_codes(received, aux_count, codes_v, codes, sem)
+    occ_local = total.shape[1] // aux_count
+    pairs_dev = (received.shape[1] - 16) // occ_local
+    total[...] = jnp.zeros_like(total)
+    load.wait()
+    for at in range(received.shape[0] // aux_count):
+        for k in range(pairs_dev):
+            r = codes[at, k] + 128 * codes[at, pairs_dev + k]
+            for p in range(aux_count):
+                part = received[at * aux_count + p, k * occ_local : (k + 1) * occ_local, :]
+                total[r, p * occ_local : (p + 1) * occ_local, :] += part.astype(jnp.float32)
+
+
+def collect_kernel(metric_in, total_in, received, out, total, metric, codes_v, codes, sems):
+    (metric_load,) = load_all(((metric_in, metric),), sems)
+    load = load_codes(received, 1, codes_v, codes, sems.at[1])
+    occ_local, aux_count = out.shape[:2]
+    rows = occ_local * aux_count
+    pairs_dev = (received.shape[1] - 16) // rows
+    load.wait()
+    for at in range(received.shape[0]):
+        for k in range(pairs_dev):
+            r = codes[at, k] + 128 * codes[at, pairs_dev + k]
+            total[r] += received[at, k * rows : (k + 1) * rows, :].astype(jnp.float32)
+    metric_load.wait()
+
+    row = lax.broadcasted_iota(jnp.int32, (rows, rows), 0)
+    column = lax.broadcasted_iota(jnp.int32, (rows, rows), 1)
+    left = (
+        lax.broadcasted_iota(jnp.int32, (rows, aux_count), 0) % aux_count
+        == lax.broadcasted_iota(jnp.int32, (rows, aux_count), 1)
+    ).astype(jnp.bfloat16)
+    right = (
+        lax.broadcasted_iota(jnp.int32, (aux_count, rows), 1) // occ_local
+        == lax.broadcasted_iota(jnp.int32, (aux_count, rows), 0)
+    ).astype(jnp.bfloat16)
+    factor = jnp.dot(left, metric[...], preferred_element_type=jnp.float32).astype(jnp.bfloat16)
+    factor = jnp.dot(factor, right, preferred_element_type=jnp.float32)
+    mix = jnp.where(row // aux_count == column % occ_local, factor, 0.0).astype(jnp.bfloat16)
+    for r in range(0, total.shape[0], 2):
+        summed = jnp.concatenate([total[r], total[r + 1]], axis=1).astype(jnp.bfloat16)
+        mixed = jnp.dot(mix, summed, preferred_element_type=jnp.float32)
+        out[:, :, r * BS : (r + 2) * BS] = mixed.reshape(
+            occ_local, aux_count, 2 * BS
+        ).astype(jnp.bfloat16)
+
+
+def flip(value, axis, bits):
+    count = lax.axis_size(axis)
+    return lax.ppermute(value, axis, [(at, at ^ bits) for at in range(count)])
+
+
+def after(value, *others):
+    return lax.optimization_barrier((value, *others))[0]
+
+
+def shared(block):
+    held, order, bits = [block], [0], lax.axis_size("aux") // 2
+    while bits:
+        held += [flip(one, "aux", bits) for one in held]
+        order += [at ^ bits for at in order]
+        bits //= 2
+    return [held[order.index(at)] for at in range(len(held))]
+
+
+def in_hbm(*operands):
+    return [pltpu.with_memory_space_constraint(operand, pltpu.HBM) for operand in operands]
+
+
+def crossed_inputs(integrals, pair_list, coef, metric, occ_slot):
+    pairs_dev = pair_list.shape[0]
+    places = lax.axis_size("place")
+    aux_count = lax.axis_size("aux")
+    devices = places * aux_count
+    occ_local = coef.shape[1] // (2 * devices)
+    block_count = coef.shape[0] // BS * 2 * places
+    rows = occ_local * aux_count
+    vmem = pl.BlockSpec(memory_space=pltpu.VMEM)
+    hbm = pl.BlockSpec(memory_space=pltpu.HBM)
+    params = pltpu.CompilerParams(vmem_limit_bytes=40 * 2**20)
+
+    blocks = integrals.reshape(pairs_dev, BS, BS)
+    far_block = flip(blocks, "half", 1)
+    near, sent_coef = pl.pallas_call(
+        functools.partial(half_kernel, occ_local, aux_count),
+        out_shape=[
+            jax.ShapeDtypeStruct((devices, pairs_dev * occ_local + 16, BS), jnp.bfloat16),
+            jax.ShapeDtypeStruct((places * occ_local + 16, pairs_dev * BS), jnp.bfloat16),
+        ],
+        in_specs=[hbm] * 4,
+        out_specs=[vmem] * 2,
+        scratch_shapes=[
+            pltpu.SMEM(pair_list.shape, jnp.int32),
+            pltpu.VMEM((1, occ_slot.shape[0]), jnp.int32),
+            pltpu.VMEM(coef.shape, jnp.bfloat16),
+            pltpu.VMEM(blocks.shape, jnp.bfloat16),
+            pltpu.SemaphoreType.DMA((4,)),
+        ],
+        compiler_params=params,
+        name="near_blocks",
+    )(*in_hbm(pair_list, occ_slot.reshape(1, -1), coef, blocks))
+    near = lax.all_to_all(near, ("place", "aux"), split_axis=0, concat_axis=0)
+    far_block = after(far_block, sent_coef)
+    far_coef = flip(after(sent_coef, far_block), "half", 1)
+    far_blocks = shared(far_block)
+
+    total_shape = jax.ShapeDtypeStruct((block_count, rows, BS), jnp.float32)
+    total = pl.pallas_call(
+        functools.partial(near_sum_kernel, aux_count),
+        out_shape=total_shape,
+        in_specs=[vmem],
+        out_specs=vmem,
+        scratch_shapes=[
+            pltpu.VMEM((places, BS), jnp.int32),
+            pltpu.SMEM((places, BS), jnp.int32),
+            pltpu.SemaphoreType.DMA,
+        ],
+        compiler_params=params,
+        name="near_sum",
+    )(near)
+    far = pl.pallas_call(
+        functools.partial(far_kernel, aux_count),
+        out_shape=jax.ShapeDtypeStruct((places, pairs_dev * rows + 16, BS), jnp.bfloat16),
+        in_specs=[vmem] * (1 + aux_count),
+        out_specs=vmem,
+        compiler_params=params,
+        name="far_blocks",
+    )(far_coef, *far_blocks)
+    far = lax.all_to_all(far, "place", split_axis=0, concat_axis=0)
+    return pl.pallas_call(
+        collect_kernel,
+        out_shape=[
+            jax.ShapeDtypeStruct((occ_local, aux_count, block_count * BS), jnp.bfloat16),
+            total_shape,
+        ],
+        in_specs=[hbm, vmem, vmem],
+        out_specs=[vmem, vmem],
+        input_output_aliases={1: 1},
+        scratch_shapes=[
+            pltpu.VMEM(metric.shape, jnp.bfloat16),
+            pltpu.VMEM((places, BS), jnp.int32),
+            pltpu.SMEM((places, BS), jnp.int32),
+            pltpu.SemaphoreType.DMA((2,)),
+        ],
+        compiler_params=params,
+        name="collect",
+    )(*in_hbm(metric), total, far)[0]
+
+
 def solution(mesh):
-    placed = (P("shell", None, "aux", None), P("shell", None), P("shell", None), P(), P())
-    return jax.shard_map(
-        per_device,
-        mesh=mesh,
-        in_specs=placed,
-        out_specs=P(("shell", "aux"), None, None),
-        check_vma=False,
-    )
+    shell_count, aux_count = mesh.shape["shell"], mesh.shape["aux"]
+    halves = Mesh(
+        mesh.devices.reshape(2, shell_count // 2, aux_count), ("half", "place", "aux")
+    )
+
+    def whole(*args):
+        occ_local = args[2].shape[1] // (shell_count * aux_count)
+        if occ_local % 16 or aux_count & (aux_count - 1):
+            program, grid, shell = relayed_half_blocks, mesh, "shell"
+        else:
+            program, grid, shell = crossed_inputs, halves, ("half", "place")
+        owners = ("shell", "aux") if grid is mesh else ("half", "place", "aux")
+        return jax.shard_map(
+            program,
+            mesh=grid,
+            in_specs=(P(shell, None, "aux", None), P(shell, None), P(shell, None), P(), P()),
+            out_specs=P(owners, None, None),
+            check_vma=False,
+        )(*args)
+
+    return whole

time: 88.8 us -> 46.3 us (0.52)
  blocking collectives: 58.8 us -> 0 us
  waiting for transfers between devices: 0.01 us -> 18.4 us
  starting transfers between devices: 3.52 us -> 19.9 us
  local copies, waits for them, and re-layouts: 12.8 us -> 0.01 us
  Pallas kernels: 0 us -> 7.67 us
  loops' own time: 6.88 us -> 0 us
  matrix products: 5.08 us -> 0 us
  other arithmetic: 0.97 us -> 0 us
    all_to_all x1 -> x0, blocking collectives: 32.8 us -> none  [per_device(): lax.all_to_all(half_blocks, 'shell', split_axis=1, concat_axis=0, tiled=T...]
    all_gather x1 -> x0, blocking collectives: 26 us -> none  [per_device(): listing = lax.all_gather(pair_list, 'shell', axis=0, tiled=True)]
    ppermute x0 -> x5, waiting for transfers between devices: none -> 10.9 us  [flip(): return lax.ppermute(value, axis, [(at, at ^ bits) for at in range(count)])]
    all_to_all x1 -> x2, starting transfers between devices: 3.52 us -> 12.3 us  [the longest x1 6.31 us: crossed_inputs(): near = lax.all_to_all(near, ('place', 'aux'), split_axis=0, concat_axis=0)]
    pallas_call x0 -> x4, Pallas kernels: none -> 7.67 us  [the longest x1 3.4 us: crossed_inputs(): pl.pallas_call(functools.partial(half_kernel, occ_local, aux_count), out_...]
    ppermute x0 -> x5, starting transfers between devices: none -> 7.61 us  [flip(): return lax.ppermute(value, axis, [(at, at ^ bits) for at in range(count)])]
    all_to_all x1 -> x2, waiting for transfers between devices: 0.01 us -> 7.5 us  [the longest x1 7.49 us: crossed_inputs(): far = lax.all_to_all(far, 'place', split_axis=0, concat_axis=0)]
    another operation x1 -> x0, loops' own time: 6.88 us -> none  [per_device(): half_blocks = lax.map(one_slot, (integrals, pair_list[:, 1]))]
  transfers between devices with their start and end apart: 1 -> 7, of which waited for: 0 -> 5; matrix products, arithmetic and copies ran while one was open for 0% -> 0% of each run, Pallas kernels for 0% -> 4%
where the time goes in v6:
time: 46.3 us; the launch traced here: 46.1 us
  starting transfers between devices  19.9 us (43%)
  waiting for transfers between devices  18.4 us (40%)
  Pallas kernels  7.67 us (17%)
    ppermute x5, waiting for transfers between devices, flip(): return lax.ppermute(value, axis, [(at, at ^ bits) for at in range(count)])  10.9 us
    ppermute x5, starting transfers between devices, flip(): return lax.ppermute(value, axis, [(at, at ^ bits) for at in range(count)])  7.61 us
    all_to_all x1, waiting for transfers between devices, crossed_inputs(): far = lax.all_to_all(far, 'place', split_axis=0, concat_axis=0)  7.49 us
    all_to_all x1, starting transfers between devices, crossed_inputs(): near = lax.all_to_all(near, ('place', 'aux'), split_axis=0, concat_axis=0)  6.31 us
    all_to_all x1, starting transfers between devices, crossed_inputs(): far = lax.all_to_all(far, 'place', split_axis=0, concat_axis=0)  6 us
    pallas_call x1, Pallas kernels, crossed_inputs(): pl.pallas_call(functools.partial(half_kernel, occ_local, aux_count), out_...  3.4 us
    pallas_call x1, Pallas kernels, crossed_inputs(): pl.pallas_call(collect_kernel, out_shape=[jax.ShapeDtypeStruct((occ_local...  2.35 us
    pallas_call x1, Pallas kernels, crossed_inputs(): pl.pallas_call(functools.partial(far_kernel, aux_count), out_shape=jax.Sh...  1.1 us
  transfers between devices with their start and end apart: 7, of which 5 were waited for; matrix products, arithmetic and copies ran while one was open for 0% of the time, Pallas kernels for 4%

profile of v6, /device:TPU:0, one launch (start us, length us, event | category | flops | bytes accessed | tf_op | source)
XLA Modules:
  0.0 46.1 jit_solution(14953152337365459192)
XLA Ops:
  0.0 0.0 copy-start
  0.0 3.4 %near_blocks.1 = (bf16[16,144,128]{2,1,0:T(8,128)(2,1)}, bf16[144,512]{1,0:T(8,128)(2,1)S(1)}) custom-call(s32[4,3]{1,0:T(4,128)} %pairs_in.1, s32[1,128]{1,0:T(1,128)} %bitcast.4, bf16[512,1024]{1,0:T(8,128)(2,1)} %coef_in.1, bf16[4,128,128]{2,1,0:T(8,128)(2,1)} %bitcast.2), custom_call_target="tpu_custom_call" | custom-call | tf_op jit(solution)/shard_map/near_blocks/pallas_call | solution.py:272
  3.4 6.3 %all-to-all-start = ((bf16[16,144,128]{2,1,0:T(8,128)(2,1)}), bf16[16,144,128]{2,1,0:T(8,128)(2,1)S(1)}, u32[]{:S(2)}, u32[]{:S(2)}) async-start(bf16[16,144,128]{2,1,0:T(8,128)(2,1)} %get-tuple-element.10), calls=%async_computation | async-start | bytes 1179648 | tf_op jit(solution)/shard_map/all_to_all | solution.py:290
  9.7 0.0 copy-done
  9.7 2.6 %collective-permute-start = (bf16[4,128,128]{2,1,0:T(8,128)(2,1)S(1)}, bf16[4,128,128]{2,1,0:T(8,128)(2,1)S(1)}, u32[]{:S(2)}, u32[]{:S(2)}) collective-permute-start(bf16[4,128,128]{2,1,0:T(8,128)(2,1)S(1)} %bitcast.3), channel_id=1, source_target_pairs={{0,16},{16,0},{1,17},{17,1},{2,18},{18,2},{3,19},{19,3},{4,20},{20... | collective-permute-start | bytes 393224 | tf_op jit(solution)/shard_map/ppermute | solution.py:238
  12.4 7.6 %collective-permute-done.refs_0_ = bf16[4,128,128]{2,1,0:T(8,128)(2,1)S(1)} collective-permute-done((bf16[4,128,128]{2,1,0:T(8,128)(2,1)S(1)}, bf16[4,128,128]{2,1,0:T(8,128)(2,1)S(1)}, u32[]{:S(2)}, u32[]{:S(2)}) %collective-permute-start) | collective-permute-done | bytes 131104 | tf_op jit(solution)/shard_map/ppermute | solution.py:238
  19.9 1.6 %collective-permute-start.3 = (bf16[4,128,128]{2,1,0:T(8,128)(2,1)S(1)}, bf16[4,128,128]{2,1,0:T(8,128)(2,1)S(1)}, u32[]{:S(2)}, u32[]{:S(2)}) collective-permute-start(bf16[4,128,128]{2,1,0:T(8,128)(2,1)S(1)} %collective-permute-done.refs_0_), channel_id=1, source_target_pairs={{0,2},{1,3},{2,0},{3,1},{4,6},{5,7},{6,4},{7,5},{8,10},{9,11},{10,... | collective-permute-start | bytes 393224 | tf_op jit(solution)/shard_map/ppermute | solution.py:238
  21.5 3.4 %collective-permute-start.1 = (bf16[144,512]{1,0:T(8,128)(2,1)S(1)}, bf16[144,512]{1,0:T(8,128)(2,1)S(1)}, u32[]{:S(2)}, u32[]{:S(2)}) collective-permute-start(bf16[144,512]{1,0:T(8,128)(2,1)S(1)} %get-tuple-element.13), channel_id=1, source_target_pairs={{0,16},{16,0},{1,17},{17,1},{2,18},{18,2},{3,19},{19,3},{4,20},{20... | collective-permute-start | bytes 442376 | tf_op jit(solution)/shard_map/ppermute | solution.py:238
  24.9 0.0 collective-permute-start.2
  24.9 1.2 %collective-permute-done.3.refs_2_ = bf16[4,128,128]{2,1,0:T(8,128)(2,1)S(1)} collective-permute-done((bf16[4,128,128]{2,1,0:T(8,128)(2,1)S(1)}, bf16[4,128,128]{2,1,0:T(8,128)(2,1)S(1)}, u32[]{:S(2)}, u32[]{:S(2)}) %collective-permute-start.3) | collective-permute-done | bytes 131104 | tf_op jit(solution)/shard_map/ppermute | solution.py:238
  26.1 0.0 collective-permute-start.4
  26.1 0.2 collective-permute-done.2.refs_1_
  26.3 2.0 %collective-permute-done.1.coefs = bf16[144,512]{1,0:T(8,128)(2,1)S(1)} collective-permute-done((bf16[144,512]{1,0:T(8,128)(2,1)S(1)}, bf16[144,512]{1,0:T(8,128)(2,1)S(1)}, u32[]{:S(2)}, u32[]{:S(2)}) %collective-permute-start.1) | collective-permute-done | bytes 147488 | tf_op jit(solution)/shard_map/ppermute | solution.py:238
  28.3 0.0 collective-permute-done.4.refs_3_
  28.3 1.1 %far_blocks.1 = bf16[4,528,128]{2,1,0:T(8,128)(2,1)} custom-call(bf16[144,512]{1,0:T(8,128)(2,1)S(1)} %collective-permute-done.1.coefs, bf16[4,128,128]{2,1,0:T(8,128)(2,1)S(1)} %collective-permute-done.refs_0_, bf16[4,128,128]{2,1,0:T(8,128)(2,1)S(1)} %collective-permute-done.2.refs_1_, bf16[4,128,128]{2,1,0:T(8,128)(2,1)S(1)} %collective-permute-done.3.refs_2_, ...), custom_call_target="tpu_custom_call" | custom-call | tf_op jit(solution)/shard_map/far_blocks/pallas_call | solution.py:309
  29.4 0.0 all-to-all-done.received
  29.4 6.0 %all-to-all-start.1 = ((bf16[4,528,128]{2,1,0:T(8,128)(2,1)}), bf16[4,528,128]{2,1,0:T(8,128)(2,1)S(1)}, u32[]{:S(2)}, u32[]{:S(2)}) async-start(bf16[4,528,128]{2,1,0:T(8,128)(2,1)} %far_blocks.1), calls=%async_computation.1 | async-start | bytes 1081344 | tf_op jit(solution)/shard_map/all_to_all | solution.py:317
  35.4 0.8 %near_sum.1.total_in = f32[32,128,128]{2,1,0:T(8,128)S(1)} custom-call(bf16[16,144,128]{2,1,0:T(8,128)(2,1)S(1)} %all-to-all-done.received), custom_call_target="tpu_custom_call" | custom-call | tf_op jit(solution)/shard_map/near_sum/pallas_call | solution.py:296
  36.2 7.5 %all-to-all-done.1.received = bf16[4,528,128]{2,1,0:T(8,128)(2,1)S(1)} async-done(((bf16[4,528,128]{2,1,0:T(8,128)(2,1)}), bf16[4,528,128]{2,1,0:T(8,128)(2,1)S(1)}, u32[]{:S(2)}, u32[]{:S(2)}) %all-to-all-start.1) | async-done | bytes 540704 | tf_op jit(solution)/shard_map/all_to_all | solution.py:317
  43.7 2.4 %collect.1 = (bf16[32,4,4096]{2,1,0:T(4,128)(2,1)}, f32[32,128,128]{2,1,0:T(8,128)S(1)}) custom-call(bf16[4,4]{1,0:T(4,128)(2,1)} %metric_in.1, f32[32,128,128]{2,1,0:T(8,128)S(1)} %near_sum.1.total_in, bf16[4,528,128]{2,1,0:T(8,128)(2,1)S(1)} %all-to-all-done.1.received), custom_call_target="tpu_custom_call", output_to_operand_aliasing={{1}: (1, {})} | custom-call | tf_op jit(solution)/shard_map/collect/pallas_call | solution.py:318
Async XLA Ops:
  0.0 9.7 %copy-start = (bf16[4,128,1,128]{3,1,2,0:T(8,128)(2,1)S(1)}, bf16[4,128,1,128]{3,1,2,0:T(8,128)(2,1)}, u32[]{:S(2)}) copy-start(bf16[4,128,1,128]{3,1,2,0:T(8,128)(2,1)} %param.5) | copy-start | bytes 393220
  3.4 26.0 %all-to-all-start = ((bf16[16,144,128]{2,1,0:T(8,128)(2,1)}), bf16[16,144,128]{2,1,0:T(8,128)(2,1)S(1)}, u32[]{:S(2)}, u32[]{:S(2)}) async-start(bf16[16,144,128]{2,1,0:T(8,128)(2,1)} %get-tuple-element.10), calls=%async_computation | async-start | bytes 1179648 | tf_op jit(solution)/shard_map/all_to_all | solution.py:290
  9.7 10.2 %collective-permute-start = (bf16[4,128,128]{2,1,0:T(8,128)(2,1)S(1)}, bf16[4,128,128]{2,1,0:T(8,128)(2,1)S(1)}, u32[]{:S(2)}, u32[]{:S(2)}) collective-permute-start(bf16[4,128,128]{2,1,0:T(8,128)(2,1)S(1)} %bitcast.3), channel_id=1, source_target_pairs={{0,16},{16,0},{1,17},{17,1},{2,18},{18,2},{3,19},{19,3},{4,20},{20... | collective-permute-start | bytes 393224 | tf_op jit(solution)/shard_map/ppermute | solution.py:238
  19.9 6.1 %collective-permute-start.3 = (bf16[4,128,128]{2,1,0:T(8,128)(2,1)S(1)}, bf16[4,128,128]{2,1,0:T(8,128)(2,1)S(1)}, u32[]{:S(2)}, u32[]{:S(2)}) collective-permute-start(bf16[4,128,128]{2,1,0:T(8,128)(2,1)S(1)} %collective-permute-done.refs_0_), channel_id=1, source_target_pairs={{0,2},{1,3},{2,0},{3,1},{4,6},{5,7},{6,4},{7,5},{8,10},{9,11},{10,... | collective-permute-start | bytes 393224 | tf_op jit(solution)/shard_map/ppermute | solution.py:238
  21.5 6.7 %collective-permute-start.1 = (bf16[144,512]{1,0:T(8,128)(2,1)S(1)}, bf16[144,512]{1,0:T(8,128)(2,1)S(1)}, u32[]{:S(2)}, u32[]{:S(2)}) collective-permute-start(bf16[144,512]{1,0:T(8,128)(2,1)S(1)} %get-tuple-element.13), channel_id=1, source_target_pairs={{0,16},{16,0},{1,17},{17,1},{2,18},{18,2},{3,19},{19,3},{4,20},{20... | collective-permute-start | bytes 442376 | tf_op jit(solution)/shard_map/ppermute | solution.py:238
  24.9 1.3 %collective-permute-start.2 = (bf16[4,128,128]{2,1,0:T(8,128)(2,1)S(1)}, bf16[4,128,128]{2,1,0:T(8,128)(2,1)S(1)}, u32[]{:S(2)}, u32[]{:S(2)}) collective-permute-start(bf16[4,128,128]{2,1,0:T(8,128)(2,1)S(1)} %collective-permute-done.refs_0_), channel_id=1, source_target_pairs={{0,1},{1,0},{2,3},{3,2},{4,5},{5,4},{6,7},{7,6},{8,9},{9,8},{10,11... | collective-permute-start | bytes 393224 | tf_op jit(solution)/shard_map/ppermute | solution.py:238
  26.1 2.2 %collective-permute-start.4 = (bf16[4,128,128]{2,1,0:T(8,128)(2,1)S(1)}, bf16[4,128,128]{2,1,0:T(8,128)(2,1)S(1)}, u32[]{:S(2)}, u32[]{:S(2)}) collective-permute-start(bf16[4,128,128]{2,1,0:T(8,128)(2,1)S(1)} %collective-permute-done.3.refs_2_), channel_id=1, source_target_pairs={{0,1},{1,0},{2,3},{3,2},{4,5},{5,4},{6,7},{7,6},{8,9},{9,8},{10,11... | collective-permute-start | bytes 393224 | tf_op jit(solution)/shard_map/ppermute | solution.py:238
  29.4 14.3 %all-to-all-start.1 = ((bf16[4,528,128]{2,1,0:T(8,128)(2,1)}), bf16[4,528,128]{2,1,0:T(8,128)(2,1)S(1)}, u32[]{:S(2)}, u32[]{:S(2)}) async-start(bf16[4,528,128]{2,1,0:T(8,128)(2,1)} %far_blocks.1), calls=%async_computation.1 | async-start | bytes 1081344 | tf_op jit(solution)/shard_map/all_to_all | solution.py:317

commit v7 on v5

--- a/solution.py
+++ b/solution.py
@@ -76,29 +76,45 @@
     )
 
 
-def pick_kernel(group, occ_local, aux_count, pairs_in, slot_in, coef_in, near, far, pairs, slot_row, coef, sems):
+def pick_kernel(
+    flips,
+    occ_local,
+    aux_count,
+    pairs_in,
+    slot_in,
+    coef_in,
+    blocks_in,
+    *refs,
+):
+    *outs, blocks, pairs, slot_row, coef, sems = refs
     pairs_dev = pairs.shape[0]
     blocks_dev = coef.shape[0] // BS
     occ_count = coef.shape[1]
     loads = [
         pltpu.make_async_copy(source, target, sems.at[at])
         for at, (source, target) in enumerate(
-            ((slot_in, slot_row), (pairs_in, pairs), (coef_in, coef))
+            ((slot_in, slot_row), (pairs_in, pairs), (coef_in, coef), (blocks_in, blocks))
         )
     ]
     for load in loads:
         load.start()
     me = lax.axis_index("shell")
     mine = lax.axis_index("aux")
-    rows = group * occ_local
-    row = lax.broadcasted_iota(jnp.int32, (2 * rows, 1), 0)
-    owner = jnp.bitwise_xor(row // occ_local, me)
-    wanted = (owner * aux_count + mine) * occ_local + row % occ_local
+    every = sum(flips, [])
+    row = lax.broadcasted_iota(jnp.int32, (len(every) * occ_local, 1), 0)
+    owner = sum(jnp.where(row // occ_local == at, f, 0) for at, f in enumerate(every))
+    wanted = (jnp.bitwise_xor(owner, me) * aux_count + mine) * occ_local + row % occ_local
     loads[0].wait()
     target = targets_of(slot_row[...], slot_row.shape[1], occ_count)
     pick = (wanted == target).astype(jnp.bfloat16)
     for load in loads[1:]:
         load.wait()
+    lane = lax.broadcasted_iota(jnp.int32, (1, BS), 1)
+    code = jnp.zeros((1, BS), jnp.int32)
+    for k in range(pairs_dev):
+        code = jnp.where(lane == k, pairs[k, 0] % 128, code)
+        code = jnp.where(lane == pairs_dev + k, pairs[k, 0] // 128, code)
+    code = jnp.broadcast_to(code.astype(jnp.float32), (16, BS)).astype(jnp.bfloat16)
     for k in range(pairs_dev):
         start = pl.multiple_of(lax.rem(pairs[k, 1], blocks_dev) * BS, BS)
         live = (pairs[k, 2] == 1).astype(jnp.float32)
@@ -109,17 +125,12 @@
             preferred_element_type=jnp.float32,
         )
         piece = (piece * live).astype(jnp.bfloat16)
-        near[:rows, k * BS : (k + 1) * BS] = piece[:rows]
-        far[:rows, k * BS : (k + 1) * BS] = piece[rows:]
-    lane = lax.broadcasted_iota(jnp.int32, (1, BS), 1)
-    code = jnp.zeros((1, BS), jnp.int32)
-    for k in range(pairs_dev):
-        code = jnp.where(lane == k, pairs[k, 0] % 128, code)
-        code = jnp.where(lane == pairs_dev + k, pairs[k, 0] // 128, code)
-    code = jnp.broadcast_to(code.astype(jnp.float32), (16, BS)).astype(jnp.bfloat16)
-    for piece in (near, far):
-        piece[rows:, :BS] = code
-        piece[rows:, BS:] = jnp.zeros((16, piece.shape[1] - BS), jnp.bfloat16)
+        first = 0
+        for out in outs:
+            rows = out.shape[0] - 16
+            out[:rows, k * BS : (k + 1) * BS] = piece[first : first + rows]
+            out[rows:, k * BS : (k + 1) * BS] = code
+            first += rows
 
 
 def block_kernel(aux_count, coefs, *refs):
@@ -144,26 +155,38 @@
         piece[pairs_dev * aux_count * occ_local :, :] = coefs[rows:, :BS]
 
 
-def collect_kernel(pairs_dev, metric_in, *refs):
-    *received, out, total, metric, codes_v, codes, sems = refs
-    occ_local, aux_count = out.shape[:2]
-    rows = occ_local * aux_count
+def add_received(total, received, codes_v, codes, sem, meanwhile):
+    rows = total.shape[1]
+    pairs_dev = (received[0].shape[0] - 16) // rows
     for at, piece in enumerate(received):
         digits = piece[pairs_dev * rows :, :].astype(jnp.float32).astype(jnp.int32)
         codes_v[at : at + 1, :] = digits[:1]
-    loads = [
-        pltpu.make_async_copy(codes_v, codes, sems.at[0]),
-        pltpu.make_async_copy(metric_in, metric, sems.at[1]),
-    ]
-    for load in loads:
-        load.start()
-    total[...] = jnp.zeros_like(total)
-    for load in loads:
-        load.wait()
+    load = pltpu.make_async_copy(codes_v, codes, sem)
+    load.start()
+    meanwhile()
+    load.wait()
     for at, piece in enumerate(received):
         for k in range(pairs_dev):
             r = codes[at, k] + 128 * codes[at, pairs_dev + k]
             total[r] += piece[k * rows : (k + 1) * rows, :].astype(jnp.float32)
+
+
+def near_sum_kernel(*refs):
+    *received, total, codes_v, codes, sem = refs
+
+    def clear():
+        total[...] = jnp.zeros_like(total)
+
+    add_received(total, received, codes_v, codes, sem, clear)
+
+
+def collect_kernel(metric_in, total_in, *refs):
+    *received, out, total, metric, codes_v, codes, sem, metric_sem = refs
+    occ_local, aux_count = out.shape[:2]
+    rows = occ_local * aux_count
+    load = pltpu.make_async_copy(metric_in, metric, metric_sem)
+    load.start()
+    add_received(total, received, codes_v, codes, sem, load.wait)
 
     row = lax.broadcasted_iota(jnp.int32, (rows, rows), 0)
     column = lax.broadcasted_iota(jnp.int32, (rows, rows), 1)
@@ -201,7 +224,8 @@
         held += [flip(one, "aux", bits) for one in held]
         order += [at ^ bits for at in order]
         bits //= 2
-        held = [after(one, *others) for one in held]
+        if others:
+            held = [after(one, *others) for one in held]
     return [held[order.index(at)] for at in range(len(held))]
 
 
@@ -216,67 +240,85 @@
     group = shell_count // 2
     occ_local = coef.shape[1] // (shell_count * aux_count)
     block_count = coef.shape[0] // BS * shell_count
-    rows = group * occ_local
-    piece_rows = pairs_dev * aux_count * occ_local
+    rows = occ_local * aux_count
+    piece = jax.ShapeDtypeStruct((pairs_dev * rows + 16, BS), jnp.bfloat16)
     vmem = pl.BlockSpec(memory_space=pltpu.VMEM)
     hbm = pl.BlockSpec(memory_space=pltpu.HBM)
     params = pltpu.CompilerParams(vmem_limit_bytes=40 * 2**20)
 
+    def transformed(name, coefs, quad, count):
+        return pl.pallas_call(
+            functools.partial(block_kernel, aux_count),
+            out_shape=[piece] * count,
+            in_specs=[vmem] * (1 + aux_count),
+            out_specs=[vmem] * count,
+            compiler_params=params,
+            name=name,
+        )(coefs, *quad)
+
+    def code_scratch(count):
+        return [
+            pltpu.VMEM((count, BS), jnp.int32),
+            pltpu.SMEM((count, BS), jnp.int32),
+            pltpu.SemaphoreType.DMA,
+        ]
+
     blocks = integrals.reshape(pairs_dev, BS, BS)
     far_block = flip(blocks, "shell", group)
-    near_coef, sent_coef = pl.pallas_call(
-        functools.partial(pick_kernel, group, occ_local, aux_count),
-        out_shape=[jax.ShapeDtypeStruct((rows + 16, pairs_dev * BS), jnp.bfloat16)] * 2,
-        in_specs=[hbm] * 3,
-        out_specs=[vmem] * 2,
+
+    flips = [list(range(group)), list(range(group, shell_count))]
+    near_coef, sent_coef, near_block = pl.pallas_call(
+        functools.partial(pick_kernel, flips, occ_local, aux_count),
+        out_shape=[
+            jax.ShapeDtypeStruct((len(f) * occ_local + 16, pairs_dev * BS), jnp.bfloat16)
+            for f in flips
+        ]
+        + [jax.ShapeDtypeStruct(blocks.shape, jnp.bfloat16)],
+        in_specs=[hbm] * 4,
+        out_specs=[vmem] * (len(flips) + 1),
         scratch_shapes=[
             pltpu.SMEM(pair_list.shape, jnp.int32),
             pltpu.VMEM((1, occ_slot.shape[0]), jnp.int32),
             pltpu.VMEM(coef.shape, jnp.bfloat16),
-            pltpu.SemaphoreType.DMA((3,)),
+            pltpu.SemaphoreType.DMA((4,)),
         ],
         compiler_params=params,
         name="pick",
-    )(*in_hbm(pair_list, occ_slot.reshape(1, -1), coef))
-    near_blocks = [blocks] + [flip(blocks, "aux", j) for j in range(1, aux_count)]
-    far_coef = flip(sent_coef, "shell", group)
-
-    def transformed(name, coefs, quad):
-        pieces = pl.pallas_call(
-            functools.partial(block_kernel, aux_count),
-            out_shape=[jax.ShapeDtypeStruct((piece_rows + 16, BS), jnp.bfloat16)] * group,
-            in_specs=[vmem] * (1 + aux_count),
-            out_specs=[vmem] * group,
-            compiler_params=params,
-            name=name,
-        )(coefs, *quad)
-        return pieces
-
-    def relayed(pieces):
-        return [pieces[0]] + [flip(pieces[f], "shell", f) for f in range(1, group)]
-
-    near = transformed("near_blocks", near_coef, near_blocks)
+    )(*in_hbm(pair_list, occ_slot.reshape(1, -1), coef, blocks))
+    near_blocks = [near_block] + [flip(blocks, "aux", j) for j in range(1, aux_count)]
+
+    near = transformed("near_blocks", near_coef, near_blocks, group)
     far_block = after(far_block, near[0])
-    near = relayed(near)
-    far_blocks = shared(far_block, far_coef, *near[1:3])
-    far = relayed(transformed("far_blocks", after(far_coef, *near), far_blocks))
+    near = [near[0]] + [flip(near[f], "shell", f) for f in range(1, group)]
+    far_coef = flip(after(sent_coef, far_block), "shell", group)
+    far_blocks = shared(far_block, *near[1:3])
+    far = transformed("far_blocks", after(far_coef, *near), far_blocks, group)
+    far = [far[0]] + [flip(far[f], "shell", f) for f in range(1, group)]
+    total_shape = jax.ShapeDtypeStruct((block_count, rows, BS), jnp.float32)
+    total = pl.pallas_call(
+        near_sum_kernel,
+        out_shape=total_shape,
+        in_specs=[vmem] * group,
+        out_specs=vmem,
+        scratch_shapes=code_scratch(group),
+        compiler_params=params,
+        name="near_sum",
+    )(*(after(one, far[0]) for one in near))
     return pl.pallas_call(
-        functools.partial(collect_kernel, pairs_dev),
-        out_shape=jax.ShapeDtypeStruct(
-            (occ_local, aux_count, block_count * BS), jnp.bfloat16
-        ),
-        in_specs=[hbm] + [vmem] * (2 * group),
-        out_specs=vmem,
-        scratch_shapes=[
-            pltpu.VMEM((block_count, occ_local * aux_count, BS), jnp.float32),
-            pltpu.VMEM(metric.shape, jnp.bfloat16),
-            pltpu.VMEM((2 * group, BS), jnp.int32),
-            pltpu.SMEM((2 * group, BS), jnp.int32),
-            pltpu.SemaphoreType.DMA((2,)),
+        collect_kernel,
+        out_shape=[
+            jax.ShapeDtypeStruct((occ_local, aux_count, block_count * BS), jnp.bfloat16),
+            total_shape,
         ],
+        in_specs=[hbm] + [vmem] * (1 + group),
+        out_specs=[vmem, vmem],
+        input_output_aliases={1: 1},
+        scratch_shapes=[pltpu.VMEM(metric.shape, jnp.bfloat16)]
+        + code_scratch(group)
+        + [pltpu.SemaphoreType.DMA],
         compiler_params=params,
         name="collect",
-    )(*in_hbm(metric), *near, *far)
+    )(*in_hbm(metric), total, *far)[0]
 
 
 def per_device(integrals, pair_list, coef, metric, occ_slot):

time: 36.9 us -> 36 us (0.976); the launches traced: 36.4 us -> 35.9 us
  waiting for transfers between devices: 14.5 us -> 10.6 us
  starting transfers between devices: 16.7 us -> 19.4 us
  Pallas kernels: 5.12 us -> 5.76 us
    ppermute x14, waiting for transfers between devices: 14.5 us -> 10.6 us  [flip(): return lax.ppermute(value, axis, [(at, at ^ bits) for at in range(count)])]
    ppermute x14, starting transfers between devices: 16.7 us -> 19.4 us  [flip(): return lax.ppermute(value, axis, [(at, at ^ bits) for at in range(count)])]
    pallas_call x4 -> x5, Pallas kernels: 5.12 us -> 5.76 us  [the longest x1 2.34 us: exchanged_inputs(): pl.pallas_call(collect_kernel, out_shape=[jax.ShapeDtypeStruct((occ_local...]
  transfers between devices with their start and end apart: 14 -> 14, of which waited for: 7 -> 4; matrix products, arithmetic and copies ran while one was open for 0% -> 0% of each run, Pallas kernels for 6% -> 9%
where the time goes in v7:
time: 36 us; the launch traced here: 35.9 us
  starting transfers between devices  19.4 us (54%)
  waiting for transfers between devices  10.6 us (29%)
  Pallas kernels  5.76 us (16%)
    ppermute x14, starting transfers between devices, flip(): return lax.ppermute(value, axis, [(at, at ^ bits) for at in range(count)])  19.4 us
    ppermute x14, waiting for transfers between devices, flip(): return lax.ppermute(value, axis, [(at, at ^ bits) for at in range(count)])  10.6 us
    pallas_call x1, Pallas kernels, exchanged_inputs(): pl.pallas_call(collect_kernel, out_shape=[jax.ShapeDtypeStruct((occ_local...  2.34 us
    pallas_call x1, Pallas kernels, exchanged_inputs(): pl.pallas_call(functools.partial(pick_kernel, flips, occ_local, aux_count...  2 us
    pallas_call x1, Pallas kernels, exchanged_inputs(): pl.pallas_call(near_sum_kernel, out_shape=total_shape, in_specs=[vmem] *...  0.84 us
  transfers between devices with their start and end apart: 14, of which 4 were waited for; matrix products, arithmetic and copies ran while one was open for 0% of the time, Pallas kernels for 9%

profile of v7, /device:TPU:0, one launch (start us, length us, event | category | flops | bytes accessed | tf_op | source)
XLA Modules:
  0.0 35.9 jit_solution(3432346414689286580)
XLA Ops:
  0.0 2.4 %collective-permute-start.2 = (bf16[4,128,128]{2,1,0:T(8,128)(2,1)}, bf16[4,128,128]{2,1,0:T(8,128)(2,1)S(1)}, u32[]{:S(2)}, u32[]{:S(2)}) collective-permute-start(bf16[4,128,128]{2,1,0:T(8,128)(2,1)} %bitcast.2), channel_id=1, source_target_pairs={{0,3},{1,2},{2,1},{3,0},{4,7},{5,6},{6,5},{7,4},{8,11},{9,10},{10,... | collective-permute-start | bytes 393224 | tf_op jit(solution)/shard_map/ppermute | solution.py:214
  2.4 0.6 %collective-permute-start.1 = (bf16[4,128,128]{2,1,0:T(8,128)(2,1)}, bf16[4,128,128]{2,1,0:T(8,128)(2,1)S(1)}, u32[]{:S(2)}, u32[]{:S(2)}) collective-permute-start(bf16[4,128,128]{2,1,0:T(8,128)(2,1)} %bitcast.3), channel_id=1, source_target_pairs={{0,2},{1,3},{2,0},{3,1},{4,6},{5,7},{6,4},{7,5},{8,10},{9,11},{10,... | collective-permute-start | bytes 393224 | tf_op jit(solution)/shard_map/ppermute | solution.py:214
  3.0 0.1 collective-permute-start
  3.1 2.8 %collective-permute-start.3 = (bf16[4,128,128]{2,1,0:T(8,128)(2,1)}, bf16[4,128,128]{2,1,0:T(8,128)(2,1)S(1)}, u32[]{:S(2)}, u32[]{:S(2)}) collective-permute-start(bf16[4,128,128]{2,1,0:T(8,128)(2,1)} %bitcast.5), channel_id=1, source_target_pairs={{0,16},{4,20},{8,24},{12,28},{16,0},{20,4},{24,8},{28,12},{1,17},{... | collective-permute-start | bytes 393224 | tf_op jit(solution)/shard_map/ppermute | solution.py:214
  5.9 2.0 %pick.1 = (bf16[144,512]{1,0:T(8,128)(2,1)S(1)}, bf16[144,512]{1,0:T(8,128)(2,1)S(1)}, bf16[4,128,128]{2,1,0:T(8,128)(2,1)S(1)}) custom-call(s32[4,3]{1,0:T(4,128)} %pairs_in.1, s32[1,128]{1,0:T(1,128)} %bitcast.7, bf16[512,1024]{1,0:T(8,128)(2,1)} %coef_in.1, bf16[4,128,128]{2,1,0:T(8,128)(2,1)} %bitcast.6), custom_call_target="tpu_custom_call" | custom-call | tf_op jit(solution)/shard_map/pick/pallas_call | solution.py:270
  7.9 1.6 %collective-permute-done.1.refs_2_ = bf16[4,128,128]{2,1,0:T(8,128)(2,1)S(1)} collective-permute-done((bf16[4,128,128]{2,1,0:T(8,128)(2,1)}, bf16[4,128,128]{2,1,0:T(8,128)(2,1)S(1)}, u32[]{:S(2)}, u32[]{:S(2)}) %collective-permute-start.1) | collective-permute-done | bytes 131104 | tf_op jit(solution)/shard_map/ppermute | solution.py:214
  9.5 0.0 collective-permute-done.refs_1_
  9.5 0.3 near_blocks.1
  9.8 2.3 %collective-permute-start.5 = (bf16[528,128]{1,0:T(8,128)(2,1)S(1)}, bf16[528,128]{1,0:T(8,128)(2,1)S(1)}, u32[]{:S(2)}, u32[]{:S(2)}) collective-permute-start(bf16[528,128]{1,0:T(8,128)(2,1)S(1)} %get-tuple-element.36), channel_id=1, source_target_pairs={{0,4},{4,0},{8,12},{12,8},{16,20},{20,16},{24,28},{28,24},{1,5},{5... | collective-permute-start | bytes 405512 | tf_op jit(solution)/shard_map/ppermute | solution.py:214
  12.1 1.6 %collective-permute-start.6 = (bf16[528,128]{1,0:T(8,128)(2,1)S(1)}, bf16[528,128]{1,0:T(8,128)(2,1)S(1)}, u32[]{:S(2)}, u32[]{:S(2)}) collective-permute-start(bf16[528,128]{1,0:T(8,128)(2,1)S(1)} %get-tuple-element.37), channel_id=1, source_target_pairs={{0,8},{4,12},{8,0},{12,4},{16,24},{20,28},{24,16},{28,20},{1,9},{5... | collective-permute-start | bytes 405512 | tf_op jit(solution)/shard_map/ppermute | solution.py:214
  13.7 1.5 %collective-permute-start.9 = (bf16[4,128,128]{2,1,0:T(8,128)(2,1)S(1)}, bf16[4,128,128]{2,1,0:T(8,128)(2,1)S(1)}, u32[]{:S(2)}, u32[]{:S(2)}) collective-permute-start(bf16[4,128,128]{2,1,0:T(8,128)(2,1)S(1)} %collective-permute-done.3.refs_0_), channel_id=1, source_target_pairs={{0,2},{1,3},{2,0},{3,1},{4,6},{5,7},{6,4},{7,5},{8,10},{9,11},{10,... | collective-permute-start | bytes 393224 | tf_op jit(solution)/shard_map/ppermute | solution.py:214
  15.2 2.6 %collective-permute-start.4 = (bf16[144,512]{1,0:T(8,128)(2,1)S(1)}, bf16[144,512]{1,0:T(8,128)(2,1)S(1)}, u32[]{:S(2)}, u32[]{:S(2)}) collective-permute-start(bf16[144,512]{1,0:T(8,128)(2,1)S(1)} %get-tuple-element.35), channel_id=1, source_target_pairs={{0,16},{4,20},{8,24},{12,28},{16,0},{20,4},{24,8},{28,12},{1,17},{... | collective-permute-start | bytes 442376 | tf_op jit(solution)/shard_map/ppermute | solution.py:214
  17.8 1.4 %collective-permute-start.7 = (bf16[528,128]{1,0:T(8,128)(2,1)S(1)}, bf16[528,128]{1,0:T(8,128)(2,1)S(1)}, u32[]{:S(2)}, u32[]{:S(2)}) collective-permute-start(bf16[528,128]{1,0:T(8,128)(2,1)S(1)} %get-tuple-element.38), channel_id=1, source_target_pairs={{0,12},{4,8},{8,4},{12,0},{16,28},{20,24},{24,20},{28,16},{1,13},{... | collective-permute-start | bytes 405512 | tf_op jit(solution)/shard_map/ppermute | solution.py:214
  19.3 0.0 collective-permute-done.9.refs_2_
  19.3 0.5 %collective-permute-start.10 = (bf16[4,128,128]{2,1,0:T(8,128)(2,1)S(1)}, bf16[4,128,128]{2,1,0:T(8,128)(2,1)S(1)}, u32[]{:S(2)}, u32[]{:S(2)}) collective-permute-start(bf16[4,128,128]{2,1,0:T(8,128)(2,1)S(1)} %collective-permute-done.9.refs_2_), channel_id=1, source_target_pairs={{0,1},{1,0},{2,3},{3,2},{4,5},{5,4},{6,7},{7,6},{8,9},{9,8},{10,11... | collective-permute-start | bytes 393224 | tf_op jit(solution)/shard_map/ppermute | solution.py:214
  19.8 5.4 %collective-permute-done.7.refs_3_ = bf16[528,128]{1,0:T(8,128)(2,1)S(1)} collective-permute-done((bf16[528,128]{1,0:T(8,128)(2,1)S(1)}, bf16[528,128]{1,0:T(8,128)(2,1)S(1)}, u32[]{:S(2)}, u32[]{:S(2)}) %collective-permute-start.7) | collective-permute-done | bytes 135200 | tf_op jit(solution)/shard_map/ppermute | solution.py:214
  25.1 0.3 far_blocks.1
  25.4 0.9 %collective-permute-start.11 = (bf16[528,128]{1,0:T(8,128)(2,1)S(1)}, bf16[528,128]{1,0:T(8,128)(2,1)S(1)}, u32[]{:S(2)}, u32[]{:S(2)}) collective-permute-start(bf16[528,128]{1,0:T(8,128)(2,1)S(1)} %get-tuple-element.51), channel_id=1, source_target_pairs={{0,4},{4,0},{8,12},{12,8},{16,20},{20,16},{24,28},{28,24},{1,5},{5... | collective-permute-start | bytes 405512 | tf_op jit(solution)/shard_map/ppermute | solution.py:214
  26.4 1.2 %collective-permute-start.12 = (bf16[528,128]{1,0:T(8,128)(2,1)S(1)}, bf16[528,128]{1,0:T(8,128)(2,1)S(1)}, u32[]{:S(2)}, u32[]{:S(2)}) collective-permute-start(bf16[528,128]{1,0:T(8,128)(2,1)S(1)} %get-tuple-element.52), channel_id=1, source_target_pairs={{0,8},{4,12},{8,0},{12,4},{16,24},{20,28},{24,16},{28,20},{1,9},{5... | collective-permute-start | bytes 405512 | tf_op jit(solution)/shard_map/ppermute | solution.py:214
  27.6 1.4 %collective-permute-start.13 = (bf16[528,128]{1,0:T(8,128)(2,1)S(1)}, bf16[528,128]{1,0:T(8,128)(2,1)S(1)}, u32[]{:S(2)}, u32[]{:S(2)}) collective-permute-start(bf16[528,128]{1,0:T(8,128)(2,1)S(1)} %get-tuple-element.53), channel_id=1, source_target_pairs={{0,12},{4,8},{8,4},{12,0},{16,28},{20,24},{24,20},{28,16},{1,13},{... | collective-permute-start | bytes 405512 | tf_op jit(solution)/shard_map/ppermute | solution.py:214
  29.0 0.8 %near_sum.1.total_in = f32[32,128,128]{2,1,0:T(8,128)S(1)} custom-call(bf16[528,128]{1,0:T(8,128)(2,1)S(1)} %get-tuple-element.47.refs_0_, bf16[528,128]{1,0:T(8,128)(2,1)S(1)} %collective-permute-done.5.refs_1_, bf16[528,128]{1,0:T(8,128)(2,1)S(1)} %collective-permute-done.6.refs_2_, bf16[528,128]{1,0:T(8,128)(2,1)S(1)} %collective-permute-done.7.refs_3_), custom_call_target="tpu_custom_call" | custom-call | tf_op jit(solution)/shard_map/near_sum/pallas_call | solution.py:298
  29.8 1.8 %collective-permute-done.11.refs_1_ = bf16[528,128]{1,0:T(8,128)(2,1)S(1)} collective-permute-done((bf16[528,128]{1,0:T(8,128)(2,1)S(1)}, bf16[528,128]{1,0:T(8,128)(2,1)S(1)}, u32[]{:S(2)}, u32[]{:S(2)}) %collective-permute-start.11) | collective-permute-done | bytes 135200 | tf_op jit(solution)/shard_map/ppermute | solution.py:214
  31.7 1.9 %collective-permute-done.13.refs_3_ = bf16[528,128]{1,0:T(8,128)(2,1)S(1)} collective-permute-done((bf16[528,128]{1,0:T(8,128)(2,1)S(1)}, bf16[528,128]{1,0:T(8,128)(2,1)S(1)}, u32[]{:S(2)}, u32[]{:S(2)}) %collective-permute-start.13) | collective-permute-done | bytes 135200 | tf_op jit(solution)/shard_map/ppermute | solution.py:214
  33.5 2.3 %collect.1 = (bf16[32,4,4096]{2,1,0:T(4,128)(2,1)}, f32[32,128,128]{2,1,0:T(8,128)S(1)}) custom-call(bf16[4,4]{1,0:T(4,128)(2,1)} %metric_in.1, f32[32,128,128]{2,1,0:T(8,128)S(1)} %near_sum.1.total_in, bf16[528,128]{1,0:T(8,128)(2,1)S(1)} %get-tuple-element.46.refs_0_, ...), custom_call_target="tpu_custom_call", output_to_operand_aliasing={{1}: (1, {})} | custom-call | tf_op jit(solution)/shard_map/collect/pallas_call | solution.py:307
  (9 shorter events, 0.0 us)
Async XLA Ops:
  0.0 7.9 %collective-permute-start.2 = (bf16[4,128,128]{2,1,0:T(8,128)(2,1)}, bf16[4,128,128]{2,1,0:T(8,128)(2,1)S(1)}, u32[]{:S(2)}, u32[]{:S(2)}) collective-permute-start(bf16[4,128,128]{2,1,0:T(8,128)(2,1)} %bitcast.2), channel_id=1, source_target_pairs={{0,3},{1,2},{2,1},{3,0},{4,7},{5,6},{6,5},{7,4},{8,11},{9,10},{10,... | collective-permute-start | bytes 393224 | tf_op jit(solution)/shard_map/ppermute | solution.py:214
  2.4 7.1 %collective-permute-start.1 = (bf16[4,128,128]{2,1,0:T(8,128)(2,1)}, bf16[4,128,128]{2,1,0:T(8,128)(2,1)S(1)}, u32[]{:S(2)}, u32[]{:S(2)}) collective-permute-start(bf16[4,128,128]{2,1,0:T(8,128)(2,1)} %bitcast.3), channel_id=1, source_target_pairs={{0,2},{1,3},{2,0},{3,1},{4,6},{5,7},{6,4},{7,5},{8,10},{9,11},{10,... | collective-permute-start | bytes 393224 | tf_op jit(solution)/shard_map/ppermute | solution.py:214
  3.0 6.5 %collective-permute-start = (bf16[4,128,128]{2,1,0:T(8,128)(2,1)}, bf16[4,128,128]{2,1,0:T(8,128)(2,1)S(1)}, u32[]{:S(2)}, u32[]{:S(2)}) collective-permute-start(bf16[4,128,128]{2,1,0:T(8,128)(2,1)} %bitcast.4), channel_id=1, source_target_pairs={{0,1},{1,0},{2,3},{3,2},{4,5},{5,4},{6,7},{7,6},{8,9},{9,8},{10,11... | collective-permute-start | bytes 393224 | tf_op jit(solution)/shard_map/ppermute | solution.py:214
  3.1 10.6 %collective-permute-start.3 = (bf16[4,128,128]{2,1,0:T(8,128)(2,1)}, bf16[4,128,128]{2,1,0:T(8,128)(2,1)S(1)}, u32[]{:S(2)}, u32[]{:S(2)}) collective-permute-start(bf16[4,128,128]{2,1,0:T(8,128)(2,1)} %bitcast.5), channel_id=1, source_target_pairs={{0,16},{4,20},{8,24},{12,28},{16,0},{20,4},{24,8},{28,12},{1,17},{... | collective-permute-start | bytes 393224 | tf_op jit(solution)/shard_map/ppermute | solution.py:214
  9.8 9.5 %collective-permute-start.5 = (bf16[528,128]{1,0:T(8,128)(2,1)S(1)}, bf16[528,128]{1,0:T(8,128)(2,1)S(1)}, u32[]{:S(2)}, u32[]{:S(2)}) collective-permute-start(bf16[528,128]{1,0:T(8,128)(2,1)S(1)} %get-tuple-element.36), channel_id=1, source_target_pairs={{0,4},{4,0},{8,12},{12,8},{16,20},{20,16},{24,28},{28,24},{1,5},{5... | collective-permute-start | bytes 405512 | tf_op jit(solution)/shard_map/ppermute | solution.py:214
  12.1 7.1 %collective-permute-start.6 = (bf16[528,128]{1,0:T(8,128)(2,1)S(1)}, bf16[528,128]{1,0:T(8,128)(2,1)S(1)}, u32[]{:S(2)}, u32[]{:S(2)}) collective-permute-start(bf16[528,128]{1,0:T(8,128)(2,1)S(1)} %get-tuple-element.37), channel_id=1, source_target_pairs={{0,8},{4,12},{8,0},{12,4},{16,24},{20,28},{24,16},{28,20},{1,9},{5... | collective-permute-start | bytes 405512 | tf_op jit(solution)/shard_map/ppermute | solution.py:214
  13.7 5.6 %collective-permute-start.9 = (bf16[4,128,128]{2,1,0:T(8,128)(2,1)S(1)}, bf16[4,128,128]{2,1,0:T(8,128)(2,1)S(1)}, u32[]{:S(2)}, u32[]{:S(2)}) collective-permute-start(bf16[4,128,128]{2,1,0:T(8,128)(2,1)S(1)} %collective-permute-done.3.refs_0_), channel_id=1, source_target_pairs={{0,2},{1,3},{2,0},{3,1},{4,6},{5,7},{6,4},{7,5},{8,10},{9,11},{10,... | collective-permute-start | bytes 393224 | tf_op jit(solution)/shard_map/ppermute | solution.py:214
  15.2 9.9 %collective-permute-start.4 = (bf16[144,512]{1,0:T(8,128)(2,1)S(1)}, bf16[144,512]{1,0:T(8,128)(2,1)S(1)}, u32[]{:S(2)}, u32[]{:S(2)}) collective-permute-start(bf16[144,512]{1,0:T(8,128)(2,1)S(1)} %get-tuple-element.35), channel_id=1, source_target_pairs={{0,16},{4,20},{8,24},{12,28},{16,0},{20,4},{24,8},{28,12},{1,17},{... | collective-permute-start | bytes 442376 | tf_op jit(solution)/shard_map/ppermute | solution.py:214
  17.8 7.3 %collective-permute-start.7 = (bf16[528,128]{1,0:T(8,128)(2,1)S(1)}, bf16[528,128]{1,0:T(8,128)(2,1)S(1)}, u32[]{:S(2)}, u32[]{:S(2)}) collective-permute-start(bf16[528,128]{1,0:T(8,128)(2,1)S(1)} %get-tuple-element.38), channel_id=1, source_target_pairs={{0,12},{4,8},{8,4},{12,0},{16,28},{20,24},{24,20},{28,16},{1,13},{... | collective-permute-start | bytes 405512 | tf_op jit(solution)/shard_map/ppermute | solution.py:214
  19.3 5.9 %collective-permute-start.8 = (bf16[4,128,128]{2,1,0:T(8,128)(2,1)S(1)}, bf16[4,128,128]{2,1,0:T(8,128)(2,1)S(1)}, u32[]{:S(2)}, u32[]{:S(2)}) collective-permute-start(bf16[4,128,128]{2,1,0:T(8,128)(2,1)S(1)} %collective-permute-done.3.refs_0_), channel_id=1, source_target_pairs={{0,1},{1,0},{2,3},{3,2},{4,5},{5,4},{6,7},{7,6},{8,9},{9,8},{10,11... | collective-permute-start | bytes 393224 | tf_op jit(solution)/shard_map/ppermute | solution.py:214
  19.3 5.9 %collective-permute-start.10 = (bf16[4,128,128]{2,1,0:T(8,128)(2,1)S(1)}, bf16[4,128,128]{2,1,0:T(8,128)(2,1)S(1)}, u32[]{:S(2)}, u32[]{:S(2)}) collective-permute-start(bf16[4,128,128]{2,1,0:T(8,128)(2,1)S(1)} %collective-permute-done.9.refs_2_), channel_id=1, source_target_pairs={{0,1},{1,0},{2,3},{3,2},{4,5},{5,4},{6,7},{7,6},{8,9},{9,8},{10,11... | collective-permute-start | bytes 393224 | tf_op jit(solution)/shard_map/ppermute | solution.py:214
  25.4 6.2 %collective-permute-start.11 = (bf16[528,128]{1,0:T(8,128)(2,1)S(1)}, bf16[528,128]{1,0:T(8,128)(2,1)S(1)}, u32[]{:S(2)}, u32[]{:S(2)}) collective-permute-start(bf16[528,128]{1,0:T(8,128)(2,1)S(1)} %get-tuple-element.51), channel_id=1, source_target_pairs={{0,4},{4,0},{8,12},{12,8},{16,20},{20,16},{24,28},{28,24},{1,5},{5... | collective-permute-start | bytes 405512 | tf_op jit(solution)/shard_map/ppermute | solution.py:214
  26.4 5.3 %collective-permute-start.12 = (bf16[528,128]{1,0:T(8,128)(2,1)S(1)}, bf16[528,128]{1,0:T(8,128)(2,1)S(1)}, u32[]{:S(2)}, u32[]{:S(2)}) collective-permute-start(bf16[528,128]{1,0:T(8,128)(2,1)S(1)} %get-tuple-element.52), channel_id=1, source_target_pairs={{0,8},{4,12},{8,0},{12,4},{16,24},{20,28},{24,16},{28,20},{1,9},{5... | collective-permute-start | bytes 405512 | tf_op jit(solution)/shard_map/ppermute | solution.py:214
  27.6 5.9 %collective-permute-start.13 = (bf16[528,128]{1,0:T(8,128)(2,1)S(1)}, bf16[528,128]{1,0:T(8,128)(2,1)S(1)}, u32[]{:S(2)}, u32[]{:S(2)}) collective-permute-start(bf16[528,128]{1,0:T(8,128)(2,1)S(1)} %get-tuple-element.53), channel_id=1, source_target_pairs={{0,12},{4,8},{8,4},{12,0},{16,28},{20,24},{24,20},{28,16},{1,13},{... | collective-permute-start | bytes 405512 | tf_op jit(solution)/shard_map/ppermute | solution.py:214

commit v8 on v7

--- a/solution.py
+++ b/solution.py
@@ -285,13 +285,14 @@
         compiler_params=params,
         name="pick",
     )(*in_hbm(pair_list, occ_slot.reshape(1, -1), coef, blocks))
-    near_blocks = [near_block] + [flip(blocks, "aux", j) for j in range(1, aux_count)]
-
+    near_blocks = shared(blocks, sent_coef)
+    near_blocks[0] = near_block
+    far_block, near_coef, sent_coef = lax.optimization_barrier((far_block, near_coef, sent_coef))
+    far_coef = flip(sent_coef, "shell", group)
     near = transformed("near_blocks", near_coef, near_blocks, group)
-    far_block = after(far_block, near[0])
+    far_blocks = shared(far_block)
+    near = [*near[:-1], after(near[-1], far_blocks[1])]
     near = [near[0]] + [flip(near[f], "shell", f) for f in range(1, group)]
-    far_coef = flip(after(sent_coef, far_block), "shell", group)
-    far_blocks = shared(far_block, *near[1:3])
     far = transformed("far_blocks", after(far_coef, *near), far_blocks, group)
     far = [far[0]] + [flip(far[f], "shell", f) for f in range(1, group)]
     total_shape = jax.ShapeDtypeStruct((block_count, rows, BS), jnp.float32)

time: 36 us -> 37.7 us (1.047)
  waiting for transfers between devices: 10.6 us -> 16.5 us
  starting transfers between devices: 19.4 us -> 15.3 us
    ppermute x14, waiting for transfers between devices: 10.6 us -> 16.5 us  [flip(): return lax.ppermute(value, axis, [(at, at ^ bits) for at in range(count)])]
    ppermute x14, starting transfers between devices: 19.4 us -> 15.3 us  [flip(): return lax.ppermute(value, axis, [(at, at ^ bits) for at in range(count)])]
  transfers between devices with their start and end apart: 14 -> 14, of which waited for: 4 -> 9; matrix products, arithmetic and copies ran while one was open for 0% -> 0% of each run, Pallas kernels for 9% -> 8%
where the time goes in v8:
time: 37.7 us; the launch traced here: 37.6 us
  waiting for transfers between devices  16.5 us (44%)
  starting transfers between devices  15.3 us (41%)
  Pallas kernels  5.76 us (15%)
    ppermute x14, waiting for transfers between devices, flip(): return lax.ppermute(value, axis, [(at, at ^ bits) for at in range(count)])  16.5 us
    ppermute x14, starting transfers between devices, flip(): return lax.ppermute(value, axis, [(at, at ^ bits) for at in range(count)])  15.3 us
    pallas_call x1, Pallas kernels, exchanged_inputs(): pl.pallas_call(collect_kernel, out_shape=[jax.ShapeDtypeStruct((occ_local...  2.33 us
    pallas_call x1, Pallas kernels, exchanged_inputs(): pl.pallas_call(functools.partial(pick_kernel, flips, occ_local, aux_count...  2 us
    pallas_call x1, Pallas kernels, exchanged_inputs(): pl.pallas_call(near_sum_kernel, out_shape=total_shape, in_specs=[vmem] *...  0.84 us
  transfers between devices with their start and end apart: 14, of which 9 were waited for; matrix products, arithmetic and copies ran while one was open for 0% of the time, Pallas kernels for 8%

profile of v8, /device:TPU:0, one launch (start us, length us, event | category | flops | bytes accessed | tf_op | source)
XLA Modules:
  0.0 37.6 jit_solution(16732072095201198288)
XLA Ops:
  0.0 3.0 %collective-permute-start.2 = (bf16[4,128,128]{2,1,0:T(8,128)(2,1)}, bf16[4,128,128]{2,1,0:T(8,128)(2,1)S(1)}, u32[]{:S(2)}, u32[]{:S(2)}) collective-permute-start(bf16[4,128,128]{2,1,0:T(8,128)(2,1)} %bitcast.2), channel_id=1, source_target_pairs={{0,2},{1,3},{2,0},{3,1},{4,6},{5,7},{6,4},{7,5},{8,10},{9,11},{10,... | collective-permute-start | bytes 393224 | tf_op jit(solution)/shard_map/ppermute | solution.py:214
  3.0 2.6 %collective-permute-start = (bf16[4,128,128]{2,1,0:T(8,128)(2,1)}, bf16[4,128,128]{2,1,0:T(8,128)(2,1)S(1)}, u32[]{:S(2)}, u32[]{:S(2)}) collective-permute-start(bf16[4,128,128]{2,1,0:T(8,128)(2,1)} %bitcast.3), channel_id=1, source_target_pairs={{0,16},{4,20},{8,24},{12,28},{16,0},{20,4},{24,8},{28,12},{1,17},{... | collective-permute-start | bytes 393224 | tf_op jit(solution)/shard_map/ppermute | solution.py:214
  5.6 2.0 %pick.1 = (bf16[144,512]{1,0:T(8,128)(2,1)S(1)}, bf16[144,512]{1,0:T(8,128)(2,1)S(1)}, bf16[4,128,128]{2,1,0:T(8,128)(2,1)S(1)}) custom-call(s32[4,3]{1,0:T(4,128)} %pairs_in.1, s32[1,128]{1,0:T(1,128)} %bitcast.6, bf16[512,1024]{1,0:T(8,128)(2,1)} %coef_in.1, bf16[4,128,128]{2,1,0:T(8,128)(2,1)} %bitcast.4), custom_call_target="tpu_custom_call" | custom-call | tf_op jit(solution)/shard_map/pick/pallas_call | solution.py:270
  7.6 0.1 collective-permute-start.1
  7.7 0.5 %collective-permute-start.3 = (bf16[4,128,128]{2,1,0:T(8,128)(2,1)S(1)}, bf16[4,128,128]{2,1,0:T(8,128)(2,1)S(1)}, u32[]{:S(2)}, u32[]{:S(2)}) collective-permute-start(bf16[4,128,128]{2,1,0:T(8,128)(2,1)S(1)} %collective-permute-done.2.refs_2_), channel_id=1, source_target_pairs={{0,1},{1,0},{2,3},{3,2},{4,5},{5,4},{6,7},{7,6},{8,9},{9,8},{10,11... | collective-permute-start | bytes 393224 | tf_op jit(solution)/shard_map/ppermute | solution.py:214
  8.1 3.7 %collective-permute-done.refs_0_ = bf16[4,128,128]{2,1,0:T(8,128)(2,1)S(1)} collective-permute-done((bf16[4,128,128]{2,1,0:T(8,128)(2,1)}, bf16[4,128,128]{2,1,0:T(8,128)(2,1)S(1)}, u32[]{:S(2)}, u32[]{:S(2)}) %collective-permute-start) | collective-permute-done | bytes 131104 | tf_op jit(solution)/shard_map/ppermute | solution.py:214
  11.9 0.5 %collective-permute-start.9 = (bf16[4,128,128]{2,1,0:T(8,128)(2,1)S(1)}, bf16[4,128,128]{2,1,0:T(8,128)(2,1)S(1)}, u32[]{:S(2)}, u32[]{:S(2)}) collective-permute-start(bf16[4,128,128]{2,1,0:T(8,128)(2,1)S(1)} %collective-permute-done.refs_0_), channel_id=1, source_target_pairs={{0,2},{1,3},{2,0},{3,1},{4,6},{5,7},{6,4},{7,5},{8,10},{9,11},{10,... | collective-permute-start | bytes 393224 | tf_op jit(solution)/shard_map/ppermute | solution.py:214
  12.3 0.3 near_blocks.1
  12.6 0.6 %collective-permute-done.7.refs_1_ = bf16[4,128,128]{2,1,0:T(8,128)(2,1)S(1)} collective-permute-done((bf16[4,128,128]{2,1,0:T(8,128)(2,1)S(1)}, bf16[4,128,128]{2,1,0:T(8,128)(2,1)S(1)}, u32[]{:S(2)}, u32[]{:S(2)}) %collective-permute-start.7) | collective-permute-done | bytes 131104 | tf_op jit(solution)/shard_map/ppermute | solution.py:214
  13.2 4.5 %collective-permute-start.8 = (bf16[528,128]{1,0:T(8,128)(2,1)S(1)}, bf16[528,128]{1,0:T(8,128)(2,1)S(1)}, u32[]{:S(2)}, u32[]{:S(2)}) collective-permute-start(bf16[528,128]{1,0:T(8,128)(2,1)S(1)} %get-tuple-element.46), channel_id=1, source_target_pairs={{0,12},{4,8},{8,4},{12,0},{16,28},{20,24},{24,20},{28,16},{1,13},{... | collective-permute-start | bytes 405512 | tf_op jit(solution)/shard_map/ppermute | solution.py:214
  17.7 0.5 %collective-permute-start.5 = (bf16[528,128]{1,0:T(8,128)(2,1)S(1)}, bf16[528,128]{1,0:T(8,128)(2,1)S(1)}, u32[]{:S(2)}, u32[]{:S(2)}) collective-permute-start(bf16[528,128]{1,0:T(8,128)(2,1)S(1)} %get-tuple-element.42), channel_id=1, source_target_pairs={{0,4},{4,0},{8,12},{12,8},{16,20},{20,16},{24,28},{28,24},{1,5},{5... | collective-permute-start | bytes 405512 | tf_op jit(solution)/shard_map/ppermute | solution.py:214
  18.3 0.1 collective-permute-start.6
  18.4 4.1 %collective-permute-done.4.coefs = bf16[144,512]{1,0:T(8,128)(2,1)S(1)} collective-permute-done((bf16[144,512]{1,0:T(8,128)(2,1)S(1)}, bf16[144,512]{1,0:T(8,128)(2,1)S(1)}, u32[]{:S(2)}, u32[]{:S(2)}) %collective-permute-start.4) | collective-permute-done | bytes 147488 | tf_op jit(solution)/shard_map/ppermute | solution.py:214
  22.5 1.5 %collective-permute-done.8.refs_3_ = bf16[528,128]{1,0:T(8,128)(2,1)S(1)} collective-permute-done((bf16[528,128]{1,0:T(8,128)(2,1)S(1)}, bf16[528,128]{1,0:T(8,128)(2,1)S(1)}, u32[]{:S(2)}, u32[]{:S(2)}) %collective-permute-start.8) | collective-permute-done | bytes 135200 | tf_op jit(solution)/shard_map/ppermute | solution.py:214
  24.0 0.3 collective-permute-done.5.refs_1_
  24.3 1.3 %collective-permute-done.6.refs_2_ = bf16[528,128]{1,0:T(8,128)(2,1)S(1)} collective-permute-done((bf16[528,128]{1,0:T(8,128)(2,1)S(1)}, bf16[528,128]{1,0:T(8,128)(2,1)S(1)}, u32[]{:S(2)}, u32[]{:S(2)}) %collective-permute-start.6) | collective-permute-done | bytes 135200 | tf_op jit(solution)/shard_map/ppermute | solution.py:214
  25.6 0.3 far_blocks.1
  25.9 1.6 %collective-permute-start.11 = (bf16[528,128]{1,0:T(8,128)(2,1)S(1)}, bf16[528,128]{1,0:T(8,128)(2,1)S(1)}, u32[]{:S(2)}, u32[]{:S(2)}) collective-permute-start(bf16[528,128]{1,0:T(8,128)(2,1)S(1)} %get-tuple-element.53), channel_id=1, source_target_pairs={{0,4},{4,0},{8,12},{12,8},{16,20},{20,16},{24,28},{28,24},{1,5},{5... | collective-permute-start | bytes 405512 | tf_op jit(solution)/shard_map/ppermute | solution.py:214
  27.5 2.0 %collective-permute-start.13 = (bf16[528,128]{1,0:T(8,128)(2,1)S(1)}, bf16[528,128]{1,0:T(8,128)(2,1)S(1)}, u32[]{:S(2)}, u32[]{:S(2)}) collective-permute-start(bf16[528,128]{1,0:T(8,128)(2,1)S(1)} %get-tuple-element.55), channel_id=1, source_target_pairs={{0,12},{4,8},{8,4},{12,0},{16,28},{20,24},{24,20},{28,16},{1,13},{... | collective-permute-start | bytes 405512 | tf_op jit(solution)/shard_map/ppermute | solution.py:214
  29.4 0.8 %near_sum.1.total_in = f32[32,128,128]{2,1,0:T(8,128)S(1)} custom-call(bf16[528,128]{1,0:T(8,128)(2,1)S(1)} %get-tuple-element.49.refs_0_, bf16[528,128]{1,0:T(8,128)(2,1)S(1)} %collective-permute-done.5.refs_1_, bf16[528,128]{1,0:T(8,128)(2,1)S(1)} %collective-permute-done.6.refs_2_, bf16[528,128]{1,0:T(8,128)(2,1)S(1)} %collective-permute-done.8.refs_3_), custom_call_target="tpu_custom_call" | custom-call | tf_op jit(solution)/shard_map/near_sum/pallas_call | solution.py:299
  30.3 1.3 %collective-permute-done.11.refs_1_ = bf16[528,128]{1,0:T(8,128)(2,1)S(1)} collective-permute-done((bf16[528,128]{1,0:T(8,128)(2,1)S(1)}, bf16[528,128]{1,0:T(8,128)(2,1)S(1)}, u32[]{:S(2)}, u32[]{:S(2)}) %collective-permute-start.11) | collective-permute-done | bytes 135200 | tf_op jit(solution)/shard_map/ppermute | solution.py:214
  31.6 2.3 %collective-permute-done.12.refs_2_ = bf16[528,128]{1,0:T(8,128)(2,1)S(1)} collective-permute-done((bf16[528,128]{1,0:T(8,128)(2,1)S(1)}, bf16[528,128]{1,0:T(8,128)(2,1)S(1)}, u32[]{:S(2)}, u32[]{:S(2)}) %collective-permute-start.12) | collective-permute-done | bytes 135200 | tf_op jit(solution)/shard_map/ppermute | solution.py:214
  33.9 1.4 %collective-permute-done.13.refs_3_ = bf16[528,128]{1,0:T(8,128)(2,1)S(1)} collective-permute-done((bf16[528,128]{1,0:T(8,128)(2,1)S(1)}, bf16[528,128]{1,0:T(8,128)(2,1)S(1)}, u32[]{:S(2)}, u32[]{:S(2)}) %collective-permute-start.13) | collective-permute-done | bytes 135200 | tf_op jit(solution)/shard_map/ppermute | solution.py:214
  35.2 2.3 %collect.1 = (bf16[32,4,4096]{2,1,0:T(4,128)(2,1)}, f32[32,128,128]{2,1,0:T(8,128)S(1)}) custom-call(bf16[4,4]{1,0:T(4,128)(2,1)} %metric_in.1, f32[32,128,128]{2,1,0:T(8,128)S(1)} %near_sum.1.total_in, bf16[528,128]{1,0:T(8,128)(2,1)S(1)} %get-tuple-element.48.refs_0_, ...), custom_call_target="tpu_custom_call", output_to_operand_aliasing={{1}: (1, {})} | custom-call | tf_op jit(solution)/shard_map/collect/pallas_call | solution.py:308
  (9 shorter events, 0.0 us)
Async XLA Ops:
  0.0 7.7 %collective-permute-start.2 = (bf16[4,128,128]{2,1,0:T(8,128)(2,1)}, bf16[4,128,128]{2,1,0:T(8,128)(2,1)S(1)}, u32[]{:S(2)}, u32[]{:S(2)}) collective-permute-start(bf16[4,128,128]{2,1,0:T(8,128)(2,1)} %bitcast.2), channel_id=1, source_target_pairs={{0,2},{1,3},{2,0},{3,1},{4,6},{5,7},{6,4},{7,5},{8,10},{9,11},{10,... | collective-permute-start | bytes 393224 | tf_op jit(solution)/shard_map/ppermute | solution.py:214
  3.0 8.9 %collective-permute-start = (bf16[4,128,128]{2,1,0:T(8,128)(2,1)}, bf16[4,128,128]{2,1,0:T(8,128)(2,1)S(1)}, u32[]{:S(2)}, u32[]{:S(2)}) collective-permute-start(bf16[4,128,128]{2,1,0:T(8,128)(2,1)} %bitcast.3), channel_id=1, source_target_pairs={{0,16},{4,20},{8,24},{12,28},{16,0},{20,4},{24,8},{28,12},{1,17},{... | collective-permute-start | bytes 393224 | tf_op jit(solution)/shard_map/ppermute | solution.py:214
  7.6 4.8 %collective-permute-start.1 = (bf16[4,128,128]{2,1,0:T(8,128)(2,1)}, bf16[4,128,128]{2,1,0:T(8,128)(2,1)S(1)}, u32[]{:S(2)}, u32[]{:S(2)}) collective-permute-start(bf16[4,128,128]{2,1,0:T(8,128)(2,1)} %bitcast.5), channel_id=1, source_target_pairs={{0,1},{1,0},{2,3},{3,2},{4,5},{5,4},{6,7},{7,6},{8,9},{9,8},{10,11... | collective-permute-start | bytes 393224 | tf_op jit(solution)/shard_map/ppermute | solution.py:214
  7.7 4.7 %collective-permute-start.3 = (bf16[4,128,128]{2,1,0:T(8,128)(2,1)S(1)}, bf16[4,128,128]{2,1,0:T(8,128)(2,1)S(1)}, u32[]{:S(2)}, u32[]{:S(2)}) collective-permute-start(bf16[4,128,128]{2,1,0:T(8,128)(2,1)S(1)} %collective-permute-done.2.refs_2_), channel_id=1, source_target_pairs={{0,1},{1,0},{2,3},{3,2},{4,5},{5,4},{6,7},{7,6},{8,9},{9,8},{10,11... | collective-permute-start | bytes 393224 | tf_op jit(solution)/shard_map/ppermute | solution.py:214
  11.9 1.3 %collective-permute-start.7 = (bf16[4,128,128]{2,1,0:T(8,128)(2,1)S(1)}, bf16[4,128,128]{2,1,0:T(8,128)(2,1)S(1)}, u32[]{:S(2)}, u32[]{:S(2)}) collective-permute-start(bf16[4,128,128]{2,1,0:T(8,128)(2,1)S(1)} %collective-permute-done.refs_0_), channel_id=1, source_target_pairs={{0,1},{1,0},{2,3},{3,2},{4,5},{5,4},{6,7},{7,6},{8,9},{9,8},{10,11... | collective-permute-start | bytes 393224 | tf_op jit(solution)/shard_map/ppermute | solution.py:214
  11.9 6.5 %collective-permute-start.9 = (bf16[4,128,128]{2,1,0:T(8,128)(2,1)S(1)}, bf16[4,128,128]{2,1,0:T(8,128)(2,1)S(1)}, u32[]{:S(2)}, u32[]{:S(2)}) collective-permute-start(bf16[4,128,128]{2,1,0:T(8,128)(2,1)S(1)} %collective-permute-done.refs_0_), channel_id=1, source_target_pairs={{0,2},{1,3},{2,0},{3,1},{4,6},{5,7},{6,4},{7,5},{8,10},{9,11},{10,... | collective-permute-start | bytes 393224 | tf_op jit(solution)/shard_map/ppermute | solution.py:214
  12.3 10.1 %collective-permute-start.4 = (bf16[144,512]{1,0:T(8,128)(2,1)S(1)}, bf16[144,512]{1,0:T(8,128)(2,1)S(1)}, u32[]{:S(2)}, u32[]{:S(2)}) collective-permute-start(bf16[144,512]{1,0:T(8,128)(2,1)S(1)} %get-tuple-element.41), channel_id=1, source_target_pairs={{0,16},{4,20},{8,24},{12,28},{16,0},{20,4},{24,8},{28,12},{1,17},{... | collective-permute-start | bytes 442376 | tf_op jit(solution)/shard_map/ppermute | solution.py:214
  13.2 10.8 %collective-permute-start.8 = (bf16[528,128]{1,0:T(8,128)(2,1)S(1)}, bf16[528,128]{1,0:T(8,128)(2,1)S(1)}, u32[]{:S(2)}, u32[]{:S(2)}) collective-permute-start(bf16[528,128]{1,0:T(8,128)(2,1)S(1)} %get-tuple-element.46), channel_id=1, source_target_pairs={{0,12},{4,8},{8,4},{12,0},{16,28},{20,24},{24,20},{28,16},{1,13},{... | collective-permute-start | bytes 405512 | tf_op jit(solution)/shard_map/ppermute | solution.py:214
  17.7 6.6 %collective-permute-start.5 = (bf16[528,128]{1,0:T(8,128)(2,1)S(1)}, bf16[528,128]{1,0:T(8,128)(2,1)S(1)}, u32[]{:S(2)}, u32[]{:S(2)}) collective-permute-start(bf16[528,128]{1,0:T(8,128)(2,1)S(1)} %get-tuple-element.42), channel_id=1, source_target_pairs={{0,4},{4,0},{8,12},{12,8},{16,20},{20,16},{24,28},{28,24},{1,5},{5... | collective-permute-start | bytes 405512 | tf_op jit(solution)/shard_map/ppermute | solution.py:214
  18.3 7.3 %collective-permute-start.6 = (bf16[528,128]{1,0:T(8,128)(2,1)S(1)}, bf16[528,128]{1,0:T(8,128)(2,1)S(1)}, u32[]{:S(2)}, u32[]{:S(2)}) collective-permute-start(bf16[528,128]{1,0:T(8,128)(2,1)S(1)} %get-tuple-element.43), channel_id=1, source_target_pairs={{0,8},{4,12},{8,0},{12,4},{16,24},{20,28},{24,16},{28,20},{1,9},{5... | collective-permute-start | bytes 405512 | tf_op jit(solution)/shard_map/ppermute | solution.py:214
  18.4 7.2 %collective-permute-start.10 = (bf16[4,128,128]{2,1,0:T(8,128)(2,1)S(1)}, bf16[4,128,128]{2,1,0:T(8,128)(2,1)S(1)}, u32[]{:S(2)}, u32[]{:S(2)}) collective-permute-start(bf16[4,128,128]{2,1,0:T(8,128)(2,1)S(1)} %collective-permute-done.9.refs_2_), channel_id=1, source_target_pairs={{0,1},{1,0},{2,3},{3,2},{4,5},{5,4},{6,7},{7,6},{8,9},{9,8},{10,11... | collective-permute-start | bytes 393224 | tf_op jit(solution)/shard_map/ppermute | solution.py:214
  25.9 5.7 %collective-permute-start.11 = (bf16[528,128]{1,0:T(8,128)(2,1)S(1)}, bf16[528,128]{1,0:T(8,128)(2,1)S(1)}, u32[]{:S(2)}, u32[]{:S(2)}) collective-permute-start(bf16[528,128]{1,0:T(8,128)(2,1)S(1)} %get-tuple-element.53), channel_id=1, source_target_pairs={{0,4},{4,0},{8,12},{12,8},{16,20},{20,16},{24,28},{28,24},{1,5},{5... | collective-permute-start | bytes 405512 | tf_op jit(solution)/shard_map/ppermute | solution.py:214
  27.5 6.4 %collective-permute-start.12 = (bf16[528,128]{1,0:T(8,128)(2,1)S(1)}, bf16[528,128]{1,0:T(8,128)(2,1)S(1)}, u32[]{:S(2)}, u32[]{:S(2)}) collective-permute-start(bf16[528,128]{1,0:T(8,128)(2,1)S(1)} %get-tuple-element.54), channel_id=1, source_target_pairs={{0,8},{4,12},{8,0},{12,4},{16,24},{20,28},{24,16},{28,20},{1,9},{5... | collective-permute-start | bytes 405512 | tf_op jit(solution)/shard_map/ppermute | solution.py:214
  27.5 7.8 %collective-permute-start.13 = (bf16[528,128]{1,0:T(8,128)(2,1)S(1)}, bf16[528,128]{1,0:T(8,128)(2,1)S(1)}, u32[]{:S(2)}, u32[]{:S(2)}) collective-permute-start(bf16[528,128]{1,0:T(8,128)(2,1)S(1)} %get-tuple-element.55), channel_id=1, source_target_pairs={{0,12},{4,8},{8,4},{12,0},{16,28},{20,24},{24,20},{28,16},{1,13},{... | collective-permute-start | bytes 405512 | tf_op jit(solution)/shard_map/ppermute | solution.py:214

commit v9 on v7

--- a/solution.py
+++ b/solution.py
@@ -76,6 +76,16 @@
     )
 
 
+def code_tile(pairs):
+    pairs_dev = pairs.shape[0]
+    lane = lax.broadcasted_iota(jnp.int32, (1, BS), 1)
+    code = jnp.zeros((1, BS), jnp.int32)
+    for k in range(pairs_dev):
+        code = jnp.where(lane == k, pairs[k, 0] % 128, code)
+        code = jnp.where(lane == pairs_dev + k, pairs[k, 0] // 128, code)
+    return jnp.broadcast_to(code.astype(jnp.float32), (16, BS)).astype(jnp.bfloat16)
+
+
 def pick_kernel(
     flips,
     occ_local,
@@ -83,17 +93,16 @@
     pairs_in,
     slot_in,
     coef_in,
-    blocks_in,
     *refs,
 ):
-    *outs, blocks, pairs, slot_row, coef, sems = refs
+    *outs, pairs, slot_row, coef, sems = refs
     pairs_dev = pairs.shape[0]
     blocks_dev = coef.shape[0] // BS
     occ_count = coef.shape[1]
     loads = [
         pltpu.make_async_copy(source, target, sems.at[at])
         for at, (source, target) in enumerate(
-            ((slot_in, slot_row), (pairs_in, pairs), (coef_in, coef), (blocks_in, blocks))
+            ((slot_in, slot_row), (pairs_in, pairs), (coef_in, coef))
         )
     ]
     for load in loads:
@@ -109,12 +118,7 @@
     pick = (wanted == target).astype(jnp.bfloat16)
     for load in loads[1:]:
         load.wait()
-    lane = lax.broadcasted_iota(jnp.int32, (1, BS), 1)
-    code = jnp.zeros((1, BS), jnp.int32)
-    for k in range(pairs_dev):
-        code = jnp.where(lane == k, pairs[k, 0] % 128, code)
-        code = jnp.where(lane == pairs_dev + k, pairs[k, 0] // 128, code)
-    code = jnp.broadcast_to(code.astype(jnp.float32), (16, BS)).astype(jnp.bfloat16)
+    code = code_tile(pairs)
     for k in range(pairs_dev):
         start = pl.multiple_of(lax.rem(pairs[k, 1], blocks_dev) * BS, BS)
         live = (pairs[k, 2] == 1).astype(jnp.float32)
@@ -131,6 +135,73 @@
             out[:rows, k * BS : (k + 1) * BS] = piece[first : first + rows]
             out[rows:, k * BS : (k + 1) * BS] = code
             first += rows
+
+
+def near_kernel(
+    occ_local,
+    aux_count,
+    pairs_in,
+    slot_in,
+    coef_in,
+    blocks_in,
+    *refs,
+):
+    *outs, pairs, slot_row, coef, blocks, sems = refs
+    pairs_dev = pairs.shape[0]
+    blocks_dev = coef.shape[0] // BS
+    occ_count = coef.shape[1]
+    loads = [
+        pltpu.make_async_copy(source, target, sems.at[at])
+        for at, (source, target) in enumerate(
+            ((slot_in, slot_row), (pairs_in, pairs), (coef_in, coef), (blocks_in, blocks))
+        )
+    ]
+    for load in loads:
+        load.start()
+    me = lax.axis_index("shell")
+    mine = lax.axis_index("aux")
+    owned = aux_count * occ_local
+    row = lax.broadcasted_iota(jnp.int32, (len(outs) * owned, 1), 0)
+    owner = jnp.bitwise_xor(row // owned, me) * aux_count + jnp.bitwise_xor(
+        row // occ_local % aux_count, mine
+    )
+    wanted = owner * occ_local + row % occ_local
+    loads[0].wait()
+    target = targets_of(slot_row[...], slot_row.shape[1], occ_count)
+    pick = (wanted == target).astype(jnp.bfloat16)
+    for load in loads[1:]:
+        load.wait()
+    code = code_tile(pairs)
+    rows = [
+        coef[pl.ds(pl.multiple_of(lax.rem(pairs[k, 1], blocks_dev) * BS, BS), BS), :]
+        for k in range(pairs_dev)
+    ]
+    ordered = lax.dot_general(
+        pick,
+        jnp.concatenate(rows, axis=0),
+        (((1,), (1,)), ((), ())),
+        preferred_element_type=jnp.float32,
+    ).astype(jnp.bfloat16)
+    for k in range(pairs_dev):
+        block = jnp.dot(
+            ordered[:, k * BS : (k + 1) * BS], blocks[k], preferred_element_type=jnp.float32
+        )
+        block = (block * (pairs[k, 2] == 1).astype(jnp.float32)).astype(jnp.bfloat16)
+        for f, out in enumerate(outs):
+            for j in range(aux_count):
+                first = f * owned + j * occ_local
+                at = (j * pairs_dev + k) * occ_local
+                out[at : at + occ_local, :] = block[first : first + occ_local, :]
+    for out in outs:
+        out[pairs_dev * owned :, :] = code
+
+
+def regroup_kernel(count, *refs):
+    received, outs = refs[:count], refs[count:]
+    rows = outs[0].shape[0] // count
+    for j, out in enumerate(outs, 1):
+        for f, piece in enumerate(received):
+            out[f * rows : (f + 1) * rows, :] = piece[j * rows : (j + 1) * rows, :]
 
 
 def block_kernel(aux_count, coefs, *refs):
@@ -155,29 +226,31 @@
         piece[pairs_dev * aux_count * occ_local :, :] = coefs[rows:, :BS]
 
 
-def add_received(total, received, codes_v, codes, sem, meanwhile):
-    rows = total.shape[1]
-    pairs_dev = (received[0].shape[0] - 16) // rows
+def load_codes(received, codes_v, codes, sem):
     for at, piece in enumerate(received):
-        digits = piece[pairs_dev * rows :, :].astype(jnp.float32).astype(jnp.int32)
+        digits = piece[piece.shape[0] - 16 :, :].astype(jnp.float32).astype(jnp.int32)
         codes_v[at : at + 1, :] = digits[:1]
     load = pltpu.make_async_copy(codes_v, codes, sem)
     load.start()
-    meanwhile()
+    return load
+
+
+def near_sum_kernel(occ_local, count, *refs):
+    *received, total, codes_v, codes, sem = refs
+    received, others = received[:count], received[count:]
+    load = load_codes(received, codes_v, codes, sem)
+    total[...] = jnp.zeros_like(total)
+    mine = lax.axis_index("aux")
+    pairs_dev = others[0].shape[0] // (count * occ_local)
     load.wait()
-    for at, piece in enumerate(received):
+    for f in range(count):
         for k in range(pairs_dev):
-            r = codes[at, k] + 128 * codes[at, pairs_dev + k]
-            total[r] += piece[k * rows : (k + 1) * rows, :].astype(jnp.float32)
-
-
-def near_sum_kernel(*refs):
-    *received, total, codes_v, codes, sem = refs
-
-    def clear():
-        total[...] = jnp.zeros_like(total)
-
-    add_received(total, received, codes_v, codes, sem, clear)
+            r = codes[f, k] + 128 * codes[f, pairs_dev + k]
+            for j in range(len(others) + 1):
+                source, first = (others[j - 1], f * pairs_dev + k) if j else (received[f], k)
+                start = pl.multiple_of(jnp.bitwise_xor(mine, j) * occ_local, occ_local)
+                part = source[first * occ_local : (first + 1) * occ_local, :]
+                total[r, pl.ds(start, occ_local), :] += part.astype(jnp.float32)
 
 
 def collect_kernel(metric_in, total_in, *refs):
@@ -186,7 +259,14 @@
     rows = occ_local * aux_count
     load = pltpu.make_async_copy(metric_in, metric, metric_sem)
     load.start()
-    add_received(total, received, codes_v, codes, sem, load.wait)
+    code_load = load_codes(received, codes_v, codes, sem)
+    pairs_dev = (received[0].shape[0] - 16) // rows
+    code_load.wait()
+    for at, piece in enumerate(received):
+        for k in range(pairs_dev):
+            r = codes[at, k] + 128 * codes[at, pairs_dev + k]
+            total[r] += piece[k * rows : (k + 1) * rows, :].astype(jnp.float32)
+    load.wait()
 
     row = lax.broadcasted_iota(jnp.int32, (rows, rows), 0)
     column = lax.broadcasted_iota(jnp.int32, (rows, rows), 1)
@@ -265,45 +345,61 @@
 
     blocks = integrals.reshape(pairs_dev, BS, BS)
     far_block = flip(blocks, "shell", group)
-
-    flips = [list(range(group)), list(range(group, shell_count))]
-    near_coef, sent_coef, near_block = pl.pallas_call(
-        functools.partial(pick_kernel, flips, occ_local, aux_count),
+    operands = (pair_list, occ_slot.reshape(1, -1), coef)
+    loaded = [
+        pltpu.SMEM(pair_list.shape, jnp.int32),
+        pltpu.VMEM((1, occ_slot.shape[0]), jnp.int32),
+        pltpu.VMEM(coef.shape, jnp.bfloat16),
+    ]
+    near = pl.pallas_call(
+        functools.partial(near_kernel, occ_local, aux_count),
+        out_shape=[piece] * group,
+        in_specs=[hbm] * 4,
+        out_specs=[vmem] * group,
+        scratch_shapes=loaded
+        + [pltpu.VMEM(blocks.shape, jnp.bfloat16), pltpu.SemaphoreType.DMA((4,))],
+        compiler_params=params,
+        name="near_blocks",
+    )(*in_hbm(*operands, blocks))
+    near = [near[0]] + [flip(near[f], "shell", f) for f in range(1, group)]
+    (sent_coef,) = pl.pallas_call(
+        functools.partial(
+            pick_kernel, [list(range(group, shell_count))], occ_local, aux_count
+        ),
         out_shape=[
-            jax.ShapeDtypeStruct((len(f) * occ_local + 16, pairs_dev * BS), jnp.bfloat16)
-            for f in flips
-        ]
-        + [jax.ShapeDtypeStruct(blocks.shape, jnp.bfloat16)],
-        in_specs=[hbm] * 4,
-        out_specs=[vmem] * (len(flips) + 1),
-        scratch_shapes=[
-            pltpu.SMEM(pair_list.shape, jnp.int32),
-            pltpu.VMEM((1, occ_slot.shape[0]), jnp.int32),
-            pltpu.VMEM(coef.shape, jnp.bfloat16),
-            pltpu.SemaphoreType.DMA((4,)),
+            jax.ShapeDtypeStruct((group * occ_local + 16, pairs_dev * BS), jnp.bfloat16)
         ],
+        in_specs=[hbm] * 3,
+        out_specs=[vmem],
+        scratch_shapes=loaded + [pltpu.SemaphoreType.DMA((3,))],
         compiler_params=params,
         name="pick",
-    )(*in_hbm(pair_list, occ_slot.reshape(1, -1), coef, blocks))
-    near_blocks = [near_block] + [flip(blocks, "aux", j) for j in range(1, aux_count)]
-
-    near = transformed("near_blocks", near_coef, near_blocks, group)
-    far_block = after(far_block, near[0])
-    near = [near[0]] + [flip(near[f], "shell", f) for f in range(1, group)]
+    )(*in_hbm(*operands))
+    far_block = after(far_block, sent_coef)
     far_coef = flip(after(sent_coef, far_block), "shell", group)
-    far_blocks = shared(far_block, *near[1:3])
-    far = transformed("far_blocks", after(far_coef, *near), far_blocks, group)
-    far = [far[0]] + [flip(far[f], "shell", f) for f in range(1, group)]
+    far_blocks = shared(far_block)
+    regrouped = pl.pallas_call(
+        functools.partial(regroup_kernel, group),
+        out_shape=[jax.ShapeDtypeStruct((group * pairs_dev * occ_local, BS), jnp.bfloat16)]
+        * (aux_count - 1),
+        in_specs=[vmem] * group,
+        out_specs=[vmem] * (aux_count - 1),
+        compiler_params=params,
+        name="regroup",
+    )(*near)
+    others = [flip(one, "aux", j) for j, one in enumerate(regrouped, 1)]
+    far = transformed("far_blocks", far_coef, far_blocks, group)
     total_shape = jax.ShapeDtypeStruct((block_count, rows, BS), jnp.float32)
     total = pl.pallas_call(
-        near_sum_kernel,
+        functools.partial(near_sum_kernel, occ_local, group),
         out_shape=total_shape,
-        in_specs=[vmem] * group,
+        in_specs=[vmem] * (group + aux_count - 1),
         out_specs=vmem,
         scratch_shapes=code_scratch(group),
         compiler_params=params,
         name="near_sum",
-    )(*(after(one, far[0]) for one in near))
+    )(*(after(one, far[0]) for one in near), *others)
+    far = [far[0]] + [flip(far[f], "shell", f) for f in range(1, group)]
     return pl.pallas_call(
         collect_kernel,
         out_shape=[

time: 36 us -> 35.9 us (level)
  the two profiles are of different devices: /device:TPU:0 before, /device:TPU:1 now
where the time goes in v9:
time: 35.9 us; the launch traced here: 35.7 us
  starting transfers between devices  21.2 us (59%)
  Pallas kernels  7.55 us (21%)
  waiting for transfers between devices  6.85 us (19%)
    ppermute x14, starting transfers between devices, flip(): return lax.ppermute(value, axis, [(at, at ^ bits) for at in range(count)])  21.2 us
    ppermute x14, waiting for transfers between devices, flip(): return lax.ppermute(value, axis, [(at, at ^ bits) for at in range(count)])  6.85 us
    pallas_call x1, Pallas kernels, exchanged_inputs(): pl.pallas_call(collect_kernel, out_shape=[jax.ShapeDtypeStruct((occ_local...  2.34 us
    pallas_call x1, Pallas kernels, exchanged_inputs(): pl.pallas_call(functools.partial(near_kernel, occ_local, aux_count), out_...  2.22 us
    pallas_call x1, Pallas kernels, exchanged_inputs(): pl.pallas_call(functools.partial(pick_kernel, [list(range(group, shell_co...  1.72 us
    pallas_call x1, Pallas kernels, exchanged_inputs(): pl.pallas_call(functools.partial(near_sum_kernel, occ_local, group), out_...  0.94 us
  transfers between devices with their start and end apart: 14, of which 3 were waited for; matrix products, arithmetic and copies ran while one was open for 0% of the time, Pallas kernels for 15%

profile of v9, /device:TPU:1, one launch (start us, length us, event | category | flops | bytes accessed | tf_op | source)
XLA Modules:
  0.0 35.7 jit_solution(2393340328142335595)
XLA Ops:
  0.0 3.1 %collective-permute-start = (bf16[4,128,128]{2,1,0:T(8,128)(2,1)}, bf16[4,128,128]{2,1,0:T(8,128)(2,1)S(1)}, u32[]{:S(2)}, u32[]{:S(2)}) collective-permute-start(bf16[4,128,128]{2,1,0:T(8,128)(2,1)} %bitcast.2), channel_id=1, source_target_pairs={{0,16},{4,20},{8,24},{12,28},{16,0},{20,4},{24,8},{28,12},{1,17},{... | collective-permute-start | bytes 393224 | tf_op jit(solution)/shard_map/ppermute | solution.py:294
  3.1 2.2 %near_blocks.1 = (bf16[528,128]{1,0:T(8,128)(2,1)S(1)}, bf16[528,128]{1,0:T(8,128)(2,1)S(1)}, bf16[528,128]{1,0:T(8,128)(2,1)S(1)}, bf16[528,128]{1,0:T(8,128)(2,1)S(1)}) custom-call(s32[4,3]{1,0:T(4,128)} %pairs_in.3, s32[1,128]{1,0:T(1,128)} %bitcast.4, bf16[512,1024]{1,0:T(8,128)(2,1)} %coef_in.3, bf16[4,128,128]{2,1,0:T(8,128)(2,1)} %bitcast.3), custom_call_target="tpu_custom_call" | custom-call | tf_op jit(solution)/shard_map/near_blocks/pallas_call | solution.py:354
  5.4 1.3 %collective-permute-start.5 = (bf16[528,128]{1,0:T(8,128)(2,1)S(1)}, bf16[528,128]{1,0:T(8,128)(2,1)S(1)}, u32[]{:S(2)}, u32[]{:S(2)}) collective-permute-start(bf16[528,128]{1,0:T(8,128)(2,1)S(1)} %get-tuple-element.28), channel_id=1, source_target_pairs={{0,4},{4,0},{8,12},{12,8},{16,20},{20,16},{24,28},{28,24},{1,5},{5... | collective-permute-start | bytes 405512 | tf_op jit(solution)/shard_map/ppermute | solution.py:294
  6.7 1.3 %collective-permute-start.6 = (bf16[528,128]{1,0:T(8,128)(2,1)S(1)}, bf16[528,128]{1,0:T(8,128)(2,1)S(1)}, u32[]{:S(2)}, u32[]{:S(2)}) collective-permute-start(bf16[528,128]{1,0:T(8,128)(2,1)S(1)} %get-tuple-element.30), channel_id=1, source_target_pairs={{0,8},{4,12},{8,0},{12,4},{16,24},{20,28},{24,16},{28,20},{1,9},{5... | collective-permute-start | bytes 405512 | tf_op jit(solution)/shard_map/ppermute | solution.py:294
  7.9 0.1 collective-permute-start.7
  8.1 1.7 %pick.1 = bf16[144,512]{1,0:T(8,128)(2,1)S(1)} custom-call(s32[4,3]{1,0:T(4,128)} %pairs_in.3, s32[1,128]{1,0:T(1,128)} %bitcast.5, bf16[512,1024]{1,0:T(8,128)(2,1)} %coef_in.3), custom_call_target="tpu_custom_call" | custom-call | tf_op jit(solution)/shard_map/pick/pallas_call | solution.py:365
  9.8 0.0 collective-permute-done.refs_0_
  9.8 1.3 %collective-permute-start.3 = (bf16[4,128,128]{2,1,0:T(8,128)(2,1)S(1)}, bf16[4,128,128]{2,1,0:T(8,128)(2,1)S(1)}, u32[]{:S(2)}, u32[]{:S(2)}) collective-permute-start(bf16[4,128,128]{2,1,0:T(8,128)(2,1)S(1)} %collective-permute-done.refs_0_), channel_id=1, source_target_pairs={{0,2},{1,3},{2,0},{3,1},{4,6},{5,7},{6,4},{7,5},{8,10},{9,11},{10,... | collective-permute-start | bytes 393224 | tf_op jit(solution)/shard_map/ppermute | solution.py:294
  11.1 0.1 collective-permute-start.1
  11.2 0.0 collective-permute-done.5.refs_1_
  11.2 2.4 %collective-permute-start.2 = (bf16[4,128,128]{2,1,0:T(8,128)(2,1)S(1)}, bf16[4,128,128]{2,1,0:T(8,128)(2,1)S(1)}, u32[]{:S(2)}, u32[]{:S(2)}) collective-permute-start(bf16[4,128,128]{2,1,0:T(8,128)(2,1)S(1)} %collective-permute-done.refs_0_), channel_id=1, source_target_pairs={{0,1},{1,0},{2,3},{3,2},{4,5},{5,4},{6,7},{7,6},{8,9},{9,8},{10,11... | collective-permute-start | bytes 393224 | tf_op jit(solution)/shard_map/ppermute | solution.py:294
  13.5 0.5 %collective-permute-done.3.refs_2_ = bf16[4,128,128]{2,1,0:T(8,128)(2,1)S(1)} collective-permute-done((bf16[4,128,128]{2,1,0:T(8,128)(2,1)S(1)}, bf16[4,128,128]{2,1,0:T(8,128)(2,1)S(1)}, u32[]{:S(2)}, u32[]{:S(2)}) %collective-permute-start.3) | collective-permute-done | bytes 131104 | tf_op jit(solution)/shard_map/ppermute | solution.py:294
  14.0 2.7 %collective-permute-start.4 = (bf16[4,128,128]{2,1,0:T(8,128)(2,1)S(1)}, bf16[4,128,128]{2,1,0:T(8,128)(2,1)S(1)}, u32[]{:S(2)}, u32[]{:S(2)}) collective-permute-start(bf16[4,128,128]{2,1,0:T(8,128)(2,1)S(1)} %collective-permute-done.3.refs_2_), channel_id=1, source_target_pairs={{0,1},{1,0},{2,3},{3,2},{4,5},{5,4},{6,7},{7,6},{8,9},{9,8},{10,11... | collective-permute-start | bytes 393224 | tf_op jit(solution)/shard_map/ppermute | solution.py:294
  16.7 1.0 %collective-permute-done.7.refs_3_ = bf16[528,128]{1,0:T(8,128)(2,1)S(1)} collective-permute-done((bf16[528,128]{1,0:T(8,128)(2,1)S(1)}, bf16[528,128]{1,0:T(8,128)(2,1)S(1)}, u32[]{:S(2)}, u32[]{:S(2)}) %collective-permute-start.7) | collective-permute-done | bytes 135200 | tf_op jit(solution)/shard_map/ppermute | solution.py:294
  17.7 0.8 %collective-permute-start.8 = (bf16[512,128]{1,0:T(8,128)(2,1)S(1)}, bf16[512,128]{1,0:T(8,128)(2,1)S(1)}, u32[]{:S(2)}, u32[]{:S(2)}) collective-permute-start(bf16[512,128]{1,0:T(8,128)(2,1)S(1)} %get-tuple-element.34), channel_id=1, source_target_pairs={{0,1},{1,0},{2,3},{3,2},{4,5},{5,4},{6,7},{7,6},{8,9},{9,8},{10,11... | collective-permute-start | bytes 393224 | tf_op jit(solution)/shard_map/ppermute | solution.py:294
  18.5 0.3 far_blocks.1
  18.8 1.0 %collective-permute-start.11 = (bf16[528,128]{1,0:T(8,128)(2,1)S(1)}, bf16[528,128]{1,0:T(8,128)(2,1)S(1)}, u32[]{:S(2)}, u32[]{:S(2)}) collective-permute-start(bf16[528,128]{1,0:T(8,128)(2,1)S(1)} %get-tuple-element.37), channel_id=1, source_target_pairs={{0,4},{4,0},{8,12},{12,8},{16,20},{20,16},{24,28},{28,24},{1,5},{5... | collective-permute-start | bytes 405512 | tf_op jit(solution)/shard_map/ppermute | solution.py:294
  19.8 1.9 %collective-permute-start.12 = (bf16[528,128]{1,0:T(8,128)(2,1)S(1)}, bf16[528,128]{1,0:T(8,128)(2,1)S(1)}, u32[]{:S(2)}, u32[]{:S(2)}) collective-permute-start(bf16[528,128]{1,0:T(8,128)(2,1)S(1)} %get-tuple-element.38), channel_id=1, source_target_pairs={{0,8},{4,12},{8,0},{12,4},{16,24},{20,28},{24,16},{28,20},{1,9},{5... | collective-permute-start | bytes 405512 | tf_op jit(solution)/shard_map/ppermute | solution.py:294
  21.7 0.1 collective-permute-start.13
  21.8 1.8 %collective-permute-start.9 = (bf16[512,128]{1,0:T(8,128)(2,1)S(1)}, bf16[512,128]{1,0:T(8,128)(2,1)S(1)}, u32[]{:S(2)}, u32[]{:S(2)}) collective-permute-start(bf16[512,128]{1,0:T(8,128)(2,1)S(1)} %get-tuple-element.35), channel_id=1, source_target_pairs={{0,2},{1,3},{2,0},{3,1},{4,6},{5,7},{6,4},{7,5},{8,10},{9,11},{10,... | collective-permute-start | bytes 393224 | tf_op jit(solution)/shard_map/ppermute | solution.py:294
  23.6 3.4 %collective-permute-start.10 = (bf16[512,128]{1,0:T(8,128)(2,1)S(1)}, bf16[512,128]{1,0:T(8,128)(2,1)S(1)}, u32[]{:S(2)}, u32[]{:S(2)}) collective-permute-start(bf16[512,128]{1,0:T(8,128)(2,1)S(1)} %get-tuple-element.36), channel_id=1, source_target_pairs={{0,3},{1,2},{2,1},{3,0},{4,7},{5,6},{6,5},{7,4},{8,11},{9,10},{10,... | collective-permute-start | bytes 393224 | tf_op jit(solution)/shard_map/ppermute | solution.py:294
  27.0 5.4 %collective-permute-done.10.refs_6_ = bf16[512,128]{1,0:T(8,128)(2,1)S(1)} collective-permute-done((bf16[512,128]{1,0:T(8,128)(2,1)S(1)}, bf16[512,128]{1,0:T(8,128)(2,1)S(1)}, u32[]{:S(2)}, u32[]{:S(2)}) %collective-permute-start.10) | collective-permute-done | bytes 131104 | tf_op jit(solution)/shard_map/ppermute | solution.py:294
  32.4 0.9 %near_sum.1.total_in = f32[32,128,128]{2,1,0:T(8,128)S(1)} custom-call(bf16[528,128]{1,0:T(8,128)(2,1)S(1)} %get-tuple-element.27.refs_0_, bf16[528,128]{1,0:T(8,128)(2,1)S(1)} %collective-permute-done.5.refs_1_, bf16[528,128]{1,0:T(8,128)(2,1)S(1)} %collective-permute-done.6.refs_2_, bf16[528,128]{1,0:T(8,128)(2,1)S(1)} %collective-permute-done.7.refs_3_, ...), custom_call_target="tpu_custom_call" | custom-call | tf_op jit(solution)/shard_map/near_sum/pallas_call | solution.py:393
  33.4 2.3 %collect.1 = (bf16[32,4,4096]{2,1,0:T(4,128)(2,1)}, f32[32,128,128]{2,1,0:T(8,128)S(1)}) custom-call(bf16[4,4]{1,0:T(4,128)(2,1)} %metric_in.1, f32[32,128,128]{2,1,0:T(8,128)S(1)} %near_sum.1.total_in, bf16[528,128]{1,0:T(8,128)(2,1)S(1)} %get-tuple-element.26.refs_0_, ...), custom_call_target="tpu_custom_call", output_to_operand_aliasing={{1}: (1, {})} | custom-call | tf_op jit(solution)/shard_map/collect/pallas_call | solution.py:403
  (10 shorter events, 0.0 us)
Async XLA Ops:
  0.0 9.8 %collective-permute-start = (bf16[4,128,128]{2,1,0:T(8,128)(2,1)}, bf16[4,128,128]{2,1,0:T(8,128)(2,1)S(1)}, u32[]{:S(2)}, u32[]{:S(2)}) collective-permute-start(bf16[4,128,128]{2,1,0:T(8,128)(2,1)} %bitcast.2), channel_id=1, source_target_pairs={{0,16},{4,20},{8,24},{12,28},{16,0},{20,4},{24,8},{28,12},{1,17},{... | collective-permute-start | bytes 393224 | tf_op jit(solution)/shard_map/ppermute | solution.py:294
  5.4 5.8 %collective-permute-start.5 = (bf16[528,128]{1,0:T(8,128)(2,1)S(1)}, bf16[528,128]{1,0:T(8,128)(2,1)S(1)}, u32[]{:S(2)}, u32[]{:S(2)}) collective-permute-start(bf16[528,128]{1,0:T(8,128)(2,1)S(1)} %get-tuple-element.28), channel_id=1, source_target_pairs={{0,4},{4,0},{8,12},{12,8},{16,20},{20,16},{24,28},{28,24},{1,5},{5... | collective-permute-start | bytes 405512 | tf_op jit(solution)/shard_map/ppermute | solution.py:294
  6.7 10.0 %collective-permute-start.6 = (bf16[528,128]{1,0:T(8,128)(2,1)S(1)}, bf16[528,128]{1,0:T(8,128)(2,1)S(1)}, u32[]{:S(2)}, u32[]{:S(2)}) collective-permute-start(bf16[528,128]{1,0:T(8,128)(2,1)S(1)} %get-tuple-element.30), channel_id=1, source_target_pairs={{0,8},{4,12},{8,0},{12,4},{16,24},{20,28},{24,16},{28,20},{1,9},{5... | collective-permute-start | bytes 405512 | tf_op jit(solution)/shard_map/ppermute | solution.py:294
  7.9 9.7 %collective-permute-start.7 = (bf16[528,128]{1,0:T(8,128)(2,1)S(1)}, bf16[528,128]{1,0:T(8,128)(2,1)S(1)}, u32[]{:S(2)}, u32[]{:S(2)}) collective-permute-start(bf16[528,128]{1,0:T(8,128)(2,1)S(1)} %get-tuple-element.32), channel_id=1, source_target_pairs={{0,12},{4,8},{8,4},{12,0},{16,28},{20,24},{24,20},{28,16},{1,13},{... | collective-permute-start | bytes 405512 | tf_op jit(solution)/shard_map/ppermute | solution.py:294
  9.8 4.2 %collective-permute-start.3 = (bf16[4,128,128]{2,1,0:T(8,128)(2,1)S(1)}, bf16[4,128,128]{2,1,0:T(8,128)(2,1)S(1)}, u32[]{:S(2)}, u32[]{:S(2)}) collective-permute-start(bf16[4,128,128]{2,1,0:T(8,128)(2,1)S(1)} %collective-permute-done.refs_0_), channel_id=1, source_target_pairs={{0,2},{1,3},{2,0},{3,1},{4,6},{5,7},{6,4},{7,5},{8,10},{9,11},{10,... | collective-permute-start | bytes 393224 | tf_op jit(solution)/shard_map/ppermute | solution.py:294
  11.1 7.3 %collective-permute-start.1 = (bf16[144,512]{1,0:T(8,128)(2,1)S(1)}, bf16[144,512]{1,0:T(8,128)(2,1)S(1)}, u32[]{:S(2)}, u32[]{:S(2)}) collective-permute-start(bf16[144,512]{1,0:T(8,128)(2,1)S(1)} %pick.1), channel_id=1, source_target_pairs={{0,16},{4,20},{8,24},{12,28},{16,0},{20,4},{24,8},{28,12},{1,17},{... | collective-permute-start | bytes 442376 | tf_op jit(solution)/shard_map/ppermute | solution.py:294
  11.2 7.3 %collective-permute-start.2 = (bf16[4,128,128]{2,1,0:T(8,128)(2,1)S(1)}, bf16[4,128,128]{2,1,0:T(8,128)(2,1)S(1)}, u32[]{:S(2)}, u32[]{:S(2)}) collective-permute-start(bf16[4,128,128]{2,1,0:T(8,128)(2,1)S(1)} %collective-permute-done.refs_0_), channel_id=1, source_target_pairs={{0,1},{1,0},{2,3},{3,2},{4,5},{5,4},{6,7},{7,6},{8,9},{9,8},{10,11... | collective-permute-start | bytes 393224 | tf_op jit(solution)/shard_map/ppermute | solution.py:294
  14.0 4.5 %collective-permute-start.4 = (bf16[4,128,128]{2,1,0:T(8,128)(2,1)S(1)}, bf16[4,128,128]{2,1,0:T(8,128)(2,1)S(1)}, u32[]{:S(2)}, u32[]{:S(2)}) collective-permute-start(bf16[4,128,128]{2,1,0:T(8,128)(2,1)S(1)} %collective-permute-done.3.refs_2_), channel_id=1, source_target_pairs={{0,1},{1,0},{2,3},{3,2},{4,5},{5,4},{6,7},{7,6},{8,9},{9,8},{10,11... | collective-permute-start | bytes 393224 | tf_op jit(solution)/shard_map/ppermute | solution.py:294
  17.7 5.9 %collective-permute-start.8 = (bf16[512,128]{1,0:T(8,128)(2,1)S(1)}, bf16[512,128]{1,0:T(8,128)(2,1)S(1)}, u32[]{:S(2)}, u32[]{:S(2)}) collective-permute-start(bf16[512,128]{1,0:T(8,128)(2,1)S(1)} %get-tuple-element.34), channel_id=1, source_target_pairs={{0,1},{1,0},{2,3},{3,2},{4,5},{5,4},{6,7},{7,6},{8,9},{9,8},{10,11... | collective-permute-start | bytes 393224 | tf_op jit(solution)/shard_map/ppermute | solution.py:294
  18.8 14.6 %collective-permute-start.11 = (bf16[528,128]{1,0:T(8,128)(2,1)S(1)}, bf16[528,128]{1,0:T(8,128)(2,1)S(1)}, u32[]{:S(2)}, u32[]{:S(2)}) collective-permute-start(bf16[528,128]{1,0:T(8,128)(2,1)S(1)} %get-tuple-element.37), channel_id=1, source_target_pairs={{0,4},{4,0},{8,12},{12,8},{16,20},{20,16},{24,28},{28,24},{1,5},{5... | collective-permute-start | bytes 405512 | tf_op jit(solution)/shard_map/ppermute | solution.py:294
  19.8 13.5 %collective-permute-start.12 = (bf16[528,128]{1,0:T(8,128)(2,1)S(1)}, bf16[528,128]{1,0:T(8,128)(2,1)S(1)}, u32[]{:S(2)}, u32[]{:S(2)}) collective-permute-start(bf16[528,128]{1,0:T(8,128)(2,1)S(1)} %get-tuple-element.38), channel_id=1, source_target_pairs={{0,8},{4,12},{8,0},{12,4},{16,24},{20,28},{24,16},{28,20},{1,9},{5... | collective-permute-start | bytes 405512 | tf_op jit(solution)/shard_map/ppermute | solution.py:294
  21.7 11.7 %collective-permute-start.13 = (bf16[528,128]{1,0:T(8,128)(2,1)S(1)}, bf16[528,128]{1,0:T(8,128)(2,1)S(1)}, u32[]{:S(2)}, u32[]{:S(2)}) collective-permute-start(bf16[528,128]{1,0:T(8,128)(2,1)S(1)} %get-tuple-element.39), channel_id=1, source_target_pairs={{0,12},{4,8},{8,4},{12,0},{16,28},{20,24},{24,20},{28,16},{1,13},{... | collective-permute-start | bytes 405512 | tf_op jit(solution)/shard_map/ppermute | solution.py:294
  21.8 5.2 %collective-permute-start.9 = (bf16[512,128]{1,0:T(8,128)(2,1)S(1)}, bf16[512,128]{1,0:T(8,128)(2,1)S(1)}, u32[]{:S(2)}, u32[]{:S(2)}) collective-permute-start(bf16[512,128]{1,0:T(8,128)(2,1)S(1)} %get-tuple-element.35), channel_id=1, source_target_pairs={{0,2},{1,3},{2,0},{3,1},{4,6},{5,7},{6,4},{7,5},{8,10},{9,11},{10,... | collective-permute-start | bytes 393224 | tf_op jit(solution)/shard_map/ppermute | solution.py:294
  23.6 8.8 %collective-permute-start.10 = (bf16[512,128]{1,0:T(8,128)(2,1)S(1)}, bf16[512,128]{1,0:T(8,128)(2,1)S(1)}, u32[]{:S(2)}, u32[]{:S(2)}) collective-permute-start(bf16[512,128]{1,0:T(8,128)(2,1)S(1)} %get-tuple-element.36), channel_id=1, source_target_pairs={{0,3},{1,2},{2,1},{3,0},{4,7},{5,6},{6,5},{7,4},{8,11},{9,10},{10,... | collective-permute-start | bytes 393224 | tf_op jit(solution)/shard_map/ppermute | solution.py:294

commit v10 on v9

--- a/solution.py
+++ b/solution.py
@@ -397,6 +397,9 @@
         out_specs=vmem,
         scratch_shapes=code_scratch(group),
         compiler_params=params,
+        cost_estimate=pl.CostEstimate(
+            flops=10**10, transcendentals=0, bytes_accessed=20 * 2**20
+        ),
         name="near_sum",
     )(*(after(one, far[0]) for one in near), *others)
     far = [far[0]] + [flip(far[f], "shell", f) for f in range(1, group)]

time: 35.9 us -> 35.7 us (level)
  the two profiles are of different devices: /device:TPU:1 before, /device:TPU:0 now
where the time goes in v10:
time: 35.7 us; the launch traced here: 35.5 us
  starting transfers between devices  15 us (42%)
  waiting for transfers between devices  12.9 us (36%)
  Pallas kernels  7.55 us (21%)
    ppermute x14, starting transfers between devices, flip(): return lax.ppermute(value, axis, [(at, at ^ bits) for at in range(count)])  15 us
    ppermute x14, waiting for transfers between devices, flip(): return lax.ppermute(value, axis, [(at, at ^ bits) for at in range(count)])  12.9 us
    pallas_call x1, Pallas kernels, exchanged_inputs(): pl.pallas_call(collect_kernel, out_shape=[jax.ShapeDtypeStruct((occ_local...  2.34 us
    pallas_call x1, Pallas kernels, exchanged_inputs(): pl.pallas_call(functools.partial(near_kernel, occ_local, aux_count), out_...  2.23 us
    pallas_call x1, Pallas kernels, exchanged_inputs(): pl.pallas_call(functools.partial(pick_kernel, [list(range(group, shell_co...  1.72 us
    pallas_call x1, Pallas kernels, exchanged_inputs(): pl.pallas_call(functools.partial(near_sum_kernel, occ_local, group), out_...  0.95 us
  transfers between devices with their start and end apart: 14, of which 6 were waited for; matrix products, arithmetic and copies ran while one was open for 0% of the time, Pallas kernels for 15%

profile of v10, /device:TPU:0, one launch (start us, length us, event | category | flops | bytes accessed | tf_op | source)
XLA Modules:
  0.0 35.5 jit_solution(12307335972489710955)
XLA Ops:
  0.0 4.0 %collective-permute-start = (bf16[4,128,128]{2,1,0:T(8,128)(2,1)}, bf16[4,128,128]{2,1,0:T(8,128)(2,1)S(1)}, u32[]{:S(2)}, u32[]{:S(2)}) collective-permute-start(bf16[4,128,128]{2,1,0:T(8,128)(2,1)} %bitcast.2), channel_id=1, source_target_pairs={{0,16},{4,20},{8,24},{12,28},{16,0},{20,4},{24,8},{28,12},{1,17},{... | collective-permute-start | bytes 393224 | tf_op jit(solution)/shard_map/ppermute | solution.py:294
  4.0 2.2 %near_blocks.1 = (bf16[528,128]{1,0:T(8,128)(2,1)S(1)}, bf16[528,128]{1,0:T(8,128)(2,1)S(1)}, bf16[528,128]{1,0:T(8,128)(2,1)S(1)}, bf16[528,128]{1,0:T(8,128)(2,1)S(1)}) custom-call(s32[4,3]{1,0:T(4,128)} %pairs_in.3, s32[1,128]{1,0:T(1,128)} %bitcast.4, bf16[512,1024]{1,0:T(8,128)(2,1)} %coef_in.3, bf16[4,128,128]{2,1,0:T(8,128)(2,1)} %bitcast.3), custom_call_target="tpu_custom_call" | custom-call | tf_op jit(solution)/shard_map/near_blocks/pallas_call | solution.py:354
  6.3 1.6 %collective-permute-start.5 = (bf16[528,128]{1,0:T(8,128)(2,1)S(1)}, bf16[528,128]{1,0:T(8,128)(2,1)S(1)}, u32[]{:S(2)}, u32[]{:S(2)}) collective-permute-start(bf16[528,128]{1,0:T(8,128)(2,1)S(1)} %get-tuple-element.28), channel_id=1, source_target_pairs={{0,4},{4,0},{8,12},{12,8},{16,20},{20,16},{24,28},{28,24},{1,5},{5... | collective-permute-start | bytes 405512 | tf_op jit(solution)/shard_map/ppermute | solution.py:294
  7.8 1.6 %collective-permute-start.6 = (bf16[528,128]{1,0:T(8,128)(2,1)S(1)}, bf16[528,128]{1,0:T(8,128)(2,1)S(1)}, u32[]{:S(2)}, u32[]{:S(2)}) collective-permute-start(bf16[528,128]{1,0:T(8,128)(2,1)S(1)} %get-tuple-element.30), channel_id=1, source_target_pairs={{0,8},{4,12},{8,0},{12,4},{16,24},{20,28},{24,16},{28,20},{1,9},{5... | collective-permute-start | bytes 405512 | tf_op jit(solution)/shard_map/ppermute | solution.py:294
  9.4 0.4 %collective-permute-start.7 = (bf16[528,128]{1,0:T(8,128)(2,1)S(1)}, bf16[528,128]{1,0:T(8,128)(2,1)S(1)}, u32[]{:S(2)}, u32[]{:S(2)}) collective-permute-start(bf16[528,128]{1,0:T(8,128)(2,1)S(1)} %get-tuple-element.32), channel_id=1, source_target_pairs={{0,12},{4,8},{8,4},{12,0},{16,28},{20,24},{24,20},{28,16},{1,13},{... | collective-permute-start | bytes 405512 | tf_op jit(solution)/shard_map/ppermute | solution.py:294
  9.8 1.7 %pick.1 = bf16[144,512]{1,0:T(8,128)(2,1)S(1)} custom-call(s32[4,3]{1,0:T(4,128)} %pairs_in.3, s32[1,128]{1,0:T(1,128)} %bitcast.5, bf16[512,1024]{1,0:T(8,128)(2,1)} %coef_in.3), custom_call_target="tpu_custom_call" | custom-call | tf_op jit(solution)/shard_map/pick/pallas_call | solution.py:365
  11.6 0.0 collective-permute-done.refs_0_
  11.6 1.6 %collective-permute-start.3 = (bf16[4,128,128]{2,1,0:T(8,128)(2,1)S(1)}, bf16[4,128,128]{2,1,0:T(8,128)(2,1)S(1)}, u32[]{:S(2)}, u32[]{:S(2)}) collective-permute-start(bf16[4,128,128]{2,1,0:T(8,128)(2,1)S(1)} %collective-permute-done.refs_0_), channel_id=1, source_target_pairs={{0,2},{1,3},{2,0},{3,1},{4,6},{5,7},{6,4},{7,5},{8,10},{9,11},{10,... | collective-permute-start | bytes 393224 | tf_op jit(solution)/shard_map/ppermute | solution.py:294
  13.2 0.3 collective-permute-start.1
  13.5 3.1 %collective-permute-done.3.refs_2_ = bf16[4,128,128]{2,1,0:T(8,128)(2,1)S(1)} collective-permute-done((bf16[4,128,128]{2,1,0:T(8,128)(2,1)S(1)}, bf16[4,128,128]{2,1,0:T(8,128)(2,1)S(1)}, u32[]{:S(2)}, u32[]{:S(2)}) %collective-permute-start.3) | collective-permute-done | bytes 131104 | tf_op jit(solution)/shard_map/ppermute | solution.py:294
  16.6 0.5 %collective-permute-done.7.refs_3_ = bf16[528,128]{1,0:T(8,128)(2,1)S(1)} collective-permute-done((bf16[528,128]{1,0:T(8,128)(2,1)S(1)}, bf16[528,128]{1,0:T(8,128)(2,1)S(1)}, u32[]{:S(2)}, u32[]{:S(2)}) %collective-permute-start.7) | collective-permute-done | bytes 135200 | tf_op jit(solution)/shard_map/ppermute | solution.py:294
  17.1 0.1 collective-permute-start.8
  17.2 1.6 %collective-permute-start.9 = (bf16[512,128]{1,0:T(8,128)(2,1)S(1)}, bf16[512,128]{1,0:T(8,128)(2,1)S(1)}, u32[]{:S(2)}, u32[]{:S(2)}) collective-permute-start(bf16[512,128]{1,0:T(8,128)(2,1)S(1)} %get-tuple-element.35), channel_id=1, source_target_pairs={{0,2},{1,3},{2,0},{3,1},{4,6},{5,7},{6,4},{7,5},{8,10},{9,11},{10,... | collective-permute-start | bytes 393224 | tf_op jit(solution)/shard_map/ppermute | solution.py:294
  18.8 0.0 collective-permute-done.2.refs_1_
  18.8 0.2 collective-permute-start.10
  19.1 4.4 %collective-permute-done.1.coefs = bf16[144,512]{1,0:T(8,128)(2,1)S(1)} collective-permute-done((bf16[144,512]{1,0:T(8,128)(2,1)S(1)}, bf16[144,512]{1,0:T(8,128)(2,1)S(1)}, u32[]{:S(2)}, u32[]{:S(2)}) %collective-permute-start.1) | collective-permute-done | bytes 147488 | tf_op jit(solution)/shard_map/ppermute | solution.py:294
  23.5 0.3 far_blocks.1
  23.8 1.6 %collective-permute-start.11 = (bf16[528,128]{1,0:T(8,128)(2,1)S(1)}, bf16[528,128]{1,0:T(8,128)(2,1)S(1)}, u32[]{:S(2)}, u32[]{:S(2)}) collective-permute-start(bf16[528,128]{1,0:T(8,128)(2,1)S(1)} %get-tuple-element.37), channel_id=1, source_target_pairs={{0,4},{4,0},{8,12},{12,8},{16,20},{20,16},{24,28},{28,24},{1,5},{5... | collective-permute-start | bytes 405512 | tf_op jit(solution)/shard_map/ppermute | solution.py:294
  25.3 2.0 %collective-permute-start.13 = (bf16[528,128]{1,0:T(8,128)(2,1)S(1)}, bf16[528,128]{1,0:T(8,128)(2,1)S(1)}, u32[]{:S(2)}, u32[]{:S(2)}) collective-permute-start(bf16[528,128]{1,0:T(8,128)(2,1)S(1)} %get-tuple-element.39), channel_id=1, source_target_pairs={{0,12},{4,8},{8,4},{12,0},{16,28},{20,24},{24,20},{28,16},{1,13},{... | collective-permute-start | bytes 405512 | tf_op jit(solution)/shard_map/ppermute | solution.py:294
  27.3 0.9 %near_sum.1.total_in = f32[32,128,128]{2,1,0:T(8,128)S(1)} custom-call(bf16[528,128]{1,0:T(8,128)(2,1)S(1)} %get-tuple-element.27.refs_0_, bf16[528,128]{1,0:T(8,128)(2,1)S(1)} %collective-permute-done.5.refs_1_, bf16[528,128]{1,0:T(8,128)(2,1)S(1)} %collective-permute-done.6.refs_2_, bf16[528,128]{1,0:T(8,128)(2,1)S(1)} %collective-permute-done.7.refs_3_, ...), custom_call_target="tpu_custom_call" | custom-call | flops 10000000000 | bytes 20971520 | tf_op jit(solution)/shard_map/near_sum/pallas_call | solution.py:393
  28.3 1.2 %collective-permute-done.11.refs_1_ = bf16[528,128]{1,0:T(8,128)(2,1)S(1)} collective-permute-done((bf16[528,128]{1,0:T(8,128)(2,1)S(1)}, bf16[528,128]{1,0:T(8,128)(2,1)S(1)}, u32[]{:S(2)}, u32[]{:S(2)}) %collective-permute-start.11) | collective-permute-done | bytes 135200 | tf_op jit(solution)/shard_map/ppermute | solution.py:294
  29.5 2.3 %collective-permute-done.12.refs_2_ = bf16[528,128]{1,0:T(8,128)(2,1)S(1)} collective-permute-done((bf16[528,128]{1,0:T(8,128)(2,1)S(1)}, bf16[528,128]{1,0:T(8,128)(2,1)S(1)}, u32[]{:S(2)}, u32[]{:S(2)}) %collective-permute-start.12) | collective-permute-done | bytes 135200 | tf_op jit(solution)/shard_map/ppermute | solution.py:294
  31.7 1.4 %collective-permute-done.13.refs_3_ = bf16[528,128]{1,0:T(8,128)(2,1)S(1)} collective-permute-done((bf16[528,128]{1,0:T(8,128)(2,1)S(1)}, bf16[528,128]{1,0:T(8,128)(2,1)S(1)}, u32[]{:S(2)}, u32[]{:S(2)}) %collective-permute-start.13) | collective-permute-done | bytes 135200 | tf_op jit(solution)/shard_map/ppermute | solution.py:294
  33.1 2.3 %collect.1 = (bf16[32,4,4096]{2,1,0:T(4,128)(2,1)}, f32[32,128,128]{2,1,0:T(8,128)S(1)}) custom-call(bf16[4,4]{1,0:T(4,128)(2,1)} %metric_in.1, f32[32,128,128]{2,1,0:T(8,128)S(1)} %near_sum.1.total_in, bf16[528,128]{1,0:T(8,128)(2,1)S(1)} %get-tuple-element.26.refs_0_, ...), custom_call_target="tpu_custom_call", output_to_operand_aliasing={{1}: (1, {})} | custom-call | tf_op jit(solution)/shard_map/collect/pallas_call | solution.py:406
  (10 shorter events, 0.1 us)
Async XLA Ops:
  0.0 11.6 %collective-permute-start = (bf16[4,128,128]{2,1,0:T(8,128)(2,1)}, bf16[4,128,128]{2,1,0:T(8,128)(2,1)S(1)}, u32[]{:S(2)}, u32[]{:S(2)}) collective-permute-start(bf16[4,128,128]{2,1,0:T(8,128)(2,1)} %bitcast.2), channel_id=1, source_target_pairs={{0,16},{4,20},{8,24},{12,28},{16,0},{20,4},{24,8},{28,12},{1,17},{... | collective-permute-start | bytes 393224 | tf_op jit(solution)/shard_map/ppermute | solution.py:294
  6.3 6.9 %collective-permute-start.5 = (bf16[528,128]{1,0:T(8,128)(2,1)S(1)}, bf16[528,128]{1,0:T(8,128)(2,1)S(1)}, u32[]{:S(2)}, u32[]{:S(2)}) collective-permute-start(bf16[528,128]{1,0:T(8,128)(2,1)S(1)} %get-tuple-element.28), channel_id=1, source_target_pairs={{0,4},{4,0},{8,12},{12,8},{16,20},{20,16},{24,28},{28,24},{1,5},{5... | collective-permute-start | bytes 405512 | tf_op jit(solution)/shard_map/ppermute | solution.py:294
  7.8 8.8 %collective-permute-start.6 = (bf16[528,128]{1,0:T(8,128)(2,1)S(1)}, bf16[528,128]{1,0:T(8,128)(2,1)S(1)}, u32[]{:S(2)}, u32[]{:S(2)}) collective-permute-start(bf16[528,128]{1,0:T(8,128)(2,1)S(1)} %get-tuple-element.30), channel_id=1, source_target_pairs={{0,8},{4,12},{8,0},{12,4},{16,24},{20,28},{24,16},{28,20},{1,9},{5... | collective-permute-start | bytes 405512 | tf_op jit(solution)/shard_map/ppermute | solution.py:294
  9.4 7.7 %collective-permute-start.7 = (bf16[528,128]{1,0:T(8,128)(2,1)S(1)}, bf16[528,128]{1,0:T(8,128)(2,1)S(1)}, u32[]{:S(2)}, u32[]{:S(2)}) collective-permute-start(bf16[528,128]{1,0:T(8,128)(2,1)S(1)} %get-tuple-element.32), channel_id=1, source_target_pairs={{0,12},{4,8},{8,4},{12,0},{16,28},{20,24},{24,20},{28,16},{1,13},{... | collective-permute-start | bytes 405512 | tf_op jit(solution)/shard_map/ppermute | solution.py:294
  11.6 5.0 %collective-permute-start.3 = (bf16[4,128,128]{2,1,0:T(8,128)(2,1)S(1)}, bf16[4,128,128]{2,1,0:T(8,128)(2,1)S(1)}, u32[]{:S(2)}, u32[]{:S(2)}) collective-permute-start(bf16[4,128,128]{2,1,0:T(8,128)(2,1)S(1)} %collective-permute-done.refs_0_), channel_id=1, source_target_pairs={{0,2},{1,3},{2,0},{3,1},{4,6},{5,7},{6,4},{7,5},{8,10},{9,11},{10,... | collective-permute-start | bytes 393224 | tf_op jit(solution)/shard_map/ppermute | solution.py:294
  13.2 5.7 %collective-permute-start.2 = (bf16[4,128,128]{2,1,0:T(8,128)(2,1)S(1)}, bf16[4,128,128]{2,1,0:T(8,128)(2,1)S(1)}, u32[]{:S(2)}, u32[]{:S(2)}) collective-permute-start(bf16[4,128,128]{2,1,0:T(8,128)(2,1)S(1)} %collective-permute-done.refs_0_), channel_id=1, source_target_pairs={{0,1},{1,0},{2,3},{3,2},{4,5},{5,4},{6,7},{7,6},{8,9},{9,8},{10,11... | collective-permute-start | bytes 393224 | tf_op jit(solution)/shard_map/ppermute | solution.py:294
  13.2 10.3 %collective-permute-start.1 = (bf16[144,512]{1,0:T(8,128)(2,1)S(1)}, bf16[144,512]{1,0:T(8,128)(2,1)S(1)}, u32[]{:S(2)}, u32[]{:S(2)}) collective-permute-start(bf16[144,512]{1,0:T(8,128)(2,1)S(1)} %pick.1), channel_id=1, source_target_pairs={{0,16},{4,20},{8,24},{12,28},{16,0},{20,4},{24,8},{28,12},{1,17},{... | collective-permute-start | bytes 442376 | tf_op jit(solution)/shard_map/ppermute | solution.py:294
  16.6 6.9 %collective-permute-start.4 = (bf16[4,128,128]{2,1,0:T(8,128)(2,1)S(1)}, bf16[4,128,128]{2,1,0:T(8,128)(2,1)S(1)}, u32[]{:S(2)}, u32[]{:S(2)}) collective-permute-start(bf16[4,128,128]{2,1,0:T(8,128)(2,1)S(1)} %collective-permute-done.3.refs_2_), channel_id=1, source_target_pairs={{0,1},{1,0},{2,3},{3,2},{4,5},{5,4},{6,7},{7,6},{8,9},{9,8},{10,11... | collective-permute-start | bytes 393224 | tf_op jit(solution)/shard_map/ppermute | solution.py:294
  17.1 8.2 %collective-permute-start.8 = (bf16[512,128]{1,0:T(8,128)(2,1)S(1)}, bf16[512,128]{1,0:T(8,128)(2,1)S(1)}, u32[]{:S(2)}, u32[]{:S(2)}) collective-permute-start(bf16[512,128]{1,0:T(8,128)(2,1)S(1)} %get-tuple-element.34), channel_id=1, source_target_pairs={{0,1},{1,0},{2,3},{3,2},{4,5},{5,4},{6,7},{7,6},{8,9},{9,8},{10,11... | collective-permute-start | bytes 393224 | tf_op jit(solution)/shard_map/ppermute | solution.py:294
  17.2 10.1 %collective-permute-start.9 = (bf16[512,128]{1,0:T(8,128)(2,1)S(1)}, bf16[512,128]{1,0:T(8,128)(2,1)S(1)}, u32[]{:S(2)}, u32[]{:S(2)}) collective-permute-start(bf16[512,128]{1,0:T(8,128)(2,1)S(1)} %get-tuple-element.35), channel_id=1, source_target_pairs={{0,2},{1,3},{2,0},{3,1},{4,6},{5,7},{6,4},{7,5},{8,10},{9,11},{10,... | collective-permute-start | bytes 393224 | tf_op jit(solution)/shard_map/ppermute | solution.py:294
  18.8 8.5 %collective-permute-start.10 = (bf16[512,128]{1,0:T(8,128)(2,1)S(1)}, bf16[512,128]{1,0:T(8,128)(2,1)S(1)}, u32[]{:S(2)}, u32[]{:S(2)}) collective-permute-start(bf16[512,128]{1,0:T(8,128)(2,1)S(1)} %get-tuple-element.36), channel_id=1, source_target_pairs={{0,3},{1,2},{2,1},{3,0},{4,7},{5,6},{6,5},{7,4},{8,11},{9,10},{10,... | collective-permute-start | bytes 393224 | tf_op jit(solution)/shard_map/ppermute | solution.py:294
  23.8 5.7 %collective-permute-start.11 = (bf16[528,128]{1,0:T(8,128)(2,1)S(1)}, bf16[528,128]{1,0:T(8,128)(2,1)S(1)}, u32[]{:S(2)}, u32[]{:S(2)}) collective-permute-start(bf16[528,128]{1,0:T(8,128)(2,1)S(1)} %get-tuple-element.37), channel_id=1, source_target_pairs={{0,4},{4,0},{8,12},{12,8},{16,20},{20,16},{24,28},{28,24},{1,5},{5... | collective-permute-start | bytes 405512 | tf_op jit(solution)/shard_map/ppermute | solution.py:294
  25.3 6.4 %collective-permute-start.12 = (bf16[528,128]{1,0:T(8,128)(2,1)S(1)}, bf16[528,128]{1,0:T(8,128)(2,1)S(1)}, u32[]{:S(2)}, u32[]{:S(2)}) collective-permute-start(bf16[528,128]{1,0:T(8,128)(2,1)S(1)} %get-tuple-element.38), channel_id=1, source_target_pairs={{0,8},{4,12},{8,0},{12,4},{16,24},{20,28},{24,16},{28,20},{1,9},{5... | collective-permute-start | bytes 405512 | tf_op jit(solution)/shard_map/ppermute | solution.py:294
  25.3 7.8 %collective-permute-start.13 = (bf16[528,128]{1,0:T(8,128)(2,1)S(1)}, bf16[528,128]{1,0:T(8,128)(2,1)S(1)}, u32[]{:S(2)}, u32[]{:S(2)}) collective-permute-start(bf16[528,128]{1,0:T(8,128)(2,1)S(1)} %get-tuple-element.39), channel_id=1, source_target_pairs={{0,12},{4,8},{8,4},{12,0},{16,28},{20,24},{24,20},{28,16},{1,13},{... | collective-permute-start | bytes 405512 | tf_op jit(solution)/shard_map/ppermute | solution.py:294

commit v11 on v9

--- a/solution.py
+++ b/solution.py
@@ -309,6 +309,10 @@
     return [held[order.index(at)] for at in range(len(held))]
 
 
+def cost(flops):
+    return pl.CostEstimate(flops=int(flops), transcendentals=0, bytes_accessed=2**20)
+
+
 def in_hbm(*operands):
     return [pltpu.with_memory_space_constraint(operand, pltpu.HBM) for operand in operands]
 
@@ -333,6 +337,7 @@
             in_specs=[vmem] * (1 + aux_count),
             out_specs=[vmem] * count,
             compiler_params=params,
+            cost_estimate=cost(3e9) if name == "far_blocks" else None,
             name=name,
         )(coefs, *quad)
 
@@ -361,7 +366,8 @@
         compiler_params=params,
         name="near_blocks",
     )(*in_hbm(*operands, blocks))
-    near = [near[0]] + [flip(near[f], "shell", f) for f in range(1, group)]
+    sent = near
+    near = [sent[0]] + [flip(sent[f], "shell", f) for f in range(1, group - 1)]
     (sent_coef,) = pl.pallas_call(
         functools.partial(
             pick_kernel, [list(range(group, shell_count))], occ_local, aux_count
@@ -378,6 +384,7 @@
     far_block = after(far_block, sent_coef)
     far_coef = flip(after(sent_coef, far_block), "shell", group)
     far_blocks = shared(far_block)
+    near.append(flip(after(sent[-1], near[-1],sent_coef), "shell", group - 1))
     regrouped = pl.pallas_call(
         functools.partial(regroup_kernel, group),
         out_shape=[jax.ShapeDtypeStruct((group * pairs_dev * occ_local, BS), jnp.bfloat16)]
@@ -397,6 +404,7 @@
         out_specs=vmem,
         scratch_shapes=code_scratch(group),
         compiler_params=params,
+        cost_estimate=cost(3e9),
         name="near_sum",
     )(*(after(one, far[0]) for one in near), *others)
     far = [far[0]] + [flip(far[f], "shell", f) for f in range(1, group)]

time: 35.9 us -> 37.2 us (1.036)
  the two profiles are of different devices: /device:TPU:1 before, /device:TPU:0 now
where the time goes in v11:
time: 37.2 us; the launch traced here: 37.1 us
  starting transfers between devices  18.8 us (51%)
  waiting for transfers between devices  10.7 us (29%)
  Pallas kernels  7.55 us (20%)
    ppermute x14, starting transfers between devices, flip(): return lax.ppermute(value, axis, [(at, at ^ bits) for at in range(count)])  18.8 us
    ppermute x14, waiting for transfers between devices, flip(): return lax.ppermute(value, axis, [(at, at ^ bits) for at in range(count)])  10.7 us
    pallas_call x1, Pallas kernels, exchanged_inputs(): pl.pallas_call(collect_kernel, out_shape=[jax.ShapeDtypeStruct((occ_local...  2.34 us
    pallas_call x1, Pallas kernels, exchanged_inputs(): pl.pallas_call(functools.partial(near_kernel, occ_local, aux_count), out_...  2.23 us
    pallas_call x1, Pallas kernels, exchanged_inputs(): pl.pallas_call(functools.partial(pick_kernel, [list(range(group, shell_co...  1.72 us
    pallas_call x1, Pallas kernels, exchanged_inputs(): pl.pallas_call(functools.partial(near_sum_kernel, occ_local, group), out_...  0.94 us
  transfers between devices with their start and end apart: 14, of which 6 were waited for; matrix products, arithmetic and copies ran while one was open for 0% of the time, Pallas kernels for 14%

profile of v11, /device:TPU:0, one launch (start us, length us, event | category | flops | bytes accessed | tf_op | source)
XLA Modules:
  0.0 37.1 jit_solution(13556165251814735561)
XLA Ops:
  0.0 4.0 %collective-permute-start = (bf16[4,128,128]{2,1,0:T(8,128)(2,1)}, bf16[4,128,128]{2,1,0:T(8,128)(2,1)S(1)}, u32[]{:S(2)}, u32[]{:S(2)}) collective-permute-start(bf16[4,128,128]{2,1,0:T(8,128)(2,1)} %bitcast.2), channel_id=1, source_target_pairs={{0,16},{4,20},{8,24},{12,28},{16,0},{20,4},{24,8},{28,12},{1,17},{... | collective-permute-start | bytes 393224 | tf_op jit(solution)/shard_map/ppermute | solution.py:294
  4.0 2.2 %near_blocks.1 = (bf16[528,128]{1,0:T(8,128)(2,1)S(1)}, bf16[528,128]{1,0:T(8,128)(2,1)S(1)}, bf16[528,128]{1,0:T(8,128)(2,1)S(1)}, bf16[528,128]{1,0:T(8,128)(2,1)S(1)}) custom-call(s32[4,3]{1,0:T(4,128)} %pairs_in.3, s32[1,128]{1,0:T(1,128)} %bitcast.4, bf16[512,1024]{1,0:T(8,128)(2,1)} %coef_in.3, bf16[4,128,128]{2,1,0:T(8,128)(2,1)} %bitcast.3), custom_call_target="tpu_custom_call" | custom-call | tf_op jit(solution)/shard_map/near_blocks/pallas_call | solution.py:359
  6.3 1.6 %collective-permute-start.6 = (bf16[528,128]{1,0:T(8,128)(2,1)S(1)}, bf16[528,128]{1,0:T(8,128)(2,1)S(1)}, u32[]{:S(2)}, u32[]{:S(2)}) collective-permute-start(bf16[528,128]{1,0:T(8,128)(2,1)S(1)} %get-tuple-element.31), channel_id=1, source_target_pairs={{0,8},{4,12},{8,0},{12,4},{16,24},{20,28},{24,16},{28,20},{1,9},{5... | collective-permute-start | bytes 405512 | tf_op jit(solution)/shard_map/ppermute | solution.py:294
  7.9 1.7 %pick.1 = bf16[144,512]{1,0:T(8,128)(2,1)S(1)} custom-call(s32[4,3]{1,0:T(4,128)} %pairs_in.3, s32[1,128]{1,0:T(1,128)} %bitcast.5, bf16[512,1024]{1,0:T(8,128)(2,1)} %coef_in.3), custom_call_target="tpu_custom_call" | custom-call | tf_op jit(solution)/shard_map/pick/pallas_call | solution.py:371
  9.6 1.0 %collective-permute-done.refs_0_ = bf16[4,128,128]{2,1,0:T(8,128)(2,1)S(1)} collective-permute-done((bf16[4,128,128]{2,1,0:T(8,128)(2,1)}, bf16[4,128,128]{2,1,0:T(8,128)(2,1)S(1)}, u32[]{:S(2)}, u32[]{:S(2)}) %collective-permute-start) | collective-permute-done | bytes 131104 | tf_op jit(solution)/shard_map/ppermute | solution.py:294
  10.7 1.6 %collective-permute-start.3 = (bf16[4,128,128]{2,1,0:T(8,128)(2,1)S(1)}, bf16[4,128,128]{2,1,0:T(8,128)(2,1)S(1)}, u32[]{:S(2)}, u32[]{:S(2)}) collective-permute-start(bf16[4,128,128]{2,1,0:T(8,128)(2,1)S(1)} %collective-permute-done.refs_0_), channel_id=1, source_target_pairs={{0,2},{1,3},{2,0},{3,1},{4,6},{5,7},{6,4},{7,5},{8,10},{9,11},{10,... | collective-permute-start | bytes 393224 | tf_op jit(solution)/shard_map/ppermute | solution.py:294
  12.2 1.5 %collective-permute-start.5 = (bf16[528,128]{1,0:T(8,128)(2,1)S(1)}, bf16[528,128]{1,0:T(8,128)(2,1)S(1)}, u32[]{:S(2)}, u32[]{:S(2)}) collective-permute-start(bf16[528,128]{1,0:T(8,128)(2,1)S(1)} %get-tuple-element.29), channel_id=1, source_target_pairs={{0,4},{4,0},{8,12},{12,8},{16,20},{20,16},{24,28},{28,24},{1,5},{5... | collective-permute-start | bytes 405512 | tf_op jit(solution)/shard_map/ppermute | solution.py:294
  13.7 4.0 %collective-permute-start.7 = (bf16[528,128]{1,0:T(8,128)(2,1)S(1)}, bf16[528,128]{1,0:T(8,128)(2,1)S(1)}, u32[]{:S(2)}, u32[]{:S(2)}) collective-permute-start(bf16[528,128]{1,0:T(8,128)(2,1)S(1)} %get-tuple-element.34), channel_id=1, source_target_pairs={{0,12},{4,8},{8,4},{12,0},{16,28},{20,24},{24,20},{28,16},{1,13},{... | collective-permute-start | bytes 405512 | tf_op jit(solution)/shard_map/ppermute | solution.py:294
  17.8 0.0 collective-permute-done.3.refs_2_
  17.8 0.5 %collective-permute-start.4 = (bf16[4,128,128]{2,1,0:T(8,128)(2,1)S(1)}, bf16[4,128,128]{2,1,0:T(8,128)(2,1)S(1)}, u32[]{:S(2)}, u32[]{:S(2)}) collective-permute-start(bf16[4,128,128]{2,1,0:T(8,128)(2,1)S(1)} %collective-permute-done.3.refs_2_), channel_id=1, source_target_pairs={{0,1},{1,0},{2,3},{3,2},{4,5},{5,4},{6,7},{7,6},{8,9},{9,8},{10,11... | collective-permute-start | bytes 393224 | tf_op jit(solution)/shard_map/ppermute | solution.py:294
  18.3 4.0 %collective-permute-done.7.refs_3_ = bf16[528,128]{1,0:T(8,128)(2,1)S(1)} collective-permute-done((bf16[528,128]{1,0:T(8,128)(2,1)S(1)}, bf16[528,128]{1,0:T(8,128)(2,1)S(1)}, u32[]{:S(2)}, u32[]{:S(2)}) %collective-permute-start.7) | collective-permute-done | bytes 135200 | tf_op jit(solution)/shard_map/ppermute | solution.py:294
  22.3 0.1 collective-permute-start.8
  22.3 0.6 %collective-permute-start.9 = (bf16[512,128]{1,0:T(8,128)(2,1)S(1)}, bf16[512,128]{1,0:T(8,128)(2,1)S(1)}, u32[]{:S(2)}, u32[]{:S(2)}) collective-permute-start(bf16[512,128]{1,0:T(8,128)(2,1)S(1)} %get-tuple-element.37), channel_id=1, source_target_pairs={{0,2},{1,3},{2,0},{3,1},{4,6},{5,7},{6,4},{7,5},{8,10},{9,11},{10,... | collective-permute-start | bytes 393224 | tf_op jit(solution)/shard_map/ppermute | solution.py:294
  22.9 1.3 %collective-permute-start.10 = (bf16[512,128]{1,0:T(8,128)(2,1)S(1)}, bf16[512,128]{1,0:T(8,128)(2,1)S(1)}, u32[]{:S(2)}, u32[]{:S(2)}) collective-permute-start(bf16[512,128]{1,0:T(8,128)(2,1)S(1)} %get-tuple-element.38), channel_id=1, source_target_pairs={{0,3},{1,2},{2,1},{3,0},{4,7},{5,6},{6,5},{7,4},{8,11},{9,10},{10,... | collective-permute-start | bytes 393224 | tf_op jit(solution)/shard_map/ppermute | solution.py:294
  24.2 0.3 far_blocks.1
  24.5 1.4 %collective-permute-start.11 = (bf16[528,128]{1,0:T(8,128)(2,1)S(1)}, bf16[528,128]{1,0:T(8,128)(2,1)S(1)}, u32[]{:S(2)}, u32[]{:S(2)}) collective-permute-start(bf16[528,128]{1,0:T(8,128)(2,1)S(1)} %get-tuple-element.39), channel_id=1, source_target_pairs={{0,4},{4,0},{8,12},{12,8},{16,20},{20,16},{24,28},{28,24},{1,5},{5... | collective-permute-start | bytes 405512 | tf_op jit(solution)/shard_map/ppermute | solution.py:294
  25.9 2.0 %collective-permute-start.12 = (bf16[528,128]{1,0:T(8,128)(2,1)S(1)}, bf16[528,128]{1,0:T(8,128)(2,1)S(1)}, u32[]{:S(2)}, u32[]{:S(2)}) collective-permute-start(bf16[528,128]{1,0:T(8,128)(2,1)S(1)} %get-tuple-element.40), channel_id=1, source_target_pairs={{0,8},{4,12},{8,0},{12,4},{16,24},{20,28},{24,16},{28,20},{1,9},{5... | collective-permute-start | bytes 405512 | tf_op jit(solution)/shard_map/ppermute | solution.py:294
  27.9 0.2 collective-permute-start.13
  28.1 0.6 %collective-permute-done.9.refs_5_ = bf16[512,128]{1,0:T(8,128)(2,1)S(1)} collective-permute-done((bf16[512,128]{1,0:T(8,128)(2,1)S(1)}, bf16[512,128]{1,0:T(8,128)(2,1)S(1)}, u32[]{:S(2)}, u32[]{:S(2)}) %collective-permute-start.9) | collective-permute-done | bytes 131104 | tf_op jit(solution)/shard_map/ppermute | solution.py:294
  28.7 1.9 %collective-permute-done.10.refs_6_ = bf16[512,128]{1,0:T(8,128)(2,1)S(1)} collective-permute-done((bf16[512,128]{1,0:T(8,128)(2,1)S(1)}, bf16[512,128]{1,0:T(8,128)(2,1)S(1)}, u32[]{:S(2)}, u32[]{:S(2)}) %collective-permute-start.10) | collective-permute-done | bytes 131104 | tf_op jit(solution)/shard_map/ppermute | solution.py:294
  30.6 0.9 %near_sum.1.total_in = f32[32,128,128]{2,1,0:T(8,128)S(1)} custom-call(bf16[528,128]{1,0:T(8,128)(2,1)S(1)} %get-tuple-element.28.refs_0_, bf16[528,128]{1,0:T(8,128)(2,1)S(1)} %collective-permute-done.5.refs_1_, bf16[528,128]{1,0:T(8,128)(2,1)S(1)} %collective-permute-done.6.refs_2_, bf16[528,128]{1,0:T(8,128)(2,1)S(1)} %collective-permute-done.7.refs_3_, ...), custom_call_target="tpu_custom_call" | custom-call | flops 3000000000 | bytes 1048576 | tf_op jit(solution)/shard_map/near_sum/pallas_call | solution.py:400
  31.6 0.8 %collective-permute-done.12.refs_2_ = bf16[528,128]{1,0:T(8,128)(2,1)S(1)} collective-permute-done((bf16[528,128]{1,0:T(8,128)(2,1)S(1)}, bf16[528,128]{1,0:T(8,128)(2,1)S(1)}, u32[]{:S(2)}, u32[]{:S(2)}) %collective-permute-start.12) | collective-permute-done | bytes 135200 | tf_op jit(solution)/shard_map/ppermute | solution.py:294
  32.3 2.4 %collective-permute-done.13.refs_3_ = bf16[528,128]{1,0:T(8,128)(2,1)S(1)} collective-permute-done((bf16[528,128]{1,0:T(8,128)(2,1)S(1)}, bf16[528,128]{1,0:T(8,128)(2,1)S(1)}, u32[]{:S(2)}, u32[]{:S(2)}) %collective-permute-start.13) | collective-permute-done | bytes 135200 | tf_op jit(solution)/shard_map/ppermute | solution.py:294
  34.7 2.3 %collect.1 = (bf16[32,4,4096]{2,1,0:T(4,128)(2,1)}, f32[32,128,128]{2,1,0:T(8,128)S(1)}) custom-call(bf16[4,4]{1,0:T(4,128)(2,1)} %metric_in.1, f32[32,128,128]{2,1,0:T(8,128)S(1)} %near_sum.1.total_in, bf16[528,128]{1,0:T(8,128)(2,1)S(1)} %get-tuple-element.27.refs_0_, ...), custom_call_target="tpu_custom_call", output_to_operand_aliasing={{1}: (1, {})} | custom-call | tf_op jit(solution)/shard_map/collect/pallas_call | solution.py:411
  (10 shorter events, 0.1 us)
Async XLA Ops:
  0.0 10.7 %collective-permute-start = (bf16[4,128,128]{2,1,0:T(8,128)(2,1)}, bf16[4,128,128]{2,1,0:T(8,128)(2,1)S(1)}, u32[]{:S(2)}, u32[]{:S(2)}) collective-permute-start(bf16[4,128,128]{2,1,0:T(8,128)(2,1)} %bitcast.2), channel_id=1, source_target_pairs={{0,16},{4,20},{8,24},{12,28},{16,0},{20,4},{24,8},{28,12},{1,17},{... | collective-permute-start | bytes 393224 | tf_op jit(solution)/shard_map/ppermute | solution.py:294
  6.3 7.5 %collective-permute-start.6 = (bf16[528,128]{1,0:T(8,128)(2,1)S(1)}, bf16[528,128]{1,0:T(8,128)(2,1)S(1)}, u32[]{:S(2)}, u32[]{:S(2)}) collective-permute-start(bf16[528,128]{1,0:T(8,128)(2,1)S(1)} %get-tuple-element.31), channel_id=1, source_target_pairs={{0,8},{4,12},{8,0},{12,4},{16,24},{20,28},{24,16},{28,20},{1,9},{5... | collective-permute-start | bytes 405512 | tf_op jit(solution)/shard_map/ppermute | solution.py:294
  10.7 7.1 %collective-permute-start.3 = (bf16[4,128,128]{2,1,0:T(8,128)(2,1)S(1)}, bf16[4,128,128]{2,1,0:T(8,128)(2,1)S(1)}, u32[]{:S(2)}, u32[]{:S(2)}) collective-permute-start(bf16[4,128,128]{2,1,0:T(8,128)(2,1)S(1)} %collective-permute-done.refs_0_), channel_id=1, source_target_pairs={{0,2},{1,3},{2,0},{3,1},{4,6},{5,7},{6,4},{7,5},{8,10},{9,11},{10,... | collective-permute-start | bytes 393224 | tf_op jit(solution)/shard_map/ppermute | solution.py:294
  12.2 12.0 %collective-permute-start.1 = (bf16[144,512]{1,0:T(8,128)(2,1)S(1)}, bf16[144,512]{1,0:T(8,128)(2,1)S(1)}, u32[]{:S(2)}, u32[]{:S(2)}) collective-permute-start(bf16[144,512]{1,0:T(8,128)(2,1)S(1)} %pick.1), channel_id=1, source_target_pairs={{0,16},{4,20},{8,24},{12,28},{16,0},{20,4},{24,8},{28,12},{1,17},{... | collective-permute-start | bytes 442376 | tf_op jit(solution)/shard_map/ppermute | solution.py:294
  12.2 6.0 %collective-permute-start.5 = (bf16[528,128]{1,0:T(8,128)(2,1)S(1)}, bf16[528,128]{1,0:T(8,128)(2,1)S(1)}, u32[]{:S(2)}, u32[]{:S(2)}) collective-permute-start(bf16[528,128]{1,0:T(8,128)(2,1)S(1)} %get-tuple-element.29), channel_id=1, source_target_pairs={{0,4},{4,0},{8,12},{12,8},{16,20},{20,16},{24,28},{28,24},{1,5},{5... | collective-permute-start | bytes 405512 | tf_op jit(solution)/shard_map/ppermute | solution.py:294
  13.7 8.5 %collective-permute-start.7 = (bf16[528,128]{1,0:T(8,128)(2,1)S(1)}, bf16[528,128]{1,0:T(8,128)(2,1)S(1)}, u32[]{:S(2)}, u32[]{:S(2)}) collective-permute-start(bf16[528,128]{1,0:T(8,128)(2,1)S(1)} %get-tuple-element.34), channel_id=1, source_target_pairs={{0,12},{4,8},{8,4},{12,0},{16,28},{20,24},{24,20},{28,16},{1,13},{... | collective-permute-start | bytes 405512 | tf_op jit(solution)/shard_map/ppermute | solution.py:294
  17.8 5.2 %collective-permute-start.2 = (bf16[4,128,128]{2,1,0:T(8,128)(2,1)S(1)}, bf16[4,128,128]{2,1,0:T(8,128)(2,1)S(1)}, u32[]{:S(2)}, u32[]{:S(2)}) collective-permute-start(bf16[4,128,128]{2,1,0:T(8,128)(2,1)S(1)} %collective-permute-done.refs_0_), channel_id=1, source_target_pairs={{0,1},{1,0},{2,3},{3,2},{4,5},{5,4},{6,7},{7,6},{8,9},{9,8},{10,11... | collective-permute-start | bytes 393224 | tf_op jit(solution)/shard_map/ppermute | solution.py:294
  17.8 6.4 %collective-permute-start.4 = (bf16[4,128,128]{2,1,0:T(8,128)(2,1)S(1)}, bf16[4,128,128]{2,1,0:T(8,128)(2,1)S(1)}, u32[]{:S(2)}, u32[]{:S(2)}) collective-permute-start(bf16[4,128,128]{2,1,0:T(8,128)(2,1)S(1)} %collective-permute-done.3.refs_2_), channel_id=1, source_target_pairs={{0,1},{1,0},{2,3},{3,2},{4,5},{5,4},{6,7},{7,6},{8,9},{9,8},{10,11... | collective-permute-start | bytes 393224 | tf_op jit(solution)/shard_map/ppermute | solution.py:294
  22.3 5.7 %collective-permute-start.8 = (bf16[512,128]{1,0:T(8,128)(2,1)S(1)}, bf16[512,128]{1,0:T(8,128)(2,1)S(1)}, u32[]{:S(2)}, u32[]{:S(2)}) collective-permute-start(bf16[512,128]{1,0:T(8,128)(2,1)S(1)} %get-tuple-element.36), channel_id=1, source_target_pairs={{0,1},{1,0},{2,3},{3,2},{4,5},{5,4},{6,7},{7,6},{8,9},{9,8},{10,11... | collective-permute-start | bytes 393224 | tf_op jit(solution)/shard_map/ppermute | solution.py:294
  22.3 6.4 %collective-permute-start.9 = (bf16[512,128]{1,0:T(8,128)(2,1)S(1)}, bf16[512,128]{1,0:T(8,128)(2,1)S(1)}, u32[]{:S(2)}, u32[]{:S(2)}) collective-permute-start(bf16[512,128]{1,0:T(8,128)(2,1)S(1)} %get-tuple-element.37), channel_id=1, source_target_pairs={{0,2},{1,3},{2,0},{3,1},{4,6},{5,7},{6,4},{7,5},{8,10},{9,11},{10,... | collective-permute-start | bytes 393224 | tf_op jit(solution)/shard_map/ppermute | solution.py:294
  22.9 7.7 %collective-permute-start.10 = (bf16[512,128]{1,0:T(8,128)(2,1)S(1)}, bf16[512,128]{1,0:T(8,128)(2,1)S(1)}, u32[]{:S(2)}, u32[]{:S(2)}) collective-permute-start(bf16[512,128]{1,0:T(8,128)(2,1)S(1)} %get-tuple-element.38), channel_id=1, source_target_pairs={{0,3},{1,2},{2,1},{3,0},{4,7},{5,6},{6,5},{7,4},{8,11},{9,10},{10,... | collective-permute-start | bytes 393224 | tf_op jit(solution)/shard_map/ppermute | solution.py:294
  24.5 7.1 %collective-permute-start.11 = (bf16[528,128]{1,0:T(8,128)(2,1)S(1)}, bf16[528,128]{1,0:T(8,128)(2,1)S(1)}, u32[]{:S(2)}, u32[]{:S(2)}) collective-permute-start(bf16[528,128]{1,0:T(8,128)(2,1)S(1)} %get-tuple-element.39), channel_id=1, source_target_pairs={{0,4},{4,0},{8,12},{12,8},{16,20},{20,16},{24,28},{28,24},{1,5},{5... | collective-permute-start | bytes 405512 | tf_op jit(solution)/shard_map/ppermute | solution.py:294
  25.9 6.4 %collective-permute-start.12 = (bf16[528,128]{1,0:T(8,128)(2,1)S(1)}, bf16[528,128]{1,0:T(8,128)(2,1)S(1)}, u32[]{:S(2)}, u32[]{:S(2)}) collective-permute-start(bf16[528,128]{1,0:T(8,128)(2,1)S(1)} %get-tuple-element.40), channel_id=1, source_target_pairs={{0,8},{4,12},{8,0},{12,4},{16,24},{20,28},{24,16},{28,20},{1,9},{5... | collective-permute-start | bytes 405512 | tf_op jit(solution)/shard_map/ppermute | solution.py:294
  27.9 6.8 %collective-permute-start.13 = (bf16[528,128]{1,0:T(8,128)(2,1)S(1)}, bf16[528,128]{1,0:T(8,128)(2,1)S(1)}, u32[]{:S(2)}, u32[]{:S(2)}) collective-permute-start(bf16[528,128]{1,0:T(8,128)(2,1)S(1)} %get-tuple-element.41), channel_id=1, source_target_pairs={{0,12},{4,8},{8,4},{12,0},{16,28},{20,24},{24,20},{28,16},{1,13},{... | collective-permute-start | bytes 405512 | tf_op jit(solution)/shard_map/ppermute | solution.py:294

commit v12 on v11

--- a/solution.py
+++ b/solution.py
@@ -366,8 +366,7 @@
         compiler_params=params,
         name="near_blocks",
     )(*in_hbm(*operands, blocks))
-    sent = near
-    near = [sent[0]] + [flip(sent[f], "shell", f) for f in range(1, group - 1)]
+    near = [near[0]] + [flip(near[f], "shell", f) for f in range(1, group)]
     (sent_coef,) = pl.pallas_call(
         functools.partial(
             pick_kernel, [list(range(group, shell_count))], occ_local, aux_count
@@ -383,8 +382,7 @@
     )(*in_hbm(*operands))
     far_block = after(far_block, sent_coef)
     far_coef = flip(after(sent_coef, far_block), "shell", group)
-    far_blocks = shared(far_block)
-    near.append(flip(after(sent[-1], near[-1],sent_coef), "shell", group - 1))
+    far_blocks = shared(far_block, near[1],near[2])
     regrouped = pl.pallas_call(
         functools.partial(regroup_kernel, group),
         out_shape=[jax.ShapeDtypeStruct((group * pairs_dev * occ_local, BS), jnp.bfloat16)]

time: 37.2 us -> 36.2 us (0.973)
  waiting for transfers between devices: 10.7 us -> 9.13 us
  starting transfers between devices: 18.8 us -> 19.2 us
    ppermute x14, waiting for transfers between devices: 10.7 us -> 9.13 us  [flip(): return lax.ppermute(value, axis, [(at, at ^ bits) for at in range(count)])]
    ppermute x14, starting transfers between devices: 18.8 us -> 19.2 us  [flip(): return lax.ppermute(value, axis, [(at, at ^ bits) for at in range(count)])]
  transfers between devices with their start and end apart: 14 -> 14, of which waited for: 6 -> 4; matrix products, arithmetic and copies ran while one was open for 0% -> 0% of each run, Pallas kernels for 14% -> 14%
where the time goes in v12:
time: 36.2 us; the launch traced here: 36 us
  starting transfers between devices  19.2 us (53%)
  waiting for transfers between devices  9.13 us (25%)
  Pallas kernels  7.55 us (21%)
    ppermute x14, starting transfers between devices, flip(): return lax.ppermute(value, axis, [(at, at ^ bits) for at in range(count)])  19.2 us
    ppermute x14, waiting for transfers between devices, flip(): return lax.ppermute(value, axis, [(at, at ^ bits) for at in range(count)])  9.13 us
    pallas_call x1, Pallas kernels, exchanged_inputs(): pl.pallas_call(collect_kernel, out_shape=[jax.ShapeDtypeStruct((occ_local...  2.34 us
    pallas_call x1, Pallas kernels, exchanged_inputs(): pl.pallas_call(functools.partial(near_kernel, occ_local, aux_count), out_...  2.23 us
    pallas_call x1, Pallas kernels, exchanged_inputs(): pl.pallas_call(functools.partial(pick_kernel, [list(range(group, shell_co...  1.72 us
    pallas_call x1, Pallas kernels, exchanged_inputs(): pl.pallas_call(functools.partial(near_sum_kernel, occ_local, group), out_...  0.94 us
  transfers between devices with their start and end apart: 14, of which 4 were waited for; matrix products, arithmetic and copies ran while one was open for 0% of the time, Pallas kernels for 14%

profile of v12, /device:TPU:0, one launch (start us, length us, event | category | flops | bytes accessed | tf_op | source)
XLA Modules:
  0.0 36.0 jit_solution(8992884897779826262)
XLA Ops:
  0.0 4.0 %collective-permute-start = (bf16[4,128,128]{2,1,0:T(8,128)(2,1)}, bf16[4,128,128]{2,1,0:T(8,128)(2,1)S(1)}, u32[]{:S(2)}, u32[]{:S(2)}) collective-permute-start(bf16[4,128,128]{2,1,0:T(8,128)(2,1)} %bitcast.2), channel_id=1, source_target_pairs={{0,16},{4,20},{8,24},{12,28},{16,0},{20,4},{24,8},{28,12},{1,17},{... | collective-permute-start | bytes 393224 | tf_op jit(solution)/shard_map/ppermute | solution.py:294
  4.0 2.2 %near_blocks.1 = (bf16[528,128]{1,0:T(8,128)(2,1)S(1)}, bf16[528,128]{1,0:T(8,128)(2,1)S(1)}, bf16[528,128]{1,0:T(8,128)(2,1)S(1)}, bf16[528,128]{1,0:T(8,128)(2,1)S(1)}) custom-call(s32[4,3]{1,0:T(4,128)} %pairs_in.3, s32[1,128]{1,0:T(1,128)} %bitcast.4, bf16[512,1024]{1,0:T(8,128)(2,1)} %coef_in.3, bf16[4,128,128]{2,1,0:T(8,128)(2,1)} %bitcast.3), custom_call_target="tpu_custom_call" | custom-call | tf_op jit(solution)/shard_map/near_blocks/pallas_call | solution.py:359
  6.3 1.6 %collective-permute-start.2 = (bf16[528,128]{1,0:T(8,128)(2,1)S(1)}, bf16[528,128]{1,0:T(8,128)(2,1)S(1)}, u32[]{:S(2)}, u32[]{:S(2)}) collective-permute-start(bf16[528,128]{1,0:T(8,128)(2,1)S(1)} %get-tuple-element.32), channel_id=1, source_target_pairs={{0,4},{4,0},{8,12},{12,8},{16,20},{20,16},{24,28},{28,24},{1,5},{5... | collective-permute-start | bytes 405512 | tf_op jit(solution)/shard_map/ppermute | solution.py:294
  7.8 1.6 %collective-permute-start.3 = (bf16[528,128]{1,0:T(8,128)(2,1)S(1)}, bf16[528,128]{1,0:T(8,128)(2,1)S(1)}, u32[]{:S(2)}, u32[]{:S(2)}) collective-permute-start(bf16[528,128]{1,0:T(8,128)(2,1)S(1)} %get-tuple-element.33), channel_id=1, source_target_pairs={{0,8},{4,12},{8,0},{12,4},{16,24},{20,28},{24,16},{28,20},{1,9},{5... | collective-permute-start | bytes 405512 | tf_op jit(solution)/shard_map/ppermute | solution.py:294
  9.4 1.7 %pick.1 = bf16[144,512]{1,0:T(8,128)(2,1)S(1)} custom-call(s32[4,3]{1,0:T(4,128)} %pairs_in.3, s32[1,128]{1,0:T(1,128)} %bitcast.5, bf16[512,1024]{1,0:T(8,128)(2,1)} %coef_in.3), custom_call_target="tpu_custom_call" | custom-call | tf_op jit(solution)/shard_map/pick/pallas_call | solution.py:370
  11.1 0.0 collective-permute-done.refs_0_
  11.1 1.6 %collective-permute-start.5 = (bf16[4,128,128]{2,1,0:T(8,128)(2,1)S(1)}, bf16[4,128,128]{2,1,0:T(8,128)(2,1)S(1)}, u32[]{:S(2)}, u32[]{:S(2)}) collective-permute-start(bf16[4,128,128]{2,1,0:T(8,128)(2,1)S(1)} %collective-permute-done.refs_0_), channel_id=1, source_target_pairs={{0,2},{1,3},{2,0},{3,1},{4,6},{5,7},{6,4},{7,5},{8,10},{9,11},{10,... | collective-permute-start | bytes 393224 | tf_op jit(solution)/shard_map/ppermute | solution.py:294
  12.7 0.3 collective-permute-start.1
  13.1 4.1 %collective-permute-start.7 = (bf16[528,128]{1,0:T(8,128)(2,1)S(1)}, bf16[528,128]{1,0:T(8,128)(2,1)S(1)}, u32[]{:S(2)}, u32[]{:S(2)}) collective-permute-start(bf16[528,128]{1,0:T(8,128)(2,1)S(1)} %get-tuple-element.44), channel_id=1, source_target_pairs={{0,12},{4,8},{8,4},{12,0},{16,28},{20,24},{24,20},{28,16},{1,13},{... | collective-permute-start | bytes 405512 | tf_op jit(solution)/shard_map/ppermute | solution.py:294
  17.2 0.0 collective-permute-start.4
  17.2 0.5 %collective-permute-start.6 = (bf16[4,128,128]{2,1,0:T(8,128)(2,1)S(1)}, bf16[4,128,128]{2,1,0:T(8,128)(2,1)S(1)}, u32[]{:S(2)}, u32[]{:S(2)}) collective-permute-start(bf16[4,128,128]{2,1,0:T(8,128)(2,1)S(1)} %collective-permute-done.5.refs_2_), channel_id=1, source_target_pairs={{0,1},{1,0},{2,3},{3,2},{4,5},{5,4},{6,7},{7,6},{8,9},{9,8},{10,11... | collective-permute-start | bytes 393224 | tf_op jit(solution)/shard_map/ppermute | solution.py:294
  17.7 3.7 %collective-permute-done.7.refs_3_ = bf16[528,128]{1,0:T(8,128)(2,1)S(1)} collective-permute-done((bf16[528,128]{1,0:T(8,128)(2,1)S(1)}, bf16[528,128]{1,0:T(8,128)(2,1)S(1)}, u32[]{:S(2)}, u32[]{:S(2)}) %collective-permute-start.7) | collective-permute-done | bytes 135200 | tf_op jit(solution)/shard_map/ppermute | solution.py:294
  21.4 0.1 collective-permute-start.8
  21.5 0.6 %collective-permute-start.9 = (bf16[512,128]{1,0:T(8,128)(2,1)S(1)}, bf16[512,128]{1,0:T(8,128)(2,1)S(1)}, u32[]{:S(2)}, u32[]{:S(2)}) collective-permute-start(bf16[512,128]{1,0:T(8,128)(2,1)S(1)} %get-tuple-element.47), channel_id=1, source_target_pairs={{0,2},{1,3},{2,0},{3,1},{4,6},{5,7},{6,4},{7,5},{8,10},{9,11},{10,... | collective-permute-start | bytes 393224 | tf_op jit(solution)/shard_map/ppermute | solution.py:294
  22.1 1.3 %collective-permute-start.10 = (bf16[512,128]{1,0:T(8,128)(2,1)S(1)}, bf16[512,128]{1,0:T(8,128)(2,1)S(1)}, u32[]{:S(2)}, u32[]{:S(2)}) collective-permute-start(bf16[512,128]{1,0:T(8,128)(2,1)S(1)} %get-tuple-element.48), channel_id=1, source_target_pairs={{0,3},{1,2},{2,1},{3,0},{4,7},{5,6},{6,5},{7,4},{8,11},{9,10},{10,... | collective-permute-start | bytes 393224 | tf_op jit(solution)/shard_map/ppermute | solution.py:294
  23.4 0.3 far_blocks.1
  23.7 0.4 %collective-permute-start.11 = (bf16[528,128]{1,0:T(8,128)(2,1)S(1)}, bf16[528,128]{1,0:T(8,128)(2,1)S(1)}, u32[]{:S(2)}, u32[]{:S(2)}) collective-permute-start(bf16[528,128]{1,0:T(8,128)(2,1)S(1)} %get-tuple-element.49), channel_id=1, source_target_pairs={{0,4},{4,0},{8,12},{12,8},{16,20},{20,16},{24,28},{28,24},{1,5},{5... | collective-permute-start | bytes 405512 | tf_op jit(solution)/shard_map/ppermute | solution.py:294
  24.1 2.0 %collective-permute-start.12 = (bf16[528,128]{1,0:T(8,128)(2,1)S(1)}, bf16[528,128]{1,0:T(8,128)(2,1)S(1)}, u32[]{:S(2)}, u32[]{:S(2)}) collective-permute-start(bf16[528,128]{1,0:T(8,128)(2,1)S(1)} %get-tuple-element.50), channel_id=1, source_target_pairs={{0,8},{4,12},{8,0},{12,4},{16,24},{20,28},{24,16},{28,20},{1,9},{5... | collective-permute-start | bytes 405512 | tf_op jit(solution)/shard_map/ppermute | solution.py:294
  26.0 1.2 %collective-permute-start.13 = (bf16[528,128]{1,0:T(8,128)(2,1)S(1)}, bf16[528,128]{1,0:T(8,128)(2,1)S(1)}, u32[]{:S(2)}, u32[]{:S(2)}) collective-permute-start(bf16[528,128]{1,0:T(8,128)(2,1)S(1)} %get-tuple-element.51), channel_id=1, source_target_pairs={{0,12},{4,8},{8,4},{12,0},{16,28},{20,24},{24,20},{28,16},{1,13},{... | collective-permute-start | bytes 405512 | tf_op jit(solution)/shard_map/ppermute | solution.py:294
  27.2 0.6 %collective-permute-done.9.refs_5_ = bf16[512,128]{1,0:T(8,128)(2,1)S(1)} collective-permute-done((bf16[512,128]{1,0:T(8,128)(2,1)S(1)}, bf16[512,128]{1,0:T(8,128)(2,1)S(1)}, u32[]{:S(2)}, u32[]{:S(2)}) %collective-permute-start.9) | collective-permute-done | bytes 131104 | tf_op jit(solution)/shard_map/ppermute | solution.py:294
  27.9 1.9 %collective-permute-done.10.refs_6_ = bf16[512,128]{1,0:T(8,128)(2,1)S(1)} collective-permute-done((bf16[512,128]{1,0:T(8,128)(2,1)S(1)}, bf16[512,128]{1,0:T(8,128)(2,1)S(1)}, u32[]{:S(2)}, u32[]{:S(2)}) %collective-permute-start.10) | collective-permute-done | bytes 131104 | tf_op jit(solution)/shard_map/ppermute | solution.py:294
  29.8 0.9 %near_sum.1.total_in = f32[32,128,128]{2,1,0:T(8,128)S(1)} custom-call(bf16[528,128]{1,0:T(8,128)(2,1)S(1)} %get-tuple-element.41.refs_0_, bf16[528,128]{1,0:T(8,128)(2,1)S(1)} %collective-permute-done.2.refs_1_, bf16[528,128]{1,0:T(8,128)(2,1)S(1)} %collective-permute-done.3.refs_2_, bf16[528,128]{1,0:T(8,128)(2,1)S(1)} %collective-permute-done.7.refs_3_, ...), custom_call_target="tpu_custom_call" | custom-call | flops 3000000000 | bytes 1048576 | tf_op jit(solution)/shard_map/near_sum/pallas_call | solution.py:398
  30.7 2.9 %collective-permute-done.13.refs_3_ = bf16[528,128]{1,0:T(8,128)(2,1)S(1)} collective-permute-done((bf16[528,128]{1,0:T(8,128)(2,1)S(1)}, bf16[528,128]{1,0:T(8,128)(2,1)S(1)}, u32[]{:S(2)}, u32[]{:S(2)}) %collective-permute-start.13) | collective-permute-done | bytes 135200 | tf_op jit(solution)/shard_map/ppermute | solution.py:294
  33.7 2.3 %collect.1 = (bf16[32,4,4096]{2,1,0:T(4,128)(2,1)}, f32[32,128,128]{2,1,0:T(8,128)S(1)}) custom-call(bf16[4,4]{1,0:T(4,128)(2,1)} %metric_in.1, f32[32,128,128]{2,1,0:T(8,128)S(1)} %near_sum.1.total_in, bf16[528,128]{1,0:T(8,128)(2,1)S(1)} %get-tuple-element.40.refs_0_, ...), custom_call_target="tpu_custom_call", output_to_operand_aliasing={{1}: (1, {})} | custom-call | tf_op jit(solution)/shard_map/collect/pallas_call | solution.py:409
  (10 shorter events, 0.0 us)
Async XLA Ops:
  0.0 11.1 %collective-permute-start = (bf16[4,128,128]{2,1,0:T(8,128)(2,1)}, bf16[4,128,128]{2,1,0:T(8,128)(2,1)S(1)}, u32[]{:S(2)}, u32[]{:S(2)}) collective-permute-start(bf16[4,128,128]{2,1,0:T(8,128)(2,1)} %bitcast.2), channel_id=1, source_target_pairs={{0,16},{4,20},{8,24},{12,28},{16,0},{20,4},{24,8},{28,12},{1,17},{... | collective-permute-start | bytes 393224 | tf_op jit(solution)/shard_map/ppermute | solution.py:294
  6.3 10.9 %collective-permute-start.2 = (bf16[528,128]{1,0:T(8,128)(2,1)S(1)}, bf16[528,128]{1,0:T(8,128)(2,1)S(1)}, u32[]{:S(2)}, u32[]{:S(2)}) collective-permute-start(bf16[528,128]{1,0:T(8,128)(2,1)S(1)} %get-tuple-element.32), channel_id=1, source_target_pairs={{0,4},{4,0},{8,12},{12,8},{16,20},{20,16},{24,28},{28,24},{1,5},{5... | collective-permute-start | bytes 405512 | tf_op jit(solution)/shard_map/ppermute | solution.py:294
  7.8 9.4 %collective-permute-start.3 = (bf16[528,128]{1,0:T(8,128)(2,1)S(1)}, bf16[528,128]{1,0:T(8,128)(2,1)S(1)}, u32[]{:S(2)}, u32[]{:S(2)}) collective-permute-start(bf16[528,128]{1,0:T(8,128)(2,1)S(1)} %get-tuple-element.33), channel_id=1, source_target_pairs={{0,8},{4,12},{8,0},{12,4},{16,24},{20,28},{24,16},{28,20},{1,9},{5... | collective-permute-start | bytes 405512 | tf_op jit(solution)/shard_map/ppermute | solution.py:294
  11.1 6.1 %collective-permute-start.5 = (bf16[4,128,128]{2,1,0:T(8,128)(2,1)S(1)}, bf16[4,128,128]{2,1,0:T(8,128)(2,1)S(1)}, u32[]{:S(2)}, u32[]{:S(2)}) collective-permute-start(bf16[4,128,128]{2,1,0:T(8,128)(2,1)S(1)} %collective-permute-done.refs_0_), channel_id=1, source_target_pairs={{0,2},{1,3},{2,0},{3,1},{4,6},{5,7},{6,4},{7,5},{8,10},{9,11},{10,... | collective-permute-start | bytes 393224 | tf_op jit(solution)/shard_map/ppermute | solution.py:294
  12.7 10.6 %collective-permute-start.1 = (bf16[144,512]{1,0:T(8,128)(2,1)S(1)}, bf16[144,512]{1,0:T(8,128)(2,1)S(1)}, u32[]{:S(2)}, u32[]{:S(2)}) collective-permute-start(bf16[144,512]{1,0:T(8,128)(2,1)S(1)} %pick.1), channel_id=1, source_target_pairs={{0,16},{4,20},{8,24},{12,28},{16,0},{20,4},{24,8},{28,12},{1,17},{... | collective-permute-start | bytes 442376 | tf_op jit(solution)/shard_map/ppermute | solution.py:294
  13.1 8.3 %collective-permute-start.7 = (bf16[528,128]{1,0:T(8,128)(2,1)S(1)}, bf16[528,128]{1,0:T(8,128)(2,1)S(1)}, u32[]{:S(2)}, u32[]{:S(2)}) collective-permute-start(bf16[528,128]{1,0:T(8,128)(2,1)S(1)} %get-tuple-element.44), channel_id=1, source_target_pairs={{0,12},{4,8},{8,4},{12,0},{16,28},{20,24},{24,20},{28,16},{1,13},{... | collective-permute-start | bytes 405512 | tf_op jit(solution)/shard_map/ppermute | solution.py:294
  17.2 4.9 %collective-permute-start.4 = (bf16[4,128,128]{2,1,0:T(8,128)(2,1)S(1)}, bf16[4,128,128]{2,1,0:T(8,128)(2,1)S(1)}, u32[]{:S(2)}, u32[]{:S(2)}) collective-permute-start(bf16[4,128,128]{2,1,0:T(8,128)(2,1)S(1)} %collective-permute-done.refs_0_), channel_id=1, source_target_pairs={{0,1},{1,0},{2,3},{3,2},{4,5},{5,4},{6,7},{7,6},{8,9},{9,8},{10,11... | collective-permute-start | bytes 393224 | tf_op jit(solution)/shard_map/ppermute | solution.py:294
  17.2 6.1 %collective-permute-start.6 = (bf16[4,128,128]{2,1,0:T(8,128)(2,1)S(1)}, bf16[4,128,128]{2,1,0:T(8,128)(2,1)S(1)}, u32[]{:S(2)}, u32[]{:S(2)}) collective-permute-start(bf16[4,128,128]{2,1,0:T(8,128)(2,1)S(1)} %collective-permute-done.5.refs_2_), channel_id=1, source_target_pairs={{0,1},{1,0},{2,3},{3,2},{4,5},{5,4},{6,7},{7,6},{8,9},{9,8},{10,11... | collective-permute-start | bytes 393224 | tf_op jit(solution)/shard_map/ppermute | solution.py:294
  21.4 4.6 %collective-permute-start.8 = (bf16[512,128]{1,0:T(8,128)(2,1)S(1)}, bf16[512,128]{1,0:T(8,128)(2,1)S(1)}, u32[]{:S(2)}, u32[]{:S(2)}) collective-permute-start(bf16[512,128]{1,0:T(8,128)(2,1)S(1)} %get-tuple-element.46), channel_id=1, source_target_pairs={{0,1},{1,0},{2,3},{3,2},{4,5},{5,4},{6,7},{7,6},{8,9},{9,8},{10,11... | collective-permute-start | bytes 393224 | tf_op jit(solution)/shard_map/ppermute | solution.py:294
  21.5 6.4 %collective-permute-start.9 = (bf16[512,128]{1,0:T(8,128)(2,1)S(1)}, bf16[512,128]{1,0:T(8,128)(2,1)S(1)}, u32[]{:S(2)}, u32[]{:S(2)}) collective-permute-start(bf16[512,128]{1,0:T(8,128)(2,1)S(1)} %get-tuple-element.47), channel_id=1, source_target_pairs={{0,2},{1,3},{2,0},{3,1},{4,6},{5,7},{6,4},{7,5},{8,10},{9,11},{10,... | collective-permute-start | bytes 393224 | tf_op jit(solution)/shard_map/ppermute | solution.py:294
  22.1 7.7 %collective-permute-start.10 = (bf16[512,128]{1,0:T(8,128)(2,1)S(1)}, bf16[512,128]{1,0:T(8,128)(2,1)S(1)}, u32[]{:S(2)}, u32[]{:S(2)}) collective-permute-start(bf16[512,128]{1,0:T(8,128)(2,1)S(1)} %get-tuple-element.48), channel_id=1, source_target_pairs={{0,3},{1,2},{2,1},{3,0},{4,7},{5,6},{6,5},{7,4},{8,11},{9,10},{10,... | collective-permute-start | bytes 393224 | tf_op jit(solution)/shard_map/ppermute | solution.py:294
  23.7 7.0 %collective-permute-start.11 = (bf16[528,128]{1,0:T(8,128)(2,1)S(1)}, bf16[528,128]{1,0:T(8,128)(2,1)S(1)}, u32[]{:S(2)}, u32[]{:S(2)}) collective-permute-start(bf16[528,128]{1,0:T(8,128)(2,1)S(1)} %get-tuple-element.49), channel_id=1, source_target_pairs={{0,4},{4,0},{8,12},{12,8},{16,20},{20,16},{24,28},{28,24},{1,5},{5... | collective-permute-start | bytes 405512 | tf_op jit(solution)/shard_map/ppermute | solution.py:294
  24.1 6.7 %collective-permute-start.12 = (bf16[528,128]{1,0:T(8,128)(2,1)S(1)}, bf16[528,128]{1,0:T(8,128)(2,1)S(1)}, u32[]{:S(2)}, u32[]{:S(2)}) collective-permute-start(bf16[528,128]{1,0:T(8,128)(2,1)S(1)} %get-tuple-element.50), channel_id=1, source_target_pairs={{0,8},{4,12},{8,0},{12,4},{16,24},{20,28},{24,16},{28,20},{1,9},{5... | collective-permute-start | bytes 405512 | tf_op jit(solution)/shard_map/ppermute | solution.py:294
  26.0 7.6 %collective-permute-start.13 = (bf16[528,128]{1,0:T(8,128)(2,1)S(1)}, bf16[528,128]{1,0:T(8,128)(2,1)S(1)}, u32[]{:S(2)}, u32[]{:S(2)}) collective-permute-start(bf16[528,128]{1,0:T(8,128)(2,1)S(1)} %get-tuple-element.51), channel_id=1, source_target_pairs={{0,12},{4,8},{8,4},{12,0},{16,28},{20,24},{24,20},{28,16},{1,13},{... | collective-permute-start | bytes 405512 | tf_op jit(solution)/shard_map/ppermute | solution.py:294

commit v13 on v12

--- a/solution.py
+++ b/solution.py
@@ -204,70 +204,70 @@
             out[f * rows : (f + 1) * rows, :] = piece[j * rows : (j + 1) * rows, :]
 
 
-def block_kernel(aux_count, coefs, *refs):
-    blocks, pieces = refs[:aux_count], refs[aux_count:]
-    pairs_dev = blocks[0].shape[0]
+def merge_kernel(first, second, out, sems):
+    count = first.shape[0]
+    skip = second.shape[0] - count
+    loads = [
+        pltpu.make_async_copy(first, out.at[:count], sems.at[0]),
+        pltpu.make_async_copy(second.at[skip:], out.at[count:], sems.at[1]),
+    ]
+    for load in loads:
+        load.start()
+    for load in loads:
+        load.wait()
+
+
+def block_kernel(aux_count, low, coefs, blocks, *refs):
+    pieces = refs[len(refs) // 2 :] if low else refs
+    pairs_dev = blocks.shape[0] // 2
     rows = coefs.shape[0] - 16
     occ_local = rows // len(pieces)
     mine = lax.axis_index("aux")
     for k in range(pairs_dev):
         left = coefs[:rows, k * BS : (k + 1) * BS]
-        for j in range(0, aux_count, 2):
-            right = jnp.concatenate([blocks[j][k], blocks[j + 1][k]], axis=1)
-            half = jnp.dot(left, right, preferred_element_type=jnp.float32).astype(jnp.bfloat16)
-            for side in range(2):
-                at = k * aux_count + jnp.bitwise_xor(mine, j + side)
-                start = pl.multiple_of(at * occ_local, occ_local)
-                for f, piece in enumerate(pieces):
-                    piece[pl.ds(start, occ_local), :] = half[
-                        f * occ_local : (f + 1) * occ_local, side * BS : (side + 1) * BS
-                    ]
-    for piece in pieces:
-        piece[pairs_dev * aux_count * occ_local :, :] = coefs[rows:, :BS]
-
-
-def load_codes(received, codes_v, codes, sem):
+        right = jnp.concatenate([blocks[k], blocks[pairs_dev + k]], axis=1)
+        half = jnp.dot(left, right, preferred_element_type=jnp.float32).astype(jnp.bfloat16)
+        for side in range(2):
+            flipped = low + side * (aux_count // 2)
+            at = k * aux_count + jnp.bitwise_xor(mine, flipped)
+            start = pl.multiple_of(at * occ_local, occ_local)
+            for f, piece in enumerate(pieces):
+                piece[pl.ds(start, occ_local), :] = half[
+                    f * occ_local : (f + 1) * occ_local, side * BS : (side + 1) * BS
+                ]
+    if low == 0:
+        for piece in pieces:
+            piece[pairs_dev * aux_count * occ_local :, :] = coefs[rows:, :BS]
+
+
+def read_codes(received, pairs_dev, codes):
     for at, piece in enumerate(received):
-        digits = piece[piece.shape[0] - 16 :, :].astype(jnp.float32).astype(jnp.int32)
-        codes_v[at : at + 1, :] = digits[:1]
-    load = pltpu.make_async_copy(codes_v, codes, sem)
+        digits = piece[piece.shape[0] - 16 :, :].astype(jnp.float32)[:1]
+        high = pltpu.roll(digits, BS - pairs_dev, 1)
+        codes[at : at + 1, :] = (digits + 128.0 * high).astype(jnp.int32)
+
+
+def near_sum_kernel(count, metric_in, *refs):
+    *received, total, mix, metric, codes, sem = refs
+    received, others = received[:count], received[count:]
+    load = pltpu.make_async_copy(metric_in, metric, sem)
     load.start()
-    return load
-
-
-def near_sum_kernel(occ_local, count, *refs):
-    *received, total, codes_v, codes, sem = refs
-    received, others = received[:count], received[count:]
-    load = load_codes(received, codes_v, codes, sem)
     total[...] = jnp.zeros_like(total)
     mine = lax.axis_index("aux")
-    pairs_dev = others[0].shape[0] // (count * occ_local)
-    load.wait()
+    rows = total.shape[1]
+    occ_local = rows // metric.shape[0]
+    pairs_dev = (received[0].shape[0] - 16) // rows
+    read_codes(received, pairs_dev, codes)
     for f in range(count):
         for k in range(pairs_dev):
-            r = codes[f, k] + 128 * codes[f, pairs_dev + k]
+            r = codes[f, k]
             for j in range(len(others) + 1):
                 source, first = (others[j - 1], f * pairs_dev + k) if j else (received[f], k)
                 start = pl.multiple_of(jnp.bitwise_xor(mine, j) * occ_local, occ_local)
                 part = source[first * occ_local : (first + 1) * occ_local, :]
                 total[r, pl.ds(start, occ_local), :] += part.astype(jnp.float32)
-
-
-def collect_kernel(metric_in, total_in, *refs):
-    *received, out, total, metric, codes_v, codes, sem, metric_sem = refs
-    occ_local, aux_count = out.shape[:2]
-    rows = occ_local * aux_count
-    load = pltpu.make_async_copy(metric_in, metric, metric_sem)
-    load.start()
-    code_load = load_codes(received, codes_v, codes, sem)
-    pairs_dev = (received[0].shape[0] - 16) // rows
-    code_load.wait()
-    for at, piece in enumerate(received):
-        for k in range(pairs_dev):
-            r = codes[at, k] + 128 * codes[at, pairs_dev + k]
-            total[r] += piece[k * rows : (k + 1) * rows, :].astype(jnp.float32)
     load.wait()
-
+    aux_count = metric.shape[0]
     row = lax.broadcasted_iota(jnp.int32, (rows, rows), 0)
     column = lax.broadcasted_iota(jnp.int32, (rows, rows), 1)
     left = (
@@ -280,14 +280,36 @@
     ).astype(jnp.bfloat16)
     factor = jnp.dot(left, metric[...], preferred_element_type=jnp.float32).astype(jnp.bfloat16)
     factor = jnp.dot(factor, right, preferred_element_type=jnp.float32)
-    mix = jnp.where(row // aux_count == column % occ_local, factor, 0.0).astype(jnp.bfloat16)
-    for r in range(0, total.shape[0], 2):
-        summed = jnp.concatenate([total[r], total[r + 1]], axis=1).astype(jnp.bfloat16)
-        mixed = jnp.dot(mix, summed, preferred_element_type=jnp.float32)
-        out[:, :, r * BS : (r + 2) * BS] = mixed.reshape(
-            occ_local, aux_count, 2 * BS
-        ).astype(jnp.bfloat16)
-
+    mix[...] = jnp.where(row // aux_count == column % occ_local, factor, 0.0).astype(jnp.bfloat16)
+
+
+def collect_kernel(mix, total_in, *refs):
+    *received, out, total, staged, codes, sems = refs
+    occ_local, aux_count = out.shape[:2]
+    rows = total.shape[1]
+    pairs_dev = (received[0].shape[0] - 16) // rows
+    read_codes(received, pairs_dev, codes)
+    for at, piece in enumerate(received):
+        for k in range(pairs_dev):
+            total[codes[at, k]] += piece[k * rows : (k + 1) * rows, :].astype(jnp.float32)
+    stores = []
+    parts = sems.shape[0]
+    each = total.shape[0] // parts
+    for part in range(parts):
+        for r in range(part * each, (part + 1) * each, 2):
+            summed = jnp.concatenate([total[r], total[r + 1]], axis=1).astype(jnp.bfloat16)
+            mixed = jnp.dot(mix[...], summed, preferred_element_type=jnp.float32)
+            staged[:, :, r * BS : (r + 2) * BS] = mixed.reshape(
+                occ_local, aux_count, 2 * BS
+            ).astype(jnp.bfloat16)
+        lanes = pl.ds(part * each * BS, each * BS)
+        store = pltpu.make_async_copy(
+            staged.at[:, :, lanes], out.at[:, :, lanes], sems.at[part]
+        )
+        store.start()
+        stores.append(store)
+    for store in stores:
+        store.wait()
 
 def flip(value, axis, bits):
     count = lax.axis_size(axis)
@@ -296,17 +318,6 @@
 
 def after(value, *others):
     return lax.optimization_barrier((value, *others))[0]
-
-
-def shared(block, *others):
-    held, order, bits = [block], [0], lax.axis_size("aux") // 2
-    while bits:
-        held += [flip(one, "aux", bits) for one in held]
-        order += [at ^ bits for at in order]
-        bits //= 2
-        if others:
-            held = [after(one, *others) for one in held]
-    return [held[order.index(at)] for at in range(len(held))]
 
 
 def cost(flops):
@@ -330,23 +341,18 @@
     hbm = pl.BlockSpec(memory_space=pltpu.HBM)
     params = pltpu.CompilerParams(vmem_limit_bytes=40 * 2**20)
 
-    def transformed(name, coefs, quad, count):
+    def merged(name, first, second):
         return pl.pallas_call(
-            functools.partial(block_kernel, aux_count),
-            out_shape=[piece] * count,
-            in_specs=[vmem] * (1 + aux_count),
-            out_specs=[vmem] * count,
+            merge_kernel,
+            out_shape=jax.ShapeDtypeStruct(
+                (2 * first.shape[0],) + first.shape[1:], jnp.bfloat16
+            ),
+            in_specs=[vmem] * 2,
+            out_specs=vmem,
+            scratch_shapes=[pltpu.SemaphoreType.DMA((2,))],
             compiler_params=params,
-            cost_estimate=cost(3e9) if name == "far_blocks" else None,
             name=name,
-        )(coefs, *quad)
-
-    def code_scratch(count):
-        return [
-            pltpu.VMEM((count, BS), jnp.int32),
-            pltpu.SMEM((count, BS), jnp.int32),
-            pltpu.SemaphoreType.DMA,
-        ]
+        )(first, second)
 
     blocks = integrals.reshape(pairs_dev, BS, BS)
     far_block = flip(blocks, "shell", group)
@@ -382,7 +388,8 @@
     )(*in_hbm(*operands))
     far_block = after(far_block, sent_coef)
     far_coef = flip(after(sent_coef, far_block), "shell", group)
-    far_blocks = shared(far_block, near[1],near[2])
+    far_pair = merged("far_pair", far_block, after(flip(far_block, "aux", 2), *near))
+    far_pairs = [far_pair, flip(far_pair, "aux", 1)]
     regrouped = pl.pallas_call(
         functools.partial(regroup_kernel, group),
         out_shape=[jax.ShapeDtypeStruct((group * pairs_dev * occ_local, BS), jnp.bfloat16)]
@@ -393,18 +400,33 @@
         name="regroup",
     )(*near)
     others = [flip(one, "aux", j) for j, one in enumerate(regrouped, 1)]
-    far = transformed("far_blocks", far_coef, far_blocks, group)
+    far = []
+    for low in range(2):
+        far = pl.pallas_call(
+            functools.partial(block_kernel, aux_count, low),
+            out_shape=[piece] * group,
+            in_specs=[vmem] * (2 + len(far)),
+            out_specs=[vmem] * group,
+            input_output_aliases={2 + f: f for f in range(len(far))},
+            compiler_params=params,
+            cost_estimate=cost(2e9) if low == 0 else None,
+            name=f"far_blocks_{low}",
+        )(far_coef, far_pairs[low], *far)
     total_shape = jax.ShapeDtypeStruct((block_count, rows, BS), jnp.float32)
-    total = pl.pallas_call(
-        functools.partial(near_sum_kernel, occ_local, group),
-        out_shape=total_shape,
-        in_specs=[vmem] * (group + aux_count - 1),
-        out_specs=vmem,
-        scratch_shapes=code_scratch(group),
+    total, mix = pl.pallas_call(
+        functools.partial(near_sum_kernel, group),
+        out_shape=[total_shape, jax.ShapeDtypeStruct((rows, rows), jnp.bfloat16)],
+        in_specs=[hbm] + [vmem] * (group + aux_count - 1),
+        out_specs=[vmem] * 2,
+        scratch_shapes=[
+            pltpu.VMEM(metric.shape, jnp.bfloat16),
+            pltpu.VMEM((8, BS), jnp.int32),
+            pltpu.SemaphoreType.DMA,
+        ],
         compiler_params=params,
         cost_estimate=cost(3e9),
         name="near_sum",
-    )(*(after(one, far[0]) for one in near), *others)
+    )(*in_hbm(metric), *(after(one, far[0]) for one in near), *others)
     far = [far[0]] + [flip(far[f], "shell", f) for f in range(1, group)]
     return pl.pallas_call(
         collect_kernel,
@@ -412,21 +434,23 @@
             jax.ShapeDtypeStruct((occ_local, aux_count, block_count * BS), jnp.bfloat16),
             total_shape,
         ],
-        in_specs=[hbm] + [vmem] * (1 + group),
-        out_specs=[vmem, vmem],
+        in_specs=[vmem] * (2 + group),
+        out_specs=[hbm, vmem],
         input_output_aliases={1: 1},
-        scratch_shapes=[pltpu.VMEM(metric.shape, jnp.bfloat16)]
-        + code_scratch(group)
-        + [pltpu.SemaphoreType.DMA],
+        scratch_shapes=[
+            pltpu.VMEM((occ_local, aux_count, block_count * BS), jnp.bfloat16),
+            pltpu.VMEM((8, BS), jnp.int32),
+            pltpu.SemaphoreType.DMA((4,)),
+        ],
         compiler_params=params,
         name="collect",
-    )(*in_hbm(metric), total, *far)[0]
+    )(mix, total, *far)[0]
 
 
 def per_device(integrals, pair_list, coef, metric, occ_slot):
     shell_count, aux_count = lax.axis_size("shell"), lax.axis_size("aux")
     occ_local = coef.shape[1] // (shell_count * aux_count)
-    if occ_local % 16 or shell_count & (shell_count - 1) or aux_count & (aux_count - 1):
+    if occ_local % 16 or shell_count & (shell_count - 1) or aux_count != 4:
         return relayed_half_blocks(integrals, pair_list, coef, metric, occ_slot)
     return exchanged_inputs(integrals, pair_list, coef, metric, occ_slot)
 

time: 36.2 us -> 33.6 us (0.928)
  starting transfers between devices: 19.2 us -> 16 us
  waiting for transfers between devices: 9.13 us -> 9.62 us
    ppermute x14 -> x13, starting transfers between devices: 19.2 us -> 16 us  [flip(): return lax.ppermute(value, axis, [(at, at ^ bits) for at in range(count)])]
    pallas_call x2 -> x4, Pallas kernels: 1.24 us -> 2.19 us  [the longest x1 1.42 us: exchanged_inputs(): pl.pallas_call(functools.partial(near_sum_kernel, group), out_shape=[tota...]
    pallas_call x1, Pallas kernels: 2.34 us -> 1.53 us  [exchanged_inputs(): pl.pallas_call(collect_kernel, out_shape=[jax.ShapeDtypeStruct((occ_local...]
    ppermute x14 -> x13, waiting for transfers between devices: 9.13 us -> 9.62 us  [flip(): return lax.ppermute(value, axis, [(at, at ^ bits) for at in range(count)])]
  transfers between devices with their start and end apart: 14 -> 13, of which waited for: 4 -> 6; matrix products, arithmetic and copies ran while one was open for 0% -> 0% of each run, Pallas kernels for 14% -> 18%
where the time goes in v13:
time: 33.6 us; the launch traced here: 33.5 us
  starting transfers between devices  16 us (48%)
  waiting for transfers between devices  9.62 us (29%)
  Pallas kernels  7.71 us (23%)
    ppermute x13, starting transfers between devices, flip(): return lax.ppermute(value, axis, [(at, at ^ bits) for at in range(count)])  16 us
    ppermute x13, waiting for transfers between devices, flip(): return lax.ppermute(value, axis, [(at, at ^ bits) for at in range(count)])  9.62 us
    pallas_call x1, Pallas kernels, exchanged_inputs(): pl.pallas_call(functools.partial(near_kernel, occ_local, aux_count), out_...  2.23 us
    pallas_call x1, Pallas kernels, exchanged_inputs(): pl.pallas_call(functools.partial(pick_kernel, [list(range(group, shell_co...  1.72 us
    pallas_call x1, Pallas kernels, exchanged_inputs(): pl.pallas_call(collect_kernel, out_shape=[jax.ShapeDtypeStruct((occ_local...  1.53 us
    pallas_call x1, Pallas kernels, exchanged_inputs(): pl.pallas_call(functools.partial(near_sum_kernel, group), out_shape=[tota...  1.42 us
  transfers between devices with their start and end apart: 13, of which 6 were waited for; matrix products, arithmetic and copies ran while one was open for 0% of the time, Pallas kernels for 18%

profile of v13, /device:TPU:0, one launch (start us, length us, event | category | flops | bytes accessed | tf_op | source)
XLA Modules:
  0.0 33.5 jit_solution(9303166751436794067)
XLA Ops:
  0.0 4.0 %collective-permute-start = (bf16[4,128,128]{2,1,0:T(8,128)(2,1)}, bf16[4,128,128]{2,1,0:T(8,128)(2,1)S(1)}, u32[]{:S(2)}, u32[]{:S(2)}) collective-permute-start(bf16[4,128,128]{2,1,0:T(8,128)(2,1)} %bitcast.2), channel_id=1, source_target_pairs={{0,16},{4,20},{8,24},{12,28},{16,0},{20,4},{24,8},{28,12},{1,17},{... | collective-permute-start | bytes 393224 | tf_op jit(solution)/shard_map/ppermute | solution.py:316
  4.0 2.2 %near_blocks.1 = (bf16[528,128]{1,0:T(8,128)(2,1)S(1)}, bf16[528,128]{1,0:T(8,128)(2,1)S(1)}, bf16[528,128]{1,0:T(8,128)(2,1)S(1)}, bf16[528,128]{1,0:T(8,128)(2,1)S(1)}) custom-call(s32[4,3]{1,0:T(4,128)} %pairs_in.3, s32[1,128]{1,0:T(1,128)} %bitcast.4, bf16[512,1024]{1,0:T(8,128)(2,1)} %coef_in.3, bf16[4,128,128]{2,1,0:T(8,128)(2,1)} %bitcast.3), custom_call_target="tpu_custom_call" | custom-call | tf_op jit(solution)/shard_map/near_blocks/pallas_call | solution.py:365
  6.3 1.6 %collective-permute-start.3 = (bf16[528,128]{1,0:T(8,128)(2,1)S(1)}, bf16[528,128]{1,0:T(8,128)(2,1)S(1)}, u32[]{:S(2)}, u32[]{:S(2)}) collective-permute-start(bf16[528,128]{1,0:T(8,128)(2,1)S(1)} %get-tuple-element.33), channel_id=1, source_target_pairs={{0,4},{4,0},{8,12},{12,8},{16,20},{20,16},{24,28},{28,24},{1,5},{5... | collective-permute-start | bytes 405512 | tf_op jit(solution)/shard_map/ppermute | solution.py:316
  7.8 1.6 %collective-permute-start.4 = (bf16[528,128]{1,0:T(8,128)(2,1)S(1)}, bf16[528,128]{1,0:T(8,128)(2,1)S(1)}, u32[]{:S(2)}, u32[]{:S(2)}) collective-permute-start(bf16[528,128]{1,0:T(8,128)(2,1)S(1)} %get-tuple-element.34), channel_id=1, source_target_pairs={{0,8},{4,12},{8,0},{12,4},{16,24},{20,28},{24,16},{28,20},{1,9},{5... | collective-permute-start | bytes 405512 | tf_op jit(solution)/shard_map/ppermute | solution.py:316
  9.4 0.4 %collective-permute-start.5 = (bf16[528,128]{1,0:T(8,128)(2,1)S(1)}, bf16[528,128]{1,0:T(8,128)(2,1)S(1)}, u32[]{:S(2)}, u32[]{:S(2)}) collective-permute-start(bf16[528,128]{1,0:T(8,128)(2,1)S(1)} %get-tuple-element.35), channel_id=1, source_target_pairs={{0,12},{4,8},{8,4},{12,0},{16,28},{20,24},{24,20},{28,16},{1,13},{... | collective-permute-start | bytes 405512 | tf_op jit(solution)/shard_map/ppermute | solution.py:316
  9.8 1.7 %pick.1 = bf16[144,512]{1,0:T(8,128)(2,1)S(1)} custom-call(s32[4,3]{1,0:T(4,128)} %pairs_in.3, s32[1,128]{1,0:T(1,128)} %bitcast.5, bf16[512,1024]{1,0:T(8,128)(2,1)} %coef_in.3), custom_call_target="tpu_custom_call" | custom-call | tf_op jit(solution)/shard_map/pick/pallas_call | solution.py:376
  11.6 1.6 %collective-permute-start.2 = (bf16[4,128,128]{2,1,0:T(8,128)(2,1)S(1)}, bf16[4,128,128]{2,1,0:T(8,128)(2,1)S(1)}, u32[]{:S(2)}, u32[]{:S(2)}) collective-permute-start(bf16[4,128,128]{2,1,0:T(8,128)(2,1)S(1)} %collective-permute-done.first), channel_id=1, source_target_pairs={{0,2},{1,3},{2,0},{3,1},{4,6},{5,7},{6,4},{7,5},{8,10},{9,11},{10,... | collective-permute-start | bytes 393224 | tf_op jit(solution)/shard_map/ppermute | solution.py:316
  13.2 0.3 %collective-permute-start.1 = (bf16[144,512]{1,0:T(8,128)(2,1)S(1)}, bf16[144,512]{1,0:T(8,128)(2,1)S(1)}, u32[]{:S(2)}, u32[]{:S(2)}) collective-permute-start(bf16[144,512]{1,0:T(8,128)(2,1)S(1)} %pick.1), channel_id=1, source_target_pairs={{0,16},{4,20},{8,24},{12,28},{16,0},{20,4},{24,8},{28,12},{1,17},{... | collective-permute-start | bytes 442376 | tf_op jit(solution)/shard_map/ppermute | solution.py:316
  13.5 0.9 %collective-permute-done.4.refs_2_ = bf16[528,128]{1,0:T(8,128)(2,1)S(1)} collective-permute-done((bf16[528,128]{1,0:T(8,128)(2,1)S(1)}, bf16[528,128]{1,0:T(8,128)(2,1)S(1)}, u32[]{:S(2)}, u32[]{:S(2)}) %collective-permute-start.4) | collective-permute-done | bytes 135200 | tf_op jit(solution)/shard_map/ppermute | solution.py:316
  14.4 4.0 %collective-permute-done.5.refs_3_ = bf16[528,128]{1,0:T(8,128)(2,1)S(1)} collective-permute-done((bf16[528,128]{1,0:T(8,128)(2,1)S(1)}, bf16[528,128]{1,0:T(8,128)(2,1)S(1)}, u32[]{:S(2)}, u32[]{:S(2)}) %collective-permute-start.5) | collective-permute-done | bytes 135200 | tf_op jit(solution)/shard_map/ppermute | solution.py:316
  18.3 0.3 %far_pair.1.blocks = bf16[8,128,128]{2,1,0:T(8,128)(2,1)S(1)} custom-call(bf16[4,128,128]{2,1,0:T(8,128)(2,1)S(1)} %collective-permute-done.first, bf16[4,128,128]{2,1,0:T(8,128)(2,1)S(1)} %collective-permute-done.2.second), custom_call_target="tpu_custom_call" | custom-call | tf_op jit(solution)/shard_map/far_pair/pallas_call | solution.py:345
  18.7 0.1 collective-permute-start.6
  18.8 0.6 %collective-permute-start.7 = (bf16[512,128]{1,0:T(8,128)(2,1)S(1)}, bf16[512,128]{1,0:T(8,128)(2,1)S(1)}, u32[]{:S(2)}, u32[]{:S(2)}) collective-permute-start(bf16[512,128]{1,0:T(8,128)(2,1)S(1)} %get-tuple-element.46), channel_id=1, source_target_pairs={{0,1},{1,0},{2,3},{3,2},{4,5},{5,4},{6,7},{7,6},{8,9},{9,8},{10,11... | collective-permute-start | bytes 393224 | tf_op jit(solution)/shard_map/ppermute | solution.py:316
  19.3 2.4 %collective-permute-start.8 = (bf16[512,128]{1,0:T(8,128)(2,1)S(1)}, bf16[512,128]{1,0:T(8,128)(2,1)S(1)}, u32[]{:S(2)}, u32[]{:S(2)}) collective-permute-start(bf16[512,128]{1,0:T(8,128)(2,1)S(1)} %get-tuple-element.47), channel_id=1, source_target_pairs={{0,2},{1,3},{2,0},{3,1},{4,6},{5,7},{6,4},{7,5},{8,10},{9,11},{10,... | collective-permute-start | bytes 393224 | tf_op jit(solution)/shard_map/ppermute | solution.py:316
  21.7 0.2 far_blocks_0.1
  21.9 0.2 far_blocks_1.1
  22.2 1.3 %collective-permute-start.10 = (bf16[528,128]{1,0:T(8,128)(2,1)S(1)}, bf16[528,128]{1,0:T(8,128)(2,1)S(1)}, u32[]{:S(2)}, u32[]{:S(2)}) collective-permute-start(bf16[528,128]{1,0:T(8,128)(2,1)S(1)} %get-tuple-element.51), channel_id=1, source_target_pairs={{0,4},{4,0},{8,12},{12,8},{16,20},{20,16},{24,28},{28,24},{1,5},{5... | collective-permute-start | bytes 405512 | tf_op jit(solution)/shard_map/ppermute | solution.py:316
  23.5 2.2 %collective-permute-start.12 = (bf16[528,128]{1,0:T(8,128)(2,1)S(1)}, bf16[528,128]{1,0:T(8,128)(2,1)S(1)}, u32[]{:S(2)}, u32[]{:S(2)}) collective-permute-start(bf16[528,128]{1,0:T(8,128)(2,1)S(1)} %get-tuple-element.53), channel_id=1, source_target_pairs={{0,12},{4,8},{8,4},{12,0},{16,28},{20,24},{24,20},{28,16},{1,13},{... | collective-permute-start | bytes 405512 | tf_op jit(solution)/shard_map/ppermute | solution.py:316
  25.7 0.3 collective-permute-done.8.refs_5_
  26.0 1.7 %collective-permute-done.9.refs_6_ = bf16[512,128]{1,0:T(8,128)(2,1)S(1)} collective-permute-done((bf16[512,128]{1,0:T(8,128)(2,1)S(1)}, bf16[512,128]{1,0:T(8,128)(2,1)S(1)}, u32[]{:S(2)}, u32[]{:S(2)}) %collective-permute-start.9) | collective-permute-done | bytes 131104 | tf_op jit(solution)/shard_map/ppermute | solution.py:316
  27.7 1.4 %near_sum.1 = (f32[32,128,128]{2,1,0:T(8,128)S(1)}, bf16[128,128]{1,0:T(8,128)(2,1)S(1)}) custom-call(bf16[4,4]{1,0:T(4,128)(2,1)} %metric_in.1, bf16[528,128]{1,0:T(8,128)(2,1)S(1)} %get-tuple-element.42.refs_0_, bf16[528,128]{1,0:T(8,128)(2,1)S(1)} %collective-permute-done.3.refs_1_, bf16[528,128]{1,0:T(8,128)(2,1)S(1)} %collective-permute-done.4.refs_2_, ...), custom_call_target="tpu_custom_call" | custom-call | flops 3000000000 | bytes 1048576 | tf_op jit(solution)/shard_map/near_sum/pallas_call | solution.py:416
  29.1 0.6 %collective-permute-done.11.refs_2_ = bf16[528,128]{1,0:T(8,128)(2,1)S(1)} collective-permute-done((bf16[528,128]{1,0:T(8,128)(2,1)S(1)}, bf16[528,128]{1,0:T(8,128)(2,1)S(1)}, u32[]{:S(2)}, u32[]{:S(2)}) %collective-permute-start.11) | collective-permute-done | bytes 135200 | tf_op jit(solution)/shard_map/ppermute | solution.py:316
  29.8 2.2 %collective-permute-done.12.refs_3_ = bf16[528,128]{1,0:T(8,128)(2,1)S(1)} collective-permute-done((bf16[528,128]{1,0:T(8,128)(2,1)S(1)}, bf16[528,128]{1,0:T(8,128)(2,1)S(1)}, u32[]{:S(2)}, u32[]{:S(2)}) %collective-permute-start.12) | collective-permute-done | bytes 135200 | tf_op jit(solution)/shard_map/ppermute | solution.py:316
  31.9 1.5 %collect.1 = (bf16[32,4,4096]{2,1,0:T(4,128)(2,1)}, f32[32,128,128]{2,1,0:T(8,128)S(1)}) custom-call(bf16[128,128]{1,0:T(8,128)(2,1)S(1)} %get-tuple-element.49.mix, f32[32,128,128]{2,1,0:T(8,128)S(1)} %get-tuple-element.50.total_in, bf16[528,128]{1,0:T(8,128)(2,1)S(1)} %get-tuple-element.41.refs_0_, ...), custom_call_target="tpu_custom_call", output_to_operand_aliasing={{1}: (1, {})} | custom-call | tf_op jit(solution)/shard_map/collect/pallas_call | solution.py:431
  (10 shorter events, 0.1 us)
Async XLA Ops:
  0.0 11.6 %collective-permute-start = (bf16[4,128,128]{2,1,0:T(8,128)(2,1)}, bf16[4,128,128]{2,1,0:T(8,128)(2,1)S(1)}, u32[]{:S(2)}, u32[]{:S(2)}) collective-permute-start(bf16[4,128,128]{2,1,0:T(8,128)(2,1)} %bitcast.2), channel_id=1, source_target_pairs={{0,16},{4,20},{8,24},{12,28},{16,0},{20,4},{24,8},{28,12},{1,17},{... | collective-permute-start | bytes 393224 | tf_op jit(solution)/shard_map/ppermute | solution.py:316
  6.3 7.2 %collective-permute-start.3 = (bf16[528,128]{1,0:T(8,128)(2,1)S(1)}, bf16[528,128]{1,0:T(8,128)(2,1)S(1)}, u32[]{:S(2)}, u32[]{:S(2)}) collective-permute-start(bf16[528,128]{1,0:T(8,128)(2,1)S(1)} %get-tuple-element.33), channel_id=1, source_target_pairs={{0,4},{4,0},{8,12},{12,8},{16,20},{20,16},{24,28},{28,24},{1,5},{5... | collective-permute-start | bytes 405512 | tf_op jit(solution)/shard_map/ppermute | solution.py:316
  7.8 6.5 %collective-permute-start.4 = (bf16[528,128]{1,0:T(8,128)(2,1)S(1)}, bf16[528,128]{1,0:T(8,128)(2,1)S(1)}, u32[]{:S(2)}, u32[]{:S(2)}) collective-permute-start(bf16[528,128]{1,0:T(8,128)(2,1)S(1)} %get-tuple-element.34), channel_id=1, source_target_pairs={{0,8},{4,12},{8,0},{12,4},{16,24},{20,28},{24,16},{28,20},{1,9},{5... | collective-permute-start | bytes 405512 | tf_op jit(solution)/shard_map/ppermute | solution.py:316
  9.4 8.9 %collective-permute-start.5 = (bf16[528,128]{1,0:T(8,128)(2,1)S(1)}, bf16[528,128]{1,0:T(8,128)(2,1)S(1)}, u32[]{:S(2)}, u32[]{:S(2)}) collective-permute-start(bf16[528,128]{1,0:T(8,128)(2,1)S(1)} %get-tuple-element.35), channel_id=1, source_target_pairs={{0,12},{4,8},{8,4},{12,0},{16,28},{20,24},{24,20},{28,16},{1,13},{... | collective-permute-start | bytes 405512 | tf_op jit(solution)/shard_map/ppermute | solution.py:316
  11.6 6.7 %collective-permute-start.2 = (bf16[4,128,128]{2,1,0:T(8,128)(2,1)S(1)}, bf16[4,128,128]{2,1,0:T(8,128)(2,1)S(1)}, u32[]{:S(2)}, u32[]{:S(2)}) collective-permute-start(bf16[4,128,128]{2,1,0:T(8,128)(2,1)S(1)} %collective-permute-done.first), channel_id=1, source_target_pairs={{0,2},{1,3},{2,0},{3,1},{4,6},{5,7},{6,4},{7,5},{8,10},{9,11},{10,... | collective-permute-start | bytes 393224 | tf_op jit(solution)/shard_map/ppermute | solution.py:316
  13.2 8.5 %collective-permute-start.1 = (bf16[144,512]{1,0:T(8,128)(2,1)S(1)}, bf16[144,512]{1,0:T(8,128)(2,1)S(1)}, u32[]{:S(2)}, u32[]{:S(2)}) collective-permute-start(bf16[144,512]{1,0:T(8,128)(2,1)S(1)} %pick.1), channel_id=1, source_target_pairs={{0,16},{4,20},{8,24},{12,28},{16,0},{20,4},{24,8},{28,12},{1,17},{... | collective-permute-start | bytes 442376 | tf_op jit(solution)/shard_map/ppermute | solution.py:316
  18.7 3.3 %collective-permute-start.6 = (bf16[8,128,128]{2,1,0:T(8,128)(2,1)S(1)}, bf16[8,128,128]{2,1,0:T(8,128)(2,1)S(1)}, u32[]{:S(2)}, u32[]{:S(2)}) collective-permute-start(bf16[8,128,128]{2,1,0:T(8,128)(2,1)S(1)} %far_pair.1.blocks), channel_id=1, source_target_pairs={{0,1},{1,0},{2,3},{3,2},{4,5},{5,4},{6,7},{7,6},{8,9},{9,8},{10,11... | collective-permute-start | bytes 786440 | tf_op jit(solution)/shard_map/ppermute | solution.py:316
  18.8 4.7 %collective-permute-start.7 = (bf16[512,128]{1,0:T(8,128)(2,1)S(1)}, bf16[512,128]{1,0:T(8,128)(2,1)S(1)}, u32[]{:S(2)}, u32[]{:S(2)}) collective-permute-start(bf16[512,128]{1,0:T(8,128)(2,1)S(1)} %get-tuple-element.46), channel_id=1, source_target_pairs={{0,1},{1,0},{2,3},{3,2},{4,5},{5,4},{6,7},{7,6},{8,9},{9,8},{10,11... | collective-permute-start | bytes 393224 | tf_op jit(solution)/shard_map/ppermute | solution.py:316
  19.3 6.6 %collective-permute-start.8 = (bf16[512,128]{1,0:T(8,128)(2,1)S(1)}, bf16[512,128]{1,0:T(8,128)(2,1)S(1)}, u32[]{:S(2)}, u32[]{:S(2)}) collective-permute-start(bf16[512,128]{1,0:T(8,128)(2,1)S(1)} %get-tuple-element.47), channel_id=1, source_target_pairs={{0,2},{1,3},{2,0},{3,1},{4,6},{5,7},{6,4},{7,5},{8,10},{9,11},{10,... | collective-permute-start | bytes 393224 | tf_op jit(solution)/shard_map/ppermute | solution.py:316
  21.7 6.0 %collective-permute-start.9 = (bf16[512,128]{1,0:T(8,128)(2,1)S(1)}, bf16[512,128]{1,0:T(8,128)(2,1)S(1)}, u32[]{:S(2)}, u32[]{:S(2)}) collective-permute-start(bf16[512,128]{1,0:T(8,128)(2,1)S(1)} %get-tuple-element.48), channel_id=1, source_target_pairs={{0,3},{1,2},{2,1},{3,0},{4,7},{5,6},{6,5},{7,4},{8,11},{9,10},{10,... | collective-permute-start | bytes 393224 | tf_op jit(solution)/shard_map/ppermute | solution.py:316
  22.2 7.0 %collective-permute-start.10 = (bf16[528,128]{1,0:T(8,128)(2,1)S(1)}, bf16[528,128]{1,0:T(8,128)(2,1)S(1)}, u32[]{:S(2)}, u32[]{:S(2)}) collective-permute-start(bf16[528,128]{1,0:T(8,128)(2,1)S(1)} %get-tuple-element.51), channel_id=1, source_target_pairs={{0,4},{4,0},{8,12},{12,8},{16,20},{20,16},{24,28},{28,24},{1,5},{5... | collective-permute-start | bytes 405512 | tf_op jit(solution)/shard_map/ppermute | solution.py:316
  23.5 6.3 %collective-permute-start.11 = (bf16[528,128]{1,0:T(8,128)(2,1)S(1)}, bf16[528,128]{1,0:T(8,128)(2,1)S(1)}, u32[]{:S(2)}, u32[]{:S(2)}) collective-permute-start(bf16[528,128]{1,0:T(8,128)(2,1)S(1)} %get-tuple-element.52), channel_id=1, source_target_pairs={{0,8},{4,12},{8,0},{12,4},{16,24},{20,28},{24,16},{28,20},{1,9},{5... | collective-permute-start | bytes 405512 | tf_op jit(solution)/shard_map/ppermute | solution.py:316
  23.5 8.5 %collective-permute-start.12 = (bf16[528,128]{1,0:T(8,128)(2,1)S(1)}, bf16[528,128]{1,0:T(8,128)(2,1)S(1)}, u32[]{:S(2)}, u32[]{:S(2)}) collective-permute-start(bf16[528,128]{1,0:T(8,128)(2,1)S(1)} %get-tuple-element.53), channel_id=1, source_target_pairs={{0,12},{4,8},{8,4},{12,0},{16,28},{20,24},{24,20},{28,16},{1,13},{... | collective-permute-start | bytes 405512 | tf_op jit(solution)/shard_map/ppermute | solution.py:316

commit v14 on v13

--- a/solution.py
+++ b/solution.py
@@ -388,7 +388,7 @@
     )(*in_hbm(*operands))
     far_block = after(far_block, sent_coef)
     far_coef = flip(after(sent_coef, far_block), "shell", group)
-    far_pair = merged("far_pair", far_block, after(flip(far_block, "aux", 2), *near))
+    far_pair = merged("far_pair", far_block, after(flip(far_block, "aux", 2), *near[:3]))
     far_pairs = [far_pair, flip(far_pair, "aux", 1)]
     regrouped = pl.pallas_call(
         functools.partial(regroup_kernel, group),

time: 33.6 us -> 35.5 us (1.057)
  starting transfers between devices: 16 us -> 18.8 us
  waiting for transfers between devices: 9.62 us -> 8.72 us
    ppermute x13, starting transfers between devices: 16 us -> 18.8 us  [flip(): return lax.ppermute(value, axis, [(at, at ^ bits) for at in range(count)])]
    ppermute x13, waiting for transfers between devices: 9.62 us -> 8.72 us  [flip(): return lax.ppermute(value, axis, [(at, at ^ bits) for at in range(count)])]
  transfers between devices with their start and end apart: 13 -> 13, of which waited for: 6 -> 4; matrix products, arithmetic and copies ran while one was open for 0% -> 0% of each run, Pallas kernels for 18% -> 18%
where the time goes in v14:
time: 35.5 us; the launch traced here: 35.3 us
  starting transfers between devices  18.8 us (53%)
  waiting for transfers between devices  8.72 us (25%)
  Pallas kernels  7.72 us (22%)
    ppermute x13, starting transfers between devices, flip(): return lax.ppermute(value, axis, [(at, at ^ bits) for at in range(count)])  18.8 us
    ppermute x13, waiting for transfers between devices, flip(): return lax.ppermute(value, axis, [(at, at ^ bits) for at in range(count)])  8.72 us
    pallas_call x1, Pallas kernels, exchanged_inputs(): pl.pallas_call(functools.partial(near_kernel, occ_local, aux_count), out_...  2.23 us
    pallas_call x1, Pallas kernels, exchanged_inputs(): pl.pallas_call(functools.partial(pick_kernel, [list(range(group, shell_co...  1.72 us
    pallas_call x1, Pallas kernels, exchanged_inputs(): pl.pallas_call(collect_kernel, out_shape=[jax.ShapeDtypeStruct((occ_local...  1.53 us
    pallas_call x1, Pallas kernels, exchanged_inputs(): pl.pallas_call(functools.partial(near_sum_kernel, group), out_shape=[tota...  1.42 us
  transfers between devices with their start and end apart: 13, of which 4 were waited for; matrix products, arithmetic and copies ran while one was open for 0% of the time, Pallas kernels for 18%

profile of v14, /device:TPU:0, one launch (start us, length us, event | category | flops | bytes accessed | tf_op | source)
XLA Modules:
  0.0 35.3 jit_solution(9023925408898216501)
XLA Ops:
  0.0 4.0 %collective-permute-start = (bf16[4,128,128]{2,1,0:T(8,128)(2,1)}, bf16[4,128,128]{2,1,0:T(8,128)(2,1)S(1)}, u32[]{:S(2)}, u32[]{:S(2)}) collective-permute-start(bf16[4,128,128]{2,1,0:T(8,128)(2,1)} %bitcast.2), channel_id=1, source_target_pairs={{0,16},{4,20},{8,24},{12,28},{16,0},{20,4},{24,8},{28,12},{1,17},{... | collective-permute-start | bytes 393224 | tf_op jit(solution)/shard_map/ppermute | solution.py:316
  4.0 2.2 %near_blocks.1 = (bf16[528,128]{1,0:T(8,128)(2,1)S(1)}, bf16[528,128]{1,0:T(8,128)(2,1)S(1)}, bf16[528,128]{1,0:T(8,128)(2,1)S(1)}, bf16[528,128]{1,0:T(8,128)(2,1)S(1)}) custom-call(s32[4,3]{1,0:T(4,128)} %pairs_in.3, s32[1,128]{1,0:T(1,128)} %bitcast.4, bf16[512,1024]{1,0:T(8,128)(2,1)} %coef_in.3, bf16[4,128,128]{2,1,0:T(8,128)(2,1)} %bitcast.3), custom_call_target="tpu_custom_call" | custom-call | tf_op jit(solution)/shard_map/near_blocks/pallas_call | solution.py:365
  6.3 1.6 %collective-permute-start.3 = (bf16[528,128]{1,0:T(8,128)(2,1)S(1)}, bf16[528,128]{1,0:T(8,128)(2,1)S(1)}, u32[]{:S(2)}, u32[]{:S(2)}) collective-permute-start(bf16[528,128]{1,0:T(8,128)(2,1)S(1)} %get-tuple-element.33), channel_id=1, source_target_pairs={{0,4},{4,0},{8,12},{12,8},{16,20},{20,16},{24,28},{28,24},{1,5},{5... | collective-permute-start | bytes 405512 | tf_op jit(solution)/shard_map/ppermute | solution.py:316
  7.8 1.6 %collective-permute-start.4 = (bf16[528,128]{1,0:T(8,128)(2,1)S(1)}, bf16[528,128]{1,0:T(8,128)(2,1)S(1)}, u32[]{:S(2)}, u32[]{:S(2)}) collective-permute-start(bf16[528,128]{1,0:T(8,128)(2,1)S(1)} %get-tuple-element.34), channel_id=1, source_target_pairs={{0,8},{4,12},{8,0},{12,4},{16,24},{20,28},{24,16},{28,20},{1,9},{5... | collective-permute-start | bytes 405512 | tf_op jit(solution)/shard_map/ppermute | solution.py:316
  9.4 1.7 %pick.1 = bf16[144,512]{1,0:T(8,128)(2,1)S(1)} custom-call(s32[4,3]{1,0:T(4,128)} %pairs_in.3, s32[1,128]{1,0:T(1,128)} %bitcast.5, bf16[512,1024]{1,0:T(8,128)(2,1)} %coef_in.3), custom_call_target="tpu_custom_call" | custom-call | tf_op jit(solution)/shard_map/pick/pallas_call | solution.py:376
  11.1 1.6 %collective-permute-start.2 = (bf16[4,128,128]{2,1,0:T(8,128)(2,1)S(1)}, bf16[4,128,128]{2,1,0:T(8,128)(2,1)S(1)}, u32[]{:S(2)}, u32[]{:S(2)}) collective-permute-start(bf16[4,128,128]{2,1,0:T(8,128)(2,1)S(1)} %collective-permute-done.first), channel_id=1, source_target_pairs={{0,2},{1,3},{2,0},{3,1},{4,6},{5,7},{6,4},{7,5},{8,10},{9,11},{10,... | collective-permute-start | bytes 393224 | tf_op jit(solution)/shard_map/ppermute | solution.py:316
  12.7 0.3 collective-permute-start.1
  13.1 4.1 %collective-permute-start.6 = (bf16[528,128]{1,0:T(8,128)(2,1)S(1)}, bf16[528,128]{1,0:T(8,128)(2,1)S(1)}, u32[]{:S(2)}, u32[]{:S(2)}) collective-permute-start(bf16[528,128]{1,0:T(8,128)(2,1)S(1)} %get-tuple-element.44), channel_id=1, source_target_pairs={{0,12},{4,8},{8,4},{12,0},{16,28},{20,24},{24,20},{28,16},{1,13},{... | collective-permute-start | bytes 405512 | tf_op jit(solution)/shard_map/ppermute | solution.py:316
  17.2 0.4 %far_pair.1.blocks = bf16[8,128,128]{2,1,0:T(8,128)(2,1)S(1)} custom-call(bf16[4,128,128]{2,1,0:T(8,128)(2,1)S(1)} %collective-permute-done.first, bf16[4,128,128]{2,1,0:T(8,128)(2,1)S(1)} %collective-permute-done.2.second), custom_call_target="tpu_custom_call" | custom-call | tf_op jit(solution)/shard_map/far_pair/pallas_call | solution.py:345
  17.6 0.1 collective-permute-start.5
  17.7 3.7 %collective-permute-done.6.refs_3_ = bf16[528,128]{1,0:T(8,128)(2,1)S(1)} collective-permute-done((bf16[528,128]{1,0:T(8,128)(2,1)S(1)}, bf16[528,128]{1,0:T(8,128)(2,1)S(1)}, u32[]{:S(2)}, u32[]{:S(2)}) %collective-permute-start.6) | collective-permute-done | bytes 135200 | tf_op jit(solution)/shard_map/ppermute | solution.py:316
  21.4 0.1 collective-permute-start.7
  21.5 0.6 %collective-permute-start.8 = (bf16[512,128]{1,0:T(8,128)(2,1)S(1)}, bf16[512,128]{1,0:T(8,128)(2,1)S(1)}, u32[]{:S(2)}, u32[]{:S(2)}) collective-permute-start(bf16[512,128]{1,0:T(8,128)(2,1)S(1)} %get-tuple-element.47), channel_id=1, source_target_pairs={{0,2},{1,3},{2,0},{3,1},{4,6},{5,7},{6,4},{7,5},{8,10},{9,11},{10,... | collective-permute-start | bytes 393224 | tf_op jit(solution)/shard_map/ppermute | solution.py:316
  22.1 1.3 %collective-permute-start.9 = (bf16[512,128]{1,0:T(8,128)(2,1)S(1)}, bf16[512,128]{1,0:T(8,128)(2,1)S(1)}, u32[]{:S(2)}, u32[]{:S(2)}) collective-permute-start(bf16[512,128]{1,0:T(8,128)(2,1)S(1)} %get-tuple-element.48), channel_id=1, source_target_pairs={{0,3},{1,2},{2,1},{3,0},{4,7},{5,6},{6,5},{7,4},{8,11},{9,10},{10,... | collective-permute-start | bytes 393224 | tf_op jit(solution)/shard_map/ppermute | solution.py:316
  23.4 0.2 far_blocks_0.1
  23.6 0.2 far_blocks_1.1
  23.8 0.4 %collective-permute-start.10 = (bf16[528,128]{1,0:T(8,128)(2,1)S(1)}, bf16[528,128]{1,0:T(8,128)(2,1)S(1)}, u32[]{:S(2)}, u32[]{:S(2)}) collective-permute-start(bf16[528,128]{1,0:T(8,128)(2,1)S(1)} %get-tuple-element.51), channel_id=1, source_target_pairs={{0,4},{4,0},{8,12},{12,8},{16,20},{20,16},{24,28},{28,24},{1,5},{5... | collective-permute-start | bytes 405512 | tf_op jit(solution)/shard_map/ppermute | solution.py:316
  24.2 2.0 %collective-permute-start.11 = (bf16[528,128]{1,0:T(8,128)(2,1)S(1)}, bf16[528,128]{1,0:T(8,128)(2,1)S(1)}, u32[]{:S(2)}, u32[]{:S(2)}) collective-permute-start(bf16[528,128]{1,0:T(8,128)(2,1)S(1)} %get-tuple-element.52), channel_id=1, source_target_pairs={{0,8},{4,12},{8,0},{12,4},{16,24},{20,28},{24,16},{28,20},{1,9},{5... | collective-permute-start | bytes 405512 | tf_op jit(solution)/shard_map/ppermute | solution.py:316
  26.2 1.2 %collective-permute-start.12 = (bf16[528,128]{1,0:T(8,128)(2,1)S(1)}, bf16[528,128]{1,0:T(8,128)(2,1)S(1)}, u32[]{:S(2)}, u32[]{:S(2)}) collective-permute-start(bf16[528,128]{1,0:T(8,128)(2,1)S(1)} %get-tuple-element.53), channel_id=1, source_target_pairs={{0,12},{4,8},{8,4},{12,0},{16,28},{20,24},{24,20},{28,16},{1,13},{... | collective-permute-start | bytes 405512 | tf_op jit(solution)/shard_map/ppermute | solution.py:316
  27.4 0.5 %collective-permute-done.8.refs_5_ = bf16[512,128]{1,0:T(8,128)(2,1)S(1)} collective-permute-done((bf16[512,128]{1,0:T(8,128)(2,1)S(1)}, bf16[512,128]{1,0:T(8,128)(2,1)S(1)}, u32[]{:S(2)}, u32[]{:S(2)}) %collective-permute-start.8) | collective-permute-done | bytes 131104 | tf_op jit(solution)/shard_map/ppermute | solution.py:316
  27.9 1.9 %collective-permute-done.9.refs_6_ = bf16[512,128]{1,0:T(8,128)(2,1)S(1)} collective-permute-done((bf16[512,128]{1,0:T(8,128)(2,1)S(1)}, bf16[512,128]{1,0:T(8,128)(2,1)S(1)}, u32[]{:S(2)}, u32[]{:S(2)}) %collective-permute-start.9) | collective-permute-done | bytes 131104 | tf_op jit(solution)/shard_map/ppermute | solution.py:316
  29.8 1.4 %near_sum.1 = (f32[32,128,128]{2,1,0:T(8,128)S(1)}, bf16[128,128]{1,0:T(8,128)(2,1)S(1)}) custom-call(bf16[4,4]{1,0:T(4,128)(2,1)} %metric_in.1, bf16[528,128]{1,0:T(8,128)(2,1)S(1)} %get-tuple-element.41.refs_0_, bf16[528,128]{1,0:T(8,128)(2,1)S(1)} %collective-permute-done.3.refs_1_, bf16[528,128]{1,0:T(8,128)(2,1)S(1)} %collective-permute-done.4.refs_2_, ...), custom_call_target="tpu_custom_call" | custom-call | flops 3000000000 | bytes 1048576 | tf_op jit(solution)/shard_map/near_sum/pallas_call | solution.py:416
  31.2 2.6 %collective-permute-done.12.refs_3_ = bf16[528,128]{1,0:T(8,128)(2,1)S(1)} collective-permute-done((bf16[528,128]{1,0:T(8,128)(2,1)S(1)}, bf16[528,128]{1,0:T(8,128)(2,1)S(1)}, u32[]{:S(2)}, u32[]{:S(2)}) %collective-permute-start.12) | collective-permute-done | bytes 135200 | tf_op jit(solution)/shard_map/ppermute | solution.py:316
  33.8 1.5 %collect.1 = (bf16[32,4,4096]{2,1,0:T(4,128)(2,1)}, f32[32,128,128]{2,1,0:T(8,128)S(1)}) custom-call(bf16[128,128]{1,0:T(8,128)(2,1)S(1)} %get-tuple-element.49.mix, f32[32,128,128]{2,1,0:T(8,128)S(1)} %get-tuple-element.50.total_in, bf16[528,128]{1,0:T(8,128)(2,1)S(1)} %get-tuple-element.40.refs_0_, ...), custom_call_target="tpu_custom_call", output_to_operand_aliasing={{1}: (1, {})} | custom-call | tf_op jit(solution)/shard_map/collect/pallas_call | solution.py:431
  (10 shorter events, 0.1 us)
Async XLA Ops:
  0.0 11.1 %collective-permute-start = (bf16[4,128,128]{2,1,0:T(8,128)(2,1)}, bf16[4,128,128]{2,1,0:T(8,128)(2,1)S(1)}, u32[]{:S(2)}, u32[]{:S(2)}) collective-permute-start(bf16[4,128,128]{2,1,0:T(8,128)(2,1)} %bitcast.2), channel_id=1, source_target_pairs={{0,16},{4,20},{8,24},{12,28},{16,0},{20,4},{24,8},{28,12},{1,17},{... | collective-permute-start | bytes 393224 | tf_op jit(solution)/shard_map/ppermute | solution.py:316
  6.3 10.9 %collective-permute-start.3 = (bf16[528,128]{1,0:T(8,128)(2,1)S(1)}, bf16[528,128]{1,0:T(8,128)(2,1)S(1)}, u32[]{:S(2)}, u32[]{:S(2)}) collective-permute-start(bf16[528,128]{1,0:T(8,128)(2,1)S(1)} %get-tuple-element.33), channel_id=1, source_target_pairs={{0,4},{4,0},{8,12},{12,8},{16,20},{20,16},{24,28},{28,24},{1,5},{5... | collective-permute-start | bytes 405512 | tf_op jit(solution)/shard_map/ppermute | solution.py:316
  7.8 9.4 %collective-permute-start.4 = (bf16[528,128]{1,0:T(8,128)(2,1)S(1)}, bf16[528,128]{1,0:T(8,128)(2,1)S(1)}, u32[]{:S(2)}, u32[]{:S(2)}) collective-permute-start(bf16[528,128]{1,0:T(8,128)(2,1)S(1)} %get-tuple-element.34), channel_id=1, source_target_pairs={{0,8},{4,12},{8,0},{12,4},{16,24},{20,28},{24,16},{28,20},{1,9},{5... | collective-permute-start | bytes 405512 | tf_op jit(solution)/shard_map/ppermute | solution.py:316
  11.1 6.1 %collective-permute-start.2 = (bf16[4,128,128]{2,1,0:T(8,128)(2,1)S(1)}, bf16[4,128,128]{2,1,0:T(8,128)(2,1)S(1)}, u32[]{:S(2)}, u32[]{:S(2)}) collective-permute-start(bf16[4,128,128]{2,1,0:T(8,128)(2,1)S(1)} %collective-permute-done.first), channel_id=1, source_target_pairs={{0,2},{1,3},{2,0},{3,1},{4,6},{5,7},{6,4},{7,5},{8,10},{9,11},{10,... | collective-permute-start | bytes 393224 | tf_op jit(solution)/shard_map/ppermute | solution.py:316
  12.7 10.6 %collective-permute-start.1 = (bf16[144,512]{1,0:T(8,128)(2,1)S(1)}, bf16[144,512]{1,0:T(8,128)(2,1)S(1)}, u32[]{:S(2)}, u32[]{:S(2)}) collective-permute-start(bf16[144,512]{1,0:T(8,128)(2,1)S(1)} %pick.1), channel_id=1, source_target_pairs={{0,16},{4,20},{8,24},{12,28},{16,0},{20,4},{24,8},{28,12},{1,17},{... | collective-permute-start | bytes 442376 | tf_op jit(solution)/shard_map/ppermute | solution.py:316
  13.1 8.3 %collective-permute-start.6 = (bf16[528,128]{1,0:T(8,128)(2,1)S(1)}, bf16[528,128]{1,0:T(8,128)(2,1)S(1)}, u32[]{:S(2)}, u32[]{:S(2)}) collective-permute-start(bf16[528,128]{1,0:T(8,128)(2,1)S(1)} %get-tuple-element.44), channel_id=1, source_target_pairs={{0,12},{4,8},{8,4},{12,0},{16,28},{20,24},{24,20},{28,16},{1,13},{... | collective-permute-start | bytes 405512 | tf_op jit(solution)/shard_map/ppermute | solution.py:316
  17.6 6.0 %collective-permute-start.5 = (bf16[8,128,128]{2,1,0:T(8,128)(2,1)S(1)}, bf16[8,128,128]{2,1,0:T(8,128)(2,1)S(1)}, u32[]{:S(2)}, u32[]{:S(2)}) collective-permute-start(bf16[8,128,128]{2,1,0:T(8,128)(2,1)S(1)} %far_pair.1.blocks), channel_id=1, source_target_pairs={{0,1},{1,0},{2,3},{3,2},{4,5},{5,4},{6,7},{7,6},{8,9},{9,8},{10,11... | collective-permute-start | bytes 786440 | tf_op jit(solution)/shard_map/ppermute | solution.py:316
  21.4 4.8 %collective-permute-start.7 = (bf16[512,128]{1,0:T(8,128)(2,1)S(1)}, bf16[512,128]{1,0:T(8,128)(2,1)S(1)}, u32[]{:S(2)}, u32[]{:S(2)}) collective-permute-start(bf16[512,128]{1,0:T(8,128)(2,1)S(1)} %get-tuple-element.46), channel_id=1, source_target_pairs={{0,1},{1,0},{2,3},{3,2},{4,5},{5,4},{6,7},{7,6},{8,9},{9,8},{10,11... | collective-permute-start | bytes 393224 | tf_op jit(solution)/shard_map/ppermute | solution.py:316
  21.5 6.4 %collective-permute-start.8 = (bf16[512,128]{1,0:T(8,128)(2,1)S(1)}, bf16[512,128]{1,0:T(8,128)(2,1)S(1)}, u32[]{:S(2)}, u32[]{:S(2)}) collective-permute-start(bf16[512,128]{1,0:T(8,128)(2,1)S(1)} %get-tuple-element.47), channel_id=1, source_target_pairs={{0,2},{1,3},{2,0},{3,1},{4,6},{5,7},{6,4},{7,5},{8,10},{9,11},{10,... | collective-permute-start | bytes 393224 | tf_op jit(solution)/shard_map/ppermute | solution.py:316
  22.1 7.7 %collective-permute-start.9 = (bf16[512,128]{1,0:T(8,128)(2,1)S(1)}, bf16[512,128]{1,0:T(8,128)(2,1)S(1)}, u32[]{:S(2)}, u32[]{:S(2)}) collective-permute-start(bf16[512,128]{1,0:T(8,128)(2,1)S(1)} %get-tuple-element.48), channel_id=1, source_target_pairs={{0,3},{1,2},{2,1},{3,0},{4,7},{5,6},{6,5},{7,4},{8,11},{9,10},{10,... | collective-permute-start | bytes 393224 | tf_op jit(solution)/shard_map/ppermute | solution.py:316
  23.8 7.4 %collective-permute-start.10 = (bf16[528,128]{1,0:T(8,128)(2,1)S(1)}, bf16[528,128]{1,0:T(8,128)(2,1)S(1)}, u32[]{:S(2)}, u32[]{:S(2)}) collective-permute-start(bf16[528,128]{1,0:T(8,128)(2,1)S(1)} %get-tuple-element.51), channel_id=1, source_target_pairs={{0,4},{4,0},{8,12},{12,8},{16,20},{20,16},{24,28},{28,24},{1,5},{5... | collective-permute-start | bytes 405512 | tf_op jit(solution)/shard_map/ppermute | solution.py:316
  24.2 7.0 %collective-permute-start.11 = (bf16[528,128]{1,0:T(8,128)(2,1)S(1)}, bf16[528,128]{1,0:T(8,128)(2,1)S(1)}, u32[]{:S(2)}, u32[]{:S(2)}) collective-permute-start(bf16[528,128]{1,0:T(8,128)(2,1)S(1)} %get-tuple-element.52), channel_id=1, source_target_pairs={{0,8},{4,12},{8,0},{12,4},{16,24},{20,28},{24,16},{28,20},{1,9},{5... | collective-permute-start | bytes 405512 | tf_op jit(solution)/shard_map/ppermute | solution.py:316
  26.2 7.6 %collective-permute-start.12 = (bf16[528,128]{1,0:T(8,128)(2,1)S(1)}, bf16[528,128]{1,0:T(8,128)(2,1)S(1)}, u32[]{:S(2)}, u32[]{:S(2)}) collective-permute-start(bf16[528,128]{1,0:T(8,128)(2,1)S(1)} %get-tuple-element.53), channel_id=1, source_target_pairs={{0,12},{4,8},{8,4},{12,0},{16,28},{20,24},{24,20},{28,16},{1,13},{... | collective-permute-start | bytes 405512 | tf_op jit(solution)/shard_map/ppermute | solution.py:316

commit v15 on v14

--- a/solution.py
+++ b/solution.py
@@ -388,7 +388,7 @@
     )(*in_hbm(*operands))
     far_block = after(far_block, sent_coef)
     far_coef = flip(after(sent_coef, far_block), "shell", group)
-    far_pair = merged("far_pair", far_block, after(flip(far_block, "aux", 2), *near[:3]))
+    far_pair = merged("far_pair", far_block, after(flip(far_block, "aux", 2), near[2],near[3]))
     far_pairs = [far_pair, flip(far_pair, "aux", 1)]
     regrouped = pl.pallas_call(
         functools.partial(regroup_kernel, group),

time: 35.5 us -> 33.7 us (0.949)
  starting transfers between devices: 18.8 us -> 15.3 us
  waiting for transfers between devices: 8.72 us -> 10.4 us
    ppermute x13, starting transfers between devices: 18.8 us -> 15.3 us  [flip(): return lax.ppermute(value, axis, [(at, at ^ bits) for at in range(count)])]
    ppermute x13, waiting for transfers between devices: 8.72 us -> 10.4 us  [flip(): return lax.ppermute(value, axis, [(at, at ^ bits) for at in range(count)])]
  transfers between devices with their start and end apart: 13 -> 13, of which waited for: 4 -> 6; matrix products, arithmetic and copies ran while one was open for 0% -> 0% of each run, Pallas kernels for 18% -> 18%
where the time goes in v15:
time: 33.7 us; the launch traced here: 33.5 us
  starting transfers between devices  15.3 us (45%)
  waiting for transfers between devices  10.4 us (31%)
  Pallas kernels  7.7 us (23%)
    ppermute x13, starting transfers between devices, flip(): return lax.ppermute(value, axis, [(at, at ^ bits) for at in range(count)])  15.3 us
    ppermute x13, waiting for transfers between devices, flip(): return lax.ppermute(value, axis, [(at, at ^ bits) for at in range(count)])  10.4 us
    pallas_call x1, Pallas kernels, exchanged_inputs(): pl.pallas_call(functools.partial(near_kernel, occ_local, aux_count), out_...  2.23 us
    pallas_call x1, Pallas kernels, exchanged_inputs(): pl.pallas_call(functools.partial(pick_kernel, [list(range(group, shell_co...  1.72 us
    pallas_call x1, Pallas kernels, exchanged_inputs(): pl.pallas_call(collect_kernel, out_shape=[jax.ShapeDtypeStruct((occ_local...  1.53 us
    pallas_call x1, Pallas kernels, exchanged_inputs(): pl.pallas_call(functools.partial(near_sum_kernel, group), out_shape=[tota...  1.42 us
  transfers between devices with their start and end apart: 13, of which 6 were waited for; matrix products, arithmetic and copies ran while one was open for 0% of the time, Pallas kernels for 18%

profile of v15, /device:TPU:0, one launch (start us, length us, event | category | flops | bytes accessed | tf_op | source)
XLA Modules:
  0.0 33.5 jit_solution(3541233058487051031)
XLA Ops:
  0.0 4.0 %collective-permute-start = (bf16[4,128,128]{2,1,0:T(8,128)(2,1)}, bf16[4,128,128]{2,1,0:T(8,128)(2,1)S(1)}, u32[]{:S(2)}, u32[]{:S(2)}) collective-permute-start(bf16[4,128,128]{2,1,0:T(8,128)(2,1)} %bitcast.2), channel_id=1, source_target_pairs={{0,16},{4,20},{8,24},{12,28},{16,0},{20,4},{24,8},{28,12},{1,17},{... | collective-permute-start | bytes 393224 | tf_op jit(solution)/shard_map/ppermute | solution.py:316
  4.0 2.2 %near_blocks.1 = (bf16[528,128]{1,0:T(8,128)(2,1)S(1)}, bf16[528,128]{1,0:T(8,128)(2,1)S(1)}, bf16[528,128]{1,0:T(8,128)(2,1)S(1)}, bf16[528,128]{1,0:T(8,128)(2,1)S(1)}) custom-call(s32[4,3]{1,0:T(4,128)} %pairs_in.3, s32[1,128]{1,0:T(1,128)} %bitcast.4, bf16[512,1024]{1,0:T(8,128)(2,1)} %coef_in.3, bf16[4,128,128]{2,1,0:T(8,128)(2,1)} %bitcast.3), custom_call_target="tpu_custom_call" | custom-call | tf_op jit(solution)/shard_map/near_blocks/pallas_call | solution.py:365
  6.3 1.6 %collective-permute-start.3 = (bf16[528,128]{1,0:T(8,128)(2,1)S(1)}, bf16[528,128]{1,0:T(8,128)(2,1)S(1)}, u32[]{:S(2)}, u32[]{:S(2)}) collective-permute-start(bf16[528,128]{1,0:T(8,128)(2,1)S(1)} %get-tuple-element.33), channel_id=1, source_target_pairs={{0,8},{4,12},{8,0},{12,4},{16,24},{20,28},{24,16},{28,20},{1,9},{5... | collective-permute-start | bytes 405512 | tf_op jit(solution)/shard_map/ppermute | solution.py:316
  7.9 1.4 %collective-permute-start.4 = (bf16[528,128]{1,0:T(8,128)(2,1)S(1)}, bf16[528,128]{1,0:T(8,128)(2,1)S(1)}, u32[]{:S(2)}, u32[]{:S(2)}) collective-permute-start(bf16[528,128]{1,0:T(8,128)(2,1)S(1)} %get-tuple-element.34), channel_id=1, source_target_pairs={{0,12},{4,8},{8,4},{12,0},{16,28},{20,24},{24,20},{28,16},{1,13},{... | collective-permute-start | bytes 405512 | tf_op jit(solution)/shard_map/ppermute | solution.py:316
  9.3 1.7 %pick.1 = bf16[144,512]{1,0:T(8,128)(2,1)S(1)} custom-call(s32[4,3]{1,0:T(4,128)} %pairs_in.3, s32[1,128]{1,0:T(1,128)} %bitcast.5, bf16[512,1024]{1,0:T(8,128)(2,1)} %coef_in.3), custom_call_target="tpu_custom_call" | custom-call | tf_op jit(solution)/shard_map/pick/pallas_call | solution.py:376
  11.0 1.6 %collective-permute-start.2 = (bf16[4,128,128]{2,1,0:T(8,128)(2,1)S(1)}, bf16[4,128,128]{2,1,0:T(8,128)(2,1)S(1)}, u32[]{:S(2)}, u32[]{:S(2)}) collective-permute-start(bf16[4,128,128]{2,1,0:T(8,128)(2,1)S(1)} %collective-permute-done.first), channel_id=1, source_target_pairs={{0,2},{1,3},{2,0},{3,1},{4,6},{5,7},{6,4},{7,5},{8,10},{9,11},{10,... | collective-permute-start | bytes 393224 | tf_op jit(solution)/shard_map/ppermute | solution.py:316
  12.6 0.3 collective-permute-start.1
  12.9 0.8 %collective-permute-start.6 = (bf16[528,128]{1,0:T(8,128)(2,1)S(1)}, bf16[528,128]{1,0:T(8,128)(2,1)S(1)}, u32[]{:S(2)}, u32[]{:S(2)}) collective-permute-start(bf16[528,128]{1,0:T(8,128)(2,1)S(1)} %get-tuple-element.42), channel_id=1, source_target_pairs={{0,4},{4,0},{8,12},{12,8},{16,20},{20,16},{24,28},{28,24},{1,5},{5... | collective-permute-start | bytes 405512 | tf_op jit(solution)/shard_map/ppermute | solution.py:316
  13.7 4.9 %collective-permute-done.4.refs_3_ = bf16[528,128]{1,0:T(8,128)(2,1)S(1)} collective-permute-done((bf16[528,128]{1,0:T(8,128)(2,1)S(1)}, bf16[528,128]{1,0:T(8,128)(2,1)S(1)}, u32[]{:S(2)}, u32[]{:S(2)}) %collective-permute-start.4) | collective-permute-done | bytes 135200 | tf_op jit(solution)/shard_map/ppermute | solution.py:316
  18.6 0.3 %far_pair.1.blocks = bf16[8,128,128]{2,1,0:T(8,128)(2,1)S(1)} custom-call(bf16[4,128,128]{2,1,0:T(8,128)(2,1)S(1)} %collective-permute-done.first, bf16[4,128,128]{2,1,0:T(8,128)(2,1)S(1)} %collective-permute-done.2.second), custom_call_target="tpu_custom_call" | custom-call | tf_op jit(solution)/shard_map/far_pair/pallas_call | solution.py:345
  19.0 0.5 %collective-permute-done.6.refs_1_ = bf16[528,128]{1,0:T(8,128)(2,1)S(1)} collective-permute-done((bf16[528,128]{1,0:T(8,128)(2,1)S(1)}, bf16[528,128]{1,0:T(8,128)(2,1)S(1)}, u32[]{:S(2)}, u32[]{:S(2)}) %collective-permute-start.6) | collective-permute-done | bytes 135200 | tf_op jit(solution)/shard_map/ppermute | solution.py:316
  19.6 1.5 %collective-permute-start.8 = (bf16[512,128]{1,0:T(8,128)(2,1)S(1)}, bf16[512,128]{1,0:T(8,128)(2,1)S(1)}, u32[]{:S(2)}, u32[]{:S(2)}) collective-permute-start(bf16[512,128]{1,0:T(8,128)(2,1)S(1)} %get-tuple-element.47), channel_id=1, source_target_pairs={{0,2},{1,3},{2,0},{3,1},{4,6},{5,7},{6,4},{7,5},{8,10},{9,11},{10,... | collective-permute-start | bytes 393224 | tf_op jit(solution)/shard_map/ppermute | solution.py:316
  21.1 0.3 collective-permute-start.9
  21.4 0.2 far_blocks_0.1
  21.7 0.2 far_blocks_1.1
  21.9 1.1 %collective-permute-start.10 = (bf16[528,128]{1,0:T(8,128)(2,1)S(1)}, bf16[528,128]{1,0:T(8,128)(2,1)S(1)}, u32[]{:S(2)}, u32[]{:S(2)}) collective-permute-start(bf16[528,128]{1,0:T(8,128)(2,1)S(1)} %get-tuple-element.51), channel_id=1, source_target_pairs={{0,4},{4,0},{8,12},{12,8},{16,20},{20,16},{24,28},{28,24},{1,5},{5... | collective-permute-start | bytes 405512 | tf_op jit(solution)/shard_map/ppermute | solution.py:316
  23.0 2.3 %collective-permute-start.11 = (bf16[528,128]{1,0:T(8,128)(2,1)S(1)}, bf16[528,128]{1,0:T(8,128)(2,1)S(1)}, u32[]{:S(2)}, u32[]{:S(2)}) collective-permute-start(bf16[528,128]{1,0:T(8,128)(2,1)S(1)} %get-tuple-element.52), channel_id=1, source_target_pairs={{0,8},{4,12},{8,0},{12,4},{16,24},{20,28},{24,16},{28,20},{1,9},{5... | collective-permute-start | bytes 405512 | tf_op jit(solution)/shard_map/ppermute | solution.py:316
  25.3 0.2 collective-permute-start.12
  25.5 0.5 %collective-permute-done.8.refs_5_ = bf16[512,128]{1,0:T(8,128)(2,1)S(1)} collective-permute-done((bf16[512,128]{1,0:T(8,128)(2,1)S(1)}, bf16[512,128]{1,0:T(8,128)(2,1)S(1)}, u32[]{:S(2)}, u32[]{:S(2)}) %collective-permute-start.8) | collective-permute-done | bytes 131104 | tf_op jit(solution)/shard_map/ppermute | solution.py:316
  25.9 1.9 %collective-permute-done.9.refs_6_ = bf16[512,128]{1,0:T(8,128)(2,1)S(1)} collective-permute-done((bf16[512,128]{1,0:T(8,128)(2,1)S(1)}, bf16[512,128]{1,0:T(8,128)(2,1)S(1)}, u32[]{:S(2)}, u32[]{:S(2)}) %collective-permute-start.9) | collective-permute-done | bytes 131104 | tf_op jit(solution)/shard_map/ppermute | solution.py:316
  27.8 1.4 %near_sum.1 = (f32[32,128,128]{2,1,0:T(8,128)S(1)}, bf16[128,128]{1,0:T(8,128)(2,1)S(1)}) custom-call(bf16[4,4]{1,0:T(4,128)(2,1)} %metric_in.1, bf16[528,128]{1,0:T(8,128)(2,1)S(1)} %get-tuple-element.41.refs_0_, bf16[528,128]{1,0:T(8,128)(2,1)S(1)} %collective-permute-done.6.refs_1_, bf16[528,128]{1,0:T(8,128)(2,1)S(1)} %collective-permute-done.3.refs_2_, ...), custom_call_target="tpu_custom_call" | custom-call | flops 3000000000 | bytes 1048576 | tf_op jit(solution)/shard_map/near_sum/pallas_call | solution.py:416
  29.3 0.4 %collective-permute-done.11.refs_2_ = bf16[528,128]{1,0:T(8,128)(2,1)S(1)} collective-permute-done((bf16[528,128]{1,0:T(8,128)(2,1)S(1)}, bf16[528,128]{1,0:T(8,128)(2,1)S(1)}, u32[]{:S(2)}, u32[]{:S(2)}) %collective-permute-start.11) | collective-permute-done | bytes 135200 | tf_op jit(solution)/shard_map/ppermute | solution.py:316
  29.7 2.3 %collective-permute-done.12.refs_3_ = bf16[528,128]{1,0:T(8,128)(2,1)S(1)} collective-permute-done((bf16[528,128]{1,0:T(8,128)(2,1)S(1)}, bf16[528,128]{1,0:T(8,128)(2,1)S(1)}, u32[]{:S(2)}, u32[]{:S(2)}) %collective-permute-start.12) | collective-permute-done | bytes 135200 | tf_op jit(solution)/shard_map/ppermute | solution.py:316
  32.0 1.5 %collect.1 = (bf16[32,4,4096]{2,1,0:T(4,128)(2,1)}, f32[32,128,128]{2,1,0:T(8,128)S(1)}) custom-call(bf16[128,128]{1,0:T(8,128)(2,1)S(1)} %get-tuple-element.49.mix, f32[32,128,128]{2,1,0:T(8,128)S(1)} %get-tuple-element.50.total_in, bf16[528,128]{1,0:T(8,128)(2,1)S(1)} %get-tuple-element.40.refs_0_, ...), custom_call_target="tpu_custom_call", output_to_operand_aliasing={{1}: (1, {})} | custom-call | tf_op jit(solution)/shard_map/collect/pallas_call | solution.py:431
  (10 shorter events, 0.2 us)
Async XLA Ops:
  0.0 11.0 %collective-permute-start = (bf16[4,128,128]{2,1,0:T(8,128)(2,1)}, bf16[4,128,128]{2,1,0:T(8,128)(2,1)S(1)}, u32[]{:S(2)}, u32[]{:S(2)}) collective-permute-start(bf16[4,128,128]{2,1,0:T(8,128)(2,1)} %bitcast.2), channel_id=1, source_target_pairs={{0,16},{4,20},{8,24},{12,28},{16,0},{20,4},{24,8},{28,12},{1,17},{... | collective-permute-start | bytes 393224 | tf_op jit(solution)/shard_map/ppermute | solution.py:316
  6.3 7.5 %collective-permute-start.3 = (bf16[528,128]{1,0:T(8,128)(2,1)S(1)}, bf16[528,128]{1,0:T(8,128)(2,1)S(1)}, u32[]{:S(2)}, u32[]{:S(2)}) collective-permute-start(bf16[528,128]{1,0:T(8,128)(2,1)S(1)} %get-tuple-element.33), channel_id=1, source_target_pairs={{0,8},{4,12},{8,0},{12,4},{16,24},{20,28},{24,16},{28,20},{1,9},{5... | collective-permute-start | bytes 405512 | tf_op jit(solution)/shard_map/ppermute | solution.py:316
  7.9 10.7 %collective-permute-start.4 = (bf16[528,128]{1,0:T(8,128)(2,1)S(1)}, bf16[528,128]{1,0:T(8,128)(2,1)S(1)}, u32[]{:S(2)}, u32[]{:S(2)}) collective-permute-start(bf16[528,128]{1,0:T(8,128)(2,1)S(1)} %get-tuple-element.34), channel_id=1, source_target_pairs={{0,12},{4,8},{8,4},{12,0},{16,28},{20,24},{24,20},{28,16},{1,13},{... | collective-permute-start | bytes 405512 | tf_op jit(solution)/shard_map/ppermute | solution.py:316
  11.0 7.6 %collective-permute-start.2 = (bf16[4,128,128]{2,1,0:T(8,128)(2,1)S(1)}, bf16[4,128,128]{2,1,0:T(8,128)(2,1)S(1)}, u32[]{:S(2)}, u32[]{:S(2)}) collective-permute-start(bf16[4,128,128]{2,1,0:T(8,128)(2,1)S(1)} %collective-permute-done.first), channel_id=1, source_target_pairs={{0,2},{1,3},{2,0},{3,1},{4,6},{5,7},{6,4},{7,5},{8,10},{9,11},{10,... | collective-permute-start | bytes 393224 | tf_op jit(solution)/shard_map/ppermute | solution.py:316
  12.6 8.8 %collective-permute-start.1 = (bf16[144,512]{1,0:T(8,128)(2,1)S(1)}, bf16[144,512]{1,0:T(8,128)(2,1)S(1)}, u32[]{:S(2)}, u32[]{:S(2)}) collective-permute-start(bf16[144,512]{1,0:T(8,128)(2,1)S(1)} %pick.1), channel_id=1, source_target_pairs={{0,16},{4,20},{8,24},{12,28},{16,0},{20,4},{24,8},{28,12},{1,17},{... | collective-permute-start | bytes 442376 | tf_op jit(solution)/shard_map/ppermute | solution.py:316
  12.9 6.5 %collective-permute-start.6 = (bf16[528,128]{1,0:T(8,128)(2,1)S(1)}, bf16[528,128]{1,0:T(8,128)(2,1)S(1)}, u32[]{:S(2)}, u32[]{:S(2)}) collective-permute-start(bf16[528,128]{1,0:T(8,128)(2,1)S(1)} %get-tuple-element.42), channel_id=1, source_target_pairs={{0,4},{4,0},{8,12},{12,8},{16,20},{20,16},{24,28},{28,24},{1,5},{5... | collective-permute-start | bytes 405512 | tf_op jit(solution)/shard_map/ppermute | solution.py:316
  18.9 2.7 %collective-permute-start.5 = (bf16[8,128,128]{2,1,0:T(8,128)(2,1)S(1)}, bf16[8,128,128]{2,1,0:T(8,128)(2,1)S(1)}, u32[]{:S(2)}, u32[]{:S(2)}) collective-permute-start(bf16[8,128,128]{2,1,0:T(8,128)(2,1)S(1)} %far_pair.1.blocks), channel_id=1, source_target_pairs={{0,1},{1,0},{2,3},{3,2},{4,5},{5,4},{6,7},{7,6},{8,9},{9,8},{10,11... | collective-permute-start | bytes 786440 | tf_op jit(solution)/shard_map/ppermute | solution.py:316
  19.5 5.8 %collective-permute-start.7 = (bf16[512,128]{1,0:T(8,128)(2,1)S(1)}, bf16[512,128]{1,0:T(8,128)(2,1)S(1)}, u32[]{:S(2)}, u32[]{:S(2)}) collective-permute-start(bf16[512,128]{1,0:T(8,128)(2,1)S(1)} %get-tuple-element.46), channel_id=1, source_target_pairs={{0,1},{1,0},{2,3},{3,2},{4,5},{5,4},{6,7},{7,6},{8,9},{9,8},{10,11... | collective-permute-start | bytes 393224 | tf_op jit(solution)/shard_map/ppermute | solution.py:316
  19.6 6.3 %collective-permute-start.8 = (bf16[512,128]{1,0:T(8,128)(2,1)S(1)}, bf16[512,128]{1,0:T(8,128)(2,1)S(1)}, u32[]{:S(2)}, u32[]{:S(2)}) collective-permute-start(bf16[512,128]{1,0:T(8,128)(2,1)S(1)} %get-tuple-element.47), channel_id=1, source_target_pairs={{0,2},{1,3},{2,0},{3,1},{4,6},{5,7},{6,4},{7,5},{8,10},{9,11},{10,... | collective-permute-start | bytes 393224 | tf_op jit(solution)/shard_map/ppermute | solution.py:316
  21.1 6.7 %collective-permute-start.9 = (bf16[512,128]{1,0:T(8,128)(2,1)S(1)}, bf16[512,128]{1,0:T(8,128)(2,1)S(1)}, u32[]{:S(2)}, u32[]{:S(2)}) collective-permute-start(bf16[512,128]{1,0:T(8,128)(2,1)S(1)} %get-tuple-element.48), channel_id=1, source_target_pairs={{0,3},{1,2},{2,1},{3,0},{4,7},{5,6},{6,5},{7,4},{8,11},{9,10},{10,... | collective-permute-start | bytes 393224 | tf_op jit(solution)/shard_map/ppermute | solution.py:316
  21.9 7.4 %collective-permute-start.10 = (bf16[528,128]{1,0:T(8,128)(2,1)S(1)}, bf16[528,128]{1,0:T(8,128)(2,1)S(1)}, u32[]{:S(2)}, u32[]{:S(2)}) collective-permute-start(bf16[528,128]{1,0:T(8,128)(2,1)S(1)} %get-tuple-element.51), channel_id=1, source_target_pairs={{0,4},{4,0},{8,12},{12,8},{16,20},{20,16},{24,28},{28,24},{1,5},{5... | collective-permute-start | bytes 405512 | tf_op jit(solution)/shard_map/ppermute | solution.py:316
  23.0 6.7 %collective-permute-start.11 = (bf16[528,128]{1,0:T(8,128)(2,1)S(1)}, bf16[528,128]{1,0:T(8,128)(2,1)S(1)}, u32[]{:S(2)}, u32[]{:S(2)}) collective-permute-start(bf16[528,128]{1,0:T(8,128)(2,1)S(1)} %get-tuple-element.52), channel_id=1, source_target_pairs={{0,8},{4,12},{8,0},{12,4},{16,24},{20,28},{24,16},{28,20},{1,9},{5... | collective-permute-start | bytes 405512 | tf_op jit(solution)/shard_map/ppermute | solution.py:316
  25.3 6.7 %collective-permute-start.12 = (bf16[528,128]{1,0:T(8,128)(2,1)S(1)}, bf16[528,128]{1,0:T(8,128)(2,1)S(1)}, u32[]{:S(2)}, u32[]{:S(2)}) collective-permute-start(bf16[528,128]{1,0:T(8,128)(2,1)S(1)} %get-tuple-element.53), channel_id=1, source_target_pairs={{0,12},{4,8},{8,4},{12,0},{16,28},{20,24},{24,20},{28,16},{1,13},{... | collective-permute-start | bytes 405512 | tf_op jit(solution)/shard_map/ppermute | solution.py:316

commit v16 on v15

--- a/solution.py
+++ b/solution.py
@@ -144,6 +144,7 @@
     slot_in,
     coef_in,
     blocks_in,
+    beside,
     *refs,
 ):
     *outs, pairs, slot_row, coef, blocks, sems = refs
@@ -160,10 +161,10 @@
         load.start()
     me = lax.axis_index("shell")
     mine = lax.axis_index("aux")
-    owned = aux_count * occ_local
+    owned = aux_count // 2 * occ_local
     row = lax.broadcasted_iota(jnp.int32, (len(outs) * owned, 1), 0)
     owner = jnp.bitwise_xor(row // owned, me) * aux_count + jnp.bitwise_xor(
-        row // occ_local % aux_count, mine
+        row // occ_local % (aux_count // 2) * 2, mine
     )
     wanted = owner * occ_local + row % occ_local
     loads[0].wait()
@@ -184,24 +185,28 @@
     ).astype(jnp.bfloat16)
     for k in range(pairs_dev):
         block = jnp.dot(
-            ordered[:, k * BS : (k + 1) * BS], blocks[k], preferred_element_type=jnp.float32
+            ordered[:, k * BS : (k + 1) * BS],
+            jnp.concatenate([blocks[k], beside[k]], axis=1),
+            preferred_element_type=jnp.float32,
         )
         block = (block * (pairs[k, 2] == 1).astype(jnp.float32)).astype(jnp.bfloat16)
         for f, out in enumerate(outs):
-            for j in range(aux_count):
+            for j in range(aux_count // 2):
                 first = f * owned + j * occ_local
-                at = (j * pairs_dev + k) * occ_local
-                out[at : at + occ_local, :] = block[first : first + occ_local, :]
+                for c in range(2):
+                    at = ((j * 2 + c) * pairs_dev + k) * occ_local
+                    out[at : at + occ_local, :] = block[
+                        first : first + occ_local, c * BS : (c + 1) * BS
+                    ]
     for out in outs:
-        out[pairs_dev * owned :, :] = code
-
-
-def regroup_kernel(count, *refs):
-    received, outs = refs[:count], refs[count:]
-    rows = outs[0].shape[0] // count
-    for j, out in enumerate(outs, 1):
-        for f, piece in enumerate(received):
-            out[f * rows : (f + 1) * rows, :] = piece[j * rows : (j + 1) * rows, :]
+        out[out.shape[0] - 16 :, :] = code
+
+
+def regroup_kernel(*refs):
+    *received, out = refs
+    rows = out.shape[0] // len(received)
+    for f, piece in enumerate(received):
+        out[f * rows : (f + 1) * rows, :] = piece[rows : 2 * rows, :]
 
 
 def merge_kernel(first, second, out, sems):
@@ -247,9 +252,8 @@
         codes[at : at + 1, :] = (digits + 128.0 * high).astype(jnp.int32)
 
 
-def near_sum_kernel(count, metric_in, *refs):
-    *received, total, mix, metric, codes, sem = refs
-    received, others = received[:count], received[count:]
+def near_sum_kernel(metric_in, *refs):
+    *received, across, total, mix, metric, codes, sem = refs
     load = pltpu.make_async_copy(metric_in, metric, sem)
     load.start()
     total[...] = jnp.zeros_like(total)
@@ -258,13 +262,14 @@
     occ_local = rows // metric.shape[0]
     pairs_dev = (received[0].shape[0] - 16) // rows
     read_codes(received, pairs_dev, codes)
-    for f in range(count):
+    for f, piece in enumerate(received):
         for k in range(pairs_dev):
             r = codes[f, k]
-            for j in range(len(others) + 1):
-                source, first = (others[j - 1], f * pairs_dev + k) if j else (received[f], k)
+            for j in range(metric.shape[0]):
+                source, first = (across, f * 2 + j - 2) if j >= 2 else (piece, j)
+                first = (first * pairs_dev + k) * occ_local
                 start = pl.multiple_of(jnp.bitwise_xor(mine, j) * occ_local, occ_local)
-                part = source[first * occ_local : (first + 1) * occ_local, :]
+                part = source[first : first + occ_local, :]
                 total[r, pl.ds(start, occ_local), :] += part.astype(jnp.float32)
     load.wait()
     aux_count = metric.shape[0]
@@ -365,13 +370,13 @@
     near = pl.pallas_call(
         functools.partial(near_kernel, occ_local, aux_count),
         out_shape=[piece] * group,
-        in_specs=[hbm] * 4,
+        in_specs=[hbm] * 4 + [vmem],
         out_specs=[vmem] * group,
         scratch_shapes=loaded
         + [pltpu.VMEM(blocks.shape, jnp.bfloat16), pltpu.SemaphoreType.DMA((4,))],
         compiler_params=params,
         name="near_blocks",
-    )(*in_hbm(*operands, blocks))
+    )(*in_hbm(*operands, blocks), flip(blocks, "aux", 1))
     near = [near[0]] + [flip(near[f], "shell", f) for f in range(1, group)]
     (sent_coef,) = pl.pallas_call(
         functools.partial(
@@ -388,18 +393,22 @@
     )(*in_hbm(*operands))
     far_block = after(far_block, sent_coef)
     far_coef = flip(after(sent_coef, far_block), "shell", group)
-    far_pair = merged("far_pair", far_block, after(flip(far_block, "aux", 2), near[2],near[3]))
+    far_pair = merged("far_pair", far_block, flip(far_block, "aux", 2))
     far_pairs = [far_pair, flip(far_pair, "aux", 1)]
-    regrouped = pl.pallas_call(
-        functools.partial(regroup_kernel, group),
-        out_shape=[jax.ShapeDtypeStruct((group * pairs_dev * occ_local, BS), jnp.bfloat16)]
-        * (aux_count - 1),
-        in_specs=[vmem] * group,
-        out_specs=[vmem] * (aux_count - 1),
-        compiler_params=params,
-        name="regroup",
-    )(*near)
-    others = [flip(one, "aux", j) for j, one in enumerate(regrouped, 1)]
+    across = flip(
+        pl.pallas_call(
+            regroup_kernel,
+            out_shape=jax.ShapeDtypeStruct(
+                (group * 2 * pairs_dev * occ_local, BS), jnp.bfloat16
+            ),
+            in_specs=[vmem] * group,
+            out_specs=vmem,
+            compiler_params=params,
+            name="regroup",
+        )(*near),
+        "aux",
+        2,
+    )
     far = []
     for low in range(2):
         far = pl.pallas_call(
@@ -414,9 +423,9 @@
         )(far_coef, far_pairs[low], *far)
     total_shape = jax.ShapeDtypeStruct((block_count, rows, BS), jnp.float32)
     total, mix = pl.pallas_call(
-        functools.partial(near_sum_kernel, group),
+        near_sum_kernel,
         out_shape=[total_shape, jax.ShapeDtypeStruct((rows, rows), jnp.bfloat16)],
-        in_specs=[hbm] + [vmem] * (group + aux_count - 1),
+        in_specs=[hbm] + [vmem] * (group + 1),
         out_specs=[vmem] * 2,
         scratch_shapes=[
             pltpu.VMEM(metric.shape, jnp.bfloat16),
@@ -426,7 +435,7 @@
         compiler_params=params,
         cost_estimate=cost(3e9),
         name="near_sum",
-    )(*in_hbm(metric), *(after(one, far[0]) for one in near), *others)
+    )(*in_hbm(metric), *(after(one, far[0]) for one in near), across)
     far = [far[0]] + [flip(far[f], "shell", f) for f in range(1, group)]
     return pl.pallas_call(
         collect_kernel,

time: 33.7 us -> 32.9 us (0.976)
  waiting for transfers between devices: 10.4 us -> 9.27 us
  starting transfers between devices: 15.3 us -> 15.9 us
    ppermute x13 -> x12, waiting for transfers between devices: 10.4 us -> 9.27 us  [flip(): return lax.ppermute(value, axis, [(at, at ^ bits) for at in range(count)])]
    ppermute x13 -> x12, starting transfers between devices: 15.3 us -> 15.9 us  [flip(): return lax.ppermute(value, axis, [(at, at ^ bits) for at in range(count)])]
  transfers between devices with their start and end apart: 13 -> 12, of which waited for: 6 -> 7; matrix products, arithmetic and copies ran while one was open for 0% -> 0% of each run, Pallas kernels for 18% -> 18%
where the time goes in v16:
time: 32.9 us; the launch traced here: 32.7 us
  starting transfers between devices  15.9 us (48%)
  waiting for transfers between devices  9.27 us (28%)
  Pallas kernels  7.38 us (22%)
    ppermute x12, starting transfers between devices, flip(): return lax.ppermute(value, axis, [(at, at ^ bits) for at in range(count)])  15.9 us
    ppermute x12, waiting for transfers between devices, flip(): return lax.ppermute(value, axis, [(at, at ^ bits) for at in range(count)])  9.27 us
    pallas_call x1, Pallas kernels, exchanged_inputs(): pl.pallas_call(functools.partial(near_kernel, occ_local, aux_count), out_...  1.98 us
    pallas_call x1, Pallas kernels, exchanged_inputs(): pl.pallas_call(functools.partial(pick_kernel, [list(range(group, shell_co...  1.72 us
    pallas_call x1, Pallas kernels, exchanged_inputs(): pl.pallas_call(collect_kernel, out_shape=[jax.ShapeDtypeStruct((occ_local...  1.53 us
    pallas_call x1, Pallas kernels, exchanged_inputs(): pl.pallas_call(near_sum_kernel, out_shape=[total_shape, jax.ShapeDtypeStr...  1.37 us
  transfers between devices with their start and end apart: 12, of which 7 were waited for; matrix products, arithmetic and copies ran while one was open for 0% of the time, Pallas kernels for 18%

profile of v16, /device:TPU:0, one launch (start us, length us, event | category | flops | bytes accessed | tf_op | source)
XLA Modules:
  0.0 32.7 jit_solution(9421544838528253273)
XLA Ops:
  0.0 0.5 %collective-permute-start = (bf16[4,128,128]{2,1,0:T(8,128)(2,1)}, bf16[4,128,128]{2,1,0:T(8,128)(2,1)S(1)}, u32[]{:S(2)}, u32[]{:S(2)}) collective-permute-start(bf16[4,128,128]{2,1,0:T(8,128)(2,1)} %bitcast.2), channel_id=1, source_target_pairs={{0,1},{1,0},{2,3},{3,2},{4,5},{5,4},{6,7},{7,6},{8,9},{9,8},{10,11... | collective-permute-start | bytes 393224 | tf_op jit(solution)/shard_map/ppermute | solution.py:321
  0.5 3.6 %collective-permute-start.1 = (bf16[4,128,128]{2,1,0:T(8,128)(2,1)}, bf16[4,128,128]{2,1,0:T(8,128)(2,1)S(1)}, u32[]{:S(2)}, u32[]{:S(2)}) collective-permute-start(bf16[4,128,128]{2,1,0:T(8,128)(2,1)} %bitcast.3), channel_id=1, source_target_pairs={{0,16},{4,20},{8,24},{12,28},{16,0},{20,4},{24,8},{28,12},{1,17},{... | collective-permute-start | bytes 393224 | tf_op jit(solution)/shard_map/ppermute | solution.py:321
  4.0 2.0 %near_blocks.1 = (bf16[528,128]{1,0:T(8,128)(2,1)S(1)}, bf16[528,128]{1,0:T(8,128)(2,1)S(1)}, bf16[528,128]{1,0:T(8,128)(2,1)S(1)}, bf16[528,128]{1,0:T(8,128)(2,1)S(1)}) custom-call(s32[4,3]{1,0:T(4,128)} %pairs_in.3, s32[1,128]{1,0:T(1,128)} %bitcast.5, bf16[512,1024]{1,0:T(8,128)(2,1)} %coef_in.3, bf16[4,128,128]{2,1,0:T(8,128)(2,1)} %bitcast.4, ...), custom_call_target="tpu_custom_call" | custom-call | tf_op jit(solution)/shard_map/near_blocks/pallas_call | solution.py:370
  6.0 1.6 %collective-permute-start.5 = (bf16[528,128]{1,0:T(8,128)(2,1)S(1)}, bf16[528,128]{1,0:T(8,128)(2,1)S(1)}, u32[]{:S(2)}, u32[]{:S(2)}) collective-permute-start(bf16[528,128]{1,0:T(8,128)(2,1)S(1)} %get-tuple-element.35), channel_id=1, source_target_pairs={{0,4},{4,0},{8,12},{12,8},{16,20},{20,16},{24,28},{28,24},{1,5},{5... | collective-permute-start | bytes 405512 | tf_op jit(solution)/shard_map/ppermute | solution.py:321
  7.6 1.6 %collective-permute-start.6 = (bf16[528,128]{1,0:T(8,128)(2,1)S(1)}, bf16[528,128]{1,0:T(8,128)(2,1)S(1)}, u32[]{:S(2)}, u32[]{:S(2)}) collective-permute-start(bf16[528,128]{1,0:T(8,128)(2,1)S(1)} %get-tuple-element.37), channel_id=1, source_target_pairs={{0,8},{4,12},{8,0},{12,4},{16,24},{20,28},{24,16},{28,20},{1,9},{5... | collective-permute-start | bytes 405512 | tf_op jit(solution)/shard_map/ppermute | solution.py:321
  9.2 0.4 %collective-permute-start.7 = (bf16[528,128]{1,0:T(8,128)(2,1)S(1)}, bf16[528,128]{1,0:T(8,128)(2,1)S(1)}, u32[]{:S(2)}, u32[]{:S(2)}) collective-permute-start(bf16[528,128]{1,0:T(8,128)(2,1)S(1)} %get-tuple-element.39), channel_id=1, source_target_pairs={{0,12},{4,8},{8,4},{12,0},{16,28},{20,24},{24,20},{28,16},{1,13},{... | collective-permute-start | bytes 405512 | tf_op jit(solution)/shard_map/ppermute | solution.py:321
  9.6 1.7 %pick.1 = bf16[144,512]{1,0:T(8,128)(2,1)S(1)} custom-call(s32[4,3]{1,0:T(4,128)} %pairs_in.3, s32[1,128]{1,0:T(1,128)} %bitcast.6, bf16[512,1024]{1,0:T(8,128)(2,1)} %coef_in.3), custom_call_target="tpu_custom_call" | custom-call | tf_op jit(solution)/shard_map/pick/pallas_call | solution.py:381
  11.3 1.6 %collective-permute-start.3 = (bf16[4,128,128]{2,1,0:T(8,128)(2,1)S(1)}, bf16[4,128,128]{2,1,0:T(8,128)(2,1)S(1)}, u32[]{:S(2)}, u32[]{:S(2)}) collective-permute-start(bf16[4,128,128]{2,1,0:T(8,128)(2,1)S(1)} %collective-permute-done.1.first), channel_id=1, source_target_pairs={{0,2},{1,3},{2,0},{3,1},{4,6},{5,7},{6,4},{7,5},{8,10},{9,11},{10,... | collective-permute-start | bytes 393224 | tf_op jit(solution)/shard_map/ppermute | solution.py:321
  12.9 1.6 %collective-permute-start.2 = (bf16[144,512]{1,0:T(8,128)(2,1)S(1)}, bf16[144,512]{1,0:T(8,128)(2,1)S(1)}, u32[]{:S(2)}, u32[]{:S(2)}) collective-permute-start(bf16[144,512]{1,0:T(8,128)(2,1)S(1)} %pick.1), channel_id=1, source_target_pairs={{0,16},{4,20},{8,24},{12,28},{16,0},{20,4},{24,8},{28,12},{1,17},{... | collective-permute-start | bytes 442376 | tf_op jit(solution)/shard_map/ppermute | solution.py:321
  14.5 2.1 %collective-permute-done.3.second = bf16[4,128,128]{2,1,0:T(8,128)(2,1)S(1)} collective-permute-done((bf16[4,128,128]{2,1,0:T(8,128)(2,1)S(1)}, bf16[4,128,128]{2,1,0:T(8,128)(2,1)S(1)}, u32[]{:S(2)}, u32[]{:S(2)}) %collective-permute-start.3) | collective-permute-done | bytes 131104 | tf_op jit(solution)/shard_map/ppermute | solution.py:321
  16.6 0.3 %far_pair.1.blocks = bf16[8,128,128]{2,1,0:T(8,128)(2,1)S(1)} custom-call(bf16[4,128,128]{2,1,0:T(8,128)(2,1)S(1)} %collective-permute-done.1.first, bf16[4,128,128]{2,1,0:T(8,128)(2,1)S(1)} %collective-permute-done.3.second), custom_call_target="tpu_custom_call" | custom-call | tf_op jit(solution)/shard_map/far_pair/pallas_call | solution.py:350
  17.0 1.8 %collective-permute-done.7.refs_3_ = bf16[528,128]{1,0:T(8,128)(2,1)S(1)} collective-permute-done((bf16[528,128]{1,0:T(8,128)(2,1)S(1)}, bf16[528,128]{1,0:T(8,128)(2,1)S(1)}, u32[]{:S(2)}, u32[]{:S(2)}) %collective-permute-start.7) | collective-permute-done | bytes 135200 | tf_op jit(solution)/shard_map/ppermute | solution.py:321
  18.9 1.6 %collective-permute-start.8 = (bf16[1024,128]{1,0:T(8,128)(2,1)S(1)}, bf16[1024,128]{1,0:T(8,128)(2,1)S(1)}, u32[]{:S(2)}, u32[]{:S(2)}) collective-permute-start(bf16[1024,128]{1,0:T(8,128)(2,1)S(1)} %regroup.1), channel_id=1, source_target_pairs={{0,2},{1,3},{2,0},{3,1},{4,6},{5,7},{6,4},{7,5},{8,10},{9,11},{10,... | collective-permute-start | bytes 786440 | tf_op jit(solution)/shard_map/ppermute | solution.py:321
  20.4 1.7 %collective-permute-done.2.coefs = bf16[144,512]{1,0:T(8,128)(2,1)S(1)} collective-permute-done((bf16[144,512]{1,0:T(8,128)(2,1)S(1)}, bf16[144,512]{1,0:T(8,128)(2,1)S(1)}, u32[]{:S(2)}, u32[]{:S(2)}) %collective-permute-start.2) | collective-permute-done | bytes 147488 | tf_op jit(solution)/shard_map/ppermute | solution.py:321
  22.1 0.2 far_blocks_0.1
  22.3 0.2 far_blocks_1.1
  22.6 1.6 %collective-permute-start.9 = (bf16[528,128]{1,0:T(8,128)(2,1)S(1)}, bf16[528,128]{1,0:T(8,128)(2,1)S(1)}, u32[]{:S(2)}, u32[]{:S(2)}) collective-permute-start(bf16[528,128]{1,0:T(8,128)(2,1)S(1)} %get-tuple-element.43), channel_id=1, source_target_pairs={{0,4},{4,0},{8,12},{12,8},{16,20},{20,16},{24,28},{28,24},{1,5},{5... | collective-permute-start | bytes 405512 | tf_op jit(solution)/shard_map/ppermute | solution.py:321
  24.2 1.9 %collective-permute-start.11 = (bf16[528,128]{1,0:T(8,128)(2,1)S(1)}, bf16[528,128]{1,0:T(8,128)(2,1)S(1)}, u32[]{:S(2)}, u32[]{:S(2)}) collective-permute-start(bf16[528,128]{1,0:T(8,128)(2,1)S(1)} %get-tuple-element.45), channel_id=1, source_target_pairs={{0,12},{4,8},{8,4},{12,0},{16,28},{20,24},{24,20},{28,16},{1,13},{... | collective-permute-start | bytes 405512 | tf_op jit(solution)/shard_map/ppermute | solution.py:321
  26.1 0.6 %collective-permute-done.8.refs_4_ = bf16[1024,128]{1,0:T(8,128)(2,1)S(1)} collective-permute-done((bf16[1024,128]{1,0:T(8,128)(2,1)S(1)}, bf16[1024,128]{1,0:T(8,128)(2,1)S(1)}, u32[]{:S(2)}, u32[]{:S(2)}) %collective-permute-start.8) | collective-permute-done | bytes 262176 | tf_op jit(solution)/shard_map/ppermute | solution.py:321
  26.7 1.4 %near_sum.1 = (f32[32,128,128]{2,1,0:T(8,128)S(1)}, bf16[128,128]{1,0:T(8,128)(2,1)S(1)}) custom-call(bf16[4,4]{1,0:T(4,128)(2,1)} %metric_in.1, bf16[528,128]{1,0:T(8,128)(2,1)S(1)} %get-tuple-element.34.refs_0_, bf16[528,128]{1,0:T(8,128)(2,1)S(1)} %collective-permute-done.5.refs_1_, bf16[528,128]{1,0:T(8,128)(2,1)S(1)} %collective-permute-done.6.refs_2_, ...), custom_call_target="tpu_custom_call" | custom-call | flops 3000000000 | bytes 1048576 | tf_op jit(solution)/shard_map/near_sum/pallas_call | solution.py:425
  28.1 1.0 %collective-permute-done.9.refs_1_ = bf16[528,128]{1,0:T(8,128)(2,1)S(1)} collective-permute-done((bf16[528,128]{1,0:T(8,128)(2,1)S(1)}, bf16[528,128]{1,0:T(8,128)(2,1)S(1)}, u32[]{:S(2)}, u32[]{:S(2)}) %collective-permute-start.9) | collective-permute-done | bytes 135200 | tf_op jit(solution)/shard_map/ppermute | solution.py:321
  29.1 0.6 %collective-permute-done.10.refs_2_ = bf16[528,128]{1,0:T(8,128)(2,1)S(1)} collective-permute-done((bf16[528,128]{1,0:T(8,128)(2,1)S(1)}, bf16[528,128]{1,0:T(8,128)(2,1)S(1)}, u32[]{:S(2)}, u32[]{:S(2)}) %collective-permute-start.10) | collective-permute-done | bytes 135200 | tf_op jit(solution)/shard_map/ppermute | solution.py:321
  29.7 1.5 %collective-permute-done.11.refs_3_ = bf16[528,128]{1,0:T(8,128)(2,1)S(1)} collective-permute-done((bf16[528,128]{1,0:T(8,128)(2,1)S(1)}, bf16[528,128]{1,0:T(8,128)(2,1)S(1)}, u32[]{:S(2)}, u32[]{:S(2)}) %collective-permute-start.11) | collective-permute-done | bytes 135200 | tf_op jit(solution)/shard_map/ppermute | solution.py:321
  31.2 1.5 %collect.1 = (bf16[32,4,4096]{2,1,0:T(4,128)(2,1)}, f32[32,128,128]{2,1,0:T(8,128)S(1)}) custom-call(bf16[128,128]{1,0:T(8,128)(2,1)S(1)} %get-tuple-element.41.mix, f32[32,128,128]{2,1,0:T(8,128)S(1)} %get-tuple-element.42.total_in, bf16[528,128]{1,0:T(8,128)(2,1)S(1)} %get-tuple-element.33.refs_0_, ...), custom_call_target="tpu_custom_call", output_to_operand_aliasing={{1}: (1, {})} | custom-call | tf_op jit(solution)/shard_map/collect/pallas_call | solution.py:440
  (8 shorter events, 0.1 us)
Async XLA Ops:
  0.0 4.0 %collective-permute-start = (bf16[4,128,128]{2,1,0:T(8,128)(2,1)}, bf16[4,128,128]{2,1,0:T(8,128)(2,1)S(1)}, u32[]{:S(2)}, u32[]{:S(2)}) collective-permute-start(bf16[4,128,128]{2,1,0:T(8,128)(2,1)} %bitcast.2), channel_id=1, source_target_pairs={{0,1},{1,0},{2,3},{3,2},{4,5},{5,4},{6,7},{7,6},{8,9},{9,8},{10,11... | collective-permute-start | bytes 393224 | tf_op jit(solution)/shard_map/ppermute | solution.py:321
  0.5 10.9 %collective-permute-start.1 = (bf16[4,128,128]{2,1,0:T(8,128)(2,1)}, bf16[4,128,128]{2,1,0:T(8,128)(2,1)S(1)}, u32[]{:S(2)}, u32[]{:S(2)}) collective-permute-start(bf16[4,128,128]{2,1,0:T(8,128)(2,1)} %bitcast.3), channel_id=1, source_target_pairs={{0,16},{4,20},{8,24},{12,28},{16,0},{20,4},{24,8},{28,12},{1,17},{... | collective-permute-start | bytes 393224 | tf_op jit(solution)/shard_map/ppermute | solution.py:321
  6.0 10.9 %collective-permute-start.5 = (bf16[528,128]{1,0:T(8,128)(2,1)S(1)}, bf16[528,128]{1,0:T(8,128)(2,1)S(1)}, u32[]{:S(2)}, u32[]{:S(2)}) collective-permute-start(bf16[528,128]{1,0:T(8,128)(2,1)S(1)} %get-tuple-element.35), channel_id=1, source_target_pairs={{0,4},{4,0},{8,12},{12,8},{16,20},{20,16},{24,28},{28,24},{1,5},{5... | collective-permute-start | bytes 405512 | tf_op jit(solution)/shard_map/ppermute | solution.py:321
  7.6 9.4 %collective-permute-start.6 = (bf16[528,128]{1,0:T(8,128)(2,1)S(1)}, bf16[528,128]{1,0:T(8,128)(2,1)S(1)}, u32[]{:S(2)}, u32[]{:S(2)}) collective-permute-start(bf16[528,128]{1,0:T(8,128)(2,1)S(1)} %get-tuple-element.37), channel_id=1, source_target_pairs={{0,8},{4,12},{8,0},{12,4},{16,24},{20,28},{24,16},{28,20},{1,9},{5... | collective-permute-start | bytes 405512 | tf_op jit(solution)/shard_map/ppermute | solution.py:321
  9.2 9.7 %collective-permute-start.7 = (bf16[528,128]{1,0:T(8,128)(2,1)S(1)}, bf16[528,128]{1,0:T(8,128)(2,1)S(1)}, u32[]{:S(2)}, u32[]{:S(2)}) collective-permute-start(bf16[528,128]{1,0:T(8,128)(2,1)S(1)} %get-tuple-element.39), channel_id=1, source_target_pairs={{0,12},{4,8},{8,4},{12,0},{16,28},{20,24},{24,20},{28,16},{1,13},{... | collective-permute-start | bytes 405512 | tf_op jit(solution)/shard_map/ppermute | solution.py:321
  11.3 5.2 %collective-permute-start.3 = (bf16[4,128,128]{2,1,0:T(8,128)(2,1)S(1)}, bf16[4,128,128]{2,1,0:T(8,128)(2,1)S(1)}, u32[]{:S(2)}, u32[]{:S(2)}) collective-permute-start(bf16[4,128,128]{2,1,0:T(8,128)(2,1)S(1)} %collective-permute-done.1.first), channel_id=1, source_target_pairs={{0,2},{1,3},{2,0},{3,1},{4,6},{5,7},{6,4},{7,5},{8,10},{9,11},{10,... | collective-permute-start | bytes 393224 | tf_op jit(solution)/shard_map/ppermute | solution.py:321
  12.9 9.2 %collective-permute-start.2 = (bf16[144,512]{1,0:T(8,128)(2,1)S(1)}, bf16[144,512]{1,0:T(8,128)(2,1)S(1)}, u32[]{:S(2)}, u32[]{:S(2)}) collective-permute-start(bf16[144,512]{1,0:T(8,128)(2,1)S(1)} %pick.1), channel_id=1, source_target_pairs={{0,16},{4,20},{8,24},{12,28},{16,0},{20,4},{24,8},{28,12},{1,17},{... | collective-permute-start | bytes 442376 | tf_op jit(solution)/shard_map/ppermute | solution.py:321
  16.9 5.4 %collective-permute-start.4 = (bf16[8,128,128]{2,1,0:T(8,128)(2,1)S(1)}, bf16[8,128,128]{2,1,0:T(8,128)(2,1)S(1)}, u32[]{:S(2)}, u32[]{:S(2)}) collective-permute-start(bf16[8,128,128]{2,1,0:T(8,128)(2,1)S(1)} %far_pair.1.blocks), channel_id=1, source_target_pairs={{0,1},{1,0},{2,3},{3,2},{4,5},{5,4},{6,7},{7,6},{8,9},{9,8},{10,11... | collective-permute-start | bytes 786440 | tf_op jit(solution)/shard_map/ppermute | solution.py:321
  18.9 7.9 %collective-permute-start.8 = (bf16[1024,128]{1,0:T(8,128)(2,1)S(1)}, bf16[1024,128]{1,0:T(8,128)(2,1)S(1)}, u32[]{:S(2)}, u32[]{:S(2)}) collective-permute-start(bf16[1024,128]{1,0:T(8,128)(2,1)S(1)} %regroup.1), channel_id=1, source_target_pairs={{0,2},{1,3},{2,0},{3,1},{4,6},{5,7},{6,4},{7,5},{8,10},{9,11},{10,... | collective-permute-start | bytes 786440 | tf_op jit(solution)/shard_map/ppermute | solution.py:321
  22.6 6.5 %collective-permute-start.9 = (bf16[528,128]{1,0:T(8,128)(2,1)S(1)}, bf16[528,128]{1,0:T(8,128)(2,1)S(1)}, u32[]{:S(2)}, u32[]{:S(2)}) collective-permute-start(bf16[528,128]{1,0:T(8,128)(2,1)S(1)} %get-tuple-element.43), channel_id=1, source_target_pairs={{0,4},{4,0},{8,12},{12,8},{16,20},{20,16},{24,28},{28,24},{1,5},{5... | collective-permute-start | bytes 405512 | tf_op jit(solution)/shard_map/ppermute | solution.py:321
  24.2 5.5 %collective-permute-start.10 = (bf16[528,128]{1,0:T(8,128)(2,1)S(1)}, bf16[528,128]{1,0:T(8,128)(2,1)S(1)}, u32[]{:S(2)}, u32[]{:S(2)}) collective-permute-start(bf16[528,128]{1,0:T(8,128)(2,1)S(1)} %get-tuple-element.44), channel_id=1, source_target_pairs={{0,8},{4,12},{8,0},{12,4},{16,24},{20,28},{24,16},{28,20},{1,9},{5... | collective-permute-start | bytes 405512 | tf_op jit(solution)/shard_map/ppermute | solution.py:321
  24.2 7.0 %collective-permute-start.11 = (bf16[528,128]{1,0:T(8,128)(2,1)S(1)}, bf16[528,128]{1,0:T(8,128)(2,1)S(1)}, u32[]{:S(2)}, u32[]{:S(2)}) collective-permute-start(bf16[528,128]{1,0:T(8,128)(2,1)S(1)} %get-tuple-element.45), channel_id=1, source_target_pairs={{0,12},{4,8},{8,4},{12,0},{16,28},{20,24},{24,20},{28,16},{1,13},{... | collective-permute-start | bytes 405512 | tf_op jit(solution)/shard_map/ppermute | solution.py:321

commit v17 on v16

--- a/solution.py
+++ b/solution.py
@@ -76,6 +76,11 @@
     )
 
 
+def place_bits(at, aux):
+    swapped = at - at % 4 + at % 2 * 2 + at // 2 % 2
+    return jnp.where(aux % 2 == 1, at, swapped)
+
+
 def code_tile(pairs):
     pairs_dev = pairs.shape[0]
     lane = lax.broadcasted_iota(jnp.int32, (1, BS), 1)
@@ -87,15 +92,18 @@
 
 
 def pick_kernel(
-    flips,
+    group,
     occ_local,
     aux_count,
     pairs_in,
     slot_in,
     coef_in,
-    *refs,
+    out,
+    pairs,
+    slot_row,
+    coef,
+    sems,
 ):
-    *outs, pairs, slot_row, coef, sems = refs
     pairs_dev = pairs.shape[0]
     blocks_dev = coef.shape[0] // BS
     occ_count = coef.shape[1]
@@ -109,9 +117,9 @@
         load.start()
     me = lax.axis_index("shell")
     mine = lax.axis_index("aux")
-    every = sum(flips, [])
-    row = lax.broadcasted_iota(jnp.int32, (len(every) * occ_local, 1), 0)
-    owner = sum(jnp.where(row // occ_local == at, f, 0) for at, f in enumerate(every))
+    rows = group * occ_local
+    row = lax.broadcasted_iota(jnp.int32, (rows, 1), 0)
+    owner = group + place_bits(row // occ_local, mine)
     wanted = (jnp.bitwise_xor(owner, me) * aux_count + mine) * occ_local + row % occ_local
     loads[0].wait()
     target = targets_of(slot_row[...], slot_row.shape[1], occ_count)
@@ -129,12 +137,8 @@
             preferred_element_type=jnp.float32,
         )
         piece = (piece * live).astype(jnp.bfloat16)
-        first = 0
-        for out in outs:
-            rows = out.shape[0] - 16
-            out[:rows, k * BS : (k + 1) * BS] = piece[first : first + rows]
-            out[rows:, k * BS : (k + 1) * BS] = code
-            first += rows
+        out[:rows, k * BS : (k + 1) * BS] = piece
+        out[rows:, k * BS : (k + 1) * BS] = code
 
 
 def near_kernel(
@@ -163,7 +167,7 @@
     mine = lax.axis_index("aux")
     owned = aux_count // 2 * occ_local
     row = lax.broadcasted_iota(jnp.int32, (len(outs) * owned, 1), 0)
-    owner = jnp.bitwise_xor(row // owned, me) * aux_count + jnp.bitwise_xor(
+    owner = jnp.bitwise_xor(place_bits(row // owned, mine), me) * aux_count + jnp.bitwise_xor(
         row // occ_local % (aux_count // 2) * 2, mine
     )
     wanted = owner * occ_local + row % occ_local
@@ -321,6 +325,16 @@
     return lax.ppermute(value, axis, [(at, at ^ bits) for at in range(count)])
 
 
+def to_place(value, at):
+    shell_count, aux_count = lax.axis_size("shell"), lax.axis_size("aux")
+    moves = []
+    for shell in range(shell_count):
+        for aux in range(aux_count):
+            bits = at if aux % 2 else at - at % 4 + at % 2 * 2 + at // 2 % 2
+            moves.append((shell * aux_count + aux, (shell ^ bits) * aux_count + aux))
+    return lax.ppermute(value, ("shell", "aux"), moves)
+
+
 def after(value, *others):
     return lax.optimization_barrier((value, *others))[0]
 
@@ -377,16 +391,14 @@
         compiler_params=params,
         name="near_blocks",
     )(*in_hbm(*operands, blocks), flip(blocks, "aux", 1))
-    near = [near[0]] + [flip(near[f], "shell", f) for f in range(1, group)]
-    (sent_coef,) = pl.pallas_call(
-        functools.partial(
-            pick_kernel, [list(range(group, shell_count))], occ_local, aux_count
+    near = [near[0]] + [to_place(near[f], f) for f in range(1, group)]
+    sent_coef = pl.pallas_call(
+        functools.partial(pick_kernel, group, occ_local, aux_count),
+        out_shape=jax.ShapeDtypeStruct(
+            (group * occ_local + 16, pairs_dev * BS), jnp.bfloat16
         ),
-        out_shape=[
-            jax.ShapeDtypeStruct((group * occ_local + 16, pairs_dev * BS), jnp.bfloat16)
-        ],
         in_specs=[hbm] * 3,
-        out_specs=[vmem],
+        out_specs=vmem,
         scratch_shapes=loaded + [pltpu.SemaphoreType.DMA((3,))],
         compiler_params=params,
         name="pick",
@@ -436,7 +448,7 @@
         cost_estimate=cost(3e9),
         name="near_sum",
     )(*in_hbm(metric), *(after(one, far[0]) for one in near), across)
-    far = [far[0]] + [flip(far[f], "shell", f) for f in range(1, group)]
+    far = [far[0]] + [to_place(far[f], f) for f in range(1, group)]
     return pl.pallas_call(
         collect_kernel,
         out_shape=[
@@ -459,7 +471,7 @@
 def per_device(integrals, pair_list, coef, metric, occ_slot):
     shell_count, aux_count = lax.axis_size("shell"), lax.axis_size("aux")
     occ_local = coef.shape[1] // (shell_count * aux_count)
-    if occ_local % 16 or shell_count & (shell_count - 1) or aux_count != 4:
+    if occ_local % 16 or shell_count < 8 or shell_count & (shell_count - 1) or aux_count != 4:
         return relayed_half_blocks(integrals, pair_list, coef, metric, occ_slot)
     return exchanged_inputs(integrals, pair_list, coef, metric, occ_slot)
 

time: 32.9 us -> 32.9 us (level)
    ppermute x12 -> x6, starting transfers between devices: 15.9 us -> 8.82 us  [flip(): return lax.ppermute(value, axis, [(at, at ^ bits) for at in range(count)])]
    ppermute x0 -> x6, starting transfers between devices: none -> 7.11 us  [to_place(): return lax.ppermute(value, ('shell', 'aux'), moves)]
    ppermute x0 -> x6, waiting for transfers between devices: none -> 4.77 us  [to_place(): return lax.ppermute(value, ('shell', 'aux'), moves)]
    ppermute x12 -> x6, waiting for transfers between devices: 9.27 us -> 4.5 us  [flip(): return lax.ppermute(value, axis, [(at, at ^ bits) for at in range(count)])]
where the time goes in v17:
time: 32.9 us; the launch traced here: 32.7 us
  starting transfers between devices  15.9 us (48%)
  waiting for transfers between devices  9.28 us (28%)
  Pallas kernels  7.38 us (22%)
    ppermute x6, starting transfers between devices, flip(): return lax.ppermute(value, axis, [(at, at ^ bits) for at in range(count)])  8.82 us
    ppermute x6, starting transfers between devices, to_place(): return lax.ppermute(value, ('shell', 'aux'), moves)  7.11 us
    ppermute x6, waiting for transfers between devices, to_place(): return lax.ppermute(value, ('shell', 'aux'), moves)  4.77 us
    ppermute x6, waiting for transfers between devices, flip(): return lax.ppermute(value, axis, [(at, at ^ bits) for at in range(count)])  4.5 us
    pallas_call x1, Pallas kernels, exchanged_inputs(): pl.pallas_call(functools.partial(near_kernel, occ_local, aux_count), out_...  1.98 us
    pallas_call x1, Pallas kernels, exchanged_inputs(): pl.pallas_call(functools.partial(pick_kernel, group, occ_local, aux_count...  1.72 us
    pallas_call x1, Pallas kernels, exchanged_inputs(): pl.pallas_call(collect_kernel, out_shape=[jax.ShapeDtypeStruct((occ_local...  1.53 us
    pallas_call x1, Pallas kernels, exchanged_inputs(): pl.pallas_call(near_sum_kernel, out_shape=[total_shape, jax.ShapeDtypeStr...  1.37 us
  transfers between devices with their start and end apart: 12, of which 7 were waited for; matrix products, arithmetic and copies ran while one was open for 0% of the time, Pallas kernels for 18%

profile of v17, /device:TPU:0, one launch (start us, length us, event | category | flops | bytes accessed | tf_op | source)
XLA Modules:
  0.0 32.7 jit_solution(4629789262161823134)
XLA Ops:
  0.0 0.5 %collective-permute-start = (bf16[4,128,128]{2,1,0:T(8,128)(2,1)}, bf16[4,128,128]{2,1,0:T(8,128)(2,1)S(1)}, u32[]{:S(2)}, u32[]{:S(2)}) collective-permute-start(bf16[4,128,128]{2,1,0:T(8,128)(2,1)} %bitcast.2), channel_id=1, source_target_pairs={{0,1},{1,0},{2,3},{3,2},{4,5},{5,4},{6,7},{7,6},{8,9},{9,8},{10,11... | collective-permute-start | bytes 393224 | tf_op jit(solution)/shard_map/ppermute | solution.py:325
  0.5 3.6 %collective-permute-start.1 = (bf16[4,128,128]{2,1,0:T(8,128)(2,1)}, bf16[4,128,128]{2,1,0:T(8,128)(2,1)S(1)}, u32[]{:S(2)}, u32[]{:S(2)}) collective-permute-start(bf16[4,128,128]{2,1,0:T(8,128)(2,1)} %bitcast.3), channel_id=1, source_target_pairs={{0,16},{4,20},{8,24},{12,28},{16,0},{20,4},{24,8},{28,12},{1,17},{... | collective-permute-start | bytes 393224 | tf_op jit(solution)/shard_map/ppermute | solution.py:325
  4.0 2.0 %near_blocks.1 = (bf16[528,128]{1,0:T(8,128)(2,1)S(1)}, bf16[528,128]{1,0:T(8,128)(2,1)S(1)}, bf16[528,128]{1,0:T(8,128)(2,1)S(1)}, bf16[528,128]{1,0:T(8,128)(2,1)S(1)}) custom-call(s32[4,3]{1,0:T(4,128)} %pairs_in.3, s32[1,128]{1,0:T(1,128)} %bitcast.5, bf16[512,1024]{1,0:T(8,128)(2,1)} %coef_in.3, bf16[4,128,128]{2,1,0:T(8,128)(2,1)} %bitcast.4, ...), custom_call_target="tpu_custom_call" | custom-call | tf_op jit(solution)/shard_map/near_blocks/pallas_call | solution.py:384
  6.0 1.6 %collective-permute-start.5 = (bf16[528,128]{1,0:T(8,128)(2,1)S(1)}, bf16[528,128]{1,0:T(8,128)(2,1)S(1)}, u32[]{:S(2)}, u32[]{:S(2)}) collective-permute-start(bf16[528,128]{1,0:T(8,128)(2,1)S(1)} %get-tuple-element.35), channel_id=1, source_target_pairs={{0,8},{1,5},{2,10},{3,7},{4,12},{5,1},{6,14},{7,3},{8,0},{9,13},{1... | collective-permute-start | bytes 405512 | tf_op jit(solution)/shard_map/ppermute | solution.py:335
  7.7 1.5 %collective-permute-start.6 = (bf16[528,128]{1,0:T(8,128)(2,1)S(1)}, bf16[528,128]{1,0:T(8,128)(2,1)S(1)}, u32[]{:S(2)}, u32[]{:S(2)}) collective-permute-start(bf16[528,128]{1,0:T(8,128)(2,1)S(1)} %get-tuple-element.37), channel_id=1, source_target_pairs={{0,4},{1,9},{2,6},{3,11},{4,0},{5,13},{6,2},{7,15},{8,12},{9,1},{1... | collective-permute-start | bytes 405512 | tf_op jit(solution)/shard_map/ppermute | solution.py:335
  9.2 0.4 %collective-permute-start.7 = (bf16[528,128]{1,0:T(8,128)(2,1)S(1)}, bf16[528,128]{1,0:T(8,128)(2,1)S(1)}, u32[]{:S(2)}, u32[]{:S(2)}) collective-permute-start(bf16[528,128]{1,0:T(8,128)(2,1)S(1)} %get-tuple-element.39), channel_id=1, source_target_pairs={{0,12},{1,13},{2,14},{3,15},{4,8},{5,9},{6,10},{7,11},{8,4},{9,5},... | collective-permute-start | bytes 405512 | tf_op jit(solution)/shard_map/ppermute | solution.py:335
  9.6 1.7 %pick.1 = bf16[144,512]{1,0:T(8,128)(2,1)S(1)} custom-call(s32[4,3]{1,0:T(4,128)} %pairs_in.3, s32[1,128]{1,0:T(1,128)} %bitcast.6, bf16[512,1024]{1,0:T(8,128)(2,1)} %coef_in.3), custom_call_target="tpu_custom_call" | custom-call | tf_op jit(solution)/shard_map/pick/pallas_call | solution.py:395
  11.3 1.6 %collective-permute-start.3 = (bf16[4,128,128]{2,1,0:T(8,128)(2,1)S(1)}, bf16[4,128,128]{2,1,0:T(8,128)(2,1)S(1)}, u32[]{:S(2)}, u32[]{:S(2)}) collective-permute-start(bf16[4,128,128]{2,1,0:T(8,128)(2,1)S(1)} %collective-permute-done.1.first), channel_id=1, source_target_pairs={{0,2},{1,3},{2,0},{3,1},{4,6},{5,7},{6,4},{7,5},{8,10},{9,11},{10,... | collective-permute-start | bytes 393224 | tf_op jit(solution)/shard_map/ppermute | solution.py:325
  12.9 1.6 %collective-permute-start.2 = (bf16[144,512]{1,0:T(8,128)(2,1)S(1)}, bf16[144,512]{1,0:T(8,128)(2,1)S(1)}, u32[]{:S(2)}, u32[]{:S(2)}) collective-permute-start(bf16[144,512]{1,0:T(8,128)(2,1)S(1)} %pick.1), channel_id=1, source_target_pairs={{0,16},{4,20},{8,24},{12,28},{16,0},{20,4},{24,8},{28,12},{1,17},{... | collective-permute-start | bytes 442376 | tf_op jit(solution)/shard_map/ppermute | solution.py:325
  14.5 2.1 %collective-permute-done.3.second = bf16[4,128,128]{2,1,0:T(8,128)(2,1)S(1)} collective-permute-done((bf16[4,128,128]{2,1,0:T(8,128)(2,1)S(1)}, bf16[4,128,128]{2,1,0:T(8,128)(2,1)S(1)}, u32[]{:S(2)}, u32[]{:S(2)}) %collective-permute-start.3) | collective-permute-done | bytes 131104 | tf_op jit(solution)/shard_map/ppermute | solution.py:325
  16.6 0.3 %far_pair.1.blocks = bf16[8,128,128]{2,1,0:T(8,128)(2,1)S(1)} custom-call(bf16[4,128,128]{2,1,0:T(8,128)(2,1)S(1)} %collective-permute-done.1.first, bf16[4,128,128]{2,1,0:T(8,128)(2,1)S(1)} %collective-permute-done.3.second), custom_call_target="tpu_custom_call" | custom-call | tf_op jit(solution)/shard_map/far_pair/pallas_call | solution.py:364
  17.0 1.8 %collective-permute-done.7.refs_3_ = bf16[528,128]{1,0:T(8,128)(2,1)S(1)} collective-permute-done((bf16[528,128]{1,0:T(8,128)(2,1)S(1)}, bf16[528,128]{1,0:T(8,128)(2,1)S(1)}, u32[]{:S(2)}, u32[]{:S(2)}) %collective-permute-start.7) | collective-permute-done | bytes 135200 | tf_op jit(solution)/shard_map/ppermute | solution.py:335
  18.9 1.6 %collective-permute-start.8 = (bf16[1024,128]{1,0:T(8,128)(2,1)S(1)}, bf16[1024,128]{1,0:T(8,128)(2,1)S(1)}, u32[]{:S(2)}, u32[]{:S(2)}) collective-permute-start(bf16[1024,128]{1,0:T(8,128)(2,1)S(1)} %regroup.1), channel_id=1, source_target_pairs={{0,2},{1,3},{2,0},{3,1},{4,6},{5,7},{6,4},{7,5},{8,10},{9,11},{10,... | collective-permute-start | bytes 786440 | tf_op jit(solution)/shard_map/ppermute | solution.py:325
  20.4 1.7 %collective-permute-done.2.coefs = bf16[144,512]{1,0:T(8,128)(2,1)S(1)} collective-permute-done((bf16[144,512]{1,0:T(8,128)(2,1)S(1)}, bf16[144,512]{1,0:T(8,128)(2,1)S(1)}, u32[]{:S(2)}, u32[]{:S(2)}) %collective-permute-start.2) | collective-permute-done | bytes 147488 | tf_op jit(solution)/shard_map/ppermute | solution.py:325
  22.1 0.2 far_blocks_0.1
  22.3 0.2 far_blocks_1.1
  22.6 0.3 collective-permute-start.9
  22.9 1.4 %collective-permute-start.10 = (bf16[528,128]{1,0:T(8,128)(2,1)S(1)}, bf16[528,128]{1,0:T(8,128)(2,1)S(1)}, u32[]{:S(2)}, u32[]{:S(2)}) collective-permute-start(bf16[528,128]{1,0:T(8,128)(2,1)S(1)} %get-tuple-element.44), channel_id=1, source_target_pairs={{0,4},{1,9},{2,6},{3,11},{4,0},{5,13},{6,2},{7,15},{8,12},{9,1},{1... | collective-permute-start | bytes 405512 | tf_op jit(solution)/shard_map/ppermute | solution.py:335
  24.2 1.9 %collective-permute-start.11 = (bf16[528,128]{1,0:T(8,128)(2,1)S(1)}, bf16[528,128]{1,0:T(8,128)(2,1)S(1)}, u32[]{:S(2)}, u32[]{:S(2)}) collective-permute-start(bf16[528,128]{1,0:T(8,128)(2,1)S(1)} %get-tuple-element.45), channel_id=1, source_target_pairs={{0,12},{1,13},{2,14},{3,15},{4,8},{5,9},{6,10},{7,11},{8,4},{9,5},... | collective-permute-start | bytes 405512 | tf_op jit(solution)/shard_map/ppermute | solution.py:335
  26.1 0.7 %collective-permute-done.8.refs_4_ = bf16[1024,128]{1,0:T(8,128)(2,1)S(1)} collective-permute-done((bf16[1024,128]{1,0:T(8,128)(2,1)S(1)}, bf16[1024,128]{1,0:T(8,128)(2,1)S(1)}, u32[]{:S(2)}, u32[]{:S(2)}) %collective-permute-start.8) | collective-permute-done | bytes 262176 | tf_op jit(solution)/shard_map/ppermute | solution.py:325
  26.8 1.4 %near_sum.1 = (f32[32,128,128]{2,1,0:T(8,128)S(1)}, bf16[128,128]{1,0:T(8,128)(2,1)S(1)}) custom-call(bf16[4,4]{1,0:T(4,128)(2,1)} %metric_in.1, bf16[528,128]{1,0:T(8,128)(2,1)S(1)} %get-tuple-element.34.refs_0_, bf16[528,128]{1,0:T(8,128)(2,1)S(1)} %collective-permute-done.5.refs_1_, bf16[528,128]{1,0:T(8,128)(2,1)S(1)} %collective-permute-done.6.refs_2_, ...), custom_call_target="tpu_custom_call" | custom-call | flops 3000000000 | bytes 1048576 | tf_op jit(solution)/shard_map/near_sum/pallas_call | solution.py:437
  28.2 0.8 %collective-permute-done.9.refs_1_ = bf16[528,128]{1,0:T(8,128)(2,1)S(1)} collective-permute-done((bf16[528,128]{1,0:T(8,128)(2,1)S(1)}, bf16[528,128]{1,0:T(8,128)(2,1)S(1)}, u32[]{:S(2)}, u32[]{:S(2)}) %collective-permute-start.9) | collective-permute-done | bytes 135200 | tf_op jit(solution)/shard_map/ppermute | solution.py:335
  29.2 2.0 %collective-permute-done.11.refs_3_ = bf16[528,128]{1,0:T(8,128)(2,1)S(1)} collective-permute-done((bf16[528,128]{1,0:T(8,128)(2,1)S(1)}, bf16[528,128]{1,0:T(8,128)(2,1)S(1)}, u32[]{:S(2)}, u32[]{:S(2)}) %collective-permute-start.11) | collective-permute-done | bytes 135200 | tf_op jit(solution)/shard_map/ppermute | solution.py:335
  31.2 1.5 %collect.1 = (bf16[32,4,4096]{2,1,0:T(4,128)(2,1)}, f32[32,128,128]{2,1,0:T(8,128)S(1)}) custom-call(bf16[128,128]{1,0:T(8,128)(2,1)S(1)} %get-tuple-element.41.mix, f32[32,128,128]{2,1,0:T(8,128)S(1)} %get-tuple-element.42.total_in, bf16[528,128]{1,0:T(8,128)(2,1)S(1)} %get-tuple-element.33.refs_0_, ...), custom_call_target="tpu_custom_call", output_to_operand_aliasing={{1}: (1, {})} | custom-call | tf_op jit(solution)/shard_map/collect/pallas_call | solution.py:452
  (8 shorter events, 0.2 us)
Async XLA Ops:
  0.0 4.0 %collective-permute-start = (bf16[4,128,128]{2,1,0:T(8,128)(2,1)}, bf16[4,128,128]{2,1,0:T(8,128)(2,1)S(1)}, u32[]{:S(2)}, u32[]{:S(2)}) collective-permute-start(bf16[4,128,128]{2,1,0:T(8,128)(2,1)} %bitcast.2), channel_id=1, source_target_pairs={{0,1},{1,0},{2,3},{3,2},{4,5},{5,4},{6,7},{7,6},{8,9},{9,8},{10,11... | collective-permute-start | bytes 393224 | tf_op jit(solution)/shard_map/ppermute | solution.py:325
  0.5 10.9 %collective-permute-start.1 = (bf16[4,128,128]{2,1,0:T(8,128)(2,1)}, bf16[4,128,128]{2,1,0:T(8,128)(2,1)S(1)}, u32[]{:S(2)}, u32[]{:S(2)}) collective-permute-start(bf16[4,128,128]{2,1,0:T(8,128)(2,1)} %bitcast.3), channel_id=1, source_target_pairs={{0,16},{4,20},{8,24},{12,28},{16,0},{20,4},{24,8},{28,12},{1,17},{... | collective-permute-start | bytes 393224 | tf_op jit(solution)/shard_map/ppermute | solution.py:325
  6.0 10.9 %collective-permute-start.5 = (bf16[528,128]{1,0:T(8,128)(2,1)S(1)}, bf16[528,128]{1,0:T(8,128)(2,1)S(1)}, u32[]{:S(2)}, u32[]{:S(2)}) collective-permute-start(bf16[528,128]{1,0:T(8,128)(2,1)S(1)} %get-tuple-element.35), channel_id=1, source_target_pairs={{0,8},{1,5},{2,10},{3,7},{4,12},{5,1},{6,14},{7,3},{8,0},{9,13},{1... | collective-permute-start | bytes 405512 | tf_op jit(solution)/shard_map/ppermute | solution.py:335
  7.7 9.3 %collective-permute-start.6 = (bf16[528,128]{1,0:T(8,128)(2,1)S(1)}, bf16[528,128]{1,0:T(8,128)(2,1)S(1)}, u32[]{:S(2)}, u32[]{:S(2)}) collective-permute-start(bf16[528,128]{1,0:T(8,128)(2,1)S(1)} %get-tuple-element.37), channel_id=1, source_target_pairs={{0,4},{1,9},{2,6},{3,11},{4,0},{5,13},{6,2},{7,15},{8,12},{9,1},{1... | collective-permute-start | bytes 405512 | tf_op jit(solution)/shard_map/ppermute | solution.py:335
  9.2 9.7 %collective-permute-start.7 = (bf16[528,128]{1,0:T(8,128)(2,1)S(1)}, bf16[528,128]{1,0:T(8,128)(2,1)S(1)}, u32[]{:S(2)}, u32[]{:S(2)}) collective-permute-start(bf16[528,128]{1,0:T(8,128)(2,1)S(1)} %get-tuple-element.39), channel_id=1, source_target_pairs={{0,12},{1,13},{2,14},{3,15},{4,8},{5,9},{6,10},{7,11},{8,4},{9,5},... | collective-permute-start | bytes 405512 | tf_op jit(solution)/shard_map/ppermute | solution.py:335
  11.3 5.2 %collective-permute-start.3 = (bf16[4,128,128]{2,1,0:T(8,128)(2,1)S(1)}, bf16[4,128,128]{2,1,0:T(8,128)(2,1)S(1)}, u32[]{:S(2)}, u32[]{:S(2)}) collective-permute-start(bf16[4,128,128]{2,1,0:T(8,128)(2,1)S(1)} %collective-permute-done.1.first), channel_id=1, source_target_pairs={{0,2},{1,3},{2,0},{3,1},{4,6},{5,7},{6,4},{7,5},{8,10},{9,11},{10,... | collective-permute-start | bytes 393224 | tf_op jit(solution)/shard_map/ppermute | solution.py:325
  12.9 9.2 %collective-permute-start.2 = (bf16[144,512]{1,0:T(8,128)(2,1)S(1)}, bf16[144,512]{1,0:T(8,128)(2,1)S(1)}, u32[]{:S(2)}, u32[]{:S(2)}) collective-permute-start(bf16[144,512]{1,0:T(8,128)(2,1)S(1)} %pick.1), channel_id=1, source_target_pairs={{0,16},{4,20},{8,24},{12,28},{16,0},{20,4},{24,8},{28,12},{1,17},{... | collective-permute-start | bytes 442376 | tf_op jit(solution)/shard_map/ppermute | solution.py:325
  16.9 5.4 %collective-permute-start.4 = (bf16[8,128,128]{2,1,0:T(8,128)(2,1)S(1)}, bf16[8,128,128]{2,1,0:T(8,128)(2,1)S(1)}, u32[]{:S(2)}, u32[]{:S(2)}) collective-permute-start(bf16[8,128,128]{2,1,0:T(8,128)(2,1)S(1)} %far_pair.1.blocks), channel_id=1, source_target_pairs={{0,1},{1,0},{2,3},{3,2},{4,5},{5,4},{6,7},{7,6},{8,9},{9,8},{10,11... | collective-permute-start | bytes 786440 | tf_op jit(solution)/shard_map/ppermute | solution.py:325
  18.9 8.0 %collective-permute-start.8 = (bf16[1024,128]{1,0:T(8,128)(2,1)S(1)}, bf16[1024,128]{1,0:T(8,128)(2,1)S(1)}, u32[]{:S(2)}, u32[]{:S(2)}) collective-permute-start(bf16[1024,128]{1,0:T(8,128)(2,1)S(1)} %regroup.1), channel_id=1, source_target_pairs={{0,2},{1,3},{2,0},{3,1},{4,6},{5,7},{6,4},{7,5},{8,10},{9,11},{10,... | collective-permute-start | bytes 786440 | tf_op jit(solution)/shard_map/ppermute | solution.py:325
  22.6 6.5 %collective-permute-start.9 = (bf16[528,128]{1,0:T(8,128)(2,1)S(1)}, bf16[528,128]{1,0:T(8,128)(2,1)S(1)}, u32[]{:S(2)}, u32[]{:S(2)}) collective-permute-start(bf16[528,128]{1,0:T(8,128)(2,1)S(1)} %get-tuple-element.43), channel_id=1, source_target_pairs={{0,8},{1,5},{2,10},{3,7},{4,12},{5,1},{6,14},{7,3},{8,0},{9,13},{1... | collective-permute-start | bytes 405512 | tf_op jit(solution)/shard_map/ppermute | solution.py:335
  22.9 6.3 %collective-permute-start.10 = (bf16[528,128]{1,0:T(8,128)(2,1)S(1)}, bf16[528,128]{1,0:T(8,128)(2,1)S(1)}, u32[]{:S(2)}, u32[]{:S(2)}) collective-permute-start(bf16[528,128]{1,0:T(8,128)(2,1)S(1)} %get-tuple-element.44), channel_id=1, source_target_pairs={{0,4},{1,9},{2,6},{3,11},{4,0},{5,13},{6,2},{7,15},{8,12},{9,1},{1... | collective-permute-start | bytes 405512 | tf_op jit(solution)/shard_map/ppermute | solution.py:335
  24.2 6.9 %collective-permute-start.11 = (bf16[528,128]{1,0:T(8,128)(2,1)S(1)}, bf16[528,128]{1,0:T(8,128)(2,1)S(1)}, u32[]{:S(2)}, u32[]{:S(2)}) collective-permute-start(bf16[528,128]{1,0:T(8,128)(2,1)S(1)} %get-tuple-element.45), channel_id=1, source_target_pairs={{0,12},{1,13},{2,14},{3,15},{4,8},{5,9},{6,10},{7,11},{8,4},{9,5},... | collective-permute-start | bytes 405512 | tf_op jit(solution)/shard_map/ppermute | solution.py:335

commit v18 on v16

--- a/solution.py
+++ b/solution.py
@@ -8,6 +8,7 @@
 from jax.sharding import PartitionSpec as P
 
 BS = 128
+TILE = 8
 
 
 def relayed_half_blocks(integrals, pair_list, coef, metric, occ_slot):
@@ -83,7 +84,7 @@
     for k in range(pairs_dev):
         code = jnp.where(lane == k, pairs[k, 0] % 128, code)
         code = jnp.where(lane == pairs_dev + k, pairs[k, 0] // 128, code)
-    return jnp.broadcast_to(code.astype(jnp.float32), (16, BS)).astype(jnp.bfloat16)
+    return jnp.broadcast_to(code.astype(jnp.float32), (TILE, BS)).astype(jnp.bfloat16)
 
 
 def pick_kernel(
@@ -131,7 +132,7 @@
         piece = (piece * live).astype(jnp.bfloat16)
         first = 0
         for out in outs:
-            rows = out.shape[0] - 16
+            rows = out.shape[0] - TILE
             out[:rows, k * BS : (k + 1) * BS] = piece[first : first + rows]
             out[rows:, k * BS : (k + 1) * BS] = code
             first += rows
@@ -161,10 +162,11 @@
         load.start()
     me = lax.axis_index("shell")
     mine = lax.axis_index("aux")
-    owned = aux_count // 2 * occ_local
+    owned = 2 * occ_local
     row = lax.broadcasted_iota(jnp.int32, (len(outs) * owned, 1), 0)
-    owner = jnp.bitwise_xor(row // owned, me) * aux_count + jnp.bitwise_xor(
-        row // occ_local % (aux_count // 2) * 2, mine
+    flips = row // owned % 2 + row // occ_local % 2 * 2
+    owner = jnp.bitwise_xor(flips, me) * aux_count + jnp.bitwise_xor(
+        row // (2 * owned) * 2, mine
     )
     wanted = owner * occ_local + row % occ_local
     loads[0].wait()
@@ -191,7 +193,7 @@
         )
         block = (block * (pairs[k, 2] == 1).astype(jnp.float32)).astype(jnp.bfloat16)
         for f, out in enumerate(outs):
-            for j in range(aux_count // 2):
+            for j in range(2):
                 first = f * owned + j * occ_local
                 for c in range(2):
                     at = ((j * 2 + c) * pairs_dev + k) * occ_local
@@ -199,14 +201,16 @@
                         first : first + occ_local, c * BS : (c + 1) * BS
                     ]
     for out in outs:
-        out[out.shape[0] - 16 :, :] = code
+        out[out.shape[0] - TILE :, :] = code
 
 
 def regroup_kernel(*refs):
     *received, out = refs
-    rows = out.shape[0] // len(received)
+    rows = (received[0].shape[0] - TILE) // 2
     for f, piece in enumerate(received):
         out[f * rows : (f + 1) * rows, :] = piece[rows : 2 * rows, :]
+    tiles = [piece[2 * rows :, :].astype(jnp.float32) for piece in received[:2]]
+    out[len(received) * rows :, :] = jnp.concatenate(tiles, axis=0).astype(jnp.bfloat16)
 
 
 def merge_kernel(first, second, out, sems):
@@ -225,7 +229,7 @@
 def block_kernel(aux_count, low, coefs, blocks, *refs):
     pieces = refs[len(refs) // 2 :] if low else refs
     pairs_dev = blocks.shape[0] // 2
-    rows = coefs.shape[0] - 16
+    rows = coefs.shape[0] - TILE
     occ_local = rows // len(pieces)
     mine = lax.axis_index("aux")
     for k in range(pairs_dev):
@@ -245,9 +249,9 @@
             piece[pairs_dev * aux_count * occ_local :, :] = coefs[rows:, :BS]
 
 
-def read_codes(received, pairs_dev, codes):
-    for at, piece in enumerate(received):
-        digits = piece[piece.shape[0] - 16 :, :].astype(jnp.float32)[:1]
+def read_codes(tiles, pairs_dev, codes):
+    for at, tile in enumerate(tiles):
+        digits = tile.astype(jnp.float32)[:1]
         high = pltpu.roll(digits, BS - pairs_dev, 1)
         codes[at : at + 1, :] = (digits + 128.0 * high).astype(jnp.int32)
 
@@ -260,17 +264,25 @@
     mine = lax.axis_index("aux")
     rows = total.shape[1]
     occ_local = rows // metric.shape[0]
-    pairs_dev = (received[0].shape[0] - 16) // rows
-    read_codes(received, pairs_dev, codes)
+    pairs_dev = (received[0].shape[0] - TILE) // rows
+    each = 2 * pairs_dev * occ_local
+    last = across[len(received) * each :, :].astype(jnp.float32)
+    tiles = [piece[2 * each :, :] for piece in received[:2]] + [last[:TILE], last[TILE:]]
+    read_codes(tiles, pairs_dev, codes)
     for f, piece in enumerate(received):
         for k in range(pairs_dev):
-            r = codes[f, k]
-            for j in range(metric.shape[0]):
-                source, first = (across, f * 2 + j - 2) if j >= 2 else (piece, j)
-                first = (first * pairs_dev + k) * occ_local
-                start = pl.multiple_of(jnp.bitwise_xor(mine, j) * occ_local, occ_local)
-                part = source[first : first + occ_local, :]
-                total[r, pl.ds(start, occ_local), :] += part.astype(jnp.float32)
+            for source, at, r in (
+                (piece, 0, codes[f % 2, k]),
+                (across, f * each, codes[2 + f % 2, k]),
+            ):
+                for c in range(2):
+                    first = at + (c * pairs_dev + k) * occ_local
+                    flipped = f // 2 * 2 + c
+                    start = pl.multiple_of(
+                        jnp.bitwise_xor(mine, flipped) * occ_local, occ_local
+                    )
+                    part = source[first : first + occ_local, :]
+                    total[r, pl.ds(start, occ_local), :] += part.astype(jnp.float32)
     load.wait()
     aux_count = metric.shape[0]
     row = lax.broadcasted_iota(jnp.int32, (rows, rows), 0)
@@ -292,8 +304,8 @@
     *received, out, total, staged, codes, sems = refs
     occ_local, aux_count = out.shape[:2]
     rows = total.shape[1]
-    pairs_dev = (received[0].shape[0] - 16) // rows
-    read_codes(received, pairs_dev, codes)
+    pairs_dev = (received[0].shape[0] - TILE) // rows
+    read_codes([piece[pairs_dev * rows :, :] for piece in received], pairs_dev, codes)
     for at, piece in enumerate(received):
         for k in range(pairs_dev):
             total[codes[at, k]] += piece[k * rows : (k + 1) * rows, :].astype(jnp.float32)
@@ -321,6 +333,16 @@
     return lax.ppermute(value, axis, [(at, at ^ bits) for at in range(count)])
 
 
+def beyond(value, shell_bits, aux_bits):
+    shell_count, aux_count = lax.axis_size("shell"), lax.axis_size("aux")
+    moves = [
+        (shell * aux_count + aux, (shell ^ shell_bits) * aux_count + (aux ^ aux_bits))
+        for shell in range(shell_count)
+        for aux in range(aux_count)
+    ]
+    return lax.ppermute(value, ("shell", "aux"), moves)
+
+
 def after(value, *others):
     return lax.optimization_barrier((value, *others))[0]
 
@@ -341,7 +363,7 @@
     occ_local = coef.shape[1] // (shell_count * aux_count)
     block_count = coef.shape[0] // BS * shell_count
     rows = occ_local * aux_count
-    piece = jax.ShapeDtypeStruct((pairs_dev * rows + 16, BS), jnp.bfloat16)
+    piece = jax.ShapeDtypeStruct((pairs_dev * rows + TILE, BS), jnp.bfloat16)
     vmem = pl.BlockSpec(memory_space=pltpu.VMEM)
     hbm = pl.BlockSpec(memory_space=pltpu.HBM)
     params = pltpu.CompilerParams(vmem_limit_bytes=40 * 2**20)
@@ -369,21 +391,21 @@
     ]
     near = pl.pallas_call(
         functools.partial(near_kernel, occ_local, aux_count),
-        out_shape=[piece] * group,
+        out_shape=[piece] * 4,
         in_specs=[hbm] * 4 + [vmem],
-        out_specs=[vmem] * group,
+        out_specs=[vmem] * 4,
         scratch_shapes=loaded
         + [pltpu.VMEM(blocks.shape, jnp.bfloat16), pltpu.SemaphoreType.DMA((4,))],
         compiler_params=params,
         name="near_blocks",
     )(*in_hbm(*operands, blocks), flip(blocks, "aux", 1))
-    near = [near[0]] + [flip(near[f], "shell", f) for f in range(1, group)]
+    near = [near[0]] + [beyond(near[f], f % 2, f // 2 * 2) for f in range(1, 4)]
     (sent_coef,) = pl.pallas_call(
         functools.partial(
             pick_kernel, [list(range(group, shell_count))], occ_local, aux_count
         ),
         out_shape=[
-            jax.ShapeDtypeStruct((group * occ_local + 16, pairs_dev * BS), jnp.bfloat16)
+            jax.ShapeDtypeStruct((group * occ_local + TILE, pairs_dev * BS), jnp.bfloat16)
         ],
         in_specs=[hbm] * 3,
         out_specs=[vmem],
@@ -399,14 +421,14 @@
         pl.pallas_call(
             regroup_kernel,
             out_shape=jax.ShapeDtypeStruct(
-                (group * 2 * pairs_dev * occ_local, BS), jnp.bfloat16
+                (4 * 2 * pairs_dev * occ_local + 2 * TILE, BS), jnp.bfloat16
             ),
-            in_specs=[vmem] * group,
+            in_specs=[vmem] * 4,
             out_specs=vmem,
             compiler_params=params,
             name="regroup",
         )(*near),
-        "aux",
+        "shell",
         2,
     )
     far = []
@@ -425,7 +447,7 @@
     total, mix = pl.pallas_call(
         near_sum_kernel,
         out_shape=[total_shape, jax.ShapeDtypeStruct((rows, rows), jnp.bfloat16)],
-        in_specs=[hbm] + [vmem] * (group + 1),
+        in_specs=[hbm] + [vmem] * 5,
         out_specs=[vmem] * 2,
         scratch_shapes=[
             pltpu.VMEM(metric.shape, jnp.bfloat16),
@@ -459,7 +481,7 @@
 def per_device(integrals, pair_list, coef, metric, occ_slot):
     shell_count, aux_count = lax.axis_size("shell"), lax.axis_size("aux")
     occ_local = coef.shape[1] // (shell_count * aux_count)
-    if occ_local % 16 or shell_count & (shell_count - 1) or aux_count != 4:
+    if occ_local % 16 or shell_count != 8 or aux_count != 4:
         return relayed_half_blocks(integrals, pair_list, coef, metric, occ_slot)
     return exchanged_inputs(integrals, pair_list, coef, metric, occ_slot)
 

time: 32.9 us -> 33.4 us (1.015)
  waiting for transfers between devices: 9.27 us -> 9.78 us
    ppermute x0 -> x3, starting transfers between devices: none -> 3.55 us  [beyond(): return lax.ppermute(value, ('shell', 'aux'), moves)]
    ppermute x12 -> x9, starting transfers between devices: 15.9 us -> 12.5 us  [flip(): return lax.ppermute(value, axis, [(at, at ^ bits) for at in range(count)])]
    ppermute x0 -> x3, waiting for transfers between devices: none -> 1.46 us  [beyond(): return lax.ppermute(value, ('shell', 'aux'), moves)]
    ppermute x12 -> x9, waiting for transfers between devices: 9.27 us -> 8.32 us  [flip(): return lax.ppermute(value, axis, [(at, at ^ bits) for at in range(count)])]
  transfers between devices with their start and end apart: 12 -> 12, of which waited for: 7 -> 6; matrix products, arithmetic and copies ran while one was open for 0% -> 0% of each run, Pallas kernels for 18% -> 18%
where the time goes in v18:
time: 33.4 us; the launch traced here: 33.2 us
  starting transfers between devices  16 us (48%)
  waiting for transfers between devices  9.78 us (29%)
  Pallas kernels  7.36 us (22%)
    ppermute x9, starting transfers between devices, flip(): return lax.ppermute(value, axis, [(at, at ^ bits) for at in range(count)])  12.5 us
    ppermute x9, waiting for transfers between devices, flip(): return lax.ppermute(value, axis, [(at, at ^ bits) for at in range(count)])  8.32 us
    ppermute x3, starting transfers between devices, beyond(): return lax.ppermute(value, ('shell', 'aux'), moves)  3.55 us
    pallas_call x1, Pallas kernels, exchanged_inputs(): pl.pallas_call(functools.partial(near_kernel, occ_local, aux_count), out_...  1.98 us
    pallas_call x1, Pallas kernels, exchanged_inputs(): pl.pallas_call(functools.partial(pick_kernel, [list(range(group, shell_co...  1.72 us
    pallas_call x1, Pallas kernels, exchanged_inputs(): pl.pallas_call(collect_kernel, out_shape=[jax.ShapeDtypeStruct((occ_local...  1.53 us
    ppermute x3, waiting for transfers between devices, beyond(): return lax.ppermute(value, ('shell', 'aux'), moves)  1.46 us
    pallas_call x1, Pallas kernels, exchanged_inputs(): pl.pallas_call(near_sum_kernel, out_shape=[total_shape, jax.ShapeDtypeStr...  1.35 us
  transfers between devices with their start and end apart: 12, of which 6 were waited for; matrix products, arithmetic and copies ran while one was open for 0% of the time, Pallas kernels for 18%

profile of v18, /device:TPU:0, one launch (start us, length us, event | category | flops | bytes accessed | tf_op | source)
XLA Modules:
  0.0 33.2 jit_solution(4960286337781883992)
XLA Ops:
  0.0 0.5 %collective-permute-start = (bf16[4,128,128]{2,1,0:T(8,128)(2,1)}, bf16[4,128,128]{2,1,0:T(8,128)(2,1)S(1)}, u32[]{:S(2)}, u32[]{:S(2)}) collective-permute-start(bf16[4,128,128]{2,1,0:T(8,128)(2,1)} %bitcast.2), channel_id=1, source_target_pairs={{0,1},{1,0},{2,3},{3,2},{4,5},{5,4},{6,7},{7,6},{8,9},{9,8},{10,11... | collective-permute-start | bytes 393224 | tf_op jit(solution)/shard_map/ppermute | solution.py:333
  0.5 3.6 %collective-permute-start.1 = (bf16[4,128,128]{2,1,0:T(8,128)(2,1)}, bf16[4,128,128]{2,1,0:T(8,128)(2,1)S(1)}, u32[]{:S(2)}, u32[]{:S(2)}) collective-permute-start(bf16[4,128,128]{2,1,0:T(8,128)(2,1)} %bitcast.3), channel_id=1, source_target_pairs={{0,16},{4,20},{8,24},{12,28},{16,0},{20,4},{24,8},{28,12},{1,17},{... | collective-permute-start | bytes 393224 | tf_op jit(solution)/shard_map/ppermute | solution.py:333
  4.0 2.0 %near_blocks.1 = (bf16[520,128]{1,0:T(8,128)(2,1)S(1)}, bf16[520,128]{1,0:T(8,128)(2,1)S(1)}, bf16[520,128]{1,0:T(8,128)(2,1)S(1)}, bf16[520,128]{1,0:T(8,128)(2,1)S(1)}) custom-call(s32[4,3]{1,0:T(4,128)} %pairs_in.3, s32[1,128]{1,0:T(1,128)} %bitcast.5, bf16[512,1024]{1,0:T(8,128)(2,1)} %coef_in.3, bf16[4,128,128]{2,1,0:T(8,128)(2,1)} %bitcast.4, ...), custom_call_target="tpu_custom_call" | custom-call | tf_op jit(solution)/shard_map/near_blocks/pallas_call | solution.py:392
  6.0 1.6 %collective-permute-start.5 = (bf16[520,128]{1,0:T(8,128)(2,1)S(1)}, bf16[520,128]{1,0:T(8,128)(2,1)S(1)}, u32[]{:S(2)}, u32[]{:S(2)}) collective-permute-start(bf16[520,128]{1,0:T(8,128)(2,1)S(1)} %get-tuple-element.35), channel_id=1, source_target_pairs={{0,4},{1,5},{2,6},{3,7},{4,0},{5,1},{6,2},{7,3},{8,12},{9,13},{10,... | collective-permute-start | bytes 399368 | tf_op jit(solution)/shard_map/ppermute | solution.py:343
  7.6 1.5 %collective-permute-start.6 = (bf16[520,128]{1,0:T(8,128)(2,1)S(1)}, bf16[520,128]{1,0:T(8,128)(2,1)S(1)}, u32[]{:S(2)}, u32[]{:S(2)}) collective-permute-start(bf16[520,128]{1,0:T(8,128)(2,1)S(1)} %get-tuple-element.37), channel_id=1, source_target_pairs={{0,2},{1,3},{2,0},{3,1},{4,6},{5,7},{6,4},{7,5},{8,10},{9,11},{10,... | collective-permute-start | bytes 399368 | tf_op jit(solution)/shard_map/ppermute | solution.py:343
  9.1 0.5 %collective-permute-start.7 = (bf16[520,128]{1,0:T(8,128)(2,1)S(1)}, bf16[520,128]{1,0:T(8,128)(2,1)S(1)}, u32[]{:S(2)}, u32[]{:S(2)}) collective-permute-start(bf16[520,128]{1,0:T(8,128)(2,1)S(1)} %get-tuple-element.39), channel_id=1, source_target_pairs={{0,6},{1,7},{2,4},{3,5},{4,2},{5,3},{6,0},{7,1},{8,14},{9,15},{10,... | collective-permute-start | bytes 399368 | tf_op jit(solution)/shard_map/ppermute | solution.py:343
  9.6 1.7 %pick.1 = bf16[136,512]{1,0:T(8,128)(2,1)S(1)} custom-call(s32[4,3]{1,0:T(4,128)} %pairs_in.3, s32[1,128]{1,0:T(1,128)} %bitcast.6, bf16[512,1024]{1,0:T(8,128)(2,1)} %coef_in.3), custom_call_target="tpu_custom_call" | custom-call | tf_op jit(solution)/shard_map/pick/pallas_call | solution.py:403
  11.3 1.6 %collective-permute-start.3 = (bf16[4,128,128]{2,1,0:T(8,128)(2,1)S(1)}, bf16[4,128,128]{2,1,0:T(8,128)(2,1)S(1)}, u32[]{:S(2)}, u32[]{:S(2)}) collective-permute-start(bf16[4,128,128]{2,1,0:T(8,128)(2,1)S(1)} %collective-permute-done.1.first), channel_id=1, source_target_pairs={{0,2},{1,3},{2,0},{3,1},{4,6},{5,7},{6,4},{7,5},{8,10},{9,11},{10,... | collective-permute-start | bytes 393224 | tf_op jit(solution)/shard_map/ppermute | solution.py:333
  12.9 1.6 %collective-permute-start.2 = (bf16[136,512]{1,0:T(8,128)(2,1)S(1)}, bf16[136,512]{1,0:T(8,128)(2,1)S(1)}, u32[]{:S(2)}, u32[]{:S(2)}) collective-permute-start(bf16[136,512]{1,0:T(8,128)(2,1)S(1)} %pick.1), channel_id=1, source_target_pairs={{0,16},{4,20},{8,24},{12,28},{16,0},{20,4},{24,8},{28,12},{1,17},{... | collective-permute-start | bytes 417800 | tf_op jit(solution)/shard_map/ppermute | solution.py:333
  14.5 1.5 %collective-permute-done.6.refs_2_ = bf16[520,128]{1,0:T(8,128)(2,1)S(1)} collective-permute-done((bf16[520,128]{1,0:T(8,128)(2,1)S(1)}, bf16[520,128]{1,0:T(8,128)(2,1)S(1)}, u32[]{:S(2)}, u32[]{:S(2)}) %collective-permute-start.6) | collective-permute-done | bytes 133152 | tf_op jit(solution)/shard_map/ppermute | solution.py:343
  15.9 1.6 %collective-permute-start.8 = (bf16[1040,128]{1,0:T(8,128)(2,1)S(1)}, bf16[1040,128]{1,0:T(8,128)(2,1)S(1)}, u32[]{:S(2)}, u32[]{:S(2)}) collective-permute-start(bf16[1040,128]{1,0:T(8,128)(2,1)S(1)} %regroup.1), channel_id=1, source_target_pairs={{0,8},{4,12},{8,0},{12,4},{16,24},{20,28},{24,16},{28,20},{1,9},{5... | collective-permute-start | bytes 798728 | tf_op jit(solution)/shard_map/ppermute | solution.py:333
  17.6 1.1 %collective-permute-done.3.second = bf16[4,128,128]{2,1,0:T(8,128)(2,1)S(1)} collective-permute-done((bf16[4,128,128]{2,1,0:T(8,128)(2,1)S(1)}, bf16[4,128,128]{2,1,0:T(8,128)(2,1)S(1)}, u32[]{:S(2)}, u32[]{:S(2)}) %collective-permute-start.3) | collective-permute-done | bytes 131104 | tf_op jit(solution)/shard_map/ppermute | solution.py:333
  18.6 0.3 far_pair.1.blocks
  19.1 2.8 %collective-permute-done.2.coefs = bf16[136,512]{1,0:T(8,128)(2,1)S(1)} collective-permute-done((bf16[136,512]{1,0:T(8,128)(2,1)S(1)}, bf16[136,512]{1,0:T(8,128)(2,1)S(1)}, u32[]{:S(2)}, u32[]{:S(2)}) %collective-permute-start.2) | collective-permute-done | bytes 139296 | tf_op jit(solution)/shard_map/ppermute | solution.py:333
  21.8 0.2 far_blocks_0.1
  22.1 0.2 far_blocks_1.1
  22.3 1.5 %collective-permute-start.9 = (bf16[520,128]{1,0:T(8,128)(2,1)S(1)}, bf16[520,128]{1,0:T(8,128)(2,1)S(1)}, u32[]{:S(2)}, u32[]{:S(2)}) collective-permute-start(bf16[520,128]{1,0:T(8,128)(2,1)S(1)} %get-tuple-element.43), channel_id=1, source_target_pairs={{0,4},{4,0},{8,12},{12,8},{16,20},{20,16},{24,28},{28,24},{1,5},{5... | collective-permute-start | bytes 399368 | tf_op jit(solution)/shard_map/ppermute | solution.py:333
  23.8 0.1 collective-permute-start.10
  24.0 1.9 %collective-permute-start.11 = (bf16[520,128]{1,0:T(8,128)(2,1)S(1)}, bf16[520,128]{1,0:T(8,128)(2,1)S(1)}, u32[]{:S(2)}, u32[]{:S(2)}) collective-permute-start(bf16[520,128]{1,0:T(8,128)(2,1)S(1)} %get-tuple-element.45), channel_id=1, source_target_pairs={{0,12},{4,8},{8,4},{12,0},{16,28},{20,24},{24,20},{28,16},{1,13},{... | collective-permute-start | bytes 399368 | tf_op jit(solution)/shard_map/ppermute | solution.py:333
  25.8 1.3 %near_sum.1 = (f32[32,128,128]{2,1,0:T(8,128)S(1)}, bf16[128,128]{1,0:T(8,128)(2,1)S(1)}) custom-call(bf16[4,4]{1,0:T(4,128)(2,1)} %metric_in.1, bf16[520,128]{1,0:T(8,128)(2,1)S(1)} %get-tuple-element.34.refs_0_, bf16[520,128]{1,0:T(8,128)(2,1)S(1)} %collective-permute-done.5.refs_1_, bf16[520,128]{1,0:T(8,128)(2,1)S(1)} %collective-permute-done.6.refs_2_, ...), custom_call_target="tpu_custom_call" | custom-call | flops 3000000000 | bytes 1048576 | tf_op jit(solution)/shard_map/near_sum/pallas_call | solution.py:447
  27.2 0.6 %collective-permute-done.9.refs_1_ = bf16[520,128]{1,0:T(8,128)(2,1)S(1)} collective-permute-done((bf16[520,128]{1,0:T(8,128)(2,1)S(1)}, bf16[520,128]{1,0:T(8,128)(2,1)S(1)}, u32[]{:S(2)}, u32[]{:S(2)}) %collective-permute-start.9) | collective-permute-done | bytes 133152 | tf_op jit(solution)/shard_map/ppermute | solution.py:333
  27.8 1.5 %collective-permute-done.10.refs_2_ = bf16[520,128]{1,0:T(8,128)(2,1)S(1)} collective-permute-done((bf16[520,128]{1,0:T(8,128)(2,1)S(1)}, bf16[520,128]{1,0:T(8,128)(2,1)S(1)}, u32[]{:S(2)}, u32[]{:S(2)}) %collective-permute-start.10) | collective-permute-done | bytes 133152 | tf_op jit(solution)/shard_map/ppermute | solution.py:333
  29.3 2.4 %collective-permute-done.11.refs_3_ = bf16[520,128]{1,0:T(8,128)(2,1)S(1)} collective-permute-done((bf16[520,128]{1,0:T(8,128)(2,1)S(1)}, bf16[520,128]{1,0:T(8,128)(2,1)S(1)}, u32[]{:S(2)}, u32[]{:S(2)}) %collective-permute-start.11) | collective-permute-done | bytes 133152 | tf_op jit(solution)/shard_map/ppermute | solution.py:333
  31.7 1.5 %collect.1 = (bf16[32,4,4096]{2,1,0:T(4,128)(2,1)}, f32[32,128,128]{2,1,0:T(8,128)S(1)}) custom-call(bf16[128,128]{1,0:T(8,128)(2,1)S(1)} %get-tuple-element.41.mix, f32[32,128,128]{2,1,0:T(8,128)S(1)} %get-tuple-element.42.total_in, bf16[520,128]{1,0:T(8,128)(2,1)S(1)} %get-tuple-element.33.refs_0_, ...), custom_call_target="tpu_custom_call", output_to_operand_aliasing={{1}: (1, {})} | custom-call | tf_op jit(solution)/shard_map/collect/pallas_call | solution.py:462
  (8 shorter events, 0.1 us)
Async XLA Ops:
  0.0 4.0 %collective-permute-start = (bf16[4,128,128]{2,1,0:T(8,128)(2,1)}, bf16[4,128,128]{2,1,0:T(8,128)(2,1)S(1)}, u32[]{:S(2)}, u32[]{:S(2)}) collective-permute-start(bf16[4,128,128]{2,1,0:T(8,128)(2,1)} %bitcast.2), channel_id=1, source_target_pairs={{0,1},{1,0},{2,3},{3,2},{4,5},{5,4},{6,7},{7,6},{8,9},{9,8},{10,11... | collective-permute-start | bytes 393224 | tf_op jit(solution)/shard_map/ppermute | solution.py:333
  0.5 10.9 %collective-permute-start.1 = (bf16[4,128,128]{2,1,0:T(8,128)(2,1)}, bf16[4,128,128]{2,1,0:T(8,128)(2,1)S(1)}, u32[]{:S(2)}, u32[]{:S(2)}) collective-permute-start(bf16[4,128,128]{2,1,0:T(8,128)(2,1)} %bitcast.3), channel_id=1, source_target_pairs={{0,16},{4,20},{8,24},{12,28},{16,0},{20,4},{24,8},{28,12},{1,17},{... | collective-permute-start | bytes 393224 | tf_op jit(solution)/shard_map/ppermute | solution.py:333
  6.0 8.4 %collective-permute-start.5 = (bf16[520,128]{1,0:T(8,128)(2,1)S(1)}, bf16[520,128]{1,0:T(8,128)(2,1)S(1)}, u32[]{:S(2)}, u32[]{:S(2)}) collective-permute-start(bf16[520,128]{1,0:T(8,128)(2,1)S(1)} %get-tuple-element.35), channel_id=1, source_target_pairs={{0,4},{1,5},{2,6},{3,7},{4,0},{5,1},{6,2},{7,3},{8,12},{9,13},{10,... | collective-permute-start | bytes 399368 | tf_op jit(solution)/shard_map/ppermute | solution.py:343
  7.6 8.3 %collective-permute-start.6 = (bf16[520,128]{1,0:T(8,128)(2,1)S(1)}, bf16[520,128]{1,0:T(8,128)(2,1)S(1)}, u32[]{:S(2)}, u32[]{:S(2)}) collective-permute-start(bf16[520,128]{1,0:T(8,128)(2,1)S(1)} %get-tuple-element.37), channel_id=1, source_target_pairs={{0,2},{1,3},{2,0},{3,1},{4,6},{5,7},{6,4},{7,5},{8,10},{9,11},{10,... | collective-permute-start | bytes 399368 | tf_op jit(solution)/shard_map/ppermute | solution.py:343
  9.1 6.8 %collective-permute-start.7 = (bf16[520,128]{1,0:T(8,128)(2,1)S(1)}, bf16[520,128]{1,0:T(8,128)(2,1)S(1)}, u32[]{:S(2)}, u32[]{:S(2)}) collective-permute-start(bf16[520,128]{1,0:T(8,128)(2,1)S(1)} %get-tuple-element.39), channel_id=1, source_target_pairs={{0,6},{1,7},{2,4},{3,5},{4,2},{5,3},{6,0},{7,1},{8,14},{9,15},{10,... | collective-permute-start | bytes 399368 | tf_op jit(solution)/shard_map/ppermute | solution.py:343
  11.3 7.3 %collective-permute-start.3 = (bf16[4,128,128]{2,1,0:T(8,128)(2,1)S(1)}, bf16[4,128,128]{2,1,0:T(8,128)(2,1)S(1)}, u32[]{:S(2)}, u32[]{:S(2)}) collective-permute-start(bf16[4,128,128]{2,1,0:T(8,128)(2,1)S(1)} %collective-permute-done.1.first), channel_id=1, source_target_pairs={{0,2},{1,3},{2,0},{3,1},{4,6},{5,7},{6,4},{7,5},{8,10},{9,11},{10,... | collective-permute-start | bytes 393224 | tf_op jit(solution)/shard_map/ppermute | solution.py:333
  12.9 8.9 %collective-permute-start.2 = (bf16[136,512]{1,0:T(8,128)(2,1)S(1)}, bf16[136,512]{1,0:T(8,128)(2,1)S(1)}, u32[]{:S(2)}, u32[]{:S(2)}) collective-permute-start(bf16[136,512]{1,0:T(8,128)(2,1)S(1)} %pick.1), channel_id=1, source_target_pairs={{0,16},{4,20},{8,24},{12,28},{16,0},{20,4},{24,8},{28,12},{1,17},{... | collective-permute-start | bytes 417800 | tf_op jit(solution)/shard_map/ppermute | solution.py:333
  15.9 9.9 %collective-permute-start.8 = (bf16[1040,128]{1,0:T(8,128)(2,1)S(1)}, bf16[1040,128]{1,0:T(8,128)(2,1)S(1)}, u32[]{:S(2)}, u32[]{:S(2)}) collective-permute-start(bf16[1040,128]{1,0:T(8,128)(2,1)S(1)} %regroup.1), channel_id=1, source_target_pairs={{0,8},{4,12},{8,0},{12,4},{16,24},{20,28},{24,16},{28,20},{1,9},{5... | collective-permute-start | bytes 798728 | tf_op jit(solution)/shard_map/ppermute | solution.py:333
  19.0 3.1 %collective-permute-start.4 = (bf16[8,128,128]{2,1,0:T(8,128)(2,1)S(1)}, bf16[8,128,128]{2,1,0:T(8,128)(2,1)S(1)}, u32[]{:S(2)}, u32[]{:S(2)}) collective-permute-start(bf16[8,128,128]{2,1,0:T(8,128)(2,1)S(1)} %far_pair.1.blocks), channel_id=1, source_target_pairs={{0,1},{1,0},{2,3},{3,2},{4,5},{5,4},{6,7},{7,6},{8,9},{9,8},{10,11... | collective-permute-start | bytes 786440 | tf_op jit(solution)/shard_map/ppermute | solution.py:333
  22.3 5.5 %collective-permute-start.9 = (bf16[520,128]{1,0:T(8,128)(2,1)S(1)}, bf16[520,128]{1,0:T(8,128)(2,1)S(1)}, u32[]{:S(2)}, u32[]{:S(2)}) collective-permute-start(bf16[520,128]{1,0:T(8,128)(2,1)S(1)} %get-tuple-element.43), channel_id=1, source_target_pairs={{0,4},{4,0},{8,12},{12,8},{16,20},{20,16},{24,28},{28,24},{1,5},{5... | collective-permute-start | bytes 399368 | tf_op jit(solution)/shard_map/ppermute | solution.py:333
  23.8 5.4 %collective-permute-start.10 = (bf16[520,128]{1,0:T(8,128)(2,1)S(1)}, bf16[520,128]{1,0:T(8,128)(2,1)S(1)}, u32[]{:S(2)}, u32[]{:S(2)}) collective-permute-start(bf16[520,128]{1,0:T(8,128)(2,1)S(1)} %get-tuple-element.44), channel_id=1, source_target_pairs={{0,8},{4,12},{8,0},{12,4},{16,24},{20,28},{24,16},{28,20},{1,9},{5... | collective-permute-start | bytes 399368 | tf_op jit(solution)/shard_map/ppermute | solution.py:333
  24.0 7.7 %collective-permute-start.11 = (bf16[520,128]{1,0:T(8,128)(2,1)S(1)}, bf16[520,128]{1,0:T(8,128)(2,1)S(1)}, u32[]{:S(2)}, u32[]{:S(2)}) collective-permute-start(bf16[520,128]{1,0:T(8,128)(2,1)S(1)} %get-tuple-element.45), channel_id=1, source_target_pairs={{0,12},{4,8},{8,4},{12,0},{16,28},{20,24},{24,20},{28,16},{1,13},{... | collective-permute-start | bytes 399368 | tf_op jit(solution)/shard_map/ppermute | solution.py:333

commit v19 on v18

--- a/solution.py
+++ b/solution.py
@@ -475,7 +475,7 @@
         ],
         compiler_params=params,
         name="collect",
-    )(mix, total, *far)[0]
+    )(mix, total, *reversed(far))[0]
 
 
 def per_device(integrals, pair_list, coef, metric, occ_slot):

time: 33.4 us -> 32.7 us (0.979)
  waiting for transfers between devices: 9.78 us -> 9.05 us
    ppermute x9, waiting for transfers between devices: 8.32 us -> 7.59 us  [flip(): return lax.ppermute(value, axis, [(at, at ^ bits) for at in range(count)])]
where the time goes in v19:
time: 32.7 us; the launch traced here: 32.5 us
  starting transfers between devices  16 us (49%)
  waiting for transfers between devices  9.05 us (28%)
  Pallas kernels  7.36 us (23%)
    ppermute x9, starting transfers between devices, flip(): return lax.ppermute(value, axis, [(at, at ^ bits) for at in range(count)])  12.5 us
    ppermute x9, waiting for transfers between devices, flip(): return lax.ppermute(value, axis, [(at, at ^ bits) for at in range(count)])  7.59 us
    ppermute x3, starting transfers between devices, beyond(): return lax.ppermute(value, ('shell', 'aux'), moves)  3.55 us
    pallas_call x1, Pallas kernels, exchanged_inputs(): pl.pallas_call(functools.partial(near_kernel, occ_local, aux_count), out_...  1.98 us
    pallas_call x1, Pallas kernels, exchanged_inputs(): pl.pallas_call(functools.partial(pick_kernel, [list(range(group, shell_co...  1.72 us
    pallas_call x1, Pallas kernels, exchanged_inputs(): pl.pallas_call(collect_kernel, out_shape=[jax.ShapeDtypeStruct((occ_local...  1.53 us
    ppermute x3, waiting for transfers between devices, beyond(): return lax.ppermute(value, ('shell', 'aux'), moves)  1.46 us
    pallas_call x1, Pallas kernels, exchanged_inputs(): pl.pallas_call(near_sum_kernel, out_shape=[total_shape, jax.ShapeDtypeStr...  1.35 us
  transfers between devices with their start and end apart: 12, of which 6 were waited for; matrix products, arithmetic and copies ran while one was open for 0% of the time, Pallas kernels for 18%

profile of v19, /device:TPU:0, one launch (start us, length us, event | category | flops | bytes accessed | tf_op | source)
XLA Modules:
  0.0 32.5 jit_solution(17107396170284702049)
XLA Ops:
  0.0 0.5 %collective-permute-start = (bf16[4,128,128]{2,1,0:T(8,128)(2,1)}, bf16[4,128,128]{2,1,0:T(8,128)(2,1)S(1)}, u32[]{:S(2)}, u32[]{:S(2)}) collective-permute-start(bf16[4,128,128]{2,1,0:T(8,128)(2,1)} %bitcast.2), channel_id=1, source_target_pairs={{0,1},{1,0},{2,3},{3,2},{4,5},{5,4},{6,7},{7,6},{8,9},{9,8},{10,11... | collective-permute-start | bytes 393224 | tf_op jit(solution)/shard_map/ppermute | solution.py:333
  0.5 3.6 %collective-permute-start.1 = (bf16[4,128,128]{2,1,0:T(8,128)(2,1)}, bf16[4,128,128]{2,1,0:T(8,128)(2,1)S(1)}, u32[]{:S(2)}, u32[]{:S(2)}) collective-permute-start(bf16[4,128,128]{2,1,0:T(8,128)(2,1)} %bitcast.3), channel_id=1, source_target_pairs={{0,16},{4,20},{8,24},{12,28},{16,0},{20,4},{24,8},{28,12},{1,17},{... | collective-permute-start | bytes 393224 | tf_op jit(solution)/shard_map/ppermute | solution.py:333
  4.0 2.0 %near_blocks.1 = (bf16[520,128]{1,0:T(8,128)(2,1)S(1)}, bf16[520,128]{1,0:T(8,128)(2,1)S(1)}, bf16[520,128]{1,0:T(8,128)(2,1)S(1)}, bf16[520,128]{1,0:T(8,128)(2,1)S(1)}) custom-call(s32[4,3]{1,0:T(4,128)} %pairs_in.3, s32[1,128]{1,0:T(1,128)} %bitcast.5, bf16[512,1024]{1,0:T(8,128)(2,1)} %coef_in.3, bf16[4,128,128]{2,1,0:T(8,128)(2,1)} %bitcast.4, ...), custom_call_target="tpu_custom_call" | custom-call | tf_op jit(solution)/shard_map/near_blocks/pallas_call | solution.py:392
  6.0 1.6 %collective-permute-start.5 = (bf16[520,128]{1,0:T(8,128)(2,1)S(1)}, bf16[520,128]{1,0:T(8,128)(2,1)S(1)}, u32[]{:S(2)}, u32[]{:S(2)}) collective-permute-start(bf16[520,128]{1,0:T(8,128)(2,1)S(1)} %get-tuple-element.35), channel_id=1, source_target_pairs={{0,4},{1,5},{2,6},{3,7},{4,0},{5,1},{6,2},{7,3},{8,12},{9,13},{10,... | collective-permute-start | bytes 399368 | tf_op jit(solution)/shard_map/ppermute | solution.py:343
  7.6 1.5 %collective-permute-start.6 = (bf16[520,128]{1,0:T(8,128)(2,1)S(1)}, bf16[520,128]{1,0:T(8,128)(2,1)S(1)}, u32[]{:S(2)}, u32[]{:S(2)}) collective-permute-start(bf16[520,128]{1,0:T(8,128)(2,1)S(1)} %get-tuple-element.37), channel_id=1, source_target_pairs={{0,2},{1,3},{2,0},{3,1},{4,6},{5,7},{6,4},{7,5},{8,10},{9,11},{10,... | collective-permute-start | bytes 399368 | tf_op jit(solution)/shard_map/ppermute | solution.py:343
  9.1 0.5 %collective-permute-start.7 = (bf16[520,128]{1,0:T(8,128)(2,1)S(1)}, bf16[520,128]{1,0:T(8,128)(2,1)S(1)}, u32[]{:S(2)}, u32[]{:S(2)}) collective-permute-start(bf16[520,128]{1,0:T(8,128)(2,1)S(1)} %get-tuple-element.39), channel_id=1, source_target_pairs={{0,6},{1,7},{2,4},{3,5},{4,2},{5,3},{6,0},{7,1},{8,14},{9,15},{10,... | collective-permute-start | bytes 399368 | tf_op jit(solution)/shard_map/ppermute | solution.py:343
  9.6 1.7 %pick.1 = bf16[136,512]{1,0:T(8,128)(2,1)S(1)} custom-call(s32[4,3]{1,0:T(4,128)} %pairs_in.3, s32[1,128]{1,0:T(1,128)} %bitcast.6, bf16[512,1024]{1,0:T(8,128)(2,1)} %coef_in.3), custom_call_target="tpu_custom_call" | custom-call | tf_op jit(solution)/shard_map/pick/pallas_call | solution.py:403
  11.3 1.6 %collective-permute-start.3 = (bf16[4,128,128]{2,1,0:T(8,128)(2,1)S(1)}, bf16[4,128,128]{2,1,0:T(8,128)(2,1)S(1)}, u32[]{:S(2)}, u32[]{:S(2)}) collective-permute-start(bf16[4,128,128]{2,1,0:T(8,128)(2,1)S(1)} %collective-permute-done.1.first), channel_id=1, source_target_pairs={{0,2},{1,3},{2,0},{3,1},{4,6},{5,7},{6,4},{7,5},{8,10},{9,11},{10,... | collective-permute-start | bytes 393224 | tf_op jit(solution)/shard_map/ppermute | solution.py:333
  12.9 1.6 %collective-permute-start.2 = (bf16[136,512]{1,0:T(8,128)(2,1)S(1)}, bf16[136,512]{1,0:T(8,128)(2,1)S(1)}, u32[]{:S(2)}, u32[]{:S(2)}) collective-permute-start(bf16[136,512]{1,0:T(8,128)(2,1)S(1)} %pick.1), channel_id=1, source_target_pairs={{0,16},{4,20},{8,24},{12,28},{16,0},{20,4},{24,8},{28,12},{1,17},{... | collective-permute-start | bytes 417800 | tf_op jit(solution)/shard_map/ppermute | solution.py:333
  14.5 1.5 %collective-permute-done.6.refs_2_ = bf16[520,128]{1,0:T(8,128)(2,1)S(1)} collective-permute-done((bf16[520,128]{1,0:T(8,128)(2,1)S(1)}, bf16[520,128]{1,0:T(8,128)(2,1)S(1)}, u32[]{:S(2)}, u32[]{:S(2)}) %collective-permute-start.6) | collective-permute-done | bytes 133152 | tf_op jit(solution)/shard_map/ppermute | solution.py:343
  15.9 1.6 %collective-permute-start.8 = (bf16[1040,128]{1,0:T(8,128)(2,1)S(1)}, bf16[1040,128]{1,0:T(8,128)(2,1)S(1)}, u32[]{:S(2)}, u32[]{:S(2)}) collective-permute-start(bf16[1040,128]{1,0:T(8,128)(2,1)S(1)} %regroup.1), channel_id=1, source_target_pairs={{0,8},{4,12},{8,0},{12,4},{16,24},{20,28},{24,16},{28,20},{1,9},{5... | collective-permute-start | bytes 798728 | tf_op jit(solution)/shard_map/ppermute | solution.py:333
  17.6 1.1 %collective-permute-done.3.second = bf16[4,128,128]{2,1,0:T(8,128)(2,1)S(1)} collective-permute-done((bf16[4,128,128]{2,1,0:T(8,128)(2,1)S(1)}, bf16[4,128,128]{2,1,0:T(8,128)(2,1)S(1)}, u32[]{:S(2)}, u32[]{:S(2)}) %collective-permute-start.3) | collective-permute-done | bytes 131104 | tf_op jit(solution)/shard_map/ppermute | solution.py:333
  18.6 0.3 %far_pair.1.blocks = bf16[8,128,128]{2,1,0:T(8,128)(2,1)S(1)} custom-call(bf16[4,128,128]{2,1,0:T(8,128)(2,1)S(1)} %collective-permute-done.1.first, bf16[4,128,128]{2,1,0:T(8,128)(2,1)S(1)} %collective-permute-done.3.second), custom_call_target="tpu_custom_call" | custom-call | tf_op jit(solution)/shard_map/far_pair/pallas_call | solution.py:372
  19.1 2.8 %collective-permute-done.2.coefs = bf16[136,512]{1,0:T(8,128)(2,1)S(1)} collective-permute-done((bf16[136,512]{1,0:T(8,128)(2,1)S(1)}, bf16[136,512]{1,0:T(8,128)(2,1)S(1)}, u32[]{:S(2)}, u32[]{:S(2)}) %collective-permute-start.2) | collective-permute-done | bytes 139296 | tf_op jit(solution)/shard_map/ppermute | solution.py:333
  21.8 0.2 far_blocks_0.1
  22.1 0.2 far_blocks_1.1
  22.3 1.1 %collective-permute-start.9 = (bf16[520,128]{1,0:T(8,128)(2,1)S(1)}, bf16[520,128]{1,0:T(8,128)(2,1)S(1)}, u32[]{:S(2)}, u32[]{:S(2)}) collective-permute-start(bf16[520,128]{1,0:T(8,128)(2,1)S(1)} %get-tuple-element.43), channel_id=1, source_target_pairs={{0,12},{4,8},{8,4},{12,0},{16,28},{20,24},{24,20},{28,16},{1,13},{... | collective-permute-start | bytes 399368 | tf_op jit(solution)/shard_map/ppermute | solution.py:333
  23.4 1.9 %collective-permute-start.10 = (bf16[520,128]{1,0:T(8,128)(2,1)S(1)}, bf16[520,128]{1,0:T(8,128)(2,1)S(1)}, u32[]{:S(2)}, u32[]{:S(2)}) collective-permute-start(bf16[520,128]{1,0:T(8,128)(2,1)S(1)} %get-tuple-element.44), channel_id=1, source_target_pairs={{0,8},{4,12},{8,0},{12,4},{16,24},{20,28},{24,16},{28,20},{1,9},{5... | collective-permute-start | bytes 399368 | tf_op jit(solution)/shard_map/ppermute | solution.py:333
  25.3 0.5 %collective-permute-start.11 = (bf16[520,128]{1,0:T(8,128)(2,1)S(1)}, bf16[520,128]{1,0:T(8,128)(2,1)S(1)}, u32[]{:S(2)}, u32[]{:S(2)}) collective-permute-start(bf16[520,128]{1,0:T(8,128)(2,1)S(1)} %get-tuple-element.45), channel_id=1, source_target_pairs={{0,4},{4,0},{8,12},{12,8},{16,20},{20,16},{24,28},{28,24},{1,5},{5... | collective-permute-start | bytes 399368 | tf_op jit(solution)/shard_map/ppermute | solution.py:333
  25.8 1.3 %near_sum.1 = (f32[32,128,128]{2,1,0:T(8,128)S(1)}, bf16[128,128]{1,0:T(8,128)(2,1)S(1)}) custom-call(bf16[4,4]{1,0:T(4,128)(2,1)} %metric_in.1, bf16[520,128]{1,0:T(8,128)(2,1)S(1)} %get-tuple-element.34.refs_0_, bf16[520,128]{1,0:T(8,128)(2,1)S(1)} %collective-permute-done.5.refs_1_, bf16[520,128]{1,0:T(8,128)(2,1)S(1)} %collective-permute-done.6.refs_2_, ...), custom_call_target="tpu_custom_call" | custom-call | flops 3000000000 | bytes 1048576 | tf_op jit(solution)/shard_map/near_sum/pallas_call | solution.py:447
  27.2 3.0 %collective-permute-done.9.refs_0_ = bf16[520,128]{1,0:T(8,128)(2,1)S(1)} collective-permute-done((bf16[520,128]{1,0:T(8,128)(2,1)S(1)}, bf16[520,128]{1,0:T(8,128)(2,1)S(1)}, u32[]{:S(2)}, u32[]{:S(2)}) %collective-permute-start.9) | collective-permute-done | bytes 133152 | tf_op jit(solution)/shard_map/ppermute | solution.py:333
  30.2 0.4 %collective-permute-done.10.refs_1_ = bf16[520,128]{1,0:T(8,128)(2,1)S(1)} collective-permute-done((bf16[520,128]{1,0:T(8,128)(2,1)S(1)}, bf16[520,128]{1,0:T(8,128)(2,1)S(1)}, u32[]{:S(2)}, u32[]{:S(2)}) %collective-permute-start.10) | collective-permute-done | bytes 133152 | tf_op jit(solution)/shard_map/ppermute | solution.py:333
  30.6 0.3 %collective-permute-done.11.refs_2_ = bf16[520,128]{1,0:T(8,128)(2,1)S(1)} collective-permute-done((bf16[520,128]{1,0:T(8,128)(2,1)S(1)}, bf16[520,128]{1,0:T(8,128)(2,1)S(1)}, u32[]{:S(2)}, u32[]{:S(2)}) %collective-permute-start.11) | collective-permute-done | bytes 133152 | tf_op jit(solution)/shard_map/ppermute | solution.py:333
  31.0 1.5 %collect.1 = (bf16[32,4,4096]{2,1,0:T(4,128)(2,1)}, f32[32,128,128]{2,1,0:T(8,128)S(1)}) custom-call(bf16[128,128]{1,0:T(8,128)(2,1)S(1)} %get-tuple-element.41.mix, f32[32,128,128]{2,1,0:T(8,128)S(1)} %get-tuple-element.42.total_in, bf16[520,128]{1,0:T(8,128)(2,1)S(1)} %collective-permute-done.9.refs_0_, ...), custom_call_target="tpu_custom_call", output_to_operand_aliasing={{1}: (1, {})} | custom-call | tf_op jit(solution)/shard_map/collect/pallas_call | solution.py:462
  (8 shorter events, 0.1 us)
Async XLA Ops:
  0.0 4.0 %collective-permute-start = (bf16[4,128,128]{2,1,0:T(8,128)(2,1)}, bf16[4,128,128]{2,1,0:T(8,128)(2,1)S(1)}, u32[]{:S(2)}, u32[]{:S(2)}) collective-permute-start(bf16[4,128,128]{2,1,0:T(8,128)(2,1)} %bitcast.2), channel_id=1, source_target_pairs={{0,1},{1,0},{2,3},{3,2},{4,5},{5,4},{6,7},{7,6},{8,9},{9,8},{10,11... | collective-permute-start | bytes 393224 | tf_op jit(solution)/shard_map/ppermute | solution.py:333
  0.5 10.9 %collective-permute-start.1 = (bf16[4,128,128]{2,1,0:T(8,128)(2,1)}, bf16[4,128,128]{2,1,0:T(8,128)(2,1)S(1)}, u32[]{:S(2)}, u32[]{:S(2)}) collective-permute-start(bf16[4,128,128]{2,1,0:T(8,128)(2,1)} %bitcast.3), channel_id=1, source_target_pairs={{0,16},{4,20},{8,24},{12,28},{16,0},{20,4},{24,8},{28,12},{1,17},{... | collective-permute-start | bytes 393224 | tf_op jit(solution)/shard_map/ppermute | solution.py:333
  6.0 8.4 %collective-permute-start.5 = (bf16[520,128]{1,0:T(8,128)(2,1)S(1)}, bf16[520,128]{1,0:T(8,128)(2,1)S(1)}, u32[]{:S(2)}, u32[]{:S(2)}) collective-permute-start(bf16[520,128]{1,0:T(8,128)(2,1)S(1)} %get-tuple-element.35), channel_id=1, source_target_pairs={{0,4},{1,5},{2,6},{3,7},{4,0},{5,1},{6,2},{7,3},{8,12},{9,13},{10,... | collective-permute-start | bytes 399368 | tf_op jit(solution)/shard_map/ppermute | solution.py:343
  7.6 8.3 %collective-permute-start.6 = (bf16[520,128]{1,0:T(8,128)(2,1)S(1)}, bf16[520,128]{1,0:T(8,128)(2,1)S(1)}, u32[]{:S(2)}, u32[]{:S(2)}) collective-permute-start(bf16[520,128]{1,0:T(8,128)(2,1)S(1)} %get-tuple-element.37), channel_id=1, source_target_pairs={{0,2},{1,3},{2,0},{3,1},{4,6},{5,7},{6,4},{7,5},{8,10},{9,11},{10,... | collective-permute-start | bytes 399368 | tf_op jit(solution)/shard_map/ppermute | solution.py:343
  9.1 6.8 %collective-permute-start.7 = (bf16[520,128]{1,0:T(8,128)(2,1)S(1)}, bf16[520,128]{1,0:T(8,128)(2,1)S(1)}, u32[]{:S(2)}, u32[]{:S(2)}) collective-permute-start(bf16[520,128]{1,0:T(8,128)(2,1)S(1)} %get-tuple-element.39), channel_id=1, source_target_pairs={{0,6},{1,7},{2,4},{3,5},{4,2},{5,3},{6,0},{7,1},{8,14},{9,15},{10,... | collective-permute-start | bytes 399368 | tf_op jit(solution)/shard_map/ppermute | solution.py:343
  11.3 7.3 %collective-permute-start.3 = (bf16[4,128,128]{2,1,0:T(8,128)(2,1)S(1)}, bf16[4,128,128]{2,1,0:T(8,128)(2,1)S(1)}, u32[]{:S(2)}, u32[]{:S(2)}) collective-permute-start(bf16[4,128,128]{2,1,0:T(8,128)(2,1)S(1)} %collective-permute-done.1.first), channel_id=1, source_target_pairs={{0,2},{1,3},{2,0},{3,1},{4,6},{5,7},{6,4},{7,5},{8,10},{9,11},{10,... | collective-permute-start | bytes 393224 | tf_op jit(solution)/shard_map/ppermute | solution.py:333
  12.9 8.9 %collective-permute-start.2 = (bf16[136,512]{1,0:T(8,128)(2,1)S(1)}, bf16[136,512]{1,0:T(8,128)(2,1)S(1)}, u32[]{:S(2)}, u32[]{:S(2)}) collective-permute-start(bf16[136,512]{1,0:T(8,128)(2,1)S(1)} %pick.1), channel_id=1, source_target_pairs={{0,16},{4,20},{8,24},{12,28},{16,0},{20,4},{24,8},{28,12},{1,17},{... | collective-permute-start | bytes 417800 | tf_op jit(solution)/shard_map/ppermute | solution.py:333
  15.9 9.9 %collective-permute-start.8 = (bf16[1040,128]{1,0:T(8,128)(2,1)S(1)}, bf16[1040,128]{1,0:T(8,128)(2,1)S(1)}, u32[]{:S(2)}, u32[]{:S(2)}) collective-permute-start(bf16[1040,128]{1,0:T(8,128)(2,1)S(1)} %regroup.1), channel_id=1, source_target_pairs={{0,8},{4,12},{8,0},{12,4},{16,24},{20,28},{24,16},{28,20},{1,9},{5... | collective-permute-start | bytes 798728 | tf_op jit(solution)/shard_map/ppermute | solution.py:333
  19.0 3.1 %collective-permute-start.4 = (bf16[8,128,128]{2,1,0:T(8,128)(2,1)S(1)}, bf16[8,128,128]{2,1,0:T(8,128)(2,1)S(1)}, u32[]{:S(2)}, u32[]{:S(2)}) collective-permute-start(bf16[8,128,128]{2,1,0:T(8,128)(2,1)S(1)} %far_pair.1.blocks), channel_id=1, source_target_pairs={{0,1},{1,0},{2,3},{3,2},{4,5},{5,4},{6,7},{7,6},{8,9},{9,8},{10,11... | collective-permute-start | bytes 786440 | tf_op jit(solution)/shard_map/ppermute | solution.py:333
  22.3 8.0 %collective-permute-start.9 = (bf16[520,128]{1,0:T(8,128)(2,1)S(1)}, bf16[520,128]{1,0:T(8,128)(2,1)S(1)}, u32[]{:S(2)}, u32[]{:S(2)}) collective-permute-start(bf16[520,128]{1,0:T(8,128)(2,1)S(1)} %get-tuple-element.43), channel_id=1, source_target_pairs={{0,12},{4,8},{8,4},{12,0},{16,28},{20,24},{24,20},{28,16},{1,13},{... | collective-permute-start | bytes 399368 | tf_op jit(solution)/shard_map/ppermute | solution.py:333
  23.4 7.2 %collective-permute-start.10 = (bf16[520,128]{1,0:T(8,128)(2,1)S(1)}, bf16[520,128]{1,0:T(8,128)(2,1)S(1)}, u32[]{:S(2)}, u32[]{:S(2)}) collective-permute-start(bf16[520,128]{1,0:T(8,128)(2,1)S(1)} %get-tuple-element.44), channel_id=1, source_target_pairs={{0,8},{4,12},{8,0},{12,4},{16,24},{20,28},{24,16},{28,20},{1,9},{5... | collective-permute-start | bytes 399368 | tf_op jit(solution)/shard_map/ppermute | solution.py:333
  25.3 5.7 %collective-permute-start.11 = (bf16[520,128]{1,0:T(8,128)(2,1)S(1)}, bf16[520,128]{1,0:T(8,128)(2,1)S(1)}, u32[]{:S(2)}, u32[]{:S(2)}) collective-permute-start(bf16[520,128]{1,0:T(8,128)(2,1)S(1)} %get-tuple-element.45), channel_id=1, source_target_pairs={{0,4},{4,0},{8,12},{12,8},{16,20},{20,16},{24,28},{28,24},{1,5},{5... | collective-permute-start | bytes 399368 | tf_op jit(solution)/shard_map/ppermute | solution.py:333

commit v20 on v16

--- a/solution.py
+++ b/solution.py
@@ -8,6 +8,7 @@
 from jax.sharding import PartitionSpec as P
 
 BS = 128
+TILE = 8
 
 
 def relayed_half_blocks(integrals, pair_list, coef, metric, occ_slot):
@@ -83,7 +84,7 @@
     for k in range(pairs_dev):
         code = jnp.where(lane == k, pairs[k, 0] % 128, code)
         code = jnp.where(lane == pairs_dev + k, pairs[k, 0] // 128, code)
-    return jnp.broadcast_to(code.astype(jnp.float32), (16, BS)).astype(jnp.bfloat16)
+    return jnp.broadcast_to(code.astype(jnp.float32), (TILE, BS)).astype(jnp.bfloat16)
 
 
 def pick_kernel(
@@ -131,7 +132,7 @@
         piece = (piece * live).astype(jnp.bfloat16)
         first = 0
         for out in outs:
-            rows = out.shape[0] - 16
+            rows = out.shape[0] - TILE
             out[:rows, k * BS : (k + 1) * BS] = piece[first : first + rows]
             out[rows:, k * BS : (k + 1) * BS] = code
             first += rows
@@ -199,7 +200,7 @@
                         first : first + occ_local, c * BS : (c + 1) * BS
                     ]
     for out in outs:
-        out[out.shape[0] - 16 :, :] = code
+        out[out.shape[0] - TILE :, :] = code
 
 
 def regroup_kernel(*refs):
@@ -225,7 +226,7 @@
 def block_kernel(aux_count, low, coefs, blocks, *refs):
     pieces = refs[len(refs) // 2 :] if low else refs
     pairs_dev = blocks.shape[0] // 2
-    rows = coefs.shape[0] - 16
+    rows = coefs.shape[0] - TILE
     occ_local = rows // len(pieces)
     mine = lax.axis_index("aux")
     for k in range(pairs_dev):
@@ -247,7 +248,7 @@
 
 def read_codes(received, pairs_dev, codes):
     for at, piece in enumerate(received):
-        digits = piece[piece.shape[0] - 16 :, :].astype(jnp.float32)[:1]
+        digits = piece[piece.shape[0] - TILE :, :].astype(jnp.float32)[:1]
         high = pltpu.roll(digits, BS - pairs_dev, 1)
         codes[at : at + 1, :] = (digits + 128.0 * high).astype(jnp.int32)
 
@@ -260,7 +261,7 @@
     mine = lax.axis_index("aux")
     rows = total.shape[1]
     occ_local = rows // metric.shape[0]
-    pairs_dev = (received[0].shape[0] - 16) // rows
+    pairs_dev = (received[0].shape[0] - TILE) // rows
     read_codes(received, pairs_dev, codes)
     for f, piece in enumerate(received):
         for k in range(pairs_dev):
@@ -292,7 +293,7 @@
     *received, out, total, staged, codes, sems = refs
     occ_local, aux_count = out.shape[:2]
     rows = total.shape[1]
-    pairs_dev = (received[0].shape[0] - 16) // rows
+    pairs_dev = (received[0].shape[0] - TILE) // rows
     read_codes(received, pairs_dev, codes)
     for at, piece in enumerate(received):
         for k in range(pairs_dev):
@@ -341,7 +342,7 @@
     occ_local = coef.shape[1] // (shell_count * aux_count)
     block_count = coef.shape[0] // BS * shell_count
     rows = occ_local * aux_count
-    piece = jax.ShapeDtypeStruct((pairs_dev * rows + 16, BS), jnp.bfloat16)
+    piece = jax.ShapeDtypeStruct((pairs_dev * rows + TILE, BS), jnp.bfloat16)
     vmem = pl.BlockSpec(memory_space=pltpu.VMEM)
     hbm = pl.BlockSpec(memory_space=pltpu.HBM)
     params = pltpu.CompilerParams(vmem_limit_bytes=40 * 2**20)
@@ -383,7 +384,7 @@
             pick_kernel, [list(range(group, shell_count))], occ_local, aux_count
         ),
         out_shape=[
-            jax.ShapeDtypeStruct((group * occ_local + 16, pairs_dev * BS), jnp.bfloat16)
+            jax.ShapeDtypeStruct((group * occ_local + TILE, pairs_dev * BS), jnp.bfloat16)
         ],
         in_specs=[hbm] * 3,
         out_specs=[vmem],
@@ -453,7 +454,7 @@
         ],
         compiler_params=params,
         name="collect",
-    )(mix, total, *far)[0]
+    )(mix, total, *reversed(far))[0]
 
 
 def per_device(integrals, pair_list, coef, metric, occ_slot):

time: 32.9 us -> 32.1 us (0.976)
  waiting for transfers between devices: 9.27 us -> 8.52 us
    ppermute x12, waiting for transfers between devices: 9.27 us -> 8.52 us  [flip(): return lax.ppermute(value, axis, [(at, at ^ bits) for at in range(count)])]
  transfers between devices with their start and end apart: 12 -> 12, of which waited for: 7 -> 6; matrix products, arithmetic and copies ran while one was open for 0% -> 0% of each run, Pallas kernels for 18% -> 18%
where the time goes in v20:
time: 32.1 us; the launch traced here: 31.9 us
  starting transfers between devices  15.9 us (50%)
  waiting for transfers between devices  8.52 us (27%)
  Pallas kernels  7.38 us (23%)
    ppermute x12, starting transfers between devices, flip(): return lax.ppermute(value, axis, [(at, at ^ bits) for at in range(count)])  15.9 us
    ppermute x12, waiting for transfers between devices, flip(): return lax.ppermute(value, axis, [(at, at ^ bits) for at in range(count)])  8.52 us
    pallas_call x1, Pallas kernels, exchanged_inputs(): pl.pallas_call(functools.partial(near_kernel, occ_local, aux_count), out_...  1.98 us
    pallas_call x1, Pallas kernels, exchanged_inputs(): pl.pallas_call(functools.partial(pick_kernel, [list(range(group, shell_co...  1.72 us
    pallas_call x1, Pallas kernels, exchanged_inputs(): pl.pallas_call(collect_kernel, out_shape=[jax.ShapeDtypeStruct((occ_local...  1.53 us
    pallas_call x1, Pallas kernels, exchanged_inputs(): pl.pallas_call(near_sum_kernel, out_shape=[total_shape, jax.ShapeDtypeStr...  1.37 us
  transfers between devices with their start and end apart: 12, of which 6 were waited for; matrix products, arithmetic and copies ran while one was open for 0% of the time, Pallas kernels for 18%

profile of v20, /device:TPU:0, one launch (start us, length us, event | category | flops | bytes accessed | tf_op | source)
XLA Modules:
  0.0 31.9 jit_solution(12193547477105824259)
XLA Ops:
  0.0 0.5 %collective-permute-start = (bf16[4,128,128]{2,1,0:T(8,128)(2,1)}, bf16[4,128,128]{2,1,0:T(8,128)(2,1)S(1)}, u32[]{:S(2)}, u32[]{:S(2)}) collective-permute-start(bf16[4,128,128]{2,1,0:T(8,128)(2,1)} %bitcast.2), channel_id=1, source_target_pairs={{0,1},{1,0},{2,3},{3,2},{4,5},{5,4},{6,7},{7,6},{8,9},{9,8},{10,11... | collective-permute-start | bytes 393224 | tf_op jit(solution)/shard_map/ppermute | solution.py:322
  0.5 3.6 %collective-permute-start.1 = (bf16[4,128,128]{2,1,0:T(8,128)(2,1)}, bf16[4,128,128]{2,1,0:T(8,128)(2,1)S(1)}, u32[]{:S(2)}, u32[]{:S(2)}) collective-permute-start(bf16[4,128,128]{2,1,0:T(8,128)(2,1)} %bitcast.3), channel_id=1, source_target_pairs={{0,16},{4,20},{8,24},{12,28},{16,0},{20,4},{24,8},{28,12},{1,17},{... | collective-permute-start | bytes 393224 | tf_op jit(solution)/shard_map/ppermute | solution.py:322
  4.0 2.0 %near_blocks.1 = (bf16[520,128]{1,0:T(8,128)(2,1)S(1)}, bf16[520,128]{1,0:T(8,128)(2,1)S(1)}, bf16[520,128]{1,0:T(8,128)(2,1)S(1)}, bf16[520,128]{1,0:T(8,128)(2,1)S(1)}) custom-call(s32[4,3]{1,0:T(4,128)} %pairs_in.3, s32[1,128]{1,0:T(1,128)} %bitcast.5, bf16[512,1024]{1,0:T(8,128)(2,1)} %coef_in.3, bf16[4,128,128]{2,1,0:T(8,128)(2,1)} %bitcast.4, ...), custom_call_target="tpu_custom_call" | custom-call | tf_op jit(solution)/shard_map/near_blocks/pallas_call | solution.py:371
  6.0 1.6 %collective-permute-start.5 = (bf16[520,128]{1,0:T(8,128)(2,1)S(1)}, bf16[520,128]{1,0:T(8,128)(2,1)S(1)}, u32[]{:S(2)}, u32[]{:S(2)}) collective-permute-start(bf16[520,128]{1,0:T(8,128)(2,1)S(1)} %get-tuple-element.35), channel_id=1, source_target_pairs={{0,4},{4,0},{8,12},{12,8},{16,20},{20,16},{24,28},{28,24},{1,5},{5... | collective-permute-start | bytes 399368 | tf_op jit(solution)/shard_map/ppermute | solution.py:322
  7.6 1.6 %collective-permute-start.6 = (bf16[520,128]{1,0:T(8,128)(2,1)S(1)}, bf16[520,128]{1,0:T(8,128)(2,1)S(1)}, u32[]{:S(2)}, u32[]{:S(2)}) collective-permute-start(bf16[520,128]{1,0:T(8,128)(2,1)S(1)} %get-tuple-element.37), channel_id=1, source_target_pairs={{0,8},{4,12},{8,0},{12,4},{16,24},{20,28},{24,16},{28,20},{1,9},{5... | collective-permute-start | bytes 399368 | tf_op jit(solution)/shard_map/ppermute | solution.py:322
  9.2 0.4 %collective-permute-start.7 = (bf16[520,128]{1,0:T(8,128)(2,1)S(1)}, bf16[520,128]{1,0:T(8,128)(2,1)S(1)}, u32[]{:S(2)}, u32[]{:S(2)}) collective-permute-start(bf16[520,128]{1,0:T(8,128)(2,1)S(1)} %get-tuple-element.39), channel_id=1, source_target_pairs={{0,12},{4,8},{8,4},{12,0},{16,28},{20,24},{24,20},{28,16},{1,13},{... | collective-permute-start | bytes 399368 | tf_op jit(solution)/shard_map/ppermute | solution.py:322
  9.6 1.7 %pick.1 = bf16[136,512]{1,0:T(8,128)(2,1)S(1)} custom-call(s32[4,3]{1,0:T(4,128)} %pairs_in.3, s32[1,128]{1,0:T(1,128)} %bitcast.6, bf16[512,1024]{1,0:T(8,128)(2,1)} %coef_in.3), custom_call_target="tpu_custom_call" | custom-call | tf_op jit(solution)/shard_map/pick/pallas_call | solution.py:382
  11.3 1.6 %collective-permute-start.3 = (bf16[4,128,128]{2,1,0:T(8,128)(2,1)S(1)}, bf16[4,128,128]{2,1,0:T(8,128)(2,1)S(1)}, u32[]{:S(2)}, u32[]{:S(2)}) collective-permute-start(bf16[4,128,128]{2,1,0:T(8,128)(2,1)S(1)} %collective-permute-done.1.first), channel_id=1, source_target_pairs={{0,2},{1,3},{2,0},{3,1},{4,6},{5,7},{6,4},{7,5},{8,10},{9,11},{10,... | collective-permute-start | bytes 393224 | tf_op jit(solution)/shard_map/ppermute | solution.py:322
  12.9 1.6 %collective-permute-start.2 = (bf16[136,512]{1,0:T(8,128)(2,1)S(1)}, bf16[136,512]{1,0:T(8,128)(2,1)S(1)}, u32[]{:S(2)}, u32[]{:S(2)}) collective-permute-start(bf16[136,512]{1,0:T(8,128)(2,1)S(1)} %pick.1), channel_id=1, source_target_pairs={{0,16},{4,20},{8,24},{12,28},{16,0},{20,4},{24,8},{28,12},{1,17},{... | collective-permute-start | bytes 417800 | tf_op jit(solution)/shard_map/ppermute | solution.py:322
  14.5 2.1 %collective-permute-done.3.second = bf16[4,128,128]{2,1,0:T(8,128)(2,1)S(1)} collective-permute-done((bf16[4,128,128]{2,1,0:T(8,128)(2,1)S(1)}, bf16[4,128,128]{2,1,0:T(8,128)(2,1)S(1)}, u32[]{:S(2)}, u32[]{:S(2)}) %collective-permute-start.3) | collective-permute-done | bytes 131104 | tf_op jit(solution)/shard_map/ppermute | solution.py:322
  16.6 0.3 %far_pair.1.blocks = bf16[8,128,128]{2,1,0:T(8,128)(2,1)S(1)} custom-call(bf16[4,128,128]{2,1,0:T(8,128)(2,1)S(1)} %collective-permute-done.1.first, bf16[4,128,128]{2,1,0:T(8,128)(2,1)S(1)} %collective-permute-done.3.second), custom_call_target="tpu_custom_call" | custom-call | tf_op jit(solution)/shard_map/far_pair/pallas_call | solution.py:351
  17.0 1.7 %collective-permute-done.7.refs_3_ = bf16[520,128]{1,0:T(8,128)(2,1)S(1)} collective-permute-done((bf16[520,128]{1,0:T(8,128)(2,1)S(1)}, bf16[520,128]{1,0:T(8,128)(2,1)S(1)}, u32[]{:S(2)}, u32[]{:S(2)}) %collective-permute-start.7) | collective-permute-done | bytes 133152 | tf_op jit(solution)/shard_map/ppermute | solution.py:322
  18.8 1.6 %collective-permute-start.8 = (bf16[1024,128]{1,0:T(8,128)(2,1)S(1)}, bf16[1024,128]{1,0:T(8,128)(2,1)S(1)}, u32[]{:S(2)}, u32[]{:S(2)}) collective-permute-start(bf16[1024,128]{1,0:T(8,128)(2,1)S(1)} %regroup.1), channel_id=1, source_target_pairs={{0,2},{1,3},{2,0},{3,1},{4,6},{5,7},{6,4},{7,5},{8,10},{9,11},{10,... | collective-permute-start | bytes 786440 | tf_op jit(solution)/shard_map/ppermute | solution.py:322
  20.4 1.4 %collective-permute-done.2.coefs = bf16[136,512]{1,0:T(8,128)(2,1)S(1)} collective-permute-done((bf16[136,512]{1,0:T(8,128)(2,1)S(1)}, bf16[136,512]{1,0:T(8,128)(2,1)S(1)}, u32[]{:S(2)}, u32[]{:S(2)}) %collective-permute-start.2) | collective-permute-done | bytes 139296 | tf_op jit(solution)/shard_map/ppermute | solution.py:322
  21.8 0.2 far_blocks_0.1
  22.0 0.2 far_blocks_1.1
  22.2 0.6 %collective-permute-start.9 = (bf16[520,128]{1,0:T(8,128)(2,1)S(1)}, bf16[520,128]{1,0:T(8,128)(2,1)S(1)}, u32[]{:S(2)}, u32[]{:S(2)}) collective-permute-start(bf16[520,128]{1,0:T(8,128)(2,1)S(1)} %get-tuple-element.43), channel_id=1, source_target_pairs={{0,12},{4,8},{8,4},{12,0},{16,28},{20,24},{24,20},{28,16},{1,13},{... | collective-permute-start | bytes 399368 | tf_op jit(solution)/shard_map/ppermute | solution.py:322
  22.9 2.4 %collective-permute-start.10 = (bf16[520,128]{1,0:T(8,128)(2,1)S(1)}, bf16[520,128]{1,0:T(8,128)(2,1)S(1)}, u32[]{:S(2)}, u32[]{:S(2)}) collective-permute-start(bf16[520,128]{1,0:T(8,128)(2,1)S(1)} %get-tuple-element.44), channel_id=1, source_target_pairs={{0,8},{4,12},{8,0},{12,4},{16,24},{20,28},{24,16},{28,20},{1,9},{5... | collective-permute-start | bytes 399368 | tf_op jit(solution)/shard_map/ppermute | solution.py:322
  25.3 0.5 %collective-permute-start.11 = (bf16[520,128]{1,0:T(8,128)(2,1)S(1)}, bf16[520,128]{1,0:T(8,128)(2,1)S(1)}, u32[]{:S(2)}, u32[]{:S(2)}) collective-permute-start(bf16[520,128]{1,0:T(8,128)(2,1)S(1)} %get-tuple-element.45), channel_id=1, source_target_pairs={{0,4},{4,0},{8,12},{12,8},{16,20},{20,16},{24,28},{28,24},{1,5},{5... | collective-permute-start | bytes 399368 | tf_op jit(solution)/shard_map/ppermute | solution.py:322
  25.8 0.9 %collective-permute-done.8.refs_4_ = bf16[1024,128]{1,0:T(8,128)(2,1)S(1)} collective-permute-done((bf16[1024,128]{1,0:T(8,128)(2,1)S(1)}, bf16[1024,128]{1,0:T(8,128)(2,1)S(1)}, u32[]{:S(2)}, u32[]{:S(2)}) %collective-permute-start.8) | collective-permute-done | bytes 262176 | tf_op jit(solution)/shard_map/ppermute | solution.py:322
  26.6 1.4 %near_sum.1 = (f32[32,128,128]{2,1,0:T(8,128)S(1)}, bf16[128,128]{1,0:T(8,128)(2,1)S(1)}) custom-call(bf16[4,4]{1,0:T(4,128)(2,1)} %metric_in.1, bf16[520,128]{1,0:T(8,128)(2,1)S(1)} %get-tuple-element.34.refs_0_, bf16[520,128]{1,0:T(8,128)(2,1)S(1)} %collective-permute-done.5.refs_1_, bf16[520,128]{1,0:T(8,128)(2,1)S(1)} %collective-permute-done.6.refs_2_, ...), custom_call_target="tpu_custom_call" | custom-call | flops 3000000000 | bytes 1048576 | tf_op jit(solution)/shard_map/near_sum/pallas_call | solution.py:426
  28.0 0.9 %collective-permute-done.9.refs_0_ = bf16[520,128]{1,0:T(8,128)(2,1)S(1)} collective-permute-done((bf16[520,128]{1,0:T(8,128)(2,1)S(1)}, bf16[520,128]{1,0:T(8,128)(2,1)S(1)}, u32[]{:S(2)}, u32[]{:S(2)}) %collective-permute-start.9) | collective-permute-done | bytes 133152 | tf_op jit(solution)/shard_map/ppermute | solution.py:322
  28.9 1.4 %collective-permute-done.10.refs_1_ = bf16[520,128]{1,0:T(8,128)(2,1)S(1)} collective-permute-done((bf16[520,128]{1,0:T(8,128)(2,1)S(1)}, bf16[520,128]{1,0:T(8,128)(2,1)S(1)}, u32[]{:S(2)}, u32[]{:S(2)}) %collective-permute-start.10) | collective-permute-done | bytes 133152 | tf_op jit(solution)/shard_map/ppermute | solution.py:322
  30.4 1.5 %collect.1 = (bf16[32,4,4096]{2,1,0:T(4,128)(2,1)}, f32[32,128,128]{2,1,0:T(8,128)S(1)}) custom-call(bf16[128,128]{1,0:T(8,128)(2,1)S(1)} %get-tuple-element.41.mix, f32[32,128,128]{2,1,0:T(8,128)S(1)} %get-tuple-element.42.total_in, bf16[520,128]{1,0:T(8,128)(2,1)S(1)} %collective-permute-done.9.refs_0_, ...), custom_call_target="tpu_custom_call", output_to_operand_aliasing={{1}: (1, {})} | custom-call | tf_op jit(solution)/shard_map/collect/pallas_call | solution.py:441
  (8 shorter events, 0.1 us)
Async XLA Ops:
  0.0 4.0 %collective-permute-start = (bf16[4,128,128]{2,1,0:T(8,128)(2,1)}, bf16[4,128,128]{2,1,0:T(8,128)(2,1)S(1)}, u32[]{:S(2)}, u32[]{:S(2)}) collective-permute-start(bf16[4,128,128]{2,1,0:T(8,128)(2,1)} %bitcast.2), channel_id=1, source_target_pairs={{0,1},{1,0},{2,3},{3,2},{4,5},{5,4},{6,7},{7,6},{8,9},{9,8},{10,11... | collective-permute-start | bytes 393224 | tf_op jit(solution)/shard_map/ppermute | solution.py:322
  0.5 10.9 %collective-permute-start.1 = (bf16[4,128,128]{2,1,0:T(8,128)(2,1)}, bf16[4,128,128]{2,1,0:T(8,128)(2,1)S(1)}, u32[]{:S(2)}, u32[]{:S(2)}) collective-permute-start(bf16[4,128,128]{2,1,0:T(8,128)(2,1)} %bitcast.3), channel_id=1, source_target_pairs={{0,16},{4,20},{8,24},{12,28},{16,0},{20,4},{24,8},{28,12},{1,17},{... | collective-permute-start | bytes 393224 | tf_op jit(solution)/shard_map/ppermute | solution.py:322
  6.0 10.9 %collective-permute-start.5 = (bf16[520,128]{1,0:T(8,128)(2,1)S(1)}, bf16[520,128]{1,0:T(8,128)(2,1)S(1)}, u32[]{:S(2)}, u32[]{:S(2)}) collective-permute-start(bf16[520,128]{1,0:T(8,128)(2,1)S(1)} %get-tuple-element.35), channel_id=1, source_target_pairs={{0,4},{4,0},{8,12},{12,8},{16,20},{20,16},{24,28},{28,24},{1,5},{5... | collective-permute-start | bytes 399368 | tf_op jit(solution)/shard_map/ppermute | solution.py:322
  7.6 9.4 %collective-permute-start.6 = (bf16[520,128]{1,0:T(8,128)(2,1)S(1)}, bf16[520,128]{1,0:T(8,128)(2,1)S(1)}, u32[]{:S(2)}, u32[]{:S(2)}) collective-permute-start(bf16[520,128]{1,0:T(8,128)(2,1)S(1)} %get-tuple-element.37), channel_id=1, source_target_pairs={{0,8},{4,12},{8,0},{12,4},{16,24},{20,28},{24,16},{28,20},{1,9},{5... | collective-permute-start | bytes 399368 | tf_op jit(solution)/shard_map/ppermute | solution.py:322
  9.2 9.6 %collective-permute-start.7 = (bf16[520,128]{1,0:T(8,128)(2,1)S(1)}, bf16[520,128]{1,0:T(8,128)(2,1)S(1)}, u32[]{:S(2)}, u32[]{:S(2)}) collective-permute-start(bf16[520,128]{1,0:T(8,128)(2,1)S(1)} %get-tuple-element.39), channel_id=1, source_target_pairs={{0,12},{4,8},{8,4},{12,0},{16,28},{20,24},{24,20},{28,16},{1,13},{... | collective-permute-start | bytes 399368 | tf_op jit(solution)/shard_map/ppermute | solution.py:322
  11.3 5.2 %collective-permute-start.3 = (bf16[4,128,128]{2,1,0:T(8,128)(2,1)S(1)}, bf16[4,128,128]{2,1,0:T(8,128)(2,1)S(1)}, u32[]{:S(2)}, u32[]{:S(2)}) collective-permute-start(bf16[4,128,128]{2,1,0:T(8,128)(2,1)S(1)} %collective-permute-done.1.first), channel_id=1, source_target_pairs={{0,2},{1,3},{2,0},{3,1},{4,6},{5,7},{6,4},{7,5},{8,10},{9,11},{10,... | collective-permute-start | bytes 393224 | tf_op jit(solution)/shard_map/ppermute | solution.py:322
  12.9 8.8 %collective-permute-start.2 = (bf16[136,512]{1,0:T(8,128)(2,1)S(1)}, bf16[136,512]{1,0:T(8,128)(2,1)S(1)}, u32[]{:S(2)}, u32[]{:S(2)}) collective-permute-start(bf16[136,512]{1,0:T(8,128)(2,1)S(1)} %pick.1), channel_id=1, source_target_pairs={{0,16},{4,20},{8,24},{12,28},{16,0},{20,4},{24,8},{28,12},{1,17},{... | collective-permute-start | bytes 417800 | tf_op jit(solution)/shard_map/ppermute | solution.py:322
  16.9 5.1 %collective-permute-start.4 = (bf16[8,128,128]{2,1,0:T(8,128)(2,1)S(1)}, bf16[8,128,128]{2,1,0:T(8,128)(2,1)S(1)}, u32[]{:S(2)}, u32[]{:S(2)}) collective-permute-start(bf16[8,128,128]{2,1,0:T(8,128)(2,1)S(1)} %far_pair.1.blocks), channel_id=1, source_target_pairs={{0,1},{1,0},{2,3},{3,2},{4,5},{5,4},{6,7},{7,6},{8,9},{9,8},{10,11... | collective-permute-start | bytes 786440 | tf_op jit(solution)/shard_map/ppermute | solution.py:322
  18.8 7.9 %collective-permute-start.8 = (bf16[1024,128]{1,0:T(8,128)(2,1)S(1)}, bf16[1024,128]{1,0:T(8,128)(2,1)S(1)}, u32[]{:S(2)}, u32[]{:S(2)}) collective-permute-start(bf16[1024,128]{1,0:T(8,128)(2,1)S(1)} %regroup.1), channel_id=1, source_target_pairs={{0,2},{1,3},{2,0},{3,1},{4,6},{5,7},{6,4},{7,5},{8,10},{9,11},{10,... | collective-permute-start | bytes 786440 | tf_op jit(solution)/shard_map/ppermute | solution.py:322
  22.2 6.7 %collective-permute-start.9 = (bf16[520,128]{1,0:T(8,128)(2,1)S(1)}, bf16[520,128]{1,0:T(8,128)(2,1)S(1)}, u32[]{:S(2)}, u32[]{:S(2)}) collective-permute-start(bf16[520,128]{1,0:T(8,128)(2,1)S(1)} %get-tuple-element.43), channel_id=1, source_target_pairs={{0,12},{4,8},{8,4},{12,0},{16,28},{20,24},{24,20},{28,16},{1,13},{... | collective-permute-start | bytes 399368 | tf_op jit(solution)/shard_map/ppermute | solution.py:322
  22.9 7.5 %collective-permute-start.10 = (bf16[520,128]{1,0:T(8,128)(2,1)S(1)}, bf16[520,128]{1,0:T(8,128)(2,1)S(1)}, u32[]{:S(2)}, u32[]{:S(2)}) collective-permute-start(bf16[520,128]{1,0:T(8,128)(2,1)S(1)} %get-tuple-element.44), channel_id=1, source_target_pairs={{0,8},{4,12},{8,0},{12,4},{16,24},{20,28},{24,16},{28,20},{1,9},{5... | collective-permute-start | bytes 399368 | tf_op jit(solution)/shard_map/ppermute | solution.py:322
  25.3 5.1 %collective-permute-start.11 = (bf16[520,128]{1,0:T(8,128)(2,1)S(1)}, bf16[520,128]{1,0:T(8,128)(2,1)S(1)}, u32[]{:S(2)}, u32[]{:S(2)}) collective-permute-start(bf16[520,128]{1,0:T(8,128)(2,1)S(1)} %get-tuple-element.45), channel_id=1, source_target_pairs={{0,4},{4,0},{8,12},{12,8},{16,20},{20,16},{24,28},{28,24},{1,5},{5... | collective-permute-start | bytes 399368 | tf_op jit(solution)/shard_map/ppermute | solution.py:322

commit v21 on v20

--- a/solution.py
+++ b/solution.py
@@ -391,9 +391,9 @@
         scratch_shapes=loaded + [pltpu.SemaphoreType.DMA((3,))],
         compiler_params=params,
         name="pick",
-    )(*in_hbm(*operands))
+    )(*in_hbm(after(pair_list, near[0]), *operands[1:]))
     far_block = after(far_block, sent_coef)
-    far_coef = flip(after(sent_coef, far_block), "shell", group)
+    far_coef = flip(sent_coef, "shell", group)
     far_pair = merged("far_pair", far_block, flip(far_block, "aux", 2))
     far_pairs = [far_pair, flip(far_pair, "aux", 1)]
     across = flip(
@@ -419,7 +419,7 @@
             out_specs=[vmem] * group,
             input_output_aliases={2 + f: f for f in range(len(far))},
             compiler_params=params,
-            cost_estimate=cost(2e9) if low == 0 else None,
+            cost_estimate=cost(3e9) if low == 0 else None,
             name=f"far_blocks_{low}",
         )(far_coef, far_pairs[low], *far)
     total_shape = jax.ShapeDtypeStruct((block_count, rows, BS), jnp.float32)

time: 32.1 us -> 33.2 us (1.034)
  waiting for transfers between devices: 8.52 us -> 9.66 us
    ppermute x12, waiting for transfers between devices: 8.52 us -> 9.66 us  [flip(): return lax.ppermute(value, axis, [(at, at ^ bits) for at in range(count)])]
where the time goes in v21:
time: 33.2 us; the launch traced here: 33 us
  starting transfers between devices  15.9 us (48%)
  waiting for transfers between devices  9.66 us (29%)
  Pallas kernels  7.38 us (22%)
    ppermute x12, starting transfers between devices, flip(): return lax.ppermute(value, axis, [(at, at ^ bits) for at in range(count)])  15.9 us
    ppermute x12, waiting for transfers between devices, flip(): return lax.ppermute(value, axis, [(at, at ^ bits) for at in range(count)])  9.66 us
    pallas_call x1, Pallas kernels, exchanged_inputs(): pl.pallas_call(functools.partial(near_kernel, occ_local, aux_count), out_...  1.98 us
    pallas_call x1, Pallas kernels, exchanged_inputs(): pl.pallas_call(functools.partial(pick_kernel, [list(range(group, shell_co...  1.73 us
    pallas_call x1, Pallas kernels, exchanged_inputs(): pl.pallas_call(collect_kernel, out_shape=[jax.ShapeDtypeStruct((occ_local...  1.53 us
    pallas_call x1, Pallas kernels, exchanged_inputs(): pl.pallas_call(near_sum_kernel, out_shape=[total_shape, jax.ShapeDtypeStr...  1.37 us
  transfers between devices with their start and end apart: 12, of which 6 were waited for; matrix products, arithmetic and copies ran while one was open for 0% of the time, Pallas kernels for 18%

profile of v21, /device:TPU:0, one launch (start us, length us, event | category | flops | bytes accessed | tf_op | source)
XLA Modules:
  0.0 33.0 jit_solution(17363859536367877367)
XLA Ops:
  0.0 0.5 %collective-permute-start = (bf16[4,128,128]{2,1,0:T(8,128)(2,1)}, bf16[4,128,128]{2,1,0:T(8,128)(2,1)S(1)}, u32[]{:S(2)}, u32[]{:S(2)}) collective-permute-start(bf16[4,128,128]{2,1,0:T(8,128)(2,1)} %bitcast.2), channel_id=1, source_target_pairs={{0,1},{1,0},{2,3},{3,2},{4,5},{5,4},{6,7},{7,6},{8,9},{9,8},{10,11... | collective-permute-start | bytes 393224 | tf_op jit(solution)/shard_map/ppermute | solution.py:322
  0.5 3.6 %collective-permute-start.2 = (bf16[4,128,128]{2,1,0:T(8,128)(2,1)}, bf16[4,128,128]{2,1,0:T(8,128)(2,1)S(1)}, u32[]{:S(2)}, u32[]{:S(2)}) collective-permute-start(bf16[4,128,128]{2,1,0:T(8,128)(2,1)} %bitcast.3), channel_id=1, source_target_pairs={{0,16},{4,20},{8,24},{12,28},{16,0},{20,4},{24,8},{28,12},{1,17},{... | collective-permute-start | bytes 393224 | tf_op jit(solution)/shard_map/ppermute | solution.py:322
  4.0 2.0 %near_blocks.1 = (bf16[520,128]{1,0:T(8,128)(2,1)S(1)}, bf16[520,128]{1,0:T(8,128)(2,1)S(1)}, bf16[520,128]{1,0:T(8,128)(2,1)S(1)}, bf16[520,128]{1,0:T(8,128)(2,1)S(1)}) custom-call(s32[4,3]{1,0:T(4,128)} %pairs_in.2, s32[1,128]{1,0:T(1,128)} %bitcast.5, bf16[512,1024]{1,0:T(8,128)(2,1)} %coef_in.3, bf16[4,128,128]{2,1,0:T(8,128)(2,1)} %bitcast.4, ...), custom_call_target="tpu_custom_call" | custom-call | tf_op jit(solution)/shard_map/near_blocks/pallas_call | solution.py:371
  6.0 1.7 %pick.1 = bf16[136,512]{1,0:T(8,128)(2,1)S(1)} custom-call(s32[4,3]{1,0:T(4,128)} %pairs_in.2, s32[1,128]{1,0:T(1,128)} %bitcast.6, bf16[512,1024]{1,0:T(8,128)(2,1)} %coef_in.3), custom_call_target="tpu_custom_call" | custom-call | tf_op jit(solution)/shard_map/pick/pallas_call | solution.py:382
  7.8 1.6 %collective-permute-start.1 = (bf16[136,512]{1,0:T(8,128)(2,1)S(1)}, bf16[136,512]{1,0:T(8,128)(2,1)S(1)}, u32[]{:S(2)}, u32[]{:S(2)}) collective-permute-start(bf16[136,512]{1,0:T(8,128)(2,1)S(1)} %pick.1), channel_id=1, source_target_pairs={{0,16},{4,20},{8,24},{12,28},{16,0},{20,4},{24,8},{28,12},{1,17},{... | collective-permute-start | bytes 417800 | tf_op jit(solution)/shard_map/ppermute | solution.py:322
  9.4 1.5 %collective-permute-start.5 = (bf16[520,128]{1,0:T(8,128)(2,1)S(1)}, bf16[520,128]{1,0:T(8,128)(2,1)S(1)}, u32[]{:S(2)}, u32[]{:S(2)}) collective-permute-start(bf16[520,128]{1,0:T(8,128)(2,1)S(1)} %get-tuple-element.35), channel_id=1, source_target_pairs={{0,4},{4,0},{8,12},{12,8},{16,20},{20,16},{24,28},{28,24},{1,5},{5... | collective-permute-start | bytes 399368 | tf_op jit(solution)/shard_map/ppermute | solution.py:322
  10.9 1.6 %collective-permute-start.6 = (bf16[520,128]{1,0:T(8,128)(2,1)S(1)}, bf16[520,128]{1,0:T(8,128)(2,1)S(1)}, u32[]{:S(2)}, u32[]{:S(2)}) collective-permute-start(bf16[520,128]{1,0:T(8,128)(2,1)S(1)} %get-tuple-element.37), channel_id=1, source_target_pairs={{0,8},{4,12},{8,0},{12,4},{16,24},{20,28},{24,16},{28,20},{1,9},{5... | collective-permute-start | bytes 399368 | tf_op jit(solution)/shard_map/ppermute | solution.py:322
  12.4 0.4 %collective-permute-start.7 = (bf16[520,128]{1,0:T(8,128)(2,1)S(1)}, bf16[520,128]{1,0:T(8,128)(2,1)S(1)}, u32[]{:S(2)}, u32[]{:S(2)}) collective-permute-start(bf16[520,128]{1,0:T(8,128)(2,1)S(1)} %get-tuple-element.39), channel_id=1, source_target_pairs={{0,12},{4,8},{8,4},{12,0},{16,28},{20,24},{24,20},{28,16},{1,13},{... | collective-permute-start | bytes 399368 | tf_op jit(solution)/shard_map/ppermute | solution.py:322
  12.9 1.5 %collective-permute-start.3 = (bf16[4,128,128]{2,1,0:T(8,128)(2,1)S(1)}, bf16[4,128,128]{2,1,0:T(8,128)(2,1)S(1)}, u32[]{:S(2)}, u32[]{:S(2)}) collective-permute-start(bf16[4,128,128]{2,1,0:T(8,128)(2,1)S(1)} %collective-permute-done.2.first), channel_id=1, source_target_pairs={{0,2},{1,3},{2,0},{3,1},{4,6},{5,7},{6,4},{7,5},{8,10},{9,11},{10,... | collective-permute-start | bytes 393224 | tf_op jit(solution)/shard_map/ppermute | solution.py:322
  14.4 3.4 %collective-permute-done.3.second = bf16[4,128,128]{2,1,0:T(8,128)(2,1)S(1)} collective-permute-done((bf16[4,128,128]{2,1,0:T(8,128)(2,1)S(1)}, bf16[4,128,128]{2,1,0:T(8,128)(2,1)S(1)}, u32[]{:S(2)}, u32[]{:S(2)}) %collective-permute-start.3) | collective-permute-done | bytes 131104 | tf_op jit(solution)/shard_map/ppermute | solution.py:322
  17.8 0.3 far_pair.1.blocks
  18.3 0.9 %collective-permute-done.6.refs_2_ = bf16[520,128]{1,0:T(8,128)(2,1)S(1)} collective-permute-done((bf16[520,128]{1,0:T(8,128)(2,1)S(1)}, bf16[520,128]{1,0:T(8,128)(2,1)S(1)}, u32[]{:S(2)}, u32[]{:S(2)}) %collective-permute-start.6) | collective-permute-done | bytes 133152 | tf_op jit(solution)/shard_map/ppermute | solution.py:322
  19.2 2.0 %collective-permute-done.7.refs_3_ = bf16[520,128]{1,0:T(8,128)(2,1)S(1)} collective-permute-done((bf16[520,128]{1,0:T(8,128)(2,1)S(1)}, bf16[520,128]{1,0:T(8,128)(2,1)S(1)}, u32[]{:S(2)}, u32[]{:S(2)}) %collective-permute-start.7) | collective-permute-done | bytes 133152 | tf_op jit(solution)/shard_map/ppermute | solution.py:322
  21.2 1.6 %collective-permute-start.8 = (bf16[1024,128]{1,0:T(8,128)(2,1)S(1)}, bf16[1024,128]{1,0:T(8,128)(2,1)S(1)}, u32[]{:S(2)}, u32[]{:S(2)}) collective-permute-start(bf16[1024,128]{1,0:T(8,128)(2,1)S(1)} %regroup.1), channel_id=1, source_target_pairs={{0,2},{1,3},{2,0},{3,1},{4,6},{5,7},{6,4},{7,5},{8,10},{9,11},{10,... | collective-permute-start | bytes 786440 | tf_op jit(solution)/shard_map/ppermute | solution.py:322
  22.8 0.2 far_blocks_0.1
  23.0 0.2 far_blocks_1.1
  23.2 0.7 %collective-permute-start.9 = (bf16[520,128]{1,0:T(8,128)(2,1)S(1)}, bf16[520,128]{1,0:T(8,128)(2,1)S(1)}, u32[]{:S(2)}, u32[]{:S(2)}) collective-permute-start(bf16[520,128]{1,0:T(8,128)(2,1)S(1)} %get-tuple-element.43), channel_id=1, source_target_pairs={{0,12},{4,8},{8,4},{12,0},{16,28},{20,24},{24,20},{28,16},{1,13},{... | collective-permute-start | bytes 399368 | tf_op jit(solution)/shard_map/ppermute | solution.py:322
  23.9 1.8 %collective-permute-start.10 = (bf16[520,128]{1,0:T(8,128)(2,1)S(1)}, bf16[520,128]{1,0:T(8,128)(2,1)S(1)}, u32[]{:S(2)}, u32[]{:S(2)}) collective-permute-start(bf16[520,128]{1,0:T(8,128)(2,1)S(1)} %get-tuple-element.44), channel_id=1, source_target_pairs={{0,8},{4,12},{8,0},{12,4},{16,24},{20,28},{24,16},{28,20},{1,9},{5... | collective-permute-start | bytes 399368 | tf_op jit(solution)/shard_map/ppermute | solution.py:322
  25.7 1.1 %collective-permute-start.11 = (bf16[520,128]{1,0:T(8,128)(2,1)S(1)}, bf16[520,128]{1,0:T(8,128)(2,1)S(1)}, u32[]{:S(2)}, u32[]{:S(2)}) collective-permute-start(bf16[520,128]{1,0:T(8,128)(2,1)S(1)} %get-tuple-element.45), channel_id=1, source_target_pairs={{0,4},{4,0},{8,12},{12,8},{16,20},{20,16},{24,28},{28,24},{1,5},{5... | collective-permute-start | bytes 399368 | tf_op jit(solution)/shard_map/ppermute | solution.py:322
  26.8 1.9 %collective-permute-done.8.refs_4_ = bf16[1024,128]{1,0:T(8,128)(2,1)S(1)} collective-permute-done((bf16[1024,128]{1,0:T(8,128)(2,1)S(1)}, bf16[1024,128]{1,0:T(8,128)(2,1)S(1)}, u32[]{:S(2)}, u32[]{:S(2)}) %collective-permute-start.8) | collective-permute-done | bytes 262176 | tf_op jit(solution)/shard_map/ppermute | solution.py:322
  28.7 1.4 %near_sum.1 = (f32[32,128,128]{2,1,0:T(8,128)S(1)}, bf16[128,128]{1,0:T(8,128)(2,1)S(1)}) custom-call(bf16[4,4]{1,0:T(4,128)(2,1)} %metric_in.1, bf16[520,128]{1,0:T(8,128)(2,1)S(1)} %get-tuple-element.34.refs_0_, bf16[520,128]{1,0:T(8,128)(2,1)S(1)} %collective-permute-done.5.refs_1_, bf16[520,128]{1,0:T(8,128)(2,1)S(1)} %collective-permute-done.6.refs_2_, ...), custom_call_target="tpu_custom_call" | custom-call | flops 3000000000 | bytes 1048576 | tf_op jit(solution)/shard_map/near_sum/pallas_call | solution.py:426
  30.1 0.2 collective-permute-done.10.refs_1_
  30.3 1.1 %collective-permute-done.11.refs_2_ = bf16[520,128]{1,0:T(8,128)(2,1)S(1)} collective-permute-done((bf16[520,128]{1,0:T(8,128)(2,1)S(1)}, bf16[520,128]{1,0:T(8,128)(2,1)S(1)}, u32[]{:S(2)}, u32[]{:S(2)}) %collective-permute-start.11) | collective-permute-done | bytes 133152 | tf_op jit(solution)/shard_map/ppermute | solution.py:322
  31.5 1.5 %collect.1 = (bf16[32,4,4096]{2,1,0:T(4,128)(2,1)}, f32[32,128,128]{2,1,0:T(8,128)S(1)}) custom-call(bf16[128,128]{1,0:T(8,128)(2,1)S(1)} %get-tuple-element.41.mix, f32[32,128,128]{2,1,0:T(8,128)S(1)} %get-tuple-element.42.total_in, bf16[520,128]{1,0:T(8,128)(2,1)S(1)} %collective-permute-done.9.refs_0_, ...), custom_call_target="tpu_custom_call", output_to_operand_aliasing={{1}: (1, {})} | custom-call | tf_op jit(solution)/shard_map/collect/pallas_call | solution.py:441
  (8 shorter events, 0.1 us)
Async XLA Ops:
  0.0 4.0 %collective-permute-start = (bf16[4,128,128]{2,1,0:T(8,128)(2,1)}, bf16[4,128,128]{2,1,0:T(8,128)(2,1)S(1)}, u32[]{:S(2)}, u32[]{:S(2)}) collective-permute-start(bf16[4,128,128]{2,1,0:T(8,128)(2,1)} %bitcast.2), channel_id=1, source_target_pairs={{0,1},{1,0},{2,3},{3,2},{4,5},{5,4},{6,7},{7,6},{8,9},{9,8},{10,11... | collective-permute-start | bytes 393224 | tf_op jit(solution)/shard_map/ppermute | solution.py:322
  0.5 12.4 %collective-permute-start.2 = (bf16[4,128,128]{2,1,0:T(8,128)(2,1)}, bf16[4,128,128]{2,1,0:T(8,128)(2,1)S(1)}, u32[]{:S(2)}, u32[]{:S(2)}) collective-permute-start(bf16[4,128,128]{2,1,0:T(8,128)(2,1)} %bitcast.3), channel_id=1, source_target_pairs={{0,16},{4,20},{8,24},{12,28},{16,0},{20,4},{24,8},{28,12},{1,17},{... | collective-permute-start | bytes 393224 | tf_op jit(solution)/shard_map/ppermute | solution.py:322
  7.8 15.0 %collective-permute-start.1 = (bf16[136,512]{1,0:T(8,128)(2,1)S(1)}, bf16[136,512]{1,0:T(8,128)(2,1)S(1)}, u32[]{:S(2)}, u32[]{:S(2)}) collective-permute-start(bf16[136,512]{1,0:T(8,128)(2,1)S(1)} %pick.1), channel_id=1, source_target_pairs={{0,16},{4,20},{8,24},{12,28},{16,0},{20,4},{24,8},{28,12},{1,17},{... | collective-permute-start | bytes 417800 | tf_op jit(solution)/shard_map/ppermute | solution.py:322
  9.4 8.9 %collective-permute-start.5 = (bf16[520,128]{1,0:T(8,128)(2,1)S(1)}, bf16[520,128]{1,0:T(8,128)(2,1)S(1)}, u32[]{:S(2)}, u32[]{:S(2)}) collective-permute-start(bf16[520,128]{1,0:T(8,128)(2,1)S(1)} %get-tuple-element.35), channel_id=1, source_target_pairs={{0,4},{4,0},{8,12},{12,8},{16,20},{20,16},{24,28},{28,24},{1,5},{5... | collective-permute-start | bytes 399368 | tf_op jit(solution)/shard_map/ppermute | solution.py:322
  10.9 8.3 %collective-permute-start.6 = (bf16[520,128]{1,0:T(8,128)(2,1)S(1)}, bf16[520,128]{1,0:T(8,128)(2,1)S(1)}, u32[]{:S(2)}, u32[]{:S(2)}) collective-permute-start(bf16[520,128]{1,0:T(8,128)(2,1)S(1)} %get-tuple-element.37), channel_id=1, source_target_pairs={{0,8},{4,12},{8,0},{12,4},{16,24},{20,28},{24,16},{28,20},{1,9},{5... | collective-permute-start | bytes 399368 | tf_op jit(solution)/shard_map/ppermute | solution.py:322
  12.4 8.7 %collective-permute-start.7 = (bf16[520,128]{1,0:T(8,128)(2,1)S(1)}, bf16[520,128]{1,0:T(8,128)(2,1)S(1)}, u32[]{:S(2)}, u32[]{:S(2)}) collective-permute-start(bf16[520,128]{1,0:T(8,128)(2,1)S(1)} %get-tuple-element.39), channel_id=1, source_target_pairs={{0,12},{4,8},{8,4},{12,0},{16,28},{20,24},{24,20},{28,16},{1,13},{... | collective-permute-start | bytes 399368 | tf_op jit(solution)/shard_map/ppermute | solution.py:322
  12.9 5.0 %collective-permute-start.3 = (bf16[4,128,128]{2,1,0:T(8,128)(2,1)S(1)}, bf16[4,128,128]{2,1,0:T(8,128)(2,1)S(1)}, u32[]{:S(2)}, u32[]{:S(2)}) collective-permute-start(bf16[4,128,128]{2,1,0:T(8,128)(2,1)S(1)} %collective-permute-done.2.first), channel_id=1, source_target_pairs={{0,2},{1,3},{2,0},{3,1},{4,6},{5,7},{6,4},{7,5},{8,10},{9,11},{10,... | collective-permute-start | bytes 393224 | tf_op jit(solution)/shard_map/ppermute | solution.py:322
  18.2 4.8 %collective-permute-start.4 = (bf16[8,128,128]{2,1,0:T(8,128)(2,1)S(1)}, bf16[8,128,128]{2,1,0:T(8,128)(2,1)S(1)}, u32[]{:S(2)}, u32[]{:S(2)}) collective-permute-start(bf16[8,128,128]{2,1,0:T(8,128)(2,1)S(1)} %far_pair.1.blocks), channel_id=1, source_target_pairs={{0,1},{1,0},{2,3},{3,2},{4,5},{5,4},{6,7},{7,6},{8,9},{9,8},{10,11... | collective-permute-start | bytes 786440 | tf_op jit(solution)/shard_map/ppermute | solution.py:322
  21.2 7.5 %collective-permute-start.8 = (bf16[1024,128]{1,0:T(8,128)(2,1)S(1)}, bf16[1024,128]{1,0:T(8,128)(2,1)S(1)}, u32[]{:S(2)}, u32[]{:S(2)}) collective-permute-start(bf16[1024,128]{1,0:T(8,128)(2,1)S(1)} %regroup.1), channel_id=1, source_target_pairs={{0,2},{1,3},{2,0},{3,1},{4,6},{5,7},{6,4},{7,5},{8,10},{9,11},{10,... | collective-permute-start | bytes 786440 | tf_op jit(solution)/shard_map/ppermute | solution.py:322
  23.2 6.9 %collective-permute-start.9 = (bf16[520,128]{1,0:T(8,128)(2,1)S(1)}, bf16[520,128]{1,0:T(8,128)(2,1)S(1)}, u32[]{:S(2)}, u32[]{:S(2)}) collective-permute-start(bf16[520,128]{1,0:T(8,128)(2,1)S(1)} %get-tuple-element.43), channel_id=1, source_target_pairs={{0,12},{4,8},{8,4},{12,0},{16,28},{20,24},{24,20},{28,16},{1,13},{... | collective-permute-start | bytes 399368 | tf_op jit(solution)/shard_map/ppermute | solution.py:322
  23.9 6.4 %collective-permute-start.10 = (bf16[520,128]{1,0:T(8,128)(2,1)S(1)}, bf16[520,128]{1,0:T(8,128)(2,1)S(1)}, u32[]{:S(2)}, u32[]{:S(2)}) collective-permute-start(bf16[520,128]{1,0:T(8,128)(2,1)S(1)} %get-tuple-element.44), channel_id=1, source_target_pairs={{0,8},{4,12},{8,0},{12,4},{16,24},{20,28},{24,16},{28,20},{1,9},{5... | collective-permute-start | bytes 399368 | tf_op jit(solution)/shard_map/ppermute | solution.py:322
  25.7 5.8 %collective-permute-start.11 = (bf16[520,128]{1,0:T(8,128)(2,1)S(1)}, bf16[520,128]{1,0:T(8,128)(2,1)S(1)}, u32[]{:S(2)}, u32[]{:S(2)}) collective-permute-start(bf16[520,128]{1,0:T(8,128)(2,1)S(1)} %get-tuple-element.45), channel_id=1, source_target_pairs={{0,4},{4,0},{8,12},{12,8},{16,20},{20,16},{24,28},{28,24},{1,5},{5... | collective-permute-start | bytes 399368 | tf_op jit(solution)/shard_map/ppermute | solution.py:322

commit v22 on v20

--- a/solution.py
+++ b/solution.py
@@ -253,7 +253,7 @@
         codes[at : at + 1, :] = (digits + 128.0 * high).astype(jnp.int32)
 
 
-def near_sum_kernel(metric_in, *refs):
+def near_sum_kernel(metric_in, own, *refs):
     *received, across, total, mix, metric, codes, sem = refs
     load = pltpu.make_async_copy(metric_in, metric, sem)
     load.start()
@@ -262,7 +262,10 @@
     rows = total.shape[1]
     occ_local = rows // metric.shape[0]
     pairs_dev = (received[0].shape[0] - TILE) // rows
-    read_codes(received, pairs_dev, codes)
+    read_codes([*received, own], pairs_dev, codes)
+    for k in range(pairs_dev):
+        part = own[k * rows : (k + 1) * rows, :]
+        total[codes[len(received), k]] += part.astype(jnp.float32)
     for f, piece in enumerate(received):
         for k in range(pairs_dev):
             r = codes[f, k]
@@ -426,7 +429,7 @@
     total, mix = pl.pallas_call(
         near_sum_kernel,
         out_shape=[total_shape, jax.ShapeDtypeStruct((rows, rows), jnp.bfloat16)],
-        in_specs=[hbm] + [vmem] * (group + 1),
+        in_specs=[hbm] + [vmem] * (group + 2),
         out_specs=[vmem] * 2,
         scratch_shapes=[
             pltpu.VMEM(metric.shape, jnp.bfloat16),
@@ -436,7 +439,7 @@
         compiler_params=params,
         cost_estimate=cost(3e9),
         name="near_sum",
-    )(*in_hbm(metric), *(after(one, far[0]) for one in near), across)
+    )(*in_hbm(metric), far[0], *near, across)
     far = [far[0]] + [flip(far[f], "shell", f) for f in range(1, group)]
     return pl.pallas_call(
         collect_kernel,
@@ -444,7 +447,7 @@
             jax.ShapeDtypeStruct((occ_local, aux_count, block_count * BS), jnp.bfloat16),
             total_shape,
         ],
-        in_specs=[vmem] * (2 + group),
+        in_specs=[vmem] * (1 + group),
         out_specs=[hbm, vmem],
         input_output_aliases={1: 1},
         scratch_shapes=[
@@ -454,7 +457,7 @@
         ],
         compiler_params=params,
         name="collect",
-    )(mix, total, *reversed(far))[0]
+    )(mix, total, far[3], far[1], far[2])[0]
 
 
 def per_device(integrals, pair_list, coef, metric, occ_slot):

time: 32.1 us -> 32.1 us (level)
  transfers between devices with their start and end apart: 12 -> 12, of which waited for: 6 -> 7; matrix products, arithmetic and copies ran while one was open for 0% -> 0% of each run, Pallas kernels for 18% -> 18%
where the time goes in v22:
time: 32.1 us; the launch traced here: 31.9 us
  starting transfers between devices  15.9 us (50%)
  waiting for transfers between devices  8.48 us (26%)
  Pallas kernels  7.37 us (23%)
    ppermute x12, starting transfers between devices, flip(): return lax.ppermute(value, axis, [(at, at ^ bits) for at in range(count)])  15.9 us
    ppermute x12, waiting for transfers between devices, flip(): return lax.ppermute(value, axis, [(at, at ^ bits) for at in range(count)])  8.48 us
    pallas_call x1, Pallas kernels, exchanged_inputs(): pl.pallas_call(functools.partial(near_kernel, occ_local, aux_count), out_...  1.98 us
    pallas_call x1, Pallas kernels, exchanged_inputs(): pl.pallas_call(functools.partial(pick_kernel, [list(range(group, shell_co...  1.72 us
    pallas_call x1, Pallas kernels, exchanged_inputs(): pl.pallas_call(collect_kernel, out_shape=[jax.ShapeDtypeStruct((occ_local...  1.48 us
    pallas_call x1, Pallas kernels, exchanged_inputs(): pl.pallas_call(near_sum_kernel, out_shape=[total_shape, jax.ShapeDtypeStr...  1.41 us
  transfers between devices with their start and end apart: 12, of which 7 were waited for; matrix products, arithmetic and copies ran while one was open for 0% of the time, Pallas kernels for 18%

profile of v22, /device:TPU:0, one launch (start us, length us, event | category | flops | bytes accessed | tf_op | source)
XLA Modules:
  0.0 31.9 jit_solution(4552908808055123357)
XLA Ops:
  0.0 0.5 %collective-permute-start.4 = (bf16[4,128,128]{2,1,0:T(8,128)(2,1)}, bf16[4,128,128]{2,1,0:T(8,128)(2,1)S(1)}, u32[]{:S(2)}, u32[]{:S(2)}) collective-permute-start(bf16[4,128,128]{2,1,0:T(8,128)(2,1)} %bitcast.2), channel_id=1, source_target_pairs={{0,1},{1,0},{2,3},{3,2},{4,5},{5,4},{6,7},{7,6},{8,9},{9,8},{10,11... | collective-permute-start | bytes 393224 | tf_op jit(solution)/shard_map/ppermute | solution.py:325
  0.5 3.6 %collective-permute-start = (bf16[4,128,128]{2,1,0:T(8,128)(2,1)}, bf16[4,128,128]{2,1,0:T(8,128)(2,1)S(1)}, u32[]{:S(2)}, u32[]{:S(2)}) collective-permute-start(bf16[4,128,128]{2,1,0:T(8,128)(2,1)} %bitcast.3), channel_id=1, source_target_pairs={{0,16},{4,20},{8,24},{12,28},{16,0},{20,4},{24,8},{28,12},{1,17},{... | collective-permute-start | bytes 393224 | tf_op jit(solution)/shard_map/ppermute | solution.py:325
  4.0 2.0 %near_blocks.1 = (bf16[520,128]{1,0:T(8,128)(2,1)S(1)}, bf16[520,128]{1,0:T(8,128)(2,1)S(1)}, bf16[520,128]{1,0:T(8,128)(2,1)S(1)}, bf16[520,128]{1,0:T(8,128)(2,1)S(1)}) custom-call(s32[4,3]{1,0:T(4,128)} %pairs_in.3, s32[1,128]{1,0:T(1,128)} %bitcast.5, bf16[512,1024]{1,0:T(8,128)(2,1)} %coef_in.3, bf16[4,128,128]{2,1,0:T(8,128)(2,1)} %bitcast.4, ...), custom_call_target="tpu_custom_call" | custom-call | tf_op jit(solution)/shard_map/near_blocks/pallas_call | solution.py:374
  6.0 1.6 %collective-permute-start.5 = (bf16[520,128]{1,0:T(8,128)(2,1)S(1)}, bf16[520,128]{1,0:T(8,128)(2,1)S(1)}, u32[]{:S(2)}, u32[]{:S(2)}) collective-permute-start(bf16[520,128]{1,0:T(8,128)(2,1)S(1)} %get-tuple-element.30), channel_id=1, source_target_pairs={{0,4},{4,0},{8,12},{12,8},{16,20},{20,16},{24,28},{28,24},{1,5},{5... | collective-permute-start | bytes 399368 | tf_op jit(solution)/shard_map/ppermute | solution.py:325
  7.6 1.6 %collective-permute-start.6 = (bf16[520,128]{1,0:T(8,128)(2,1)S(1)}, bf16[520,128]{1,0:T(8,128)(2,1)S(1)}, u32[]{:S(2)}, u32[]{:S(2)}) collective-permute-start(bf16[520,128]{1,0:T(8,128)(2,1)S(1)} %get-tuple-element.31), channel_id=1, source_target_pairs={{0,8},{4,12},{8,0},{12,4},{16,24},{20,28},{24,16},{28,20},{1,9},{5... | collective-permute-start | bytes 399368 | tf_op jit(solution)/shard_map/ppermute | solution.py:325
  9.2 0.4 %collective-permute-start.7 = (bf16[520,128]{1,0:T(8,128)(2,1)S(1)}, bf16[520,128]{1,0:T(8,128)(2,1)S(1)}, u32[]{:S(2)}, u32[]{:S(2)}) collective-permute-start(bf16[520,128]{1,0:T(8,128)(2,1)S(1)} %get-tuple-element.32), channel_id=1, source_target_pairs={{0,12},{4,8},{8,4},{12,0},{16,28},{20,24},{24,20},{28,16},{1,13},{... | collective-permute-start | bytes 399368 | tf_op jit(solution)/shard_map/ppermute | solution.py:325
  9.6 1.7 %pick.1 = bf16[136,512]{1,0:T(8,128)(2,1)S(1)} custom-call(s32[4,3]{1,0:T(4,128)} %pairs_in.3, s32[1,128]{1,0:T(1,128)} %bitcast.6, bf16[512,1024]{1,0:T(8,128)(2,1)} %coef_in.3), custom_call_target="tpu_custom_call" | custom-call | tf_op jit(solution)/shard_map/pick/pallas_call | solution.py:385
  11.3 1.6 %collective-permute-start.2 = (bf16[4,128,128]{2,1,0:T(8,128)(2,1)S(1)}, bf16[4,128,128]{2,1,0:T(8,128)(2,1)S(1)}, u32[]{:S(2)}, u32[]{:S(2)}) collective-permute-start(bf16[4,128,128]{2,1,0:T(8,128)(2,1)S(1)} %collective-permute-done.first), channel_id=1, source_target_pairs={{0,2},{1,3},{2,0},{3,1},{4,6},{5,7},{6,4},{7,5},{8,10},{9,11},{10,... | collective-permute-start | bytes 393224 | tf_op jit(solution)/shard_map/ppermute | solution.py:325
  12.9 1.6 %collective-permute-start.1 = (bf16[136,512]{1,0:T(8,128)(2,1)S(1)}, bf16[136,512]{1,0:T(8,128)(2,1)S(1)}, u32[]{:S(2)}, u32[]{:S(2)}) collective-permute-start(bf16[136,512]{1,0:T(8,128)(2,1)S(1)} %pick.1), channel_id=1, source_target_pairs={{0,16},{4,20},{8,24},{12,28},{16,0},{20,4},{24,8},{28,12},{1,17},{... | collective-permute-start | bytes 417800 | tf_op jit(solution)/shard_map/ppermute | solution.py:325
  14.5 2.1 %collective-permute-done.2.second = bf16[4,128,128]{2,1,0:T(8,128)(2,1)S(1)} collective-permute-done((bf16[4,128,128]{2,1,0:T(8,128)(2,1)S(1)}, bf16[4,128,128]{2,1,0:T(8,128)(2,1)S(1)}, u32[]{:S(2)}, u32[]{:S(2)}) %collective-permute-start.2) | collective-permute-done | bytes 131104 | tf_op jit(solution)/shard_map/ppermute | solution.py:325
  16.6 0.3 %far_pair.1.blocks = bf16[8,128,128]{2,1,0:T(8,128)(2,1)S(1)} custom-call(bf16[4,128,128]{2,1,0:T(8,128)(2,1)S(1)} %collective-permute-done.first, bf16[4,128,128]{2,1,0:T(8,128)(2,1)S(1)} %collective-permute-done.2.second), custom_call_target="tpu_custom_call" | custom-call | tf_op jit(solution)/shard_map/far_pair/pallas_call | solution.py:354
  17.0 1.7 %collective-permute-done.7.refs_3_ = bf16[520,128]{1,0:T(8,128)(2,1)S(1)} collective-permute-done((bf16[520,128]{1,0:T(8,128)(2,1)S(1)}, bf16[520,128]{1,0:T(8,128)(2,1)S(1)}, u32[]{:S(2)}, u32[]{:S(2)}) %collective-permute-start.7) | collective-permute-done | bytes 133152 | tf_op jit(solution)/shard_map/ppermute | solution.py:325
  18.8 1.6 %collective-permute-start.8 = (bf16[1024,128]{1,0:T(8,128)(2,1)S(1)}, bf16[1024,128]{1,0:T(8,128)(2,1)S(1)}, u32[]{:S(2)}, u32[]{:S(2)}) collective-permute-start(bf16[1024,128]{1,0:T(8,128)(2,1)S(1)} %regroup.1), channel_id=1, source_target_pairs={{0,2},{1,3},{2,0},{3,1},{4,6},{5,7},{6,4},{7,5},{8,10},{9,11},{10,... | collective-permute-start | bytes 786440 | tf_op jit(solution)/shard_map/ppermute | solution.py:325
  20.4 1.4 %collective-permute-done.1.coefs = bf16[136,512]{1,0:T(8,128)(2,1)S(1)} collective-permute-done((bf16[136,512]{1,0:T(8,128)(2,1)S(1)}, bf16[136,512]{1,0:T(8,128)(2,1)S(1)}, u32[]{:S(2)}, u32[]{:S(2)}) %collective-permute-start.1) | collective-permute-done | bytes 139296 | tf_op jit(solution)/shard_map/ppermute | solution.py:325
  21.8 0.2 far_blocks_0.1
  22.0 0.2 far_blocks_1.1
  22.2 0.6 %collective-permute-start.9 = (bf16[520,128]{1,0:T(8,128)(2,1)S(1)}, bf16[520,128]{1,0:T(8,128)(2,1)S(1)}, u32[]{:S(2)}, u32[]{:S(2)}) collective-permute-start(bf16[520,128]{1,0:T(8,128)(2,1)S(1)} %get-tuple-element.35), channel_id=1, source_target_pairs={{0,12},{4,8},{8,4},{12,0},{16,28},{20,24},{24,20},{28,16},{1,13},{... | collective-permute-start | bytes 399368 | tf_op jit(solution)/shard_map/ppermute | solution.py:325
  22.9 1.2 %collective-permute-start.10 = (bf16[520,128]{1,0:T(8,128)(2,1)S(1)}, bf16[520,128]{1,0:T(8,128)(2,1)S(1)}, u32[]{:S(2)}, u32[]{:S(2)}) collective-permute-start(bf16[520,128]{1,0:T(8,128)(2,1)S(1)} %get-tuple-element.36), channel_id=1, source_target_pairs={{0,4},{4,0},{8,12},{12,8},{16,20},{20,16},{24,28},{28,24},{1,5},{5... | collective-permute-start | bytes 399368 | tf_op jit(solution)/shard_map/ppermute | solution.py:325
  24.0 1.7 %collective-permute-start.11 = (bf16[520,128]{1,0:T(8,128)(2,1)S(1)}, bf16[520,128]{1,0:T(8,128)(2,1)S(1)}, u32[]{:S(2)}, u32[]{:S(2)}) collective-permute-start(bf16[520,128]{1,0:T(8,128)(2,1)S(1)} %get-tuple-element.37), channel_id=1, source_target_pairs={{0,8},{4,12},{8,0},{12,4},{16,24},{20,28},{24,16},{28,20},{1,9},{5... | collective-permute-start | bytes 399368 | tf_op jit(solution)/shard_map/ppermute | solution.py:325
  25.8 0.9 %collective-permute-done.8.refs_4_ = bf16[1024,128]{1,0:T(8,128)(2,1)S(1)} collective-permute-done((bf16[1024,128]{1,0:T(8,128)(2,1)S(1)}, bf16[1024,128]{1,0:T(8,128)(2,1)S(1)}, u32[]{:S(2)}, u32[]{:S(2)}) %collective-permute-start.8) | collective-permute-done | bytes 262176 | tf_op jit(solution)/shard_map/ppermute | solution.py:325
  26.6 1.4 %near_sum.1 = (f32[32,128,128]{2,1,0:T(8,128)S(1)}, bf16[128,128]{1,0:T(8,128)(2,1)S(1)}) custom-call(bf16[4,4]{1,0:T(4,128)(2,1)} %metric_in.1, bf16[520,128]{1,0:T(8,128)(2,1)S(1)} %get-tuple-element.28.own, bf16[520,128]{1,0:T(8,128)(2,1)S(1)} %get-tuple-element.29.refs_0_, bf16[520,128]{1,0:T(8,128)(2,1)S(1)} %collective-permute-done.5.refs_1_, ...), custom_call_target="tpu_custom_call" | custom-call | flops 3000000000 | bytes 1048576 | tf_op jit(solution)/shard_map/near_sum/pallas_call | solution.py:429
  28.1 1.2 %collective-permute-done.9.refs_0_ = bf16[520,128]{1,0:T(8,128)(2,1)S(1)} collective-permute-done((bf16[520,128]{1,0:T(8,128)(2,1)S(1)}, bf16[520,128]{1,0:T(8,128)(2,1)S(1)}, u32[]{:S(2)}, u32[]{:S(2)}) %collective-permute-start.9) | collective-permute-done | bytes 133152 | tf_op jit(solution)/shard_map/ppermute | solution.py:325
  29.2 1.0 %collective-permute-done.10.refs_1_ = bf16[520,128]{1,0:T(8,128)(2,1)S(1)} collective-permute-done((bf16[520,128]{1,0:T(8,128)(2,1)S(1)}, bf16[520,128]{1,0:T(8,128)(2,1)S(1)}, u32[]{:S(2)}, u32[]{:S(2)}) %collective-permute-start.10) | collective-permute-done | bytes 133152 | tf_op jit(solution)/shard_map/ppermute | solution.py:325
  30.4 1.5 %collect.1 = (bf16[32,4,4096]{2,1,0:T(4,128)(2,1)}, f32[32,128,128]{2,1,0:T(8,128)S(1)}) custom-call(bf16[128,128]{1,0:T(8,128)(2,1)S(1)} %get-tuple-element.33.mix, f32[32,128,128]{2,1,0:T(8,128)S(1)} %get-tuple-element.34.total_in, bf16[520,128]{1,0:T(8,128)(2,1)S(1)} %collective-permute-done.9.refs_0_, ...), custom_call_target="tpu_custom_call", output_to_operand_aliasing={{1}: (1, {})} | custom-call | tf_op jit(solution)/shard_map/collect/pallas_call | solution.py:444
  (8 shorter events, 0.3 us)
Async XLA Ops:
  0.0 4.0 %collective-permute-start.4 = (bf16[4,128,128]{2,1,0:T(8,128)(2,1)}, bf16[4,128,128]{2,1,0:T(8,128)(2,1)S(1)}, u32[]{:S(2)}, u32[]{:S(2)}) collective-permute-start(bf16[4,128,128]{2,1,0:T(8,128)(2,1)} %bitcast.2), channel_id=1, source_target_pairs={{0,1},{1,0},{2,3},{3,2},{4,5},{5,4},{6,7},{7,6},{8,9},{9,8},{10,11... | collective-permute-start | bytes 393224 | tf_op jit(solution)/shard_map/ppermute | solution.py:325
  0.5 10.9 %collective-permute-start = (bf16[4,128,128]{2,1,0:T(8,128)(2,1)}, bf16[4,128,128]{2,1,0:T(8,128)(2,1)S(1)}, u32[]{:S(2)}, u32[]{:S(2)}) collective-permute-start(bf16[4,128,128]{2,1,0:T(8,128)(2,1)} %bitcast.3), channel_id=1, source_target_pairs={{0,16},{4,20},{8,24},{12,28},{16,0},{20,4},{24,8},{28,12},{1,17},{... | collective-permute-start | bytes 393224 | tf_op jit(solution)/shard_map/ppermute | solution.py:325
  6.0 10.9 %collective-permute-start.5 = (bf16[520,128]{1,0:T(8,128)(2,1)S(1)}, bf16[520,128]{1,0:T(8,128)(2,1)S(1)}, u32[]{:S(2)}, u32[]{:S(2)}) collective-permute-start(bf16[520,128]{1,0:T(8,128)(2,1)S(1)} %get-tuple-element.30), channel_id=1, source_target_pairs={{0,4},{4,0},{8,12},{12,8},{16,20},{20,16},{24,28},{28,24},{1,5},{5... | collective-permute-start | bytes 399368 | tf_op jit(solution)/shard_map/ppermute | solution.py:325
  7.6 9.4 %collective-permute-start.6 = (bf16[520,128]{1,0:T(8,128)(2,1)S(1)}, bf16[520,128]{1,0:T(8,128)(2,1)S(1)}, u32[]{:S(2)}, u32[]{:S(2)}) collective-permute-start(bf16[520,128]{1,0:T(8,128)(2,1)S(1)} %get-tuple-element.31), channel_id=1, source_target_pairs={{0,8},{4,12},{8,0},{12,4},{16,24},{20,28},{24,16},{28,20},{1,9},{5... | collective-permute-start | bytes 399368 | tf_op jit(solution)/shard_map/ppermute | solution.py:325
  9.2 9.6 %collective-permute-start.7 = (bf16[520,128]{1,0:T(8,128)(2,1)S(1)}, bf16[520,128]{1,0:T(8,128)(2,1)S(1)}, u32[]{:S(2)}, u32[]{:S(2)}) collective-permute-start(bf16[520,128]{1,0:T(8,128)(2,1)S(1)} %get-tuple-element.32), channel_id=1, source_target_pairs={{0,12},{4,8},{8,4},{12,0},{16,28},{20,24},{24,20},{28,16},{1,13},{... | collective-permute-start | bytes 399368 | tf_op jit(solution)/shard_map/ppermute | solution.py:325
  11.3 5.2 %collective-permute-start.2 = (bf16[4,128,128]{2,1,0:T(8,128)(2,1)S(1)}, bf16[4,128,128]{2,1,0:T(8,128)(2,1)S(1)}, u32[]{:S(2)}, u32[]{:S(2)}) collective-permute-start(bf16[4,128,128]{2,1,0:T(8,128)(2,1)S(1)} %collective-permute-done.first), channel_id=1, source_target_pairs={{0,2},{1,3},{2,0},{3,1},{4,6},{5,7},{6,4},{7,5},{8,10},{9,11},{10,... | collective-permute-start | bytes 393224 | tf_op jit(solution)/shard_map/ppermute | solution.py:325
  12.9 8.8 %collective-permute-start.1 = (bf16[136,512]{1,0:T(8,128)(2,1)S(1)}, bf16[136,512]{1,0:T(8,128)(2,1)S(1)}, u32[]{:S(2)}, u32[]{:S(2)}) collective-permute-start(bf16[136,512]{1,0:T(8,128)(2,1)S(1)} %pick.1), channel_id=1, source_target_pairs={{0,16},{4,20},{8,24},{12,28},{16,0},{20,4},{24,8},{28,12},{1,17},{... | collective-permute-start | bytes 417800 | tf_op jit(solution)/shard_map/ppermute | solution.py:325
  16.9 5.1 %collective-permute-start.3 = (bf16[8,128,128]{2,1,0:T(8,128)(2,1)S(1)}, bf16[8,128,128]{2,1,0:T(8,128)(2,1)S(1)}, u32[]{:S(2)}, u32[]{:S(2)}) collective-permute-start(bf16[8,128,128]{2,1,0:T(8,128)(2,1)S(1)} %far_pair.1.blocks), channel_id=1, source_target_pairs={{0,1},{1,0},{2,3},{3,2},{4,5},{5,4},{6,7},{7,6},{8,9},{9,8},{10,11... | collective-permute-start | bytes 786440 | tf_op jit(solution)/shard_map/ppermute | solution.py:325
  18.8 7.9 %collective-permute-start.8 = (bf16[1024,128]{1,0:T(8,128)(2,1)S(1)}, bf16[1024,128]{1,0:T(8,128)(2,1)S(1)}, u32[]{:S(2)}, u32[]{:S(2)}) collective-permute-start(bf16[1024,128]{1,0:T(8,128)(2,1)S(1)} %regroup.1), channel_id=1, source_target_pairs={{0,2},{1,3},{2,0},{3,1},{4,6},{5,7},{6,4},{7,5},{8,10},{9,11},{10,... | collective-permute-start | bytes 786440 | tf_op jit(solution)/shard_map/ppermute | solution.py:325
  22.2 7.0 %collective-permute-start.9 = (bf16[520,128]{1,0:T(8,128)(2,1)S(1)}, bf16[520,128]{1,0:T(8,128)(2,1)S(1)}, u32[]{:S(2)}, u32[]{:S(2)}) collective-permute-start(bf16[520,128]{1,0:T(8,128)(2,1)S(1)} %get-tuple-element.35), channel_id=1, source_target_pairs={{0,12},{4,8},{8,4},{12,0},{16,28},{20,24},{24,20},{28,16},{1,13},{... | collective-permute-start | bytes 399368 | tf_op jit(solution)/shard_map/ppermute | solution.py:325
  22.9 7.4 %collective-permute-start.10 = (bf16[520,128]{1,0:T(8,128)(2,1)S(1)}, bf16[520,128]{1,0:T(8,128)(2,1)S(1)}, u32[]{:S(2)}, u32[]{:S(2)}) collective-permute-start(bf16[520,128]{1,0:T(8,128)(2,1)S(1)} %get-tuple-element.36), channel_id=1, source_target_pairs={{0,4},{4,0},{8,12},{12,8},{16,20},{20,16},{24,28},{28,24},{1,5},{5... | collective-permute-start | bytes 399368 | tf_op jit(solution)/shard_map/ppermute | solution.py:325
  24.0 6.4 %collective-permute-start.11 = (bf16[520,128]{1,0:T(8,128)(2,1)S(1)}, bf16[520,128]{1,0:T(8,128)(2,1)S(1)}, u32[]{:S(2)}, u32[]{:S(2)}) collective-permute-start(bf16[520,128]{1,0:T(8,128)(2,1)S(1)} %get-tuple-element.37), channel_id=1, source_target_pairs={{0,8},{4,12},{8,0},{12,4},{16,24},{20,28},{24,16},{28,20},{1,9},{5... | collective-permute-start | bytes 399368 | tf_op jit(solution)/shard_map/ppermute | solution.py:325

commit v23 on v22

--- a/solution.py
+++ b/solution.py
@@ -457,7 +457,7 @@
         ],
         compiler_params=params,
         name="collect",
-    )(mix, total, far[3], far[1], far[2])[0]
+    )(mix, total, far[1], far[3], far[2])[0]
 
 
 def per_device(integrals, pair_list, coef, metric, occ_slot):

time: 32.1 us -> 32.3 us (level)
  no operation moved by 1% of the time
where the time goes in v23:
time: 32.3 us; the launch traced here: 32.1 us
  starting transfers between devices  15.9 us (49%)
  waiting for transfers between devices  8.68 us (27%)
  Pallas kernels  7.37 us (23%)
    ppermute x12, starting transfers between devices, flip(): return lax.ppermute(value, axis, [(at, at ^ bits) for at in range(count)])  15.9 us
    ppermute x12, waiting for transfers between devices, flip(): return lax.ppermute(value, axis, [(at, at ^ bits) for at in range(count)])  8.68 us
    pallas_call x1, Pallas kernels, exchanged_inputs(): pl.pallas_call(functools.partial(near_kernel, occ_local, aux_count), out_...  1.98 us
    pallas_call x1, Pallas kernels, exchanged_inputs(): pl.pallas_call(functools.partial(pick_kernel, [list(range(group, shell_co...  1.72 us
    pallas_call x1, Pallas kernels, exchanged_inputs(): pl.pallas_call(collect_kernel, out_shape=[jax.ShapeDtypeStruct((occ_local...  1.48 us
    pallas_call x1, Pallas kernels, exchanged_inputs(): pl.pallas_call(near_sum_kernel, out_shape=[total_shape, jax.ShapeDtypeStr...  1.41 us
  transfers between devices with their start and end apart: 12, of which 7 were waited for; matrix products, arithmetic and copies ran while one was open for 0% of the time, Pallas kernels for 18%

profile of v23, /device:TPU:0, one launch (start us, length us, event | category | flops | bytes accessed | tf_op | source)
XLA Modules:
  0.0 32.1 jit_solution(13243308223471984743)
XLA Ops:
  0.0 0.5 %collective-permute-start.4 = (bf16[4,128,128]{2,1,0:T(8,128)(2,1)}, bf16[4,128,128]{2,1,0:T(8,128)(2,1)S(1)}, u32[]{:S(2)}, u32[]{:S(2)}) collective-permute-start(bf16[4,128,128]{2,1,0:T(8,128)(2,1)} %bitcast.2), channel_id=1, source_target_pairs={{0,1},{1,0},{2,3},{3,2},{4,5},{5,4},{6,7},{7,6},{8,9},{9,8},{10,11... | collective-permute-start | bytes 393224 | tf_op jit(solution)/shard_map/ppermute | solution.py:325
  0.5 3.6 %collective-permute-start = (bf16[4,128,128]{2,1,0:T(8,128)(2,1)}, bf16[4,128,128]{2,1,0:T(8,128)(2,1)S(1)}, u32[]{:S(2)}, u32[]{:S(2)}) collective-permute-start(bf16[4,128,128]{2,1,0:T(8,128)(2,1)} %bitcast.3), channel_id=1, source_target_pairs={{0,16},{4,20},{8,24},{12,28},{16,0},{20,4},{24,8},{28,12},{1,17},{... | collective-permute-start | bytes 393224 | tf_op jit(solution)/shard_map/ppermute | solution.py:325
  4.0 2.0 %near_blocks.1 = (bf16[520,128]{1,0:T(8,128)(2,1)S(1)}, bf16[520,128]{1,0:T(8,128)(2,1)S(1)}, bf16[520,128]{1,0:T(8,128)(2,1)S(1)}, bf16[520,128]{1,0:T(8,128)(2,1)S(1)}) custom-call(s32[4,3]{1,0:T(4,128)} %pairs_in.3, s32[1,128]{1,0:T(1,128)} %bitcast.5, bf16[512,1024]{1,0:T(8,128)(2,1)} %coef_in.3, bf16[4,128,128]{2,1,0:T(8,128)(2,1)} %bitcast.4, ...), custom_call_target="tpu_custom_call" | custom-call | tf_op jit(solution)/shard_map/near_blocks/pallas_call | solution.py:374
  6.0 1.6 %collective-permute-start.5 = (bf16[520,128]{1,0:T(8,128)(2,1)S(1)}, bf16[520,128]{1,0:T(8,128)(2,1)S(1)}, u32[]{:S(2)}, u32[]{:S(2)}) collective-permute-start(bf16[520,128]{1,0:T(8,128)(2,1)S(1)} %get-tuple-element.30), channel_id=1, source_target_pairs={{0,4},{4,0},{8,12},{12,8},{16,20},{20,16},{24,28},{28,24},{1,5},{5... | collective-permute-start | bytes 399368 | tf_op jit(solution)/shard_map/ppermute | solution.py:325
  7.6 1.6 %collective-permute-start.6 = (bf16[520,128]{1,0:T(8,128)(2,1)S(1)}, bf16[520,128]{1,0:T(8,128)(2,1)S(1)}, u32[]{:S(2)}, u32[]{:S(2)}) collective-permute-start(bf16[520,128]{1,0:T(8,128)(2,1)S(1)} %get-tuple-element.31), channel_id=1, source_target_pairs={{0,8},{4,12},{8,0},{12,4},{16,24},{20,28},{24,16},{28,20},{1,9},{5... | collective-permute-start | bytes 399368 | tf_op jit(solution)/shard_map/ppermute | solution.py:325
  9.2 0.4 %collective-permute-start.7 = (bf16[520,128]{1,0:T(8,128)(2,1)S(1)}, bf16[520,128]{1,0:T(8,128)(2,1)S(1)}, u32[]{:S(2)}, u32[]{:S(2)}) collective-permute-start(bf16[520,128]{1,0:T(8,128)(2,1)S(1)} %get-tuple-element.32), channel_id=1, source_target_pairs={{0,12},{4,8},{8,4},{12,0},{16,28},{20,24},{24,20},{28,16},{1,13},{... | collective-permute-start | bytes 399368 | tf_op jit(solution)/shard_map/ppermute | solution.py:325
  9.6 1.7 %pick.1 = bf16[136,512]{1,0:T(8,128)(2,1)S(1)} custom-call(s32[4,3]{1,0:T(4,128)} %pairs_in.3, s32[1,128]{1,0:T(1,128)} %bitcast.6, bf16[512,1024]{1,0:T(8,128)(2,1)} %coef_in.3), custom_call_target="tpu_custom_call" | custom-call | tf_op jit(solution)/shard_map/pick/pallas_call | solution.py:385
  11.3 1.6 %collective-permute-start.2 = (bf16[4,128,128]{2,1,0:T(8,128)(2,1)S(1)}, bf16[4,128,128]{2,1,0:T(8,128)(2,1)S(1)}, u32[]{:S(2)}, u32[]{:S(2)}) collective-permute-start(bf16[4,128,128]{2,1,0:T(8,128)(2,1)S(1)} %collective-permute-done.first), channel_id=1, source_target_pairs={{0,2},{1,3},{2,0},{3,1},{4,6},{5,7},{6,4},{7,5},{8,10},{9,11},{10,... | collective-permute-start | bytes 393224 | tf_op jit(solution)/shard_map/ppermute | solution.py:325
  12.9 1.6 %collective-permute-start.1 = (bf16[136,512]{1,0:T(8,128)(2,1)S(1)}, bf16[136,512]{1,0:T(8,128)(2,1)S(1)}, u32[]{:S(2)}, u32[]{:S(2)}) collective-permute-start(bf16[136,512]{1,0:T(8,128)(2,1)S(1)} %pick.1), channel_id=1, source_target_pairs={{0,16},{4,20},{8,24},{12,28},{16,0},{20,4},{24,8},{28,12},{1,17},{... | collective-permute-start | bytes 417800 | tf_op jit(solution)/shard_map/ppermute | solution.py:325
  14.5 2.1 %collective-permute-done.2.second = bf16[4,128,128]{2,1,0:T(8,128)(2,1)S(1)} collective-permute-done((bf16[4,128,128]{2,1,0:T(8,128)(2,1)S(1)}, bf16[4,128,128]{2,1,0:T(8,128)(2,1)S(1)}, u32[]{:S(2)}, u32[]{:S(2)}) %collective-permute-start.2) | collective-permute-done | bytes 131104 | tf_op jit(solution)/shard_map/ppermute | solution.py:325
  16.6 0.3 %far_pair.1.blocks = bf16[8,128,128]{2,1,0:T(8,128)(2,1)S(1)} custom-call(bf16[4,128,128]{2,1,0:T(8,128)(2,1)S(1)} %collective-permute-done.first, bf16[4,128,128]{2,1,0:T(8,128)(2,1)S(1)} %collective-permute-done.2.second), custom_call_target="tpu_custom_call" | custom-call | tf_op jit(solution)/shard_map/far_pair/pallas_call | solution.py:354
  17.0 1.7 %collective-permute-done.7.refs_3_ = bf16[520,128]{1,0:T(8,128)(2,1)S(1)} collective-permute-done((bf16[520,128]{1,0:T(8,128)(2,1)S(1)}, bf16[520,128]{1,0:T(8,128)(2,1)S(1)}, u32[]{:S(2)}, u32[]{:S(2)}) %collective-permute-start.7) | collective-permute-done | bytes 133152 | tf_op jit(solution)/shard_map/ppermute | solution.py:325
  18.8 1.6 %collective-permute-start.8 = (bf16[1024,128]{1,0:T(8,128)(2,1)S(1)}, bf16[1024,128]{1,0:T(8,128)(2,1)S(1)}, u32[]{:S(2)}, u32[]{:S(2)}) collective-permute-start(bf16[1024,128]{1,0:T(8,128)(2,1)S(1)} %regroup.1), channel_id=1, source_target_pairs={{0,2},{1,3},{2,0},{3,1},{4,6},{5,7},{6,4},{7,5},{8,10},{9,11},{10,... | collective-permute-start | bytes 786440 | tf_op jit(solution)/shard_map/ppermute | solution.py:325
  20.4 1.4 %collective-permute-done.1.coefs = bf16[136,512]{1,0:T(8,128)(2,1)S(1)} collective-permute-done((bf16[136,512]{1,0:T(8,128)(2,1)S(1)}, bf16[136,512]{1,0:T(8,128)(2,1)S(1)}, u32[]{:S(2)}, u32[]{:S(2)}) %collective-permute-start.1) | collective-permute-done | bytes 139296 | tf_op jit(solution)/shard_map/ppermute | solution.py:325
  22.0 0.2 far_blocks_1.1
  22.2 1.6 %collective-permute-start.9 = (bf16[520,128]{1,0:T(8,128)(2,1)S(1)}, bf16[520,128]{1,0:T(8,128)(2,1)S(1)}, u32[]{:S(2)}, u32[]{:S(2)}) collective-permute-start(bf16[520,128]{1,0:T(8,128)(2,1)S(1)} %get-tuple-element.35), channel_id=1, source_target_pairs={{0,4},{4,0},{8,12},{12,8},{16,20},{20,16},{24,28},{28,24},{1,5},{5... | collective-permute-start | bytes 399368 | tf_op jit(solution)/shard_map/ppermute | solution.py:325
  23.8 0.2 collective-permute-start.10
  24.0 1.7 %collective-permute-start.11 = (bf16[520,128]{1,0:T(8,128)(2,1)S(1)}, bf16[520,128]{1,0:T(8,128)(2,1)S(1)}, u32[]{:S(2)}, u32[]{:S(2)}) collective-permute-start(bf16[520,128]{1,0:T(8,128)(2,1)S(1)} %get-tuple-element.37), channel_id=1, source_target_pairs={{0,8},{4,12},{8,0},{12,4},{16,24},{20,28},{24,16},{28,20},{1,9},{5... | collective-permute-start | bytes 399368 | tf_op jit(solution)/shard_map/ppermute | solution.py:325
  25.8 0.9 %collective-permute-done.8.refs_4_ = bf16[1024,128]{1,0:T(8,128)(2,1)S(1)} collective-permute-done((bf16[1024,128]{1,0:T(8,128)(2,1)S(1)}, bf16[1024,128]{1,0:T(8,128)(2,1)S(1)}, u32[]{:S(2)}, u32[]{:S(2)}) %collective-permute-start.8) | collective-permute-done | bytes 262176 | tf_op jit(solution)/shard_map/ppermute | solution.py:325
  26.6 1.4 %near_sum.1 = (f32[32,128,128]{2,1,0:T(8,128)S(1)}, bf16[128,128]{1,0:T(8,128)(2,1)S(1)}) custom-call(bf16[4,4]{1,0:T(4,128)(2,1)} %metric_in.1, bf16[520,128]{1,0:T(8,128)(2,1)S(1)} %get-tuple-element.28.own, bf16[520,128]{1,0:T(8,128)(2,1)S(1)} %get-tuple-element.29.refs_0_, bf16[520,128]{1,0:T(8,128)(2,1)S(1)} %collective-permute-done.5.refs_1_, ...), custom_call_target="tpu_custom_call" | custom-call | flops 3000000000 | bytes 1048576 | tf_op jit(solution)/shard_map/near_sum/pallas_call | solution.py:429
  28.1 1.0 %collective-permute-done.9.refs_0_ = bf16[520,128]{1,0:T(8,128)(2,1)S(1)} collective-permute-done((bf16[520,128]{1,0:T(8,128)(2,1)S(1)}, bf16[520,128]{1,0:T(8,128)(2,1)S(1)}, u32[]{:S(2)}, u32[]{:S(2)}) %collective-permute-start.9) | collective-permute-done | bytes 133152 | tf_op jit(solution)/shard_map/ppermute | solution.py:325
  29.0 1.1 %collective-permute-done.10.refs_1_ = bf16[520,128]{1,0:T(8,128)(2,1)S(1)} collective-permute-done((bf16[520,128]{1,0:T(8,128)(2,1)S(1)}, bf16[520,128]{1,0:T(8,128)(2,1)S(1)}, u32[]{:S(2)}, u32[]{:S(2)}) %collective-permute-start.10) | collective-permute-done | bytes 133152 | tf_op jit(solution)/shard_map/ppermute | solution.py:325
  30.1 0.5 %collective-permute-done.11.refs_2_ = bf16[520,128]{1,0:T(8,128)(2,1)S(1)} collective-permute-done((bf16[520,128]{1,0:T(8,128)(2,1)S(1)}, bf16[520,128]{1,0:T(8,128)(2,1)S(1)}, u32[]{:S(2)}, u32[]{:S(2)}) %collective-permute-start.11) | collective-permute-done | bytes 133152 | tf_op jit(solution)/shard_map/ppermute | solution.py:325
  30.6 1.5 %collect.1 = (bf16[32,4,4096]{2,1,0:T(4,128)(2,1)}, f32[32,128,128]{2,1,0:T(8,128)S(1)}) custom-call(bf16[128,128]{1,0:T(8,128)(2,1)S(1)} %get-tuple-element.33.mix, f32[32,128,128]{2,1,0:T(8,128)S(1)} %get-tuple-element.34.total_in, bf16[520,128]{1,0:T(8,128)(2,1)S(1)} %collective-permute-done.9.refs_0_, ...), custom_call_target="tpu_custom_call", output_to_operand_aliasing={{1}: (1, {})} | custom-call | tf_op jit(solution)/shard_map/collect/pallas_call | solution.py:444
  (8 shorter events, 0.3 us)
Async XLA Ops:
  0.0 4.0 %collective-permute-start.4 = (bf16[4,128,128]{2,1,0:T(8,128)(2,1)}, bf16[4,128,128]{2,1,0:T(8,128)(2,1)S(1)}, u32[]{:S(2)}, u32[]{:S(2)}) collective-permute-start(bf16[4,128,128]{2,1,0:T(8,128)(2,1)} %bitcast.2), channel_id=1, source_target_pairs={{0,1},{1,0},{2,3},{3,2},{4,5},{5,4},{6,7},{7,6},{8,9},{9,8},{10,11... | collective-permute-start | bytes 393224 | tf_op jit(solution)/shard_map/ppermute | solution.py:325
  0.5 10.9 %collective-permute-start = (bf16[4,128,128]{2,1,0:T(8,128)(2,1)}, bf16[4,128,128]{2,1,0:T(8,128)(2,1)S(1)}, u32[]{:S(2)}, u32[]{:S(2)}) collective-permute-start(bf16[4,128,128]{2,1,0:T(8,128)(2,1)} %bitcast.3), channel_id=1, source_target_pairs={{0,16},{4,20},{8,24},{12,28},{16,0},{20,4},{24,8},{28,12},{1,17},{... | collective-permute-start | bytes 393224 | tf_op jit(solution)/shard_map/ppermute | solution.py:325
  6.0 10.9 %collective-permute-start.5 = (bf16[520,128]{1,0:T(8,128)(2,1)S(1)}, bf16[520,128]{1,0:T(8,128)(2,1)S(1)}, u32[]{:S(2)}, u32[]{:S(2)}) collective-permute-start(bf16[520,128]{1,0:T(8,128)(2,1)S(1)} %get-tuple-element.30), channel_id=1, source_target_pairs={{0,4},{4,0},{8,12},{12,8},{16,20},{20,16},{24,28},{28,24},{1,5},{5... | collective-permute-start | bytes 399368 | tf_op jit(solution)/shard_map/ppermute | solution.py:325
  7.6 9.4 %collective-permute-start.6 = (bf16[520,128]{1,0:T(8,128)(2,1)S(1)}, bf16[520,128]{1,0:T(8,128)(2,1)S(1)}, u32[]{:S(2)}, u32[]{:S(2)}) collective-permute-start(bf16[520,128]{1,0:T(8,128)(2,1)S(1)} %get-tuple-element.31), channel_id=1, source_target_pairs={{0,8},{4,12},{8,0},{12,4},{16,24},{20,28},{24,16},{28,20},{1,9},{5... | collective-permute-start | bytes 399368 | tf_op jit(solution)/shard_map/ppermute | solution.py:325
  9.2 9.6 %collective-permute-start.7 = (bf16[520,128]{1,0:T(8,128)(2,1)S(1)}, bf16[520,128]{1,0:T(8,128)(2,1)S(1)}, u32[]{:S(2)}, u32[]{:S(2)}) collective-permute-start(bf16[520,128]{1,0:T(8,128)(2,1)S(1)} %get-tuple-element.32), channel_id=1, source_target_pairs={{0,12},{4,8},{8,4},{12,0},{16,28},{20,24},{24,20},{28,16},{1,13},{... | collective-permute-start | bytes 399368 | tf_op jit(solution)/shard_map/ppermute | solution.py:325
  11.3 5.2 %collective-permute-start.2 = (bf16[4,128,128]{2,1,0:T(8,128)(2,1)S(1)}, bf16[4,128,128]{2,1,0:T(8,128)(2,1)S(1)}, u32[]{:S(2)}, u32[]{:S(2)}) collective-permute-start(bf16[4,128,128]{2,1,0:T(8,128)(2,1)S(1)} %collective-permute-done.first), channel_id=1, source_target_pairs={{0,2},{1,3},{2,0},{3,1},{4,6},{5,7},{6,4},{7,5},{8,10},{9,11},{10,... | collective-permute-start | bytes 393224 | tf_op jit(solution)/shard_map/ppermute | solution.py:325
  12.9 8.8 %collective-permute-start.1 = (bf16[136,512]{1,0:T(8,128)(2,1)S(1)}, bf16[136,512]{1,0:T(8,128)(2,1)S(1)}, u32[]{:S(2)}, u32[]{:S(2)}) collective-permute-start(bf16[136,512]{1,0:T(8,128)(2,1)S(1)} %pick.1), channel_id=1, source_target_pairs={{0,16},{4,20},{8,24},{12,28},{16,0},{20,4},{24,8},{28,12},{1,17},{... | collective-permute-start | bytes 417800 | tf_op jit(solution)/shard_map/ppermute | solution.py:325
  16.9 5.1 %collective-permute-start.3 = (bf16[8,128,128]{2,1,0:T(8,128)(2,1)S(1)}, bf16[8,128,128]{2,1,0:T(8,128)(2,1)S(1)}, u32[]{:S(2)}, u32[]{:S(2)}) collective-permute-start(bf16[8,128,128]{2,1,0:T(8,128)(2,1)S(1)} %far_pair.1.blocks), channel_id=1, source_target_pairs={{0,1},{1,0},{2,3},{3,2},{4,5},{5,4},{6,7},{7,6},{8,9},{9,8},{10,11... | collective-permute-start | bytes 786440 | tf_op jit(solution)/shard_map/ppermute | solution.py:325
  18.8 7.9 %collective-permute-start.8 = (bf16[1024,128]{1,0:T(8,128)(2,1)S(1)}, bf16[1024,128]{1,0:T(8,128)(2,1)S(1)}, u32[]{:S(2)}, u32[]{:S(2)}) collective-permute-start(bf16[1024,128]{1,0:T(8,128)(2,1)S(1)} %regroup.1), channel_id=1, source_target_pairs={{0,2},{1,3},{2,0},{3,1},{4,6},{5,7},{6,4},{7,5},{8,10},{9,11},{10,... | collective-permute-start | bytes 786440 | tf_op jit(solution)/shard_map/ppermute | solution.py:325
  22.2 6.8 %collective-permute-start.9 = (bf16[520,128]{1,0:T(8,128)(2,1)S(1)}, bf16[520,128]{1,0:T(8,128)(2,1)S(1)}, u32[]{:S(2)}, u32[]{:S(2)}) collective-permute-start(bf16[520,128]{1,0:T(8,128)(2,1)S(1)} %get-tuple-element.35), channel_id=1, source_target_pairs={{0,4},{4,0},{8,12},{12,8},{16,20},{20,16},{24,28},{28,24},{1,5},{5... | collective-permute-start | bytes 399368 | tf_op jit(solution)/shard_map/ppermute | solution.py:325
  23.8 6.3 %collective-permute-start.10 = (bf16[520,128]{1,0:T(8,128)(2,1)S(1)}, bf16[520,128]{1,0:T(8,128)(2,1)S(1)}, u32[]{:S(2)}, u32[]{:S(2)}) collective-permute-start(bf16[520,128]{1,0:T(8,128)(2,1)S(1)} %get-tuple-element.36), channel_id=1, source_target_pairs={{0,12},{4,8},{8,4},{12,0},{16,28},{20,24},{24,20},{28,16},{1,13},{... | collective-permute-start | bytes 399368 | tf_op jit(solution)/shard_map/ppermute | solution.py:325
  24.0 6.6 %collective-permute-start.11 = (bf16[520,128]{1,0:T(8,128)(2,1)S(1)}, bf16[520,128]{1,0:T(8,128)(2,1)S(1)}, u32[]{:S(2)}, u32[]{:S(2)}) collective-permute-start(bf16[520,128]{1,0:T(8,128)(2,1)S(1)} %get-tuple-element.37), channel_id=1, source_target_pairs={{0,8},{4,12},{8,0},{12,4},{16,24},{20,28},{24,16},{28,20},{1,9},{5... | collective-permute-start | bytes 399368 | tf_op jit(solution)/shard_map/ppermute | solution.py:325

commit v24 on v22

--- a/solution.py
+++ b/solution.py
@@ -87,57 +87,6 @@
     return jnp.broadcast_to(code.astype(jnp.float32), (TILE, BS)).astype(jnp.bfloat16)
 
 
-def pick_kernel(
-    flips,
-    occ_local,
-    aux_count,
-    pairs_in,
-    slot_in,
-    coef_in,
-    *refs,
-):
-    *outs, pairs, slot_row, coef, sems = refs
-    pairs_dev = pairs.shape[0]
-    blocks_dev = coef.shape[0] // BS
-    occ_count = coef.shape[1]
-    loads = [
-        pltpu.make_async_copy(source, target, sems.at[at])
-        for at, (source, target) in enumerate(
-            ((slot_in, slot_row), (pairs_in, pairs), (coef_in, coef))
-        )
-    ]
-    for load in loads:
-        load.start()
-    me = lax.axis_index("shell")
-    mine = lax.axis_index("aux")
-    every = sum(flips, [])
-    row = lax.broadcasted_iota(jnp.int32, (len(every) * occ_local, 1), 0)
-    owner = sum(jnp.where(row // occ_local == at, f, 0) for at, f in enumerate(every))
-    wanted = (jnp.bitwise_xor(owner, me) * aux_count + mine) * occ_local + row % occ_local
-    loads[0].wait()
-    target = targets_of(slot_row[...], slot_row.shape[1], occ_count)
-    pick = (wanted == target).astype(jnp.bfloat16)
-    for load in loads[1:]:
-        load.wait()
-    code = code_tile(pairs)
-    for k in range(pairs_dev):
-        start = pl.multiple_of(lax.rem(pairs[k, 1], blocks_dev) * BS, BS)
-        live = (pairs[k, 2] == 1).astype(jnp.float32)
-        piece = lax.dot_general(
-            pick,
-            coef[pl.ds(start, BS), :],
-            (((1,), (1,)), ((), ())),
-            preferred_element_type=jnp.float32,
-        )
-        piece = (piece * live).astype(jnp.bfloat16)
-        first = 0
-        for out in outs:
-            rows = out.shape[0] - TILE
-            out[:rows, k * BS : (k + 1) * BS] = piece[first : first + rows]
-            out[rows:, k * BS : (k + 1) * BS] = code
-            first += rows
-
-
 def near_kernel(
     occ_local,
     aux_count,
@@ -148,7 +97,7 @@
     beside,
     *refs,
 ):
-    *outs, pairs, slot_row, coef, blocks, sems = refs
+    *outs, far, pairs, slot_row, coef, blocks, sems = refs
     pairs_dev = pairs.shape[0]
     blocks_dev = coef.shape[0] // BS
     occ_count = coef.shape[1]
@@ -168,9 +117,14 @@
         row // occ_local % (aux_count // 2) * 2, mine
     )
     wanted = owner * occ_local + row % occ_local
+    far_rows = far.shape[0] - TILE
+    row = lax.broadcasted_iota(jnp.int32, (far_rows, 1), 0)
+    owner = jnp.bitwise_xor(len(outs) + row // occ_local, me) * aux_count + mine
+    far_wanted = owner * occ_local + row % occ_local
     loads[0].wait()
     target = targets_of(slot_row[...], slot_row.shape[1], occ_count)
     pick = (wanted == target).astype(jnp.bfloat16)
+    far_pick = (far_wanted == target).astype(jnp.bfloat16)
     for load in loads[1:]:
         load.wait()
     code = code_tile(pairs)
@@ -178,19 +132,22 @@
         coef[pl.ds(pl.multiple_of(lax.rem(pairs[k, 1], blocks_dev) * BS, BS), BS), :]
         for k in range(pairs_dev)
     ]
-    ordered = lax.dot_general(
-        pick,
-        jnp.concatenate(rows, axis=0),
-        (((1,), (1,)), ((), ())),
-        preferred_element_type=jnp.float32,
-    ).astype(jnp.bfloat16)
+    rows = jnp.concatenate(rows, axis=0)
+    contract = (((1,), (1,)), ((), ()))
+    ordered = lax.dot_general(pick, rows, contract, preferred_element_type=jnp.float32)
+    ordered = ordered.astype(jnp.bfloat16)
+    far_coef = lax.dot_general(far_pick, rows, contract, preferred_element_type=jnp.float32)
     for k in range(pairs_dev):
         block = jnp.dot(
             ordered[:, k * BS : (k + 1) * BS],
             jnp.concatenate([blocks[k], beside[k]], axis=1),
             preferred_element_type=jnp.float32,
         )
-        block = (block * (pairs[k, 2] == 1).astype(jnp.float32)).astype(jnp.bfloat16)
+        live = (pairs[k, 2] == 1).astype(jnp.float32)
+        block = (block * live).astype(jnp.bfloat16)
+        lanes = slice(k * BS, (k + 1) * BS)
+        far[:far_rows, lanes] = (far_coef[:, lanes] * live).astype(jnp.bfloat16)
+        far[far_rows:, lanes] = code
         for f, out in enumerate(outs):
             for j in range(aux_count // 2):
                 first = f * owned + j * occ_local
@@ -371,30 +328,18 @@
         pltpu.VMEM((1, occ_slot.shape[0]), jnp.int32),
         pltpu.VMEM(coef.shape, jnp.bfloat16),
     ]
-    near = pl.pallas_call(
+    *near, sent_coef = pl.pallas_call(
         functools.partial(near_kernel, occ_local, aux_count),
-        out_shape=[piece] * group,
+        out_shape=[piece] * group
+        + [jax.ShapeDtypeStruct((group * occ_local + TILE, pairs_dev * BS), jnp.bfloat16)],
         in_specs=[hbm] * 4 + [vmem],
-        out_specs=[vmem] * group,
+        out_specs=[vmem] * (group + 1),
         scratch_shapes=loaded
         + [pltpu.VMEM(blocks.shape, jnp.bfloat16), pltpu.SemaphoreType.DMA((4,))],
         compiler_params=params,
         name="near_blocks",
     )(*in_hbm(*operands, blocks), flip(blocks, "aux", 1))
     near = [near[0]] + [flip(near[f], "shell", f) for f in range(1, group)]
-    (sent_coef,) = pl.pallas_call(
-        functools.partial(
-            pick_kernel, [list(range(group, shell_count))], occ_local, aux_count
-        ),
-        out_shape=[
-            jax.ShapeDtypeStruct((group * occ_local + TILE, pairs_dev * BS), jnp.bfloat16)
-        ],
-        in_specs=[hbm] * 3,
-        out_specs=[vmem],
-        scratch_shapes=loaded + [pltpu.SemaphoreType.DMA((3,))],
-        compiler_params=params,
-        name="pick",
-    )(*in_hbm(*operands))
     far_block = after(far_block, sent_coef)
     far_coef = flip(after(sent_coef, far_block), "shell", group)
     far_pair = merged("far_pair", far_block, flip(far_block, "aux", 2))

time: 32.1 us -> 32 us (level)
  waiting for transfers between devices: 8.48 us -> 11.5 us
  Pallas kernels: 7.37 us -> 5.87 us
  starting transfers between devices: 15.9 us -> 14.4 us
    ppermute x12, waiting for transfers between devices: 8.48 us -> 11.5 us  [flip(): return lax.ppermute(value, axis, [(at, at ^ bits) for at in range(count)])]
    pallas_call x1 -> x0, Pallas kernels: 1.72 us -> none  [exchanged_inputs(): pl.pallas_call(functools.partial(pick_kernel, [list(range(group, shell_co...]
    ppermute x12, starting transfers between devices: 15.9 us -> 14.4 us  [flip(): return lax.ppermute(value, axis, [(at, at ^ bits) for at in range(count)])]
  transfers between devices with their start and end apart: 12 -> 12, of which waited for: 7 -> 8; matrix products, arithmetic and copies ran while one was open for 0% -> 0% of each run, Pallas kernels for 18% -> 14%
where the time goes in v24:
time: 32 us; the launch traced here: 31.9 us
  starting transfers between devices  14.4 us (45%)
  waiting for transfers between devices  11.5 us (36%)
  Pallas kernels  5.87 us (18%)
    ppermute x12, starting transfers between devices, flip(): return lax.ppermute(value, axis, [(at, at ^ bits) for at in range(count)])  14.4 us
    ppermute x12, waiting for transfers between devices, flip(): return lax.ppermute(value, axis, [(at, at ^ bits) for at in range(count)])  11.5 us
    pallas_call x1, Pallas kernels, exchanged_inputs(): pl.pallas_call(functools.partial(near_kernel, occ_local, aux_count), out_...  2.2 us
    pallas_call x1, Pallas kernels, exchanged_inputs(): pl.pallas_call(collect_kernel, out_shape=[jax.ShapeDtypeStruct((occ_local...  1.48 us
    pallas_call x1, Pallas kernels, exchanged_inputs(): pl.pallas_call(near_sum_kernel, out_shape=[total_shape, jax.ShapeDtypeStr...  1.41 us
  transfers between devices with their start and end apart: 12, of which 8 were waited for; matrix products, arithmetic and copies ran while one was open for 0% of the time, Pallas kernels for 14%

profile of v24, /device:TPU:0, one launch (start us, length us, event | category | flops | bytes accessed | tf_op | source)
XLA Modules:
  0.0 31.9 jit_solution(17670859813352150692)
XLA Ops:
  0.0 0.5 %collective-permute-start = (bf16[4,128,128]{2,1,0:T(8,128)(2,1)}, bf16[4,128,128]{2,1,0:T(8,128)(2,1)S(1)}, u32[]{:S(2)}, u32[]{:S(2)}) collective-permute-start(bf16[4,128,128]{2,1,0:T(8,128)(2,1)} %bitcast.2), channel_id=1, source_target_pairs={{0,1},{1,0},{2,3},{3,2},{4,5},{5,4},{6,7},{7,6},{8,9},{9,8},{10,11... | collective-permute-start | bytes 393224 | tf_op jit(solution)/shard_map/ppermute | solution.py:282
  0.5 3.6 %collective-permute-start.1 = (bf16[4,128,128]{2,1,0:T(8,128)(2,1)}, bf16[4,128,128]{2,1,0:T(8,128)(2,1)S(1)}, u32[]{:S(2)}, u32[]{:S(2)}) collective-permute-start(bf16[4,128,128]{2,1,0:T(8,128)(2,1)} %bitcast.3), channel_id=1, source_target_pairs={{0,16},{4,20},{8,24},{12,28},{16,0},{20,4},{24,8},{28,12},{1,17},{... | collective-permute-start | bytes 393224 | tf_op jit(solution)/shard_map/ppermute | solution.py:282
  4.0 2.2 %near_blocks.1 = (bf16[520,128]{1,0:T(8,128)(2,1)S(1)}, bf16[520,128]{1,0:T(8,128)(2,1)S(1)}, bf16[520,128]{1,0:T(8,128)(2,1)S(1)}, bf16[520,128]{1,0:T(8,128)(2,1)S(1)}, bf16[136,512]{1,0:T(8,128)(2,1)S(1)}) custom-call(s32[4,3]{1,0:T(4,128)} %pairs_in.1, s32[1,128]{1,0:T(1,128)} %bitcast.5, bf16[512,1024]{1,0:T(8,128)(2,1)} %coef_in.1, ...), custom_call_target="tpu_custom_call" | custom-call | tf_op jit(solution)/shard_map/near_blocks/pallas_call | solution.py:331
  6.3 1.6 %collective-permute-start.5 = (bf16[520,128]{1,0:T(8,128)(2,1)S(1)}, bf16[520,128]{1,0:T(8,128)(2,1)S(1)}, u32[]{:S(2)}, u32[]{:S(2)}) collective-permute-start(bf16[520,128]{1,0:T(8,128)(2,1)S(1)} %get-tuple-element.32), channel_id=1, source_target_pairs={{0,4},{4,0},{8,12},{12,8},{16,20},{20,16},{24,28},{28,24},{1,5},{5... | collective-permute-start | bytes 399368 | tf_op jit(solution)/shard_map/ppermute | solution.py:282
  7.8 1.6 %collective-permute-start.6 = (bf16[520,128]{1,0:T(8,128)(2,1)S(1)}, bf16[520,128]{1,0:T(8,128)(2,1)S(1)}, u32[]{:S(2)}, u32[]{:S(2)}) collective-permute-start(bf16[520,128]{1,0:T(8,128)(2,1)S(1)} %get-tuple-element.33), channel_id=1, source_target_pairs={{0,8},{4,12},{8,0},{12,4},{16,24},{20,28},{24,16},{28,20},{1,9},{5... | collective-permute-start | bytes 399368 | tf_op jit(solution)/shard_map/ppermute | solution.py:282
  9.4 0.4 %collective-permute-start.7 = (bf16[520,128]{1,0:T(8,128)(2,1)S(1)}, bf16[520,128]{1,0:T(8,128)(2,1)S(1)}, u32[]{:S(2)}, u32[]{:S(2)}) collective-permute-start(bf16[520,128]{1,0:T(8,128)(2,1)S(1)} %get-tuple-element.34), channel_id=1, source_target_pairs={{0,12},{4,8},{8,4},{12,0},{16,28},{20,24},{24,20},{28,16},{1,13},{... | collective-permute-start | bytes 399368 | tf_op jit(solution)/shard_map/ppermute | solution.py:282
  9.8 1.5 %collective-permute-done.1.first = bf16[4,128,128]{2,1,0:T(8,128)(2,1)S(1)} collective-permute-done((bf16[4,128,128]{2,1,0:T(8,128)(2,1)}, bf16[4,128,128]{2,1,0:T(8,128)(2,1)S(1)}, u32[]{:S(2)}, u32[]{:S(2)}) %collective-permute-start.1) | collective-permute-done | bytes 131104 | tf_op jit(solution)/shard_map/ppermute | solution.py:282
  11.3 1.6 %collective-permute-start.3 = (bf16[4,128,128]{2,1,0:T(8,128)(2,1)S(1)}, bf16[4,128,128]{2,1,0:T(8,128)(2,1)S(1)}, u32[]{:S(2)}, u32[]{:S(2)}) collective-permute-start(bf16[4,128,128]{2,1,0:T(8,128)(2,1)S(1)} %collective-permute-done.1.first), channel_id=1, source_target_pairs={{0,2},{1,3},{2,0},{3,1},{4,6},{5,7},{6,4},{7,5},{8,10},{9,11},{10,... | collective-permute-start | bytes 393224 | tf_op jit(solution)/shard_map/ppermute | solution.py:282
  12.9 3.7 %collective-permute-done.3.second = bf16[4,128,128]{2,1,0:T(8,128)(2,1)S(1)} collective-permute-done((bf16[4,128,128]{2,1,0:T(8,128)(2,1)S(1)}, bf16[4,128,128]{2,1,0:T(8,128)(2,1)S(1)}, u32[]{:S(2)}, u32[]{:S(2)}) %collective-permute-start.3) | collective-permute-done | bytes 131104 | tf_op jit(solution)/shard_map/ppermute | solution.py:282
  16.6 0.3 %far_pair.1.blocks = bf16[8,128,128]{2,1,0:T(8,128)(2,1)S(1)} custom-call(bf16[4,128,128]{2,1,0:T(8,128)(2,1)S(1)} %collective-permute-done.1.first, bf16[4,128,128]{2,1,0:T(8,128)(2,1)S(1)} %collective-permute-done.3.second), custom_call_target="tpu_custom_call" | custom-call | tf_op jit(solution)/shard_map/far_pair/pallas_call | solution.py:311
  17.0 2.0 %collective-permute-done.7.refs_3_ = bf16[520,128]{1,0:T(8,128)(2,1)S(1)} collective-permute-done((bf16[520,128]{1,0:T(8,128)(2,1)S(1)}, bf16[520,128]{1,0:T(8,128)(2,1)S(1)}, u32[]{:S(2)}, u32[]{:S(2)}) %collective-permute-start.7) | collective-permute-done | bytes 133152 | tf_op jit(solution)/shard_map/ppermute | solution.py:282
  19.0 1.6 %collective-permute-start.8 = (bf16[1024,128]{1,0:T(8,128)(2,1)S(1)}, bf16[1024,128]{1,0:T(8,128)(2,1)S(1)}, u32[]{:S(2)}, u32[]{:S(2)}) collective-permute-start(bf16[1024,128]{1,0:T(8,128)(2,1)S(1)} %regroup.1), channel_id=1, source_target_pairs={{0,2},{1,3},{2,0},{3,1},{4,6},{5,7},{6,4},{7,5},{8,10},{9,11},{10,... | collective-permute-start | bytes 786440 | tf_op jit(solution)/shard_map/ppermute | solution.py:282
  20.6 1.1 %collective-permute-done.2.coefs = bf16[136,512]{1,0:T(8,128)(2,1)S(1)} collective-permute-done((bf16[136,512]{1,0:T(8,128)(2,1)S(1)}, bf16[136,512]{1,0:T(8,128)(2,1)S(1)}, u32[]{:S(2)}, u32[]{:S(2)}) %collective-permute-start.2) | collective-permute-done | bytes 139296 | tf_op jit(solution)/shard_map/ppermute | solution.py:282
  21.8 0.2 far_blocks_0.1
  22.0 0.2 far_blocks_1.1
  22.2 0.9 %collective-permute-start.9 = (bf16[520,128]{1,0:T(8,128)(2,1)S(1)}, bf16[520,128]{1,0:T(8,128)(2,1)S(1)}, u32[]{:S(2)}, u32[]{:S(2)}) collective-permute-start(bf16[520,128]{1,0:T(8,128)(2,1)S(1)} %get-tuple-element.37), channel_id=1, source_target_pairs={{0,12},{4,8},{8,4},{12,0},{16,28},{20,24},{24,20},{28,16},{1,13},{... | collective-permute-start | bytes 399368 | tf_op jit(solution)/shard_map/ppermute | solution.py:282
  23.1 1.1 %collective-permute-start.10 = (bf16[520,128]{1,0:T(8,128)(2,1)S(1)}, bf16[520,128]{1,0:T(8,128)(2,1)S(1)}, u32[]{:S(2)}, u32[]{:S(2)}) collective-permute-start(bf16[520,128]{1,0:T(8,128)(2,1)S(1)} %get-tuple-element.38), channel_id=1, source_target_pairs={{0,4},{4,0},{8,12},{12,8},{16,20},{20,16},{24,28},{28,24},{1,5},{5... | collective-permute-start | bytes 399368 | tf_op jit(solution)/shard_map/ppermute | solution.py:282
  24.1 1.6 %collective-permute-start.11 = (bf16[520,128]{1,0:T(8,128)(2,1)S(1)}, bf16[520,128]{1,0:T(8,128)(2,1)S(1)}, u32[]{:S(2)}, u32[]{:S(2)}) collective-permute-start(bf16[520,128]{1,0:T(8,128)(2,1)S(1)} %get-tuple-element.39), channel_id=1, source_target_pairs={{0,8},{4,12},{8,0},{12,4},{16,24},{20,28},{24,16},{28,20},{1,9},{5... | collective-permute-start | bytes 399368 | tf_op jit(solution)/shard_map/ppermute | solution.py:282
  25.8 1.3 %collective-permute-done.8.refs_4_ = bf16[1024,128]{1,0:T(8,128)(2,1)S(1)} collective-permute-done((bf16[1024,128]{1,0:T(8,128)(2,1)S(1)}, bf16[1024,128]{1,0:T(8,128)(2,1)S(1)}, u32[]{:S(2)}, u32[]{:S(2)}) %collective-permute-start.8) | collective-permute-done | bytes 262176 | tf_op jit(solution)/shard_map/ppermute | solution.py:282
  27.1 1.4 %near_sum.1 = (f32[32,128,128]{2,1,0:T(8,128)S(1)}, bf16[128,128]{1,0:T(8,128)(2,1)S(1)}) custom-call(bf16[4,4]{1,0:T(4,128)(2,1)} %metric_in.1, bf16[520,128]{1,0:T(8,128)(2,1)S(1)} %get-tuple-element.30.own, bf16[520,128]{1,0:T(8,128)(2,1)S(1)} %get-tuple-element.31.refs_0_, bf16[520,128]{1,0:T(8,128)(2,1)S(1)} %collective-permute-done.5.refs_1_, ...), custom_call_target="tpu_custom_call" | custom-call | flops 3000000000 | bytes 1048576 | tf_op jit(solution)/shard_map/near_sum/pallas_call | solution.py:374
  28.5 1.0 %collective-permute-done.9.refs_0_ = bf16[520,128]{1,0:T(8,128)(2,1)S(1)} collective-permute-done((bf16[520,128]{1,0:T(8,128)(2,1)S(1)}, bf16[520,128]{1,0:T(8,128)(2,1)S(1)}, u32[]{:S(2)}, u32[]{:S(2)}) %collective-permute-start.9) | collective-permute-done | bytes 133152 | tf_op jit(solution)/shard_map/ppermute | solution.py:282
  29.6 0.7 %collective-permute-done.10.refs_1_ = bf16[520,128]{1,0:T(8,128)(2,1)S(1)} collective-permute-done((bf16[520,128]{1,0:T(8,128)(2,1)S(1)}, bf16[520,128]{1,0:T(8,128)(2,1)S(1)}, u32[]{:S(2)}, u32[]{:S(2)}) %collective-permute-start.10) | collective-permute-done | bytes 133152 | tf_op jit(solution)/shard_map/ppermute | solution.py:282
  30.2 0.2 collective-permute-done.11.refs_2_
  30.4 1.5 %collect.1 = (bf16[32,4,4096]{2,1,0:T(4,128)(2,1)}, f32[32,128,128]{2,1,0:T(8,128)S(1)}) custom-call(bf16[128,128]{1,0:T(8,128)(2,1)S(1)} %get-tuple-element.35.mix, f32[32,128,128]{2,1,0:T(8,128)S(1)} %get-tuple-element.36.total_in, bf16[520,128]{1,0:T(8,128)(2,1)S(1)} %collective-permute-done.9.refs_0_, ...), custom_call_target="tpu_custom_call", output_to_operand_aliasing={{1}: (1, {})} | custom-call | tf_op jit(solution)/shard_map/collect/pallas_call | solution.py:389
  (7 shorter events, 0.1 us)
Async XLA Ops:
  0.0 4.0 %collective-permute-start = (bf16[4,128,128]{2,1,0:T(8,128)(2,1)}, bf16[4,128,128]{2,1,0:T(8,128)(2,1)S(1)}, u32[]{:S(2)}, u32[]{:S(2)}) collective-permute-start(bf16[4,128,128]{2,1,0:T(8,128)(2,1)} %bitcast.2), channel_id=1, source_target_pairs={{0,1},{1,0},{2,3},{3,2},{4,5},{5,4},{6,7},{7,6},{8,9},{9,8},{10,11... | collective-permute-start | bytes 393224 | tf_op jit(solution)/shard_map/ppermute | solution.py:282
  0.5 10.9 %collective-permute-start.1 = (bf16[4,128,128]{2,1,0:T(8,128)(2,1)}, bf16[4,128,128]{2,1,0:T(8,128)(2,1)S(1)}, u32[]{:S(2)}, u32[]{:S(2)}) collective-permute-start(bf16[4,128,128]{2,1,0:T(8,128)(2,1)} %bitcast.3), channel_id=1, source_target_pairs={{0,16},{4,20},{8,24},{12,28},{16,0},{20,4},{24,8},{28,12},{1,17},{... | collective-permute-start | bytes 393224 | tf_op jit(solution)/shard_map/ppermute | solution.py:282
  6.3 10.7 %collective-permute-start.5 = (bf16[520,128]{1,0:T(8,128)(2,1)S(1)}, bf16[520,128]{1,0:T(8,128)(2,1)S(1)}, u32[]{:S(2)}, u32[]{:S(2)}) collective-permute-start(bf16[520,128]{1,0:T(8,128)(2,1)S(1)} %get-tuple-element.32), channel_id=1, source_target_pairs={{0,4},{4,0},{8,12},{12,8},{16,20},{20,16},{24,28},{28,24},{1,5},{5... | collective-permute-start | bytes 399368 | tf_op jit(solution)/shard_map/ppermute | solution.py:282
  7.8 9.2 %collective-permute-start.6 = (bf16[520,128]{1,0:T(8,128)(2,1)S(1)}, bf16[520,128]{1,0:T(8,128)(2,1)S(1)}, u32[]{:S(2)}, u32[]{:S(2)}) collective-permute-start(bf16[520,128]{1,0:T(8,128)(2,1)S(1)} %get-tuple-element.33), channel_id=1, source_target_pairs={{0,8},{4,12},{8,0},{12,4},{16,24},{20,28},{24,16},{28,20},{1,9},{5... | collective-permute-start | bytes 399368 | tf_op jit(solution)/shard_map/ppermute | solution.py:282
  9.4 9.6 %collective-permute-start.7 = (bf16[520,128]{1,0:T(8,128)(2,1)S(1)}, bf16[520,128]{1,0:T(8,128)(2,1)S(1)}, u32[]{:S(2)}, u32[]{:S(2)}) collective-permute-start(bf16[520,128]{1,0:T(8,128)(2,1)S(1)} %get-tuple-element.34), channel_id=1, source_target_pairs={{0,12},{4,8},{8,4},{12,0},{16,28},{20,24},{24,20},{28,16},{1,13},{... | collective-permute-start | bytes 399368 | tf_op jit(solution)/shard_map/ppermute | solution.py:282
  11.3 5.2 %collective-permute-start.3 = (bf16[4,128,128]{2,1,0:T(8,128)(2,1)S(1)}, bf16[4,128,128]{2,1,0:T(8,128)(2,1)S(1)}, u32[]{:S(2)}, u32[]{:S(2)}) collective-permute-start(bf16[4,128,128]{2,1,0:T(8,128)(2,1)S(1)} %collective-permute-done.1.first), channel_id=1, source_target_pairs={{0,2},{1,3},{2,0},{3,1},{4,6},{5,7},{6,4},{7,5},{8,10},{9,11},{10,... | collective-permute-start | bytes 393224 | tf_op jit(solution)/shard_map/ppermute | solution.py:282
  12.9 8.9 %collective-permute-start.2 = (bf16[136,512]{1,0:T(8,128)(2,1)S(1)}, bf16[136,512]{1,0:T(8,128)(2,1)S(1)}, u32[]{:S(2)}, u32[]{:S(2)}) collective-permute-start(bf16[136,512]{1,0:T(8,128)(2,1)S(1)} %get-tuple-element.25), channel_id=1, source_target_pairs={{0,16},{4,20},{8,24},{12,28},{16,0},{20,4},{24,8},{28,12},{1,17},{... | collective-permute-start | bytes 417800 | tf_op jit(solution)/shard_map/ppermute | solution.py:282
  16.9 5.1 %collective-permute-start.4 = (bf16[8,128,128]{2,1,0:T(8,128)(2,1)S(1)}, bf16[8,128,128]{2,1,0:T(8,128)(2,1)S(1)}, u32[]{:S(2)}, u32[]{:S(2)}) collective-permute-start(bf16[8,128,128]{2,1,0:T(8,128)(2,1)S(1)} %far_pair.1.blocks), channel_id=1, source_target_pairs={{0,1},{1,0},{2,3},{3,2},{4,5},{5,4},{6,7},{7,6},{8,9},{9,8},{10,11... | collective-permute-start | bytes 786440 | tf_op jit(solution)/shard_map/ppermute | solution.py:282
  19.0 8.1 %collective-permute-start.8 = (bf16[1024,128]{1,0:T(8,128)(2,1)S(1)}, bf16[1024,128]{1,0:T(8,128)(2,1)S(1)}, u32[]{:S(2)}, u32[]{:S(2)}) collective-permute-start(bf16[1024,128]{1,0:T(8,128)(2,1)S(1)} %regroup.1), channel_id=1, source_target_pairs={{0,2},{1,3},{2,0},{3,1},{4,6},{5,7},{6,4},{7,5},{8,10},{9,11},{10,... | collective-permute-start | bytes 786440 | tf_op jit(solution)/shard_map/ppermute | solution.py:282
  22.2 7.3 %collective-permute-start.9 = (bf16[520,128]{1,0:T(8,128)(2,1)S(1)}, bf16[520,128]{1,0:T(8,128)(2,1)S(1)}, u32[]{:S(2)}, u32[]{:S(2)}) collective-permute-start(bf16[520,128]{1,0:T(8,128)(2,1)S(1)} %get-tuple-element.37), channel_id=1, source_target_pairs={{0,12},{4,8},{8,4},{12,0},{16,28},{20,24},{24,20},{28,16},{1,13},{... | collective-permute-start | bytes 399368 | tf_op jit(solution)/shard_map/ppermute | solution.py:282
  23.1 7.1 %collective-permute-start.10 = (bf16[520,128]{1,0:T(8,128)(2,1)S(1)}, bf16[520,128]{1,0:T(8,128)(2,1)S(1)}, u32[]{:S(2)}, u32[]{:S(2)}) collective-permute-start(bf16[520,128]{1,0:T(8,128)(2,1)S(1)} %get-tuple-element.38), channel_id=1, source_target_pairs={{0,4},{4,0},{8,12},{12,8},{16,20},{20,16},{24,28},{28,24},{1,5},{5... | collective-permute-start | bytes 399368 | tf_op jit(solution)/shard_map/ppermute | solution.py:282
  24.1 6.3 %collective-permute-start.11 = (bf16[520,128]{1,0:T(8,128)(2,1)S(1)}, bf16[520,128]{1,0:T(8,128)(2,1)S(1)}, u32[]{:S(2)}, u32[]{:S(2)}) collective-permute-start(bf16[520,128]{1,0:T(8,128)(2,1)S(1)} %get-tuple-element.39), channel_id=1, source_target_pairs={{0,8},{4,12},{8,0},{12,4},{16,24},{20,28},{24,16},{28,20},{1,9},{5... | collective-permute-start | bytes 399368 | tf_op jit(solution)/shard_map/ppermute | solution.py:282

commit v25 on v24

--- a/solution.py
+++ b/solution.py
@@ -162,6 +162,7 @@
 
 def regroup_kernel(*refs):
     *received, out = refs
+    received = received[::-1]
     rows = out.shape[0] // len(received)
     for f, piece in enumerate(received):
         out[f * rows : (f + 1) * rows, :] = piece[rows : 2 * rows, :]
@@ -212,6 +213,7 @@
 
 def near_sum_kernel(metric_in, own, *refs):
     *received, across, total, mix, metric, codes, sem = refs
+    received = received[::-1]
     load = pltpu.make_async_copy(metric_in, metric, sem)
     load.start()
     total[...] = jnp.zeros_like(total)
@@ -354,7 +356,7 @@
             out_specs=vmem,
             compiler_params=params,
             name="regroup",
-        )(*near),
+        )(*reversed(near)),
         "aux",
         2,
     )
@@ -384,7 +386,7 @@
         compiler_params=params,
         cost_estimate=cost(3e9),
         name="near_sum",
-    )(*in_hbm(metric), far[0], *near, across)
+    )(*in_hbm(metric), far[0], *reversed(near), across)
     far = [far[0]] + [flip(far[f], "shell", f) for f in range(1, group)]
     return pl.pallas_call(
         collect_kernel,

time: 32 us -> 32 us (level)
  starting transfers between devices: 14.4 us -> 15 us
  waiting for transfers between devices: 11.5 us -> 10.9 us
    ppermute x12, waiting for transfers between devices: 11.5 us -> 10.9 us  [flip(): return lax.ppermute(value, axis, [(at, at ^ bits) for at in range(count)])]
    ppermute x12, starting transfers between devices: 14.4 us -> 15 us  [flip(): return lax.ppermute(value, axis, [(at, at ^ bits) for at in range(count)])]
where the time goes in v25:
time: 32 us; the launch traced here: 31.9 us
  starting transfers between devices  15 us (47%)
  waiting for transfers between devices  10.9 us (34%)
  Pallas kernels  5.87 us (18%)
    ppermute x12, starting transfers between devices, flip(): return lax.ppermute(value, axis, [(at, at ^ bits) for at in range(count)])  15 us
    ppermute x12, waiting for transfers between devices, flip(): return lax.ppermute(value, axis, [(at, at ^ bits) for at in range(count)])  10.9 us
    pallas_call x1, Pallas kernels, exchanged_inputs(): pl.pallas_call(functools.partial(near_kernel, occ_local, aux_count), out_...  2.2 us
    pallas_call x1, Pallas kernels, exchanged_inputs(): pl.pallas_call(collect_kernel, out_shape=[jax.ShapeDtypeStruct((occ_local...  1.48 us
    pallas_call x1, Pallas kernels, exchanged_inputs(): pl.pallas_call(near_sum_kernel, out_shape=[total_shape, jax.ShapeDtypeStr...  1.41 us
  transfers between devices with their start and end apart: 12, of which 8 were waited for; matrix products, arithmetic and copies ran while one was open for 0% of the time, Pallas kernels for 14%

profile of v25, /device:TPU:0, one launch (start us, length us, event | category | flops | bytes accessed | tf_op | source)
XLA Modules:
  0.0 31.9 jit_solution(7795523351875884565)
XLA Ops:
  0.0 0.5 %collective-permute-start = (bf16[4,128,128]{2,1,0:T(8,128)(2,1)}, bf16[4,128,128]{2,1,0:T(8,128)(2,1)S(1)}, u32[]{:S(2)}, u32[]{:S(2)}) collective-permute-start(bf16[4,128,128]{2,1,0:T(8,128)(2,1)} %bitcast.2), channel_id=1, source_target_pairs={{0,1},{1,0},{2,3},{3,2},{4,5},{5,4},{6,7},{7,6},{8,9},{9,8},{10,11... | collective-permute-start | bytes 393224 | tf_op jit(solution)/shard_map/ppermute | solution.py:284
  0.5 3.6 %collective-permute-start.1 = (bf16[4,128,128]{2,1,0:T(8,128)(2,1)}, bf16[4,128,128]{2,1,0:T(8,128)(2,1)S(1)}, u32[]{:S(2)}, u32[]{:S(2)}) collective-permute-start(bf16[4,128,128]{2,1,0:T(8,128)(2,1)} %bitcast.3), channel_id=1, source_target_pairs={{0,16},{4,20},{8,24},{12,28},{16,0},{20,4},{24,8},{28,12},{1,17},{... | collective-permute-start | bytes 393224 | tf_op jit(solution)/shard_map/ppermute | solution.py:284
  4.0 2.2 %near_blocks.1 = (bf16[520,128]{1,0:T(8,128)(2,1)S(1)}, bf16[520,128]{1,0:T(8,128)(2,1)S(1)}, bf16[520,128]{1,0:T(8,128)(2,1)S(1)}, bf16[520,128]{1,0:T(8,128)(2,1)S(1)}, bf16[136,512]{1,0:T(8,128)(2,1)S(1)}) custom-call(s32[4,3]{1,0:T(4,128)} %pairs_in.1, s32[1,128]{1,0:T(1,128)} %bitcast.5, bf16[512,1024]{1,0:T(8,128)(2,1)} %coef_in.1, ...), custom_call_target="tpu_custom_call" | custom-call | tf_op jit(solution)/shard_map/near_blocks/pallas_call | solution.py:333
  6.3 2.6 %collective-permute-start.5 = (bf16[520,128]{1,0:T(8,128)(2,1)S(1)}, bf16[520,128]{1,0:T(8,128)(2,1)S(1)}, u32[]{:S(2)}, u32[]{:S(2)}) collective-permute-start(bf16[520,128]{1,0:T(8,128)(2,1)S(1)} %get-tuple-element.31), channel_id=1, source_target_pairs={{0,12},{4,8},{8,4},{12,0},{16,28},{20,24},{24,20},{28,16},{1,13},{... | collective-permute-start | bytes 399368 | tf_op jit(solution)/shard_map/ppermute | solution.py:284
  8.8 0.4 %collective-permute-start.6 = (bf16[520,128]{1,0:T(8,128)(2,1)S(1)}, bf16[520,128]{1,0:T(8,128)(2,1)S(1)}, u32[]{:S(2)}, u32[]{:S(2)}) collective-permute-start(bf16[520,128]{1,0:T(8,128)(2,1)S(1)} %get-tuple-element.32), channel_id=1, source_target_pairs={{0,8},{4,12},{8,0},{12,4},{16,24},{20,28},{24,16},{28,20},{1,9},{5... | collective-permute-start | bytes 399368 | tf_op jit(solution)/shard_map/ppermute | solution.py:284
  9.3 0.5 %collective-permute-start.7 = (bf16[520,128]{1,0:T(8,128)(2,1)S(1)}, bf16[520,128]{1,0:T(8,128)(2,1)S(1)}, u32[]{:S(2)}, u32[]{:S(2)}) collective-permute-start(bf16[520,128]{1,0:T(8,128)(2,1)S(1)} %get-tuple-element.33), channel_id=1, source_target_pairs={{0,4},{4,0},{8,12},{12,8},{16,20},{20,16},{24,28},{28,24},{1,5},{5... | collective-permute-start | bytes 399368 | tf_op jit(solution)/shard_map/ppermute | solution.py:284
  9.8 1.5 %collective-permute-done.1.first = bf16[4,128,128]{2,1,0:T(8,128)(2,1)S(1)} collective-permute-done((bf16[4,128,128]{2,1,0:T(8,128)(2,1)}, bf16[4,128,128]{2,1,0:T(8,128)(2,1)S(1)}, u32[]{:S(2)}, u32[]{:S(2)}) %collective-permute-start.1) | collective-permute-done | bytes 131104 | tf_op jit(solution)/shard_map/ppermute | solution.py:284
  11.3 1.6 %collective-permute-start.3 = (bf16[4,128,128]{2,1,0:T(8,128)(2,1)S(1)}, bf16[4,128,128]{2,1,0:T(8,128)(2,1)S(1)}, u32[]{:S(2)}, u32[]{:S(2)}) collective-permute-start(bf16[4,128,128]{2,1,0:T(8,128)(2,1)S(1)} %collective-permute-done.1.first), channel_id=1, source_target_pairs={{0,2},{1,3},{2,0},{3,1},{4,6},{5,7},{6,4},{7,5},{8,10},{9,11},{10,... | collective-permute-start | bytes 393224 | tf_op jit(solution)/shard_map/ppermute | solution.py:284
  12.9 3.7 %collective-permute-done.3.second = bf16[4,128,128]{2,1,0:T(8,128)(2,1)S(1)} collective-permute-done((bf16[4,128,128]{2,1,0:T(8,128)(2,1)S(1)}, bf16[4,128,128]{2,1,0:T(8,128)(2,1)S(1)}, u32[]{:S(2)}, u32[]{:S(2)}) %collective-permute-start.3) | collective-permute-done | bytes 131104 | tf_op jit(solution)/shard_map/ppermute | solution.py:284
  16.6 0.3 %far_pair.1.blocks = bf16[8,128,128]{2,1,0:T(8,128)(2,1)S(1)} custom-call(bf16[4,128,128]{2,1,0:T(8,128)(2,1)S(1)} %collective-permute-done.1.first, bf16[4,128,128]{2,1,0:T(8,128)(2,1)S(1)} %collective-permute-done.3.second), custom_call_target="tpu_custom_call" | custom-call | tf_op jit(solution)/shard_map/far_pair/pallas_call | solution.py:313
  17.0 1.3 %collective-permute-done.6.refs_1_ = bf16[520,128]{1,0:T(8,128)(2,1)S(1)} collective-permute-done((bf16[520,128]{1,0:T(8,128)(2,1)S(1)}, bf16[520,128]{1,0:T(8,128)(2,1)S(1)}, u32[]{:S(2)}, u32[]{:S(2)}) %collective-permute-start.6) | collective-permute-done | bytes 133152 | tf_op jit(solution)/shard_map/ppermute | solution.py:284
  18.3 2.2 %collective-permute-start.8 = (bf16[1024,128]{1,0:T(8,128)(2,1)S(1)}, bf16[1024,128]{1,0:T(8,128)(2,1)S(1)}, u32[]{:S(2)}, u32[]{:S(2)}) collective-permute-start(bf16[1024,128]{1,0:T(8,128)(2,1)S(1)} %regroup.1), channel_id=1, source_target_pairs={{0,2},{1,3},{2,0},{3,1},{4,6},{5,7},{6,4},{7,5},{8,10},{9,11},{10,... | collective-permute-start | bytes 786440 | tf_op jit(solution)/shard_map/ppermute | solution.py:284
  20.5 1.2 %collective-permute-done.2.coefs = bf16[136,512]{1,0:T(8,128)(2,1)S(1)} collective-permute-done((bf16[136,512]{1,0:T(8,128)(2,1)S(1)}, bf16[136,512]{1,0:T(8,128)(2,1)S(1)}, u32[]{:S(2)}, u32[]{:S(2)}) %collective-permute-start.2) | collective-permute-done | bytes 139296 | tf_op jit(solution)/shard_map/ppermute | solution.py:284
  21.8 0.2 far_blocks_0.1
  22.0 0.2 far_blocks_1.1
  22.2 0.6 %collective-permute-start.9 = (bf16[520,128]{1,0:T(8,128)(2,1)S(1)}, bf16[520,128]{1,0:T(8,128)(2,1)S(1)}, u32[]{:S(2)}, u32[]{:S(2)}) collective-permute-start(bf16[520,128]{1,0:T(8,128)(2,1)S(1)} %get-tuple-element.37), channel_id=1, source_target_pairs={{0,12},{4,8},{8,4},{12,0},{16,28},{20,24},{24,20},{28,16},{1,13},{... | collective-permute-start | bytes 399368 | tf_op jit(solution)/shard_map/ppermute | solution.py:284
  22.8 1.4 %collective-permute-start.10 = (bf16[520,128]{1,0:T(8,128)(2,1)S(1)}, bf16[520,128]{1,0:T(8,128)(2,1)S(1)}, u32[]{:S(2)}, u32[]{:S(2)}) collective-permute-start(bf16[520,128]{1,0:T(8,128)(2,1)S(1)} %get-tuple-element.38), channel_id=1, source_target_pairs={{0,4},{4,0},{8,12},{12,8},{16,20},{20,16},{24,28},{28,24},{1,5},{5... | collective-permute-start | bytes 399368 | tf_op jit(solution)/shard_map/ppermute | solution.py:284
  24.2 1.6 %collective-permute-start.11 = (bf16[520,128]{1,0:T(8,128)(2,1)S(1)}, bf16[520,128]{1,0:T(8,128)(2,1)S(1)}, u32[]{:S(2)}, u32[]{:S(2)}) collective-permute-start(bf16[520,128]{1,0:T(8,128)(2,1)S(1)} %get-tuple-element.39), channel_id=1, source_target_pairs={{0,8},{4,12},{8,0},{12,4},{16,24},{20,28},{24,16},{28,20},{1,9},{5... | collective-permute-start | bytes 399368 | tf_op jit(solution)/shard_map/ppermute | solution.py:284
  25.8 1.3 %collective-permute-done.8.refs_4_ = bf16[1024,128]{1,0:T(8,128)(2,1)S(1)} collective-permute-done((bf16[1024,128]{1,0:T(8,128)(2,1)S(1)}, bf16[1024,128]{1,0:T(8,128)(2,1)S(1)}, u32[]{:S(2)}, u32[]{:S(2)}) %collective-permute-start.8) | collective-permute-done | bytes 262176 | tf_op jit(solution)/shard_map/ppermute | solution.py:284
  27.0 1.4 %near_sum.1 = (f32[32,128,128]{2,1,0:T(8,128)S(1)}, bf16[128,128]{1,0:T(8,128)(2,1)S(1)}) custom-call(bf16[4,4]{1,0:T(4,128)(2,1)} %metric_in.1, bf16[520,128]{1,0:T(8,128)(2,1)S(1)} %get-tuple-element.30.own, bf16[520,128]{1,0:T(8,128)(2,1)S(1)} %collective-permute-done.5.refs_0_, bf16[520,128]{1,0:T(8,128)(2,1)S(1)} %collective-permute-done.6.refs_1_, ...), custom_call_target="tpu_custom_call" | custom-call | flops 3000000000 | bytes 1048576 | tf_op jit(solution)/shard_map/near_sum/pallas_call | solution.py:376
  28.4 0.8 %collective-permute-done.9.refs_0_ = bf16[520,128]{1,0:T(8,128)(2,1)S(1)} collective-permute-done((bf16[520,128]{1,0:T(8,128)(2,1)S(1)}, bf16[520,128]{1,0:T(8,128)(2,1)S(1)}, u32[]{:S(2)}, u32[]{:S(2)}) %collective-permute-start.9) | collective-permute-done | bytes 133152 | tf_op jit(solution)/shard_map/ppermute | solution.py:284
  29.2 1.0 %collective-permute-done.10.refs_1_ = bf16[520,128]{1,0:T(8,128)(2,1)S(1)} collective-permute-done((bf16[520,128]{1,0:T(8,128)(2,1)S(1)}, bf16[520,128]{1,0:T(8,128)(2,1)S(1)}, u32[]{:S(2)}, u32[]{:S(2)}) %collective-permute-start.10) | collective-permute-done | bytes 133152 | tf_op jit(solution)/shard_map/ppermute | solution.py:284
  30.2 0.1 collective-permute-done.11.refs_2_
  30.4 1.5 %collect.1 = (bf16[32,4,4096]{2,1,0:T(4,128)(2,1)}, f32[32,128,128]{2,1,0:T(8,128)S(1)}) custom-call(bf16[128,128]{1,0:T(8,128)(2,1)S(1)} %get-tuple-element.35.mix, f32[32,128,128]{2,1,0:T(8,128)S(1)} %get-tuple-element.36.total_in, bf16[520,128]{1,0:T(8,128)(2,1)S(1)} %collective-permute-done.9.refs_0_, ...), custom_call_target="tpu_custom_call", output_to_operand_aliasing={{1}: (1, {})} | custom-call | tf_op jit(solution)/shard_map/collect/pallas_call | solution.py:391
  (7 shorter events, 0.1 us)
Async XLA Ops:
  0.0 4.0 %collective-permute-start = (bf16[4,128,128]{2,1,0:T(8,128)(2,1)}, bf16[4,128,128]{2,1,0:T(8,128)(2,1)S(1)}, u32[]{:S(2)}, u32[]{:S(2)}) collective-permute-start(bf16[4,128,128]{2,1,0:T(8,128)(2,1)} %bitcast.2), channel_id=1, source_target_pairs={{0,1},{1,0},{2,3},{3,2},{4,5},{5,4},{6,7},{7,6},{8,9},{9,8},{10,11... | collective-permute-start | bytes 393224 | tf_op jit(solution)/shard_map/ppermute | solution.py:284
  0.5 10.9 %collective-permute-start.1 = (bf16[4,128,128]{2,1,0:T(8,128)(2,1)}, bf16[4,128,128]{2,1,0:T(8,128)(2,1)S(1)}, u32[]{:S(2)}, u32[]{:S(2)}) collective-permute-start(bf16[4,128,128]{2,1,0:T(8,128)(2,1)} %bitcast.3), channel_id=1, source_target_pairs={{0,16},{4,20},{8,24},{12,28},{16,0},{20,4},{24,8},{28,12},{1,17},{... | collective-permute-start | bytes 393224 | tf_op jit(solution)/shard_map/ppermute | solution.py:284
  6.3 10.7 %collective-permute-start.5 = (bf16[520,128]{1,0:T(8,128)(2,1)S(1)}, bf16[520,128]{1,0:T(8,128)(2,1)S(1)}, u32[]{:S(2)}, u32[]{:S(2)}) collective-permute-start(bf16[520,128]{1,0:T(8,128)(2,1)S(1)} %get-tuple-element.31), channel_id=1, source_target_pairs={{0,12},{4,8},{8,4},{12,0},{16,28},{20,24},{24,20},{28,16},{1,13},{... | collective-permute-start | bytes 399368 | tf_op jit(solution)/shard_map/ppermute | solution.py:284
  8.8 9.4 %collective-permute-start.6 = (bf16[520,128]{1,0:T(8,128)(2,1)S(1)}, bf16[520,128]{1,0:T(8,128)(2,1)S(1)}, u32[]{:S(2)}, u32[]{:S(2)}) collective-permute-start(bf16[520,128]{1,0:T(8,128)(2,1)S(1)} %get-tuple-element.32), channel_id=1, source_target_pairs={{0,8},{4,12},{8,0},{12,4},{16,24},{20,28},{24,16},{28,20},{1,9},{5... | collective-permute-start | bytes 399368 | tf_op jit(solution)/shard_map/ppermute | solution.py:284
  9.3 9.0 %collective-permute-start.7 = (bf16[520,128]{1,0:T(8,128)(2,1)S(1)}, bf16[520,128]{1,0:T(8,128)(2,1)S(1)}, u32[]{:S(2)}, u32[]{:S(2)}) collective-permute-start(bf16[520,128]{1,0:T(8,128)(2,1)S(1)} %get-tuple-element.33), channel_id=1, source_target_pairs={{0,4},{4,0},{8,12},{12,8},{16,20},{20,16},{24,28},{28,24},{1,5},{5... | collective-permute-start | bytes 399368 | tf_op jit(solution)/shard_map/ppermute | solution.py:284
  11.3 5.2 %collective-permute-start.3 = (bf16[4,128,128]{2,1,0:T(8,128)(2,1)S(1)}, bf16[4,128,128]{2,1,0:T(8,128)(2,1)S(1)}, u32[]{:S(2)}, u32[]{:S(2)}) collective-permute-start(bf16[4,128,128]{2,1,0:T(8,128)(2,1)S(1)} %collective-permute-done.1.first), channel_id=1, source_target_pairs={{0,2},{1,3},{2,0},{3,1},{4,6},{5,7},{6,4},{7,5},{8,10},{9,11},{10,... | collective-permute-start | bytes 393224 | tf_op jit(solution)/shard_map/ppermute | solution.py:284
  12.9 8.9 %collective-permute-start.2 = (bf16[136,512]{1,0:T(8,128)(2,1)S(1)}, bf16[136,512]{1,0:T(8,128)(2,1)S(1)}, u32[]{:S(2)}, u32[]{:S(2)}) collective-permute-start(bf16[136,512]{1,0:T(8,128)(2,1)S(1)} %get-tuple-element.25), channel_id=1, source_target_pairs={{0,16},{4,20},{8,24},{12,28},{16,0},{20,4},{24,8},{28,12},{1,17},{... | collective-permute-start | bytes 417800 | tf_op jit(solution)/shard_map/ppermute | solution.py:284
  16.9 5.1 %collective-permute-start.4 = (bf16[8,128,128]{2,1,0:T(8,128)(2,1)S(1)}, bf16[8,128,128]{2,1,0:T(8,128)(2,1)S(1)}, u32[]{:S(2)}, u32[]{:S(2)}) collective-permute-start(bf16[8,128,128]{2,1,0:T(8,128)(2,1)S(1)} %far_pair.1.blocks), channel_id=1, source_target_pairs={{0,1},{1,0},{2,3},{3,2},{4,5},{5,4},{6,7},{7,6},{8,9},{9,8},{10,11... | collective-permute-start | bytes 786440 | tf_op jit(solution)/shard_map/ppermute | solution.py:284
  18.3 8.7 %collective-permute-start.8 = (bf16[1024,128]{1,0:T(8,128)(2,1)S(1)}, bf16[1024,128]{1,0:T(8,128)(2,1)S(1)}, u32[]{:S(2)}, u32[]{:S(2)}) collective-permute-start(bf16[1024,128]{1,0:T(8,128)(2,1)S(1)} %regroup.1), channel_id=1, source_target_pairs={{0,2},{1,3},{2,0},{3,1},{4,6},{5,7},{6,4},{7,5},{8,10},{9,11},{10,... | collective-permute-start | bytes 786440 | tf_op jit(solution)/shard_map/ppermute | solution.py:284
  22.2 7.0 %collective-permute-start.9 = (bf16[520,128]{1,0:T(8,128)(2,1)S(1)}, bf16[520,128]{1,0:T(8,128)(2,1)S(1)}, u32[]{:S(2)}, u32[]{:S(2)}) collective-permute-start(bf16[520,128]{1,0:T(8,128)(2,1)S(1)} %get-tuple-element.37), channel_id=1, source_target_pairs={{0,12},{4,8},{8,4},{12,0},{16,28},{20,24},{24,20},{28,16},{1,13},{... | collective-permute-start | bytes 399368 | tf_op jit(solution)/shard_map/ppermute | solution.py:284
  22.8 7.4 %collective-permute-start.10 = (bf16[520,128]{1,0:T(8,128)(2,1)S(1)}, bf16[520,128]{1,0:T(8,128)(2,1)S(1)}, u32[]{:S(2)}, u32[]{:S(2)}) collective-permute-start(bf16[520,128]{1,0:T(8,128)(2,1)S(1)} %get-tuple-element.38), channel_id=1, source_target_pairs={{0,4},{4,0},{8,12},{12,8},{16,20},{20,16},{24,28},{28,24},{1,5},{5... | collective-permute-start | bytes 399368 | tf_op jit(solution)/shard_map/ppermute | solution.py:284
  24.2 6.2 %collective-permute-start.11 = (bf16[520,128]{1,0:T(8,128)(2,1)S(1)}, bf16[520,128]{1,0:T(8,128)(2,1)S(1)}, u32[]{:S(2)}, u32[]{:S(2)}) collective-permute-start(bf16[520,128]{1,0:T(8,128)(2,1)S(1)} %get-tuple-element.39), channel_id=1, source_target_pairs={{0,8},{4,12},{8,0},{12,4},{16,24},{20,28},{24,16},{28,20},{1,9},{5... | collective-permute-start | bytes 399368 | tf_op jit(solution)/shard_map/ppermute | solution.py:284

commit v26 on v24

--- a/solution.py
+++ b/solution.py
@@ -117,7 +117,7 @@
         row // occ_local % (aux_count // 2) * 2, mine
     )
     wanted = owner * occ_local + row % occ_local
-    far_rows = far.shape[0] - TILE
+    far_rows = far.shape[0]
     row = lax.broadcasted_iota(jnp.int32, (far_rows, 1), 0)
     owner = jnp.bitwise_xor(len(outs) + row // occ_local, me) * aux_count + mine
     far_wanted = owner * occ_local + row % occ_local
@@ -146,8 +146,7 @@
         live = (pairs[k, 2] == 1).astype(jnp.float32)
         block = (block * live).astype(jnp.bfloat16)
         lanes = slice(k * BS, (k + 1) * BS)
-        far[:far_rows, lanes] = (far_coef[:, lanes] * live).astype(jnp.bfloat16)
-        far[far_rows:, lanes] = code
+        far[:, lanes] = (far_coef[:, lanes] * live).astype(jnp.bfloat16)
         for f, out in enumerate(outs):
             for j in range(aux_count // 2):
                 first = f * owned + j * occ_local
@@ -180,10 +179,14 @@
         load.wait()
 
 
-def block_kernel(aux_count, low, coefs, blocks, *refs):
+def tile_kernel(pairs, out):
+    out[...] = code_tile(pairs)
+
+
+def block_kernel(aux_count, low, coefs, blocks, tile, *refs):
     pieces = refs[len(refs) // 2 :] if low else refs
     pairs_dev = blocks.shape[0] // 2
-    rows = coefs.shape[0] - TILE
+    rows = coefs.shape[0]
     occ_local = rows // len(pieces)
     mine = lax.axis_index("aux")
     for k in range(pairs_dev):
@@ -200,7 +203,7 @@
                 ]
     if low == 0:
         for piece in pieces:
-            piece[pairs_dev * aux_count * occ_local :, :] = coefs[rows:, :BS]
+            piece[pairs_dev * aux_count * occ_local :, :] = tile[...]
 
 
 def read_codes(received, pairs_dev, codes):
@@ -321,6 +324,7 @@
         )(first, second)
 
     blocks = integrals.reshape(pairs_dev, BS, BS)
+    far_list = flip(pair_list, "shell", group)
     far_block = flip(blocks, "shell", group)
     operands = (pair_list, occ_slot.reshape(1, -1), coef)
     loaded = [
@@ -331,7 +335,7 @@
     *near, sent_coef = pl.pallas_call(
         functools.partial(near_kernel, occ_local, aux_count),
         out_shape=[piece] * group
-        + [jax.ShapeDtypeStruct((group * occ_local + TILE, pairs_dev * BS), jnp.bfloat16)],
+        + [jax.ShapeDtypeStruct((group * occ_local, pairs_dev * BS), jnp.bfloat16)],
         in_specs=[hbm] * 4 + [vmem],
         out_specs=[vmem] * (group + 1),
         scratch_shapes=loaded
@@ -340,7 +344,14 @@
         name="near_blocks",
     )(*in_hbm(*operands, blocks), flip(blocks, "aux", 1))
     near = [near[0]] + [flip(near[f], "shell", f) for f in range(1, group)]
-    far_block = after(far_block, sent_coef)
+    far_tile = pl.pallas_call(
+        tile_kernel,
+        out_shape=jax.ShapeDtypeStruct((TILE, BS), jnp.bfloat16),
+        in_specs=[pl.BlockSpec(memory_space=pltpu.SMEM)],
+        out_specs=vmem,
+        name="far_tile",
+    )(far_list)
+    far_block = after(far_block, sent_coef, far_tile)
     far_coef = flip(after(sent_coef, far_block), "shell", group)
     far_pair = merged("far_pair", far_block, flip(far_block, "aux", 2))
     far_pairs = [far_pair, flip(far_pair, "aux", 1)]
@@ -363,13 +374,13 @@
         far = pl.pallas_call(
             functools.partial(block_kernel, aux_count, low),
             out_shape=[piece] * group,
-            in_specs=[vmem] * (2 + len(far)),
+            in_specs=[vmem] * (3 + len(far)),
             out_specs=[vmem] * group,
-            input_output_aliases={2 + f: f for f in range(len(far))},
+            input_output_aliases={3 + f: f for f in range(len(far))},
             compiler_params=params,
             cost_estimate=cost(2e9) if low == 0 else None,
             name=f"far_blocks_{low}",
-        )(far_coef, far_pairs[low], *far)
+        )(far_coef, far_pairs[low], far_tile, *far)
     total_shape = jax.ShapeDtypeStruct((block_count, rows, BS), jnp.float32)
     total, mix = pl.pallas_call(
         near_sum_kernel,

time: 32 us -> 37.4 us (1.17)
  starting transfers between devices: 14.4 us -> 19.2 us
  waiting for transfers between devices: 11.5 us -> 9.36 us
  Pallas kernels: 5.87 us -> 7.18 us
  local copies, waits for them, and re-layouts: 0 us -> 1.25 us
    ppermute x12 -> x13, starting transfers between devices: 14.4 us -> 19.2 us  [flip(): return lax.ppermute(value, axis, [(at, at ^ bits) for at in range(count)])]
    ppermute x12 -> x13, waiting for transfers between devices: 11.5 us -> 9.36 us  [flip(): return lax.ppermute(value, axis, [(at, at ^ bits) for at in range(count)])]
    pallas_call x0 -> x1, Pallas kernels: none -> 1.3 us  [exchanged_inputs(): pl.pallas_call(tile_kernel, out_shape=jax.ShapeDtypeStruct((TILE, BS), jn...]
    unnamed x0 -> x4, local copies, waits for them, and re-layouts: none -> 1.25 us
  transfers between devices with their start and end apart: 12 -> 13, of which waited for: 8 -> 6; matrix products, arithmetic and copies ran while one was open for 0% -> 0% of each run, Pallas kernels for 14% -> 15%
where the time goes in v26:
time: 37.4 us; the launch traced here: 37.1 us
  starting transfers between devices  19.2 us (51%)
  waiting for transfers between devices  9.36 us (25%)
  Pallas kernels  7.18 us (19%)
  local copies, waits for them, and re-layouts  1.25 us (3%)
    ppermute x13, starting transfers between devices, flip(): return lax.ppermute(value, axis, [(at, at ^ bits) for at in range(count)])  19.2 us
    ppermute x13, waiting for transfers between devices, flip(): return lax.ppermute(value, axis, [(at, at ^ bits) for at in range(count)])  9.36 us
    pallas_call x1, Pallas kernels, exchanged_inputs(): pl.pallas_call(functools.partial(near_kernel, occ_local, aux_count), out_...  2.2 us
    pallas_call x1, Pallas kernels, exchanged_inputs(): pl.pallas_call(collect_kernel, out_shape=[jax.ShapeDtypeStruct((occ_local...  1.48 us
    pallas_call x1, Pallas kernels, exchanged_inputs(): pl.pallas_call(near_sum_kernel, out_shape=[total_shape, jax.ShapeDtypeStr...  1.41 us
    pallas_call x1, Pallas kernels, exchanged_inputs(): pl.pallas_call(tile_kernel, out_shape=jax.ShapeDtypeStruct((TILE, BS), jn...  1.3 us
    unnamed x4, local copies, waits for them, and re-layouts  1.25 us
  transfers between devices with their start and end apart: 13, of which 6 were waited for; matrix products, arithmetic and copies ran while one was open for 0% of the time, Pallas kernels for 15%

profile of v26, /device:TPU:0, one launch (start us, length us, event | category | flops | bytes accessed | tf_op | source)
XLA Modules:
  0.0 37.1 jit_solution(13294516852203357688)
XLA Ops:
  0.0 0.5 %collective-permute-start = (bf16[4,128,128]{2,1,0:T(8,128)(2,1)}, bf16[4,128,128]{2,1,0:T(8,128)(2,1)S(1)}, u32[]{:S(2)}, u32[]{:S(2)}) collective-permute-start(bf16[4,128,128]{2,1,0:T(8,128)(2,1)} %bitcast.2), channel_id=1, source_target_pairs={{0,1},{1,0},{2,3},{3,2},{4,5},{5,4},{6,7},{7,6},{8,9},{9,8},{10,11... | collective-permute-start | bytes 393224 | tf_op jit(solution)/shard_map/ppermute | solution.py:285
  0.5 3.6 %collective-permute-start.1 = (bf16[4,128,128]{2,1,0:T(8,128)(2,1)}, bf16[4,128,128]{2,1,0:T(8,128)(2,1)S(1)}, u32[]{:S(2)}, u32[]{:S(2)}) collective-permute-start(bf16[4,128,128]{2,1,0:T(8,128)(2,1)} %bitcast.3), channel_id=1, source_target_pairs={{0,16},{4,20},{8,24},{12,28},{16,0},{20,4},{24,8},{28,12},{1,17},{... | collective-permute-start | bytes 393224 | tf_op jit(solution)/shard_map/ppermute | solution.py:285
  4.0 2.2 %near_blocks.1 = (bf16[520,128]{1,0:T(8,128)(2,1)S(1)}, bf16[520,128]{1,0:T(8,128)(2,1)S(1)}, bf16[520,128]{1,0:T(8,128)(2,1)S(1)}, bf16[520,128]{1,0:T(8,128)(2,1)S(1)}, bf16[128,512]{1,0:T(8,128)(2,1)S(1)}) custom-call(s32[4,3]{1,0:T(4,128)} %pairs_in.1, s32[1,128]{1,0:T(1,128)} %bitcast.5, bf16[512,1024]{1,0:T(8,128)(2,1)} %coef_in.1, ...), custom_call_target="tpu_custom_call" | custom-call | tf_op jit(solution)/shard_map/near_blocks/pallas_call | solution.py:335
  6.3 1.6 %collective-permute-start.6 = (bf16[520,128]{1,0:T(8,128)(2,1)S(1)}, bf16[520,128]{1,0:T(8,128)(2,1)S(1)}, u32[]{:S(2)}, u32[]{:S(2)}) collective-permute-start(bf16[520,128]{1,0:T(8,128)(2,1)S(1)} %get-tuple-element.32), channel_id=1, source_target_pairs={{0,4},{4,0},{8,12},{12,8},{16,20},{20,16},{24,28},{28,24},{1,5},{5... | collective-permute-start | bytes 399368 | tf_op jit(solution)/shard_map/ppermute | solution.py:285
  7.8 1.6 %collective-permute-start.7 = (bf16[520,128]{1,0:T(8,128)(2,1)S(1)}, bf16[520,128]{1,0:T(8,128)(2,1)S(1)}, u32[]{:S(2)}, u32[]{:S(2)}) collective-permute-start(bf16[520,128]{1,0:T(8,128)(2,1)S(1)} %get-tuple-element.33), channel_id=1, source_target_pairs={{0,8},{4,12},{8,0},{12,4},{16,24},{20,28},{24,16},{28,20},{1,9},{5... | collective-permute-start | bytes 399368 | tf_op jit(solution)/shard_map/ppermute | solution.py:285
  9.4 0.4 %collective-permute-start.8 = (bf16[520,128]{1,0:T(8,128)(2,1)S(1)}, bf16[520,128]{1,0:T(8,128)(2,1)S(1)}, u32[]{:S(2)}, u32[]{:S(2)}) collective-permute-start(bf16[520,128]{1,0:T(8,128)(2,1)S(1)} %get-tuple-element.34), channel_id=1, source_target_pairs={{0,12},{4,8},{8,4},{12,0},{16,28},{20,24},{24,20},{28,16},{1,13},{... | collective-permute-start | bytes 399368 | tf_op jit(solution)/shard_map/ppermute | solution.py:285
  9.8 1.6 %collective-permute-start.2 = (s32[4,3]{1,0:T(4,128)}, s32[4,3]{1,0:T(4,128)S(1)}, u32[]{:S(2)}, u32[]{:S(2)}) collective-permute-start(s32[4,3]{1,0:T(4,128)} %pairs_in.1), channel_id=1, source_target_pairs={{0,16},{4,20},{8,24},{12,28},{16,0},{20,4},{24,8},{28,12},{1,17},{... | collective-permute-start | bytes 152 | tf_op jit(solution)/shard_map/ppermute | solution.py:285
  11.4 3.8 %collective-permute-done.2.pairs = s32[4,3]{1,0:T(4,128)S(1)} collective-permute-done((s32[4,3]{1,0:T(4,128)}, s32[4,3]{1,0:T(4,128)S(1)}, u32[]{:S(2)}, u32[]{:S(2)}) %collective-permute-start.2) | collective-permute-done | bytes 80 | tf_op jit(solution)/shard_map/ppermute | solution.py:285
  15.2 0.6 %copy-done.1 = s32[4,3]{1,0:T(4,128)} copy-done((s32[4,3]{1,0:T(4,128)}, s32[4,3]{1,0:T(4,128)S(1)}, u32[]{:S(2)}) %copy-start.1) | copy-done | bytes 72
  15.8 1.3 %far_tile.1.tile = bf16[8,128]{1,0:T(8,128)(2,1)} custom-call(s32[4,3]{1,0:T(4,128)} %copy-done.1), custom_call_target="tpu_custom_call" | custom-call | tf_op jit(solution)/shard_map/far_tile/pallas_call | solution.py:347
  17.1 1.5 %collective-permute-start.4 = (bf16[4,128,128]{2,1,0:T(8,128)(2,1)S(1)}, bf16[4,128,128]{2,1,0:T(8,128)(2,1)S(1)}, u32[]{:S(2)}, u32[]{:S(2)}) collective-permute-start(bf16[4,128,128]{2,1,0:T(8,128)(2,1)S(1)} %collective-permute-done.1.first), channel_id=1, source_target_pairs={{0,2},{1,3},{2,0},{3,1},{4,6},{5,7},{6,4},{7,5},{8,10},{9,11},{10,... | collective-permute-start | bytes 393224 | tf_op jit(solution)/shard_map/ppermute | solution.py:285
  18.6 3.4 %collective-permute-start.3 = (bf16[128,512]{1,0:T(8,128)(2,1)S(1)}, bf16[128,512]{1,0:T(8,128)(2,1)S(1)}, u32[]{:S(2)}, u32[]{:S(2)}) collective-permute-start(bf16[128,512]{1,0:T(8,128)(2,1)S(1)} %get-tuple-element.25), channel_id=1, source_target_pairs={{0,16},{4,20},{8,24},{12,28},{16,0},{20,4},{24,8},{28,12},{1,17},{... | collective-permute-start | bytes 393224 | tf_op jit(solution)/shard_map/ppermute | solution.py:285
  22.1 0.3 far_pair.1.blocks
  22.5 1.6 %collective-permute-start.9 = (bf16[1024,128]{1,0:T(8,128)(2,1)S(1)}, bf16[1024,128]{1,0:T(8,128)(2,1)S(1)}, u32[]{:S(2)}, u32[]{:S(2)}) collective-permute-start(bf16[1024,128]{1,0:T(8,128)(2,1)S(1)} %regroup.1), channel_id=1, source_target_pairs={{0,2},{1,3},{2,0},{3,1},{4,6},{5,7},{6,4},{7,5},{8,10},{9,11},{10,... | collective-permute-start | bytes 786440 | tf_op jit(solution)/shard_map/ppermute | solution.py:285
  24.1 3.1 %collective-permute-done.3.coefs = bf16[128,512]{1,0:T(8,128)(2,1)S(1)} collective-permute-done((bf16[128,512]{1,0:T(8,128)(2,1)S(1)}, bf16[128,512]{1,0:T(8,128)(2,1)S(1)}, u32[]{:S(2)}, u32[]{:S(2)}) %collective-permute-start.3) | collective-permute-done | bytes 131104 | tf_op jit(solution)/shard_map/ppermute | solution.py:285
  27.2 0.7 %copy-done = bf16[8,128]{1,0:T(8,128)(2,1)S(1)} copy-done((bf16[8,128]{1,0:T(8,128)(2,1)S(1)}, bf16[8,128]{1,0:T(8,128)(2,1)}, u32[]{:S(2)}) %copy-start) | copy-done | bytes 2072
  28.1 0.2 far_blocks_1.1
  28.4 1.2 %collective-permute-start.11 = (bf16[520,128]{1,0:T(8,128)(2,1)S(1)}, bf16[520,128]{1,0:T(8,128)(2,1)S(1)}, u32[]{:S(2)}, u32[]{:S(2)}) collective-permute-start(bf16[520,128]{1,0:T(8,128)(2,1)S(1)} %get-tuple-element.38), channel_id=1, source_target_pairs={{0,4},{4,0},{8,12},{12,8},{16,20},{20,16},{24,28},{28,24},{1,5},{5... | collective-permute-start | bytes 399368 | tf_op jit(solution)/shard_map/ppermute | solution.py:285
  29.6 2.3 %collective-permute-start.12 = (bf16[520,128]{1,0:T(8,128)(2,1)S(1)}, bf16[520,128]{1,0:T(8,128)(2,1)S(1)}, u32[]{:S(2)}, u32[]{:S(2)}) collective-permute-start(bf16[520,128]{1,0:T(8,128)(2,1)S(1)} %get-tuple-element.39), channel_id=1, source_target_pairs={{0,8},{4,12},{8,0},{12,4},{16,24},{20,28},{24,16},{28,20},{1,9},{5... | collective-permute-start | bytes 399368 | tf_op jit(solution)/shard_map/ppermute | solution.py:285
  31.9 1.4 %near_sum.1 = (f32[32,128,128]{2,1,0:T(8,128)S(1)}, bf16[128,128]{1,0:T(8,128)(2,1)S(1)}) custom-call(bf16[4,4]{1,0:T(4,128)(2,1)} %metric_in.1, bf16[520,128]{1,0:T(8,128)(2,1)S(1)} %get-tuple-element.30.own, bf16[520,128]{1,0:T(8,128)(2,1)S(1)} %get-tuple-element.31.refs_0_, bf16[520,128]{1,0:T(8,128)(2,1)S(1)} %collective-permute-done.6.refs_1_, ...), custom_call_target="tpu_custom_call" | custom-call | flops 3000000000 | bytes 1048576 | tf_op jit(solution)/shard_map/near_sum/pallas_call | solution.py:385
  33.3 1.1 %collective-permute-done.10.refs_0_ = bf16[520,128]{1,0:T(8,128)(2,1)S(1)} collective-permute-done((bf16[520,128]{1,0:T(8,128)(2,1)S(1)}, bf16[520,128]{1,0:T(8,128)(2,1)S(1)}, u32[]{:S(2)}, u32[]{:S(2)}) %collective-permute-start.10) | collective-permute-done | bytes 133152 | tf_op jit(solution)/shard_map/ppermute | solution.py:285
  34.4 0.7 %collective-permute-done.11.refs_1_ = bf16[520,128]{1,0:T(8,128)(2,1)S(1)} collective-permute-done((bf16[520,128]{1,0:T(8,128)(2,1)S(1)}, bf16[520,128]{1,0:T(8,128)(2,1)S(1)}, u32[]{:S(2)}, u32[]{:S(2)}) %collective-permute-start.11) | collective-permute-done | bytes 133152 | tf_op jit(solution)/shard_map/ppermute | solution.py:285
  35.2 0.5 %collective-permute-done.12.refs_2_ = bf16[520,128]{1,0:T(8,128)(2,1)S(1)} collective-permute-done((bf16[520,128]{1,0:T(8,128)(2,1)S(1)}, bf16[520,128]{1,0:T(8,128)(2,1)S(1)}, u32[]{:S(2)}, u32[]{:S(2)}) %collective-permute-start.12) | collective-permute-done | bytes 133152 | tf_op jit(solution)/shard_map/ppermute | solution.py:285
  35.7 1.5 %collect.1 = (bf16[32,4,4096]{2,1,0:T(4,128)(2,1)}, f32[32,128,128]{2,1,0:T(8,128)S(1)}) custom-call(bf16[128,128]{1,0:T(8,128)(2,1)S(1)} %get-tuple-element.35.mix, f32[32,128,128]{2,1,0:T(8,128)S(1)} %get-tuple-element.36.total_in, bf16[520,128]{1,0:T(8,128)(2,1)S(1)} %collective-permute-done.10.refs_0_, ...), custom_call_target="tpu_custom_call", output_to_operand_aliasing={{1}: (1, {})} | custom-call | tf_op jit(solution)/shard_map/collect/pallas_call | solution.py:400
  (14 shorter events, 0.5 us)
Async XLA Ops:
  0.0 4.0 %collective-permute-start = (bf16[4,128,128]{2,1,0:T(8,128)(2,1)}, bf16[4,128,128]{2,1,0:T(8,128)(2,1)S(1)}, u32[]{:S(2)}, u32[]{:S(2)}) collective-permute-start(bf16[4,128,128]{2,1,0:T(8,128)(2,1)} %bitcast.2), channel_id=1, source_target_pairs={{0,1},{1,0},{2,3},{3,2},{4,5},{5,4},{6,7},{7,6},{8,9},{9,8},{10,11... | collective-permute-start | bytes 393224 | tf_op jit(solution)/shard_map/ppermute | solution.py:285
  0.5 16.6 %collective-permute-start.1 = (bf16[4,128,128]{2,1,0:T(8,128)(2,1)}, bf16[4,128,128]{2,1,0:T(8,128)(2,1)S(1)}, u32[]{:S(2)}, u32[]{:S(2)}) collective-permute-start(bf16[4,128,128]{2,1,0:T(8,128)(2,1)} %bitcast.3), channel_id=1, source_target_pairs={{0,16},{4,20},{8,24},{12,28},{16,0},{20,4},{24,8},{28,12},{1,17},{... | collective-permute-start | bytes 393224 | tf_op jit(solution)/shard_map/ppermute | solution.py:285
  6.3 16.2 %collective-permute-start.6 = (bf16[520,128]{1,0:T(8,128)(2,1)S(1)}, bf16[520,128]{1,0:T(8,128)(2,1)S(1)}, u32[]{:S(2)}, u32[]{:S(2)}) collective-permute-start(bf16[520,128]{1,0:T(8,128)(2,1)S(1)} %get-tuple-element.32), channel_id=1, source_target_pairs={{0,4},{4,0},{8,12},{12,8},{16,20},{20,16},{24,28},{28,24},{1,5},{5... | collective-permute-start | bytes 399368 | tf_op jit(solution)/shard_map/ppermute | solution.py:285
  7.8 14.7 %collective-permute-start.7 = (bf16[520,128]{1,0:T(8,128)(2,1)S(1)}, bf16[520,128]{1,0:T(8,128)(2,1)S(1)}, u32[]{:S(2)}, u32[]{:S(2)}) collective-permute-start(bf16[520,128]{1,0:T(8,128)(2,1)S(1)} %get-tuple-element.33), channel_id=1, source_target_pairs={{0,8},{4,12},{8,0},{12,4},{16,24},{20,28},{24,16},{28,20},{1,9},{5... | collective-permute-start | bytes 399368 | tf_op jit(solution)/shard_map/ppermute | solution.py:285
  9.4 13.1 %collective-permute-start.8 = (bf16[520,128]{1,0:T(8,128)(2,1)S(1)}, bf16[520,128]{1,0:T(8,128)(2,1)S(1)}, u32[]{:S(2)}, u32[]{:S(2)}) collective-permute-start(bf16[520,128]{1,0:T(8,128)(2,1)S(1)} %get-tuple-element.34), channel_id=1, source_target_pairs={{0,12},{4,8},{8,4},{12,0},{16,28},{20,24},{24,20},{28,16},{1,13},{... | collective-permute-start | bytes 399368 | tf_op jit(solution)/shard_map/ppermute | solution.py:285
  9.8 5.4 %collective-permute-start.2 = (s32[4,3]{1,0:T(4,128)}, s32[4,3]{1,0:T(4,128)S(1)}, u32[]{:S(2)}, u32[]{:S(2)}) collective-permute-start(s32[4,3]{1,0:T(4,128)} %pairs_in.1), channel_id=1, source_target_pairs={{0,16},{4,20},{8,24},{12,28},{16,0},{20,4},{24,8},{28,12},{1,17},{... | collective-permute-start | bytes 152 | tf_op jit(solution)/shard_map/ppermute | solution.py:285
  15.2 0.6 %copy-start.1 = (s32[4,3]{1,0:T(4,128)}, s32[4,3]{1,0:T(4,128)S(1)}, u32[]{:S(2)}) copy-start(s32[4,3]{1,0:T(4,128)S(1)} %collective-permute-done.2.pairs) | copy-start | bytes 148
  17.1 5.0 %collective-permute-start.4 = (bf16[4,128,128]{2,1,0:T(8,128)(2,1)S(1)}, bf16[4,128,128]{2,1,0:T(8,128)(2,1)S(1)}, u32[]{:S(2)}, u32[]{:S(2)}) collective-permute-start(bf16[4,128,128]{2,1,0:T(8,128)(2,1)S(1)} %collective-permute-done.1.first), channel_id=1, source_target_pairs={{0,2},{1,3},{2,0},{3,1},{4,6},{5,7},{6,4},{7,5},{8,10},{9,11},{10,... | collective-permute-start | bytes 393224 | tf_op jit(solution)/shard_map/ppermute | solution.py:285
  18.6 8.6 %collective-permute-start.3 = (bf16[128,512]{1,0:T(8,128)(2,1)S(1)}, bf16[128,512]{1,0:T(8,128)(2,1)S(1)}, u32[]{:S(2)}, u32[]{:S(2)}) collective-permute-start(bf16[128,512]{1,0:T(8,128)(2,1)S(1)} %get-tuple-element.25), channel_id=1, source_target_pairs={{0,16},{4,20},{8,24},{12,28},{16,0},{20,4},{24,8},{28,12},{1,17},{... | collective-permute-start | bytes 393224 | tf_op jit(solution)/shard_map/ppermute | solution.py:285
  22.4 5.7 %collective-permute-start.5 = (bf16[8,128,128]{2,1,0:T(8,128)(2,1)S(1)}, bf16[8,128,128]{2,1,0:T(8,128)(2,1)S(1)}, u32[]{:S(2)}, u32[]{:S(2)}) collective-permute-start(bf16[8,128,128]{2,1,0:T(8,128)(2,1)S(1)} %far_pair.1.blocks), channel_id=1, source_target_pairs={{0,1},{1,0},{2,3},{3,2},{4,5},{5,4},{6,7},{7,6},{8,9},{9,8},{10,11... | collective-permute-start | bytes 786440 | tf_op jit(solution)/shard_map/ppermute | solution.py:285
  22.5 9.4 %collective-permute-start.9 = (bf16[1024,128]{1,0:T(8,128)(2,1)S(1)}, bf16[1024,128]{1,0:T(8,128)(2,1)S(1)}, u32[]{:S(2)}, u32[]{:S(2)}) collective-permute-start(bf16[1024,128]{1,0:T(8,128)(2,1)S(1)} %regroup.1), channel_id=1, source_target_pairs={{0,2},{1,3},{2,0},{3,1},{4,6},{5,7},{6,4},{7,5},{8,10},{9,11},{10,... | collective-permute-start | bytes 786440 | tf_op jit(solution)/shard_map/ppermute | solution.py:285
  27.2 0.7 %copy-start = (bf16[8,128]{1,0:T(8,128)(2,1)S(1)}, bf16[8,128]{1,0:T(8,128)(2,1)}, u32[]{:S(2)}) copy-start(bf16[8,128]{1,0:T(8,128)(2,1)} %far_tile.1.tile) | copy-start | bytes 6148
  28.4 6.1 %collective-permute-start.10 = (bf16[520,128]{1,0:T(8,128)(2,1)S(1)}, bf16[520,128]{1,0:T(8,128)(2,1)S(1)}, u32[]{:S(2)}, u32[]{:S(2)}) collective-permute-start(bf16[520,128]{1,0:T(8,128)(2,1)S(1)} %get-tuple-element.37), channel_id=1, source_target_pairs={{0,12},{4,8},{8,4},{12,0},{16,28},{20,24},{24,20},{28,16},{1,13},{... | collective-permute-start | bytes 399368 | tf_op jit(solution)/shard_map/ppermute | solution.py:285
  28.4 6.7 %collective-permute-start.11 = (bf16[520,128]{1,0:T(8,128)(2,1)S(1)}, bf16[520,128]{1,0:T(8,128)(2,1)S(1)}, u32[]{:S(2)}, u32[]{:S(2)}) collective-permute-start(bf16[520,128]{1,0:T(8,128)(2,1)S(1)} %get-tuple-element.38), channel_id=1, source_target_pairs={{0,4},{4,0},{8,12},{12,8},{16,20},{20,16},{24,28},{28,24},{1,5},{5... | collective-permute-start | bytes 399368 | tf_op jit(solution)/shard_map/ppermute | solution.py:285
  29.6 6.1 %collective-permute-start.12 = (bf16[520,128]{1,0:T(8,128)(2,1)S(1)}, bf16[520,128]{1,0:T(8,128)(2,1)S(1)}, u32[]{:S(2)}, u32[]{:S(2)}) collective-permute-start(bf16[520,128]{1,0:T(8,128)(2,1)S(1)} %get-tuple-element.39), channel_id=1, source_target_pairs={{0,8},{4,12},{8,0},{12,4},{16,24},{20,28},{24,16},{28,20},{1,9},{5... | collective-permute-start | bytes 399368 | tf_op jit(solution)/shard_map/ppermute | solution.py:285

commit v27 on v24

--- a/solution.py
+++ b/solution.py
@@ -398,7 +398,7 @@
         scratch_shapes=[
             pltpu.VMEM((occ_local, aux_count, block_count * BS), jnp.bfloat16),
             pltpu.VMEM((8, BS), jnp.int32),
-            pltpu.SemaphoreType.DMA((4,)),
+            pltpu.SemaphoreType.DMA((8,)),
         ],
         compiler_params=params,
         name="collect",

time: 32 us -> 32 us (level)
  no operation moved by 1% of the time
where the time goes in v27:
time: 32 us; the launch traced here: 31.9 us
  starting transfers between devices  14.4 us (45%)
  waiting for transfers between devices  11.5 us (36%)
  Pallas kernels  5.86 us (18%)
    ppermute x12, starting transfers between devices, flip(): return lax.ppermute(value, axis, [(at, at ^ bits) for at in range(count)])  14.4 us
    ppermute x12, waiting for transfers between devices, flip(): return lax.ppermute(value, axis, [(at, at ^ bits) for at in range(count)])  11.5 us
    pallas_call x1, Pallas kernels, exchanged_inputs(): pl.pallas_call(functools.partial(near_kernel, occ_local, aux_count), out_...  2.2 us
    pallas_call x1, Pallas kernels, exchanged_inputs(): pl.pallas_call(collect_kernel, out_shape=[jax.ShapeDtypeStruct((occ_local...  1.47 us
    pallas_call x1, Pallas kernels, exchanged_inputs(): pl.pallas_call(near_sum_kernel, out_shape=[total_shape, jax.ShapeDtypeStr...  1.41 us
  transfers between devices with their start and end apart: 12, of which 8 were waited for; matrix products, arithmetic and copies ran while one was open for 0% of the time, Pallas kernels for 14%

profile of v27, /device:TPU:0, one launch (start us, length us, event | category | flops | bytes accessed | tf_op | source)
XLA Modules:
  0.0 31.9 jit_solution(3518033287497981347)
XLA Ops:
  0.0 0.5 %collective-permute-start = (bf16[4,128,128]{2,1,0:T(8,128)(2,1)}, bf16[4,128,128]{2,1,0:T(8,128)(2,1)S(1)}, u32[]{:S(2)}, u32[]{:S(2)}) collective-permute-start(bf16[4,128,128]{2,1,0:T(8,128)(2,1)} %bitcast.2), channel_id=1, source_target_pairs={{0,1},{1,0},{2,3},{3,2},{4,5},{5,4},{6,7},{7,6},{8,9},{9,8},{10,11... | collective-permute-start | bytes 393224 | tf_op jit(solution)/shard_map/ppermute | solution.py:282
  0.5 3.6 %collective-permute-start.1 = (bf16[4,128,128]{2,1,0:T(8,128)(2,1)}, bf16[4,128,128]{2,1,0:T(8,128)(2,1)S(1)}, u32[]{:S(2)}, u32[]{:S(2)}) collective-permute-start(bf16[4,128,128]{2,1,0:T(8,128)(2,1)} %bitcast.3), channel_id=1, source_target_pairs={{0,16},{4,20},{8,24},{12,28},{16,0},{20,4},{24,8},{28,12},{1,17},{... | collective-permute-start | bytes 393224 | tf_op jit(solution)/shard_map/ppermute | solution.py:282
  4.0 2.2 %near_blocks.1 = (bf16[520,128]{1,0:T(8,128)(2,1)S(1)}, bf16[520,128]{1,0:T(8,128)(2,1)S(1)}, bf16[520,128]{1,0:T(8,128)(2,1)S(1)}, bf16[520,128]{1,0:T(8,128)(2,1)S(1)}, bf16[136,512]{1,0:T(8,128)(2,1)S(1)}) custom-call(s32[4,3]{1,0:T(4,128)} %pairs_in.1, s32[1,128]{1,0:T(1,128)} %bitcast.5, bf16[512,1024]{1,0:T(8,128)(2,1)} %coef_in.1, ...), custom_call_target="tpu_custom_call" | custom-call | tf_op jit(solution)/shard_map/near_blocks/pallas_call | solution.py:331
  6.3 1.6 %collective-permute-start.5 = (bf16[520,128]{1,0:T(8,128)(2,1)S(1)}, bf16[520,128]{1,0:T(8,128)(2,1)S(1)}, u32[]{:S(2)}, u32[]{:S(2)}) collective-permute-start(bf16[520,128]{1,0:T(8,128)(2,1)S(1)} %get-tuple-element.32), channel_id=1, source_target_pairs={{0,4},{4,0},{8,12},{12,8},{16,20},{20,16},{24,28},{28,24},{1,5},{5... | collective-permute-start | bytes 399368 | tf_op jit(solution)/shard_map/ppermute | solution.py:282
  7.8 1.6 %collective-permute-start.6 = (bf16[520,128]{1,0:T(8,128)(2,1)S(1)}, bf16[520,128]{1,0:T(8,128)(2,1)S(1)}, u32[]{:S(2)}, u32[]{:S(2)}) collective-permute-start(bf16[520,128]{1,0:T(8,128)(2,1)S(1)} %get-tuple-element.33), channel_id=1, source_target_pairs={{0,8},{4,12},{8,0},{12,4},{16,24},{20,28},{24,16},{28,20},{1,9},{5... | collective-permute-start | bytes 399368 | tf_op jit(solution)/shard_map/ppermute | solution.py:282
  9.4 0.4 %collective-permute-start.7 = (bf16[520,128]{1,0:T(8,128)(2,1)S(1)}, bf16[520,128]{1,0:T(8,128)(2,1)S(1)}, u32[]{:S(2)}, u32[]{:S(2)}) collective-permute-start(bf16[520,128]{1,0:T(8,128)(2,1)S(1)} %get-tuple-element.34), channel_id=1, source_target_pairs={{0,12},{4,8},{8,4},{12,0},{16,28},{20,24},{24,20},{28,16},{1,13},{... | collective-permute-start | bytes 399368 | tf_op jit(solution)/shard_map/ppermute | solution.py:282
  9.8 1.5 %collective-permute-done.1.first = bf16[4,128,128]{2,1,0:T(8,128)(2,1)S(1)} collective-permute-done((bf16[4,128,128]{2,1,0:T(8,128)(2,1)}, bf16[4,128,128]{2,1,0:T(8,128)(2,1)S(1)}, u32[]{:S(2)}, u32[]{:S(2)}) %collective-permute-start.1) | collective-permute-done | bytes 131104 | tf_op jit(solution)/shard_map/ppermute | solution.py:282
  11.3 1.6 %collective-permute-start.3 = (bf16[4,128,128]{2,1,0:T(8,128)(2,1)S(1)}, bf16[4,128,128]{2,1,0:T(8,128)(2,1)S(1)}, u32[]{:S(2)}, u32[]{:S(2)}) collective-permute-start(bf16[4,128,128]{2,1,0:T(8,128)(2,1)S(1)} %collective-permute-done.1.first), channel_id=1, source_target_pairs={{0,2},{1,3},{2,0},{3,1},{4,6},{5,7},{6,4},{7,5},{8,10},{9,11},{10,... | collective-permute-start | bytes 393224 | tf_op jit(solution)/shard_map/ppermute | solution.py:282
  12.9 3.7 %collective-permute-done.3.second = bf16[4,128,128]{2,1,0:T(8,128)(2,1)S(1)} collective-permute-done((bf16[4,128,128]{2,1,0:T(8,128)(2,1)S(1)}, bf16[4,128,128]{2,1,0:T(8,128)(2,1)S(1)}, u32[]{:S(2)}, u32[]{:S(2)}) %collective-permute-start.3) | collective-permute-done | bytes 131104 | tf_op jit(solution)/shard_map/ppermute | solution.py:282
  16.6 0.3 %far_pair.1.blocks = bf16[8,128,128]{2,1,0:T(8,128)(2,1)S(1)} custom-call(bf16[4,128,128]{2,1,0:T(8,128)(2,1)S(1)} %collective-permute-done.1.first, bf16[4,128,128]{2,1,0:T(8,128)(2,1)S(1)} %collective-permute-done.3.second), custom_call_target="tpu_custom_call" | custom-call | tf_op jit(solution)/shard_map/far_pair/pallas_call | solution.py:311
  17.0 2.0 %collective-permute-done.7.refs_3_ = bf16[520,128]{1,0:T(8,128)(2,1)S(1)} collective-permute-done((bf16[520,128]{1,0:T(8,128)(2,1)S(1)}, bf16[520,128]{1,0:T(8,128)(2,1)S(1)}, u32[]{:S(2)}, u32[]{:S(2)}) %collective-permute-start.7) | collective-permute-done | bytes 133152 | tf_op jit(solution)/shard_map/ppermute | solution.py:282
  19.0 1.6 %collective-permute-start.8 = (bf16[1024,128]{1,0:T(8,128)(2,1)S(1)}, bf16[1024,128]{1,0:T(8,128)(2,1)S(1)}, u32[]{:S(2)}, u32[]{:S(2)}) collective-permute-start(bf16[1024,128]{1,0:T(8,128)(2,1)S(1)} %regroup.1), channel_id=1, source_target_pairs={{0,2},{1,3},{2,0},{3,1},{4,6},{5,7},{6,4},{7,5},{8,10},{9,11},{10,... | collective-permute-start | bytes 786440 | tf_op jit(solution)/shard_map/ppermute | solution.py:282
  20.6 1.1 %collective-permute-done.2.coefs = bf16[136,512]{1,0:T(8,128)(2,1)S(1)} collective-permute-done((bf16[136,512]{1,0:T(8,128)(2,1)S(1)}, bf16[136,512]{1,0:T(8,128)(2,1)S(1)}, u32[]{:S(2)}, u32[]{:S(2)}) %collective-permute-start.2) | collective-permute-done | bytes 139296 | tf_op jit(solution)/shard_map/ppermute | solution.py:282
  21.8 0.2 far_blocks_0.1
  22.0 0.2 far_blocks_1.1
  22.2 0.9 %collective-permute-start.9 = (bf16[520,128]{1,0:T(8,128)(2,1)S(1)}, bf16[520,128]{1,0:T(8,128)(2,1)S(1)}, u32[]{:S(2)}, u32[]{:S(2)}) collective-permute-start(bf16[520,128]{1,0:T(8,128)(2,1)S(1)} %get-tuple-element.37), channel_id=1, source_target_pairs={{0,12},{4,8},{8,4},{12,0},{16,28},{20,24},{24,20},{28,16},{1,13},{... | collective-permute-start | bytes 399368 | tf_op jit(solution)/shard_map/ppermute | solution.py:282
  23.1 1.1 %collective-permute-start.10 = (bf16[520,128]{1,0:T(8,128)(2,1)S(1)}, bf16[520,128]{1,0:T(8,128)(2,1)S(1)}, u32[]{:S(2)}, u32[]{:S(2)}) collective-permute-start(bf16[520,128]{1,0:T(8,128)(2,1)S(1)} %get-tuple-element.38), channel_id=1, source_target_pairs={{0,4},{4,0},{8,12},{12,8},{16,20},{20,16},{24,28},{28,24},{1,5},{5... | collective-permute-start | bytes 399368 | tf_op jit(solution)/shard_map/ppermute | solution.py:282
  24.1 1.6 %collective-permute-start.11 = (bf16[520,128]{1,0:T(8,128)(2,1)S(1)}, bf16[520,128]{1,0:T(8,128)(2,1)S(1)}, u32[]{:S(2)}, u32[]{:S(2)}) collective-permute-start(bf16[520,128]{1,0:T(8,128)(2,1)S(1)} %get-tuple-element.39), channel_id=1, source_target_pairs={{0,8},{4,12},{8,0},{12,4},{16,24},{20,28},{24,16},{28,20},{1,9},{5... | collective-permute-start | bytes 399368 | tf_op jit(solution)/shard_map/ppermute | solution.py:282
  25.8 1.3 %collective-permute-done.8.refs_4_ = bf16[1024,128]{1,0:T(8,128)(2,1)S(1)} collective-permute-done((bf16[1024,128]{1,0:T(8,128)(2,1)S(1)}, bf16[1024,128]{1,0:T(8,128)(2,1)S(1)}, u32[]{:S(2)}, u32[]{:S(2)}) %collective-permute-start.8) | collective-permute-done | bytes 262176 | tf_op jit(solution)/shard_map/ppermute | solution.py:282
  27.1 1.4 %near_sum.1 = (f32[32,128,128]{2,1,0:T(8,128)S(1)}, bf16[128,128]{1,0:T(8,128)(2,1)S(1)}) custom-call(bf16[4,4]{1,0:T(4,128)(2,1)} %metric_in.1, bf16[520,128]{1,0:T(8,128)(2,1)S(1)} %get-tuple-element.30.own, bf16[520,128]{1,0:T(8,128)(2,1)S(1)} %get-tuple-element.31.refs_0_, bf16[520,128]{1,0:T(8,128)(2,1)S(1)} %collective-permute-done.5.refs_1_, ...), custom_call_target="tpu_custom_call" | custom-call | flops 3000000000 | bytes 1048576 | tf_op jit(solution)/shard_map/near_sum/pallas_call | solution.py:374
  28.5 1.0 %collective-permute-done.9.refs_0_ = bf16[520,128]{1,0:T(8,128)(2,1)S(1)} collective-permute-done((bf16[520,128]{1,0:T(8,128)(2,1)S(1)}, bf16[520,128]{1,0:T(8,128)(2,1)S(1)}, u32[]{:S(2)}, u32[]{:S(2)}) %collective-permute-start.9) | collective-permute-done | bytes 133152 | tf_op jit(solution)/shard_map/ppermute | solution.py:282
  29.6 0.7 %collective-permute-done.10.refs_1_ = bf16[520,128]{1,0:T(8,128)(2,1)S(1)} collective-permute-done((bf16[520,128]{1,0:T(8,128)(2,1)S(1)}, bf16[520,128]{1,0:T(8,128)(2,1)S(1)}, u32[]{:S(2)}, u32[]{:S(2)}) %collective-permute-start.10) | collective-permute-done | bytes 133152 | tf_op jit(solution)/shard_map/ppermute | solution.py:282
  30.2 0.2 collective-permute-done.11.refs_2_
  30.4 1.5 %collect.1 = (bf16[32,4,4096]{2,1,0:T(4,128)(2,1)}, f32[32,128,128]{2,1,0:T(8,128)S(1)}) custom-call(bf16[128,128]{1,0:T(8,128)(2,1)S(1)} %get-tuple-element.35.mix, f32[32,128,128]{2,1,0:T(8,128)S(1)} %get-tuple-element.36.total_in, bf16[520,128]{1,0:T(8,128)(2,1)S(1)} %collective-permute-done.9.refs_0_, ...), custom_call_target="tpu_custom_call", output_to_operand_aliasing={{1}: (1, {})} | custom-call | tf_op jit(solution)/shard_map/collect/pallas_call | solution.py:389
  (7 shorter events, 0.1 us)
Async XLA Ops:
  0.0 4.0 %collective-permute-start = (bf16[4,128,128]{2,1,0:T(8,128)(2,1)}, bf16[4,128,128]{2,1,0:T(8,128)(2,1)S(1)}, u32[]{:S(2)}, u32[]{:S(2)}) collective-permute-start(bf16[4,128,128]{2,1,0:T(8,128)(2,1)} %bitcast.2), channel_id=1, source_target_pairs={{0,1},{1,0},{2,3},{3,2},{4,5},{5,4},{6,7},{7,6},{8,9},{9,8},{10,11... | collective-permute-start | bytes 393224 | tf_op jit(solution)/shard_map/ppermute | solution.py:282
  0.5 10.9 %collective-permute-start.1 = (bf16[4,128,128]{2,1,0:T(8,128)(2,1)}, bf16[4,128,128]{2,1,0:T(8,128)(2,1)S(1)}, u32[]{:S(2)}, u32[]{:S(2)}) collective-permute-start(bf16[4,128,128]{2,1,0:T(8,128)(2,1)} %bitcast.3), channel_id=1, source_target_pairs={{0,16},{4,20},{8,24},{12,28},{16,0},{20,4},{24,8},{28,12},{1,17},{... | collective-permute-start | bytes 393224 | tf_op jit(solution)/shard_map/ppermute | solution.py:282
  6.3 10.7 %collective-permute-start.5 = (bf16[520,128]{1,0:T(8,128)(2,1)S(1)}, bf16[520,128]{1,0:T(8,128)(2,1)S(1)}, u32[]{:S(2)}, u32[]{:S(2)}) collective-permute-start(bf16[520,128]{1,0:T(8,128)(2,1)S(1)} %get-tuple-element.32), channel_id=1, source_target_pairs={{0,4},{4,0},{8,12},{12,8},{16,20},{20,16},{24,28},{28,24},{1,5},{5... | collective-permute-start | bytes 399368 | tf_op jit(solution)/shard_map/ppermute | solution.py:282
  7.8 9.2 %collective-permute-start.6 = (bf16[520,128]{1,0:T(8,128)(2,1)S(1)}, bf16[520,128]{1,0:T(8,128)(2,1)S(1)}, u32[]{:S(2)}, u32[]{:S(2)}) collective-permute-start(bf16[520,128]{1,0:T(8,128)(2,1)S(1)} %get-tuple-element.33), channel_id=1, source_target_pairs={{0,8},{4,12},{8,0},{12,4},{16,24},{20,28},{24,16},{28,20},{1,9},{5... | collective-permute-start | bytes 399368 | tf_op jit(solution)/shard_map/ppermute | solution.py:282
  9.4 9.6 %collective-permute-start.7 = (bf16[520,128]{1,0:T(8,128)(2,1)S(1)}, bf16[520,128]{1,0:T(8,128)(2,1)S(1)}, u32[]{:S(2)}, u32[]{:S(2)}) collective-permute-start(bf16[520,128]{1,0:T(8,128)(2,1)S(1)} %get-tuple-element.34), channel_id=1, source_target_pairs={{0,12},{4,8},{8,4},{12,0},{16,28},{20,24},{24,20},{28,16},{1,13},{... | collective-permute-start | bytes 399368 | tf_op jit(solution)/shard_map/ppermute | solution.py:282
  11.3 5.2 %collective-permute-start.3 = (bf16[4,128,128]{2,1,0:T(8,128)(2,1)S(1)}, bf16[4,128,128]{2,1,0:T(8,128)(2,1)S(1)}, u32[]{:S(2)}, u32[]{:S(2)}) collective-permute-start(bf16[4,128,128]{2,1,0:T(8,128)(2,1)S(1)} %collective-permute-done.1.first), channel_id=1, source_target_pairs={{0,2},{1,3},{2,0},{3,1},{4,6},{5,7},{6,4},{7,5},{8,10},{9,11},{10,... | collective-permute-start | bytes 393224 | tf_op jit(solution)/shard_map/ppermute | solution.py:282
  12.9 8.9 %collective-permute-start.2 = (bf16[136,512]{1,0:T(8,128)(2,1)S(1)}, bf16[136,512]{1,0:T(8,128)(2,1)S(1)}, u32[]{:S(2)}, u32[]{:S(2)}) collective-permute-start(bf16[136,512]{1,0:T(8,128)(2,1)S(1)} %get-tuple-element.25), channel_id=1, source_target_pairs={{0,16},{4,20},{8,24},{12,28},{16,0},{20,4},{24,8},{28,12},{1,17},{... | collective-permute-start | bytes 417800 | tf_op jit(solution)/shard_map/ppermute | solution.py:282
  16.9 5.1 %collective-permute-start.4 = (bf16[8,128,128]{2,1,0:T(8,128)(2,1)S(1)}, bf16[8,128,128]{2,1,0:T(8,128)(2,1)S(1)}, u32[]{:S(2)}, u32[]{:S(2)}) collective-permute-start(bf16[8,128,128]{2,1,0:T(8,128)(2,1)S(1)} %far_pair.1.blocks), channel_id=1, source_target_pairs={{0,1},{1,0},{2,3},{3,2},{4,5},{5,4},{6,7},{7,6},{8,9},{9,8},{10,11... | collective-permute-start | bytes 786440 | tf_op jit(solution)/shard_map/ppermute | solution.py:282
  19.0 8.1 %collective-permute-start.8 = (bf16[1024,128]{1,0:T(8,128)(2,1)S(1)}, bf16[1024,128]{1,0:T(8,128)(2,1)S(1)}, u32[]{:S(2)}, u32[]{:S(2)}) collective-permute-start(bf16[1024,128]{1,0:T(8,128)(2,1)S(1)} %regroup.1), channel_id=1, source_target_pairs={{0,2},{1,3},{2,0},{3,1},{4,6},{5,7},{6,4},{7,5},{8,10},{9,11},{10,... | collective-permute-start | bytes 786440 | tf_op jit(solution)/shard_map/ppermute | solution.py:282
  22.2 7.3 %collective-permute-start.9 = (bf16[520,128]{1,0:T(8,128)(2,1)S(1)}, bf16[520,128]{1,0:T(8,128)(2,1)S(1)}, u32[]{:S(2)}, u32[]{:S(2)}) collective-permute-start(bf16[520,128]{1,0:T(8,128)(2,1)S(1)} %get-tuple-element.37), channel_id=1, source_target_pairs={{0,12},{4,8},{8,4},{12,0},{16,28},{20,24},{24,20},{28,16},{1,13},{... | collective-permute-start | bytes 399368 | tf_op jit(solution)/shard_map/ppermute | solution.py:282
  23.1 7.1 %collective-permute-start.10 = (bf16[520,128]{1,0:T(8,128)(2,1)S(1)}, bf16[520,128]{1,0:T(8,128)(2,1)S(1)}, u32[]{:S(2)}, u32[]{:S(2)}) collective-permute-start(bf16[520,128]{1,0:T(8,128)(2,1)S(1)} %get-tuple-element.38), channel_id=1, source_target_pairs={{0,4},{4,0},{8,12},{12,8},{16,20},{20,16},{24,28},{28,24},{1,5},{5... | collective-permute-start | bytes 399368 | tf_op jit(solution)/shard_map/ppermute | solution.py:282
  24.1 6.3 %collective-permute-start.11 = (bf16[520,128]{1,0:T(8,128)(2,1)S(1)}, bf16[520,128]{1,0:T(8,128)(2,1)S(1)}, u32[]{:S(2)}, u32[]{:S(2)}) collective-permute-start(bf16[520,128]{1,0:T(8,128)(2,1)S(1)} %get-tuple-element.39), channel_id=1, source_target_pairs={{0,8},{4,12},{8,0},{12,4},{16,24},{20,28},{24,16},{28,20},{1,9},{5... | collective-permute-start | bytes 399368 | tf_op jit(solution)/shard_map/ppermute | solution.py:282
